TPU v7x, 32 devices: a whole 2x2x4 slice. The times are simulated.
32 devices in a mesh: parts: 2 (over y), term: 4 (over z), env: 2 (over x), blk: 2 (over core).
Axes of the slice: x: 2, y: 2, z: 4, core: 2. Of those that a mesh axis runs over, the one named last changes fastest.
Arguments:
- psi: bfloat16 [16, 256, 256], P(('parts', 'blk')), parts along dimension 0, may hold values from -6 to 6
- left_env: bfloat16 [64, 8, 256, 256], P(('parts', 'term'), 'blk', 'env'), parts along dimension 0, may hold values from -0.0625 to 0.0625
- right_env: bfloat16 [64, 8, 256, 256], P(('parts', 'term'), 'blk', 'env'), parts along dimension 0, may hold values from -0.375 to 0.375
- pairing: int32 [64, 8], P(('parts', 'term'), 'blk'), parts along dimension 0, may hold values from 0 to 7
- sector_dims: int32 [16], P('parts'), parts along dimension 0, may hold values from 1 to 256, 1536 in all
- precond: float32 [16, 256, 256], P(('parts', 'blk')), parts along dimension 0, may hold values from 0.3 to 3
Outputs:
- sigmas: float32 [3, 16, 256, 256], P(None, ('parts', 'blk'), 'term'), parts along dimension 1
- subspace: float32 [6, 3], P('parts'), parts along dimension 0
There are 2 independent parts, one for each index of `parts`. A program takes and returns all parts, laid end to end along the dimension named above; each array names one. Nothing has to cross between parts.
All inputs are finite; a program needn't handle non-finite values.
Results may differ from a plain program's by a relative error of at most 0.0057.
Values may be sent and summed in bfloat16 or wider, within the bound.
No kernel may reach another device: no remote copies, remote signals or barrier semaphores. Data moves between devices by JAX's collectives and lax.ppermute only.
A program may use at most 64 MiB of HBM per device.

v0:
```python
import jax
import jax.numpy as jnp
from jax import lax
from jax.sharding import PartitionSpec as P

ITERS = 3


eps = 1e-06


def on_device(psi, left_env, right_env, pairing, sector_dims, precond):
    sec_local, states, width = psi.shape
    n_env = lax.axis_size("env")
    n_term = lax.axis_size("term")
    n_blk = lax.axis_size("blk")
    count = sec_local * n_blk * states * width
    env_rows = states // n_env
    term_rows = states // n_term
    env_pos = lax.axis_index("env")
    term_pos = lax.axis_index("term")
    blk_pos = lax.axis_index("blk")
    sector_ids = blk_pos * sec_local + jnp.arange(sec_local, dtype=jnp.int32)
    all_ids = jnp.arange(sec_local * n_blk, dtype=jnp.int32)
    live = jnp.sum(
        jnp.where(all_ids[None, :] == sector_ids[:, None], sector_dims[None, :], 0), axis=1
    )
    row_ids = jnp.arange(states, dtype=jnp.int32)
    mask = (
        (row_ids[None, :, None] < live[:, None, None])
        & (row_ids[None, None, :] < live[:, None, None])
    ).astype(jnp.float32)
    right_full = lax.all_gather(right_env, "env", axis=2, tiled=True)
    start = psi.astype(jnp.float32) * mask
    start_total = lax.psum(jnp.sum(start * start), "blk")
    first = start * lax.rsqrt(start_total / count + eps)
    first_rows = lax.dynamic_slice_in_dim(first, env_pos * env_rows, env_rows, 1).astype(
        jnp.bfloat16
    )

    def reduce_means(values):
        return lax.psum(values, "blk") / count

    basis = [first]
    sigma_list = []
    rows_bf = first_rows
    for step in range(ITERS):
        every = lax.all_gather(rows_bf, "blk", axis=0, tiled=True)
        chosen = every[pairing]
        inner = jnp.einsum(
            "tkcj,tkbj->tkcb", chosen, right_full, preferred_element_type=jnp.float32
        ).astype(jnp.bfloat16)
        sigma = (
            lax.psum(
                jnp.einsum("tkca,tkcb->kab", left_env, inner, preferred_element_type=jnp.float32),
                ("term", "env"),
            )
            * mask
        )
        sigma_list.append(sigma)
        if step + 1 < ITERS:
            proj = reduce_means(jnp.stack([jnp.sum(other * sigma) for other in basis]))
            resid = sigma
            for index in range(len(basis)):
                resid = resid - proj[index] * basis[index]
            trial = resid * precond
            back = reduce_means(jnp.stack([jnp.sum(other * trial) for other in basis]))
            for index in range(len(basis)):
                trial = trial - back[index] * basis[index]
            square = reduce_means(jnp.sum(trial * trial)[None])
            vec = trial * lax.rsqrt(square[0] + eps)
            basis.append(vec)
            rows_bf = lax.dynamic_slice_in_dim(vec, env_pos * env_rows, env_rows, 1).astype(
                jnp.bfloat16
            )
    flat = [jnp.sum(basis[j] * sigma_list[i]) for i in range(ITERS) for j in range(ITERS)]
    subspace = reduce_means(jnp.stack(flat)).reshape(ITERS, ITERS)
    sigma_list, subspace = (sigma_list, subspace)
    stacked = jnp.stack(sigma_list)
    return (lax.dynamic_slice_in_dim(stacked, term_pos * term_rows, term_rows, 2), subspace)


def solution(mesh):
    placed = (
        P(("parts", "blk"), None, None),
        P(("parts", "term"), "blk", "env", None),
        P(("parts", "term"), "blk", "env", None),
        P(("parts", "term"), "blk"),
        P("parts"),
        P(("parts", "blk"), None, None),
    )
    return jax.shard_map(
        on_device,
        mesh=mesh,
        in_specs=placed,
        out_specs=(P(None, ("parts", "blk"), "term", None), P("parts", None)),
        check_vma=False,
    )
```

profile of v0, /device:TPU:1, one launch (start us, length us, event | category | flops | bytes accessed | tf_op | source)
XLA Modules:
  0.0 407.4 jit_solution(11767998865989722233)
XLA Ops:
  7.2 3.3 copy.45
  10.6 1.0 copy-done.3
  11.5 0.2 copy.42
  11.8 0.2 select_reduce_fusion
  12.0 1.0 multiply_reduce_fusion.14
  13.0 3.1 psum.77
  17.0 0.3 fusion.50
  17.3 0.1 copy.43
  17.5 2.2 all_gather.12
  19.7 2.0 gather_fusion
  21.7 47.8 %all-gather.2.cloned.1.call-done = bf16[8,4,256,256]{3,2,0,1:T(8,128)(2,1)} async-done(((bf16[8,4,128,256]{3,2,0,1:T(8,128)(2,1)}), bf16[8,4,256,256]{3,2,0,1:T(8,128)(2,1)}) %all-gather.2.cloned.1.call-update) | async-done | bytes 4194320 | tf_op jit(solution)/shard_map/all_gather | solution.py:33
  69.5 5.9 %fusion.29 = f32[4,256,256]{1,2,0:T(8,128)} fusion(bf16[8,4,128,256]{3,2,1,0:T(8,128)(2,1)S(1)} %copy-done, bf16[8,4,256,256]{3,2,0,1:T(8,128)(2,1)} %all-gather.2.cloned.1.call-done, bf16[8,4,128,256]{3,2,1,0:T(8,128)(2,1)} %bitcast.49), kind=kOutput, calls=%fused_computation.27 | convolution fusion | flops 1074790400 | bytes 9437184 | tf_op jit(solution)/shard_map/tkca,tkcb->kab/dot_general | solution.py:55
  75.5 2.5 copy.49
  78.1 74.9 %all-reduce.4.cloned.1.call-done = f32[4,256,256]{1,2,0:T(8,128)} async-done(((f32[4,256,256]{1,2,0:T(8,128)}), f32[4,256,256]{1,2,0:T(8,128)}) %all-reduce.4.cloned.1.call-update) | async-done | bytes 1048592 | tf_op jit(solution)/shard_map/psum | solution.py:54
  153.0 2.3 multiply_reduce_fusion.13
  155.3 4.1 %psum.79 = f32[1]{0:T(128)} all-reduce(f32[1]{0:T(128)} %bitcast.5), channel_id=1, replica_groups=mesh['parts'=2,'term'=4,'env'=2,'blk'=2] {'blk'}, use_global_device_ids=true, to_apply=%region_5.6 | all-reduce | flops 1 | bytes 8 | tf_op jit(solution)/shard_map/psum | solution.py:42
  160.0 2.7 multiply_reduce_fusion.12
  162.7 3.1 psum.80
  166.5 2.8 multiply_reduce_fusion.11
  169.2 3.2 psum.81
  173.1 2.0 broadcast_multiply_fusion.1
  175.2 1.0 copy-done.1
  176.3 2.2 all_gather.14
  178.5 2.0 gather_fusion.1
  180.5 5.9 %fusion.36 = f32[4,256,256]{1,2,0:T(8,128)} fusion(bf16[8,4,128,256]{3,2,1,0:T(8,128)(2,1)S(1)} %copy-done, bf16[8,4,256,256]{3,2,0,1:T(8,128)(2,1)} %all-gather.2.cloned.1.call-done, bf16[8,4,128,256]{3,2,1,0:T(8,128)(2,1)} %bitcast.51), kind=kOutput, calls=%fused_computation.28 | convolution fusion | flops 1074790400 | bytes 9437184 | tf_op jit(solution)/shard_map/tkca,tkcb->kab/dot_general | solution.py:55
  186.5 76.7 %all-reduce.6.cloned.1.call-done = f32[4,256,256]{1,2,0:T(8,128)} async-done(((f32[4,256,256]{1,2,0:T(8,128)}), f32[4,256,256]{1,2,0:T(8,128)}) %all-reduce.6.cloned.1.call-update) | async-done | bytes 1048592 | tf_op jit(solution)/shard_map/psum | solution.py:54
  263.1 2.7 multiply_reduce_fusion.10
  265.8 1.3 pad_maximum_fusion
  267.1 3.5 psum.83
  270.6 0.6 fusion.55
  271.2 5.3 %multiply_reduce_fusion.8 = (f32[]{:T(128)}, f32[]{:T(128)}, f32[4,256,256]{1,2,0:T(8,128)}) fusion(bf16[4,256,256]{1,2,0:T(8,128)(2,1)S(1)} %copy.42, f32[]{:T(128)S(6)} %rsqrt.15, pred[4,256]{1,0:T(4,128)(4,1)S(1)} %iota_compare_fusion, f32[4,256,256]{1,2,0:T(8,128)} %copy-done.1, f32[4,256,256]{1,2,0:T(8,128)} %copy.49, f32[]{:T(128)} %bitcast.19, ...), kind=kLoop, calls=%fused_computation.39 | loop fusion | flops 3670014 | bytes 4719636 | tf_op jit(solution)/shard_map/reduce_sum | solution.py:67
  276.4 1.4 pad_maximum_fusion.1
  277.8 2.5 psum.84
  280.2 0.6 fusion.54
  280.8 4.0 multiply_reduce_fusion.6
  284.8 3.1 psum.85
  288.6 3.2 broadcast_multiply_fusion
  291.7 1.0 copy-done.2
  292.9 2.4 all_gather.15
  295.3 2.0 gather_fusion.2
  297.3 5.9 %fusion.43 = f32[4,256,256]{1,2,0:T(8,128)} fusion(bf16[8,4,128,256]{3,2,1,0:T(8,128)(2,1)S(1)} %copy-done, bf16[8,4,256,256]{3,2,0,1:T(8,128)(2,1)} %all-gather.2.cloned.1.call-done, bf16[8,4,128,256]{3,2,1,0:T(8,128)(2,1)} %bitcast.50), kind=kOutput, calls=%fused_computation.29 | convolution fusion | flops 1074790400 | bytes 9437184 | tf_op jit(solution)/shard_map/tkca,tkcb->kab/dot_general | solution.py:55
  303.1 76.7 %all-reduce.8.cloned.1.call-done = f32[4,256,256]{1,2,0:T(8,128)} async-done(((f32[4,256,256]{1,2,0:T(8,128)}), f32[4,256,256]{1,2,0:T(8,128)}) %all-reduce.8.cloned.1.call-update) | async-done | bytes 1048592 | tf_op jit(solution)/shard_map/psum | solution.py:54
  379.8 5.5 %multiply_reduce_fusion = (f32[]{:T(128)}, f32[]{:T(128)}, f32[]{:T(128)}, f32[]{:T(128)}, f32[]{:T(128)}, /*index=5*/f32[]{:T(128)}, f32[1,4,256,256]{2,3,1,0:T...) fusion(f32[4,256,256]{1,2,0:T(8,128)} %copy-done.2, f32[4,256,256]{1,2,0:T(8,128)} %all-reduce.8.cloned.1.call-done, ...), kind=kLoop, calls=%fused_computation.30 | loop fusion | flops 4980730 | bytes 8913948 | tf_op jit(solution)/shard_map/reduce_sum | solution.py:76
  385.3 5.7 %stack.78 = f32[9]{0:T(128)S(1)} concatenate(f32[1]{0:T(128)} %bitcast.5, f32[1]{0:T(128)} %bitcast.31, f32[1]{0:T(128)} %bitcast.32, f32[1]{0:T(128)} %bitcast.16, f32[1]{0:T(128)} %bitcast.17, f32[1]{0:T(128)} %bitcast.33, f32[1]{0:T(128)} %bitcast.34, f32[1]{0:T(128)} %bitcast.35, f32[1]{0:T(128)} %bitcast.36), dimensions={0} | concatenate | bytes 72 | tf_op jit(solution)/shard_map/stack | solution.py:77
  391.1 3.5 psum.87
  394.5 3.0 fusion.28
  397.5 2.7 copy.59
  400.3 0.7 reshape.63
  (31 shorter events, 0.9 us)
Async XLA Ops:
  7.2 62.4 %copy-start = (bf16[8,4,128,256]{3,2,1,0:T(8,128)(2,1)S(1)}, bf16[8,4,128,256]{3,2,1,0:T(8,128)(2,1)}, u32[]{:S(2)}) copy-start(bf16[8,4,128,256]{3,2,1,0:T(8,128)(2,1)} %param.7) | copy-start | bytes 6291460
  7.2 62.3 %all-gather.2.cloned.1.call-start = ((), (), s32[]{:S(2)}) async-start(), calls=%async_computation | async-start | bytes 6291456 | tf_op jit(solution)/shard_map/all_gather | solution.py:33
  10.5 1.0 copy-start.3
  10.5 1.3 copy-start.5
  10.5 5.6 %copy-start.4 = (s32[8,4]{0,1:T(4,128)S(1)}, s32[8,4]{0,1:T(4,128)}, u32[]{:S(2)}) copy-start(s32[8,4]{0,1:T(4,128)} %param.9) | copy-start | bytes 388
  10.5 142.4 %all-reduce.4.cloned.1.call-start = ((), (), s32[]{:S(2)}) async-start(), calls=%async_computation.1 | async-start | bytes 2097152 | tf_op jit(solution)/shard_map/psum | solution.py:54
  75.5 187.6 %all-reduce.6.cloned.1.call-start = ((), (), s32[]{:S(2)}) async-start(), calls=%async_computation.2 | async-start | bytes 2097152 | tf_op jit(solution)/shard_map/psum | solution.py:54
  175.2 1.0 copy-start.1
  186.4 193.4 %all-reduce.8.cloned.1.call-start = ((), (), s32[]{:S(2)}) async-start(), calls=%async_computation.3 | async-start | bytes 2097152 | tf_op jit(solution)/shard_map/psum | solution.py:54
  291.7 1.0 copy-start.2
Sparse Core Ops, SparseCore 0:
  10.7 58.8 all-gather.1
  75.6 77.2 all-reduce.3
  186.5 76.5 all-reduce.5
  303.3 76.5 all-reduce.7
where the time goes:
time: 409 us; the launch traced here: 407 us
  waiting for transfers between devices  276 us (67%)
  other arithmetic  37.6 us (9%)
  blocking collectives  32.7 us (8%)
  local copies, waits for them, and re-layouts  26 us (6%)
  matrix products  17.7 us (4%)
  between operations  17.3 us (4%)
    psum x3, waiting for transfers between devices, on_device(): lax.psum(jnp.einsum('tkca,tkcb->kab', left_env, inner, preferred_element_...  228 us
    all_gather x1, waiting for transfers between devices, on_device(): right_full = lax.all_gather(right_env, 'env', axis=2, tiled=True)  47.8 us
    psum x7, blocking collectives, reduce_means(): return lax.psum(values, 'blk') / count  22.9 us
    dot_general x3, matrix products, on_device(): jnp.einsum('tkca,tkcb->kab', left_env, inner, preferred_element_type=jnp....  17.7 us
    unnamed x16, local copies, waits for them, and re-layouts  11.7 us
  transfers between devices with their start and end apart: 4, of which 4 were waited for; matrix products, arithmetic and copies ran while one was open for 2% of the time, Pallas kernels for 0%

commit v1 on v0

v1 whole, which is shorter than its diff:
```python
import functools

import jax
import jax.numpy as jnp
from jax import lax
from jax.experimental import pallas as pl
from jax.experimental.pallas import tpu as pltpu
from jax.sharding import PartitionSpec as P

ITERS = 3
EPS = 1e-06
F32, BF16 = jnp.float32, jnp.bfloat16
ROWS = 32
VMEM_LIMIT = 40 * 1024 * 1024


def _specs(*shapes):
    return [pl.BlockSpec(memory_space=s) for s in shapes]


ANY, VM, SM = pl.ANY, pltpu.VMEM, pltpu.SMEM


def _fold(x):
    return jnp.sum(x.reshape(x.shape[0] // 8, 8, x.shape[1]), axis=0)


def _over(n_sec, states, width, n_acc, body):
    blocks = states // ROWS

    def step(i, accs):
        sec, rows = i // blocks, pl.ds(pl.multiple_of((i % blocks) * ROWS, ROWS), ROWS)
        return tuple(a + b for a, b in zip(accs, body(sec, rows)))

    zero = tuple(jnp.zeros((8, width), F32) for _ in range(n_acc))
    return tuple(jnp.sum(a) for a in lax.fori_loop(0, n_sec * blocks, step, zero, unroll=2))


def _write_vb(vb, sec, rows, value, env_pos, swap):
    half = value.shape[1] // 2
    low = value.astype(BF16)
    if swap:
        turned = jnp.concatenate([value[:, half:], value[:, :half]], axis=1).astype(BF16)
        low = jnp.where(env_pos == 0, low, turned)
    vb[sec, rows, :] = low


def _put_scalars(ref, values):
    shape = ref.shape
    row = lax.broadcasted_iota(jnp.int32, shape, 0)
    out = jnp.zeros(shape, F32)
    for index, value in enumerate(values):
        out = jnp.where(row == index, value, out)
    ref[...] = out


def _emit(cfg, meta, acc, outs):
    if cfg["direct"]:
        n, part = cfg["n_term"], cfg["part"]
        z = meta[1]
        for s in range(n):
            rows = pl.ds(pl.multiple_of((z ^ s) * part, part), part)
            for k in range(cfg["sec"]):
                outs[s][k] = acc[k, rows, :].astype(outs[s].dtype)
    else:
        outs[0][...] = acc[...]


def _first_kernel(cfg, meta, psi, psi_o, pre, pre_o, right, v0, pret, inner, vb, work):
    sec, states, width = psi.shape
    n_sec = sec * cfg["n_blk"]
    blk, env_pos = meta[2], meta[0]
    base = blk * sec
    for part, (p_ref, c_ref) in enumerate(((psi, pre), (psi_o, pre_o))):
        for k in range(p_ref.shape[0]):
            at = lax.rem(base + part * sec + k, n_sec)
            live = meta[cfg["dims_at"] + at]
            row = lax.broadcasted_iota(jnp.int32, (states, width), 0)
            col = lax.broadcasted_iota(jnp.int32, (states, width), 1)
            value = jnp.where((row < live) & (col < live), p_ref[k].astype(F32).T, 0.0)
            work[at] = value
            pret[at] = c_ref[k].T
    (total,) = _over(n_sec, states, width, 1, lambda s, r: (_fold(work[s, r, :] * work[s, r, :]),))
    scale = lax.rsqrt(total / (n_sec * states * width) + EPS)

    def make(s, r):
        value = work[s, r, :] * scale
        v0[s, r, :] = value
        _write_vb(vb, s, r, value, env_pos, cfg["swap"])
        return ()

    _over(n_sec, states, width, 0, make)
    terms = right.shape[0]

    def one(i, carry):
        k, t = i % sec, i // sec
        chosen = vb[meta[cfg["pair_at"] + t * sec + k]]
        inner[t, k] = jnp.dot(right[t, k], chosen, preferred_element_type=F32).astype(BF16)
        return carry

    lax.fori_loop(0, terms * sec, one, 0, unroll=4)


def _second_kernel(cfg, n_left, meta, inner, *rest):
    lefts, outs, acc = rest[:n_left], rest[n_left:-1], rest[-1]
    terms, sec = inner.shape[:2]

    def one(k, carry):
        total = None
        for t in range(terms):
            left = jnp.concatenate([ref[t, k] for ref in lefts], axis=0)
            got = jnp.dot(inner[t, k], left, preferred_element_type=F32)
            total = got if total is None else total + got
        acc[k] = total
        return carry

    lax.fori_loop(0, sec, one, 0)
    _emit(cfg, meta, acc, outs)


def _step_kernel(cfg, step, n_left, n_shard, last, meta, *refs):
    it = iter(refs)
    take = lambda n: [next(it) for _ in range(n)]
    shards = take(n_shard)
    basis_h, (pre_h,), olds_h, (right_h,), left_h = take(step), take(1), take(step - 1), take(1), take(n_left)
    v_h, sig_h, dots = take(3)
    outs = take(cfg["n_out"])
    basis, (pre,), olds, (right,), lefts = take(step), take(1), take(step - 1), take(1), take(n_left)
    vnew, sig, vb, acc, sem = take(5)
    env_pos = meta[0]
    n_sec, states, width = vnew.shape
    sec = cfg["sec"]
    count = n_sec * states * width
    copies = []
    for i, (a, b) in enumerate(zip([*basis_h, pre_h, *olds_h, right_h, *left_h], [*basis, pre, *olds, right, *lefts])):
        copies.append(pltpu.make_async_copy(a, b, sem.at[i]))
        copies[-1].start()
    n_in = len(copies)
    v_out = pltpu.make_async_copy(vnew, v_h, sem.at[n_in])
    sig_out = pltpu.make_async_copy(sig, sig_h, sem.at[n_in + 1])
    for i, shard in enumerate(shards):
        s0, r0 = meta[cfg["shard_at"] + 2 * i], meta[cfg["shard_at"] + 2 * i + 1]
        rows = shard.shape[1]
        for k in range(shard.shape[0]):
            sig[s0 + k, pl.ds(pl.multiple_of(r0, rows), rows), :] = shard[k].astype(BF16)
    sig_out.start()
    for c in copies[:step]:
        c.wait()
    over = functools.partial(_over, n_sec, states, width)
    sums = over(step, lambda s, r: tuple(_fold(b[s, r, :] * sig[s, r, :].astype(F32)) for b in basis))
    proj = [x / count for x in sums]
    copies[step].wait()

    def trial_pass(s, r):
        resid = sig[s, r, :].astype(F32)
        held = [b[s, r, :] for b in basis]
        for h, b in zip(proj, held):
            resid = resid - h * b
        trial = resid * pre[s, r, :]
        vnew[s, r, :] = trial
        return tuple(_fold(b * trial) for b in held)

    back = [x / count for x in over(step, trial_pass)]

    def shift_pass(s, r):
        trial = vnew[s, r, :]
        for g, b in zip(back, basis):
            trial = trial - g * b[s, r, :]
        vnew[s, r, :] = trial
        return (_fold(trial * trial),)

    (square,) = over(1, shift_pass)
    scale = lax.rsqrt(square / count + EPS)
    for c in copies[step + 1 : 2 * step]:
        c.wait()

    def final_pass(s, r):
        value = vnew[s, r, :] * scale
        vnew[s, r, :] = value
        _write_vb(vb, s, r, value, env_pos, cfg["swap"])
        return tuple(_fold(value * o[s, r, :].astype(F32)) for o in [*olds, sig])

    cross = [x / count for x in over(step, final_pass)]
    v_out.start()
    scalars = proj + cross
    for c in copies[2 * step :]:
        c.wait()
    terms = right.shape[0]

    def one(k, carry):
        total = None
        for t in range(terms):
            chosen = vb[meta[cfg["pair_at"] + t * sec + k]]
            inner = jnp.dot(right[t, k], chosen, preferred_element_type=F32).astype(BF16)
            left = jnp.concatenate([ref[t, k] for ref in lefts], axis=0)
            got = jnp.dot(inner, left, preferred_element_type=F32)
            total = got if total is None else total + got
        acc[k] = total
        return carry

    lax.fori_loop(0, sec, one, 0)
    if last:
        rows_b = acc.shape[1]
        first = meta[2] * sec
        mine = []
        for b in [*basis, vnew]:
            def part(k, total, b=b):
                rows = pl.ds(pl.multiple_of(env_pos * rows_b, rows_b), rows_b)
                return total + _fold(b[first + k, rows, :] * acc[k])

            mine.append(jnp.sum(lax.fori_loop(0, sec, part, jnp.zeros((8, width), F32))) / count)
        scalars = scalars + mine
        for k in range(sec):
            acc[k, :, :] = acc[k, :, :]
        if cfg["direct"]:
            n, part = cfg["n_term"], width // cfg["n_term"]
            turned = cfg["turned"]
            for k in range(sec):
                outs[n][k] = acc[k].T
            z = meta[1]
            for s in range(n):
                rows = pl.ds(pl.multiple_of((z ^ s) * part, part), part)
                for k in range(sec):
                    outs[s][k] = outs[n][k, rows, :].astype(outs[s].dtype)
        else:
            for k in range(sec):
                outs[0][k] = acc[k].T
    else:
        _emit(cfg, meta, acc, outs)
    _put_scalars(dots, scalars)
    v_out.wait()
    sig_out.wait()


def solution(mesh):
    n_env, n_term, n_blk = (mesh.shape[a] for a in ("env", "term", "blk"))

    def on_device(psi, left_env, right_env, pairing, sector_dims, precond):
        return _on_device(n_env, n_term, n_blk, psi, left_env, right_env, pairing, sector_dims, precond)

    placed = (
        P(("parts", "blk"), None, None),
        P(("parts", "term"), "blk", "env", None),
        P(("parts", "term"), "blk", "env", None),
        P(("parts", "term"), "blk"),
        P("parts"),
        P(("parts", "blk"), None, None),
    )
    return jax.shard_map(
        on_device,
        mesh=mesh,
        in_specs=placed,
        out_specs=(P(None, ("parts", "blk"), "term", None), P("parts", None)),
        check_vma=False,
    )


def _xor(axis, n, s):
    return functools.partial(lax.ppermute, axis_name=axis, perm=[(i, i ^ s) for i in range(n)])


def _on_device(n_env, n_term, n_blk, psi, left_env, right_env, pairing, sector_dims, precond):
    sec, states, width = psi.shape
    terms = left_env.shape[0]
    n_sec = sec * n_blk
    half = right_env.shape[2]
    direct = n_env == 2 and n_blk == 2 and n_term in (2, 4)
    part = half // n_term
    cfg = dict(direct=direct, swap=direct, n_term=n_term, n_blk=n_blk, sec=sec, part=part, turned=None)
    env_pos, term_pos, blk_pos = (lax.axis_index(a) for a in ("env", "term", "blk"))
    other_env = _xor("env", 2, 1)
    other_blk = _xor("blk", 2, 1)

    places = []
    if direct:
        for b in range(2):
            for e in range(2):
                for s in range(n_term):
                    places += [(blk_pos ^ b) * sec, (env_pos ^ e) * half + (term_pos ^ s) * part]
    else:
        places = [0, 0]
    flat = jnp.stack([jnp.asarray(x, jnp.int32) for x in [env_pos, term_pos, blk_pos, *places]])
    meta = jnp.concatenate([flat, pairing.reshape(-1), sector_dims.reshape(-1)])
    cfg["shard_at"] = 3
    cfg["pair_at"] = 3 + len(places)
    cfg["dims_at"] = cfg["pair_at"] + terms * sec

    if direct:
        lefts = [left_env, other_env(left_env)]
        psi_o, pre_o = other_blk(psi), other_blk(precond)
    else:
        lefts = [lax.all_gather(left_env, "env", axis=2, tiled=True)]
        others = [lax.dynamic_slice_in_dim(
            lax.all_gather(x, "blk", axis=0, tiled=True), ((blk_pos + 1) % n_blk) * sec, sec * (n_blk - 1), 0
        ) for x in (psi, precond)] if n_blk == 2 else [psi, precond]
        psi_o, pre_o = others
    n_left = len(lefts)

    full = (n_sec, states, width)
    sds = jax.ShapeDtypeStruct
    params = pltpu.CompilerParams(vmem_limit_bytes=VMEM_LIMIT)
    v0, pret, inner = pl.pallas_call(
        functools.partial(_first_kernel, cfg),
        out_shape=(sds(full, F32), sds(full, F32), sds((terms, sec, half, states), BF16)),
        in_specs=_specs(SM, VM, VM, VM, VM, VM),
        out_specs=_specs(VM, VM, VM),
        scratch_shapes=[pltpu.VMEM(full, BF16), pltpu.VMEM(full, F32)],
        compiler_params=params,
        name="start_vector",
    )(meta, psi, psi_o, precond, pre_o, right_env)

    if direct:
        piece_shapes = [sds((sec, part, width), F32)] + [sds((sec, part, width), BF16)] * (n_term - 1)
    else:
        piece_shapes = [sds((sec, half, width), F32)]
    pieces = pl.pallas_call(
        functools.partial(_second_kernel, cfg, n_left),
        out_shape=tuple(piece_shapes),
        in_specs=_specs(SM, *[VM] * (1 + n_left)),
        out_specs=tuple(_specs(*[VM] * len(piece_shapes))),
        scratch_shapes=[pltpu.VMEM((sec, half, width), F32)],
        compiler_params=params,
        name="first_sigma",
    )(meta, inner, *lefts)

    live_own = lax.dynamic_slice_in_dim(sector_dims, blk_pos * sec, sec)[:, None, None]

    def reduce(pieces):
        if direct:
            got = [_xor("term", n_term, s)(pieces[s]) for s in range(1, n_term)]
            total = pieces[0]
            for g in got:
                total = total + g.astype(F32)
            row = env_pos * half + term_pos * part + lax.broadcasted_iota(jnp.int32, total.shape, 1)
            col = lax.broadcasted_iota(jnp.int32, total.shape, 2)
            return jnp.where((row < live_own) & (col < live_own), total, 0.0).astype(BF16)
        flat_sum = lax.psum_scatter(pieces[0].reshape(sec * half, width), "term", scatter_dimension=0, tiled=True)
        return flat_sum

    def gather(shard):
        if direct:
            along = [shard] + [_xor("term", n_term, s)(shard) for s in range(1, n_term)]
            along = along + [other_env(a) for a in along]
            return along + [other_blk(a) for a in along]
        whole = lax.all_gather(shard, "term", axis=0, tiled=True).reshape(sec, half, width)
        whole = lax.all_gather(whole, "env", axis=1, tiled=True)
        row = lax.broadcasted_iota(jnp.int32, whole.shape, 1)
        col = lax.broadcasted_iota(jnp.int32, whole.shape, 2)
        whole = jnp.where((row < live_own) & (col < live_own), whole, 0.0).astype(BF16)
        return [lax.all_gather(whole, "blk", axis=0, tiled=True)]

    basis, olds, rows_out = [v0], [], []
    chunk = states // n_term
    dots_all = []
    for step in range(1, ITERS):
        last = step + 1 == ITERS
        shards = gather(reduce(pieces))
        if last:
            if direct:
                outs = [sds((sec, chunk, half), F32)] + [sds((sec, chunk, half), BF16)] * (n_term - 1)
                outs.append(sds((sec, states, half), F32))
            else:
                outs = [sds((sec, states, half), F32)]
        else:
            outs = piece_shapes
        cfg_step = dict(cfg, n_out=len(outs))
        moved = [sds(full, F32)] * step + [sds(full, F32)] + [sds(full, BF16)] * (step - 1)
        moved += [sds(right_env.shape, BF16)] + [sds(x.shape, BF16) for x in lefts]
        results = pl.pallas_call(
            functools.partial(_step_kernel, cfg_step, step, n_left, len(shards), last),
            out_shape=(sds(full, F32), sds(full, BF16), sds((16, 128), F32), *outs),
            in_specs=_specs(SM, *[VM] * len(shards), *[ANY] * len(moved)),
            out_specs=tuple(_specs(ANY, ANY, VM, *[VM] * len(outs))),
            scratch_shapes=[pltpu.VMEM(m.shape, m.dtype) for m in moved]
            + [
                pltpu.VMEM(full, F32),
                pltpu.VMEM(full, BF16),
                pltpu.VMEM(full, BF16),
                pltpu.VMEM((sec, half, width), F32),
                pltpu.SemaphoreType.DMA((len(moved) + 2,)),
            ],
            compiler_params=params,
            name=f"vector_and_sigma_{step}",
        )(meta, *shards, *basis, pret, *olds, right_env, *lefts)
        vec, sig, dots = results[:3]
        pieces = results[3:]
        basis.append(vec)
        olds.append(sig)
        dots_all.append(dots)
        mine = lax.dynamic_slice(sig, (blk_pos * sec, 0, term_pos * chunk), (sec, states, chunk))
        rows_out.append(jnp.swapaxes(mine, 1, 2).astype(F32))

    tail = dots_all[-1]
    n_mid = 2 * (ITERS - 1)
    if direct:
        total, scal = pieces[0], tail
        for s in range(1, n_term):
            total = total + _xor("term", n_term, s)(pieces[s]).astype(F32)
            scal = scal + _xor("term", n_term, s)(tail)
        row = term_pos * chunk + lax.broadcasted_iota(jnp.int32, total.shape, 1)
        col = env_pos * half + lax.broadcasted_iota(jnp.int32, total.shape, 2)
        own = jnp.where((row < live_own) & (col < live_own), total, 0.0)
        theirs = other_env(own.astype(BF16)).astype(F32)
        scal = scal + other_env(scal)
        scal = scal + other_blk(scal)
        both = jnp.where(env_pos == 0, jnp.concatenate([own, theirs], 2), jnp.concatenate([theirs, own], 2))
    else:
        own = lax.psum_scatter(pieces[0], "term", scatter_dimension=1, tiled=True)
        both = lax.all_gather(own, "env", axis=2, tiled=True)
        row = term_pos * chunk + lax.broadcasted_iota(jnp.int32, both.shape, 1)
        col = lax.broadcasted_iota(jnp.int32, both.shape, 2)
        both = jnp.where((row < live_own) & (col < live_own), both, 0.0)
        scal = lax.psum(tail, ("term", "env", "blk"))
    rows_out.append(both)
    first, second = dots_all[0][:, 0], tail[:, 0]
    subspace = jnp.stack([
        jnp.stack([first[0], first[1], second[2]]),
        jnp.stack([second[0], second[1], second[3]]),
        scal[n_mid : n_mid + ITERS, 0],
    ])
    return jnp.stack(rows_out), subspace
```

time: 409 us -> 175 us (0.43)
  waiting for transfers between devices: 276 us -> 45.5 us
  starting transfers between devices: 0.16 us -> 50.7 us
  blocking collectives: 32.7 us -> 0 us
  other arithmetic: 37.6 us -> 8.55 us
  Pallas kernels: 0 us -> 25.7 us
  matrix products: 17.7 us -> 0 us
  between operations: 17.3 us -> 0.94 us
  local copies, waits for them, and re-layouts: 26 us -> 41.5 us
    psum x3 -> x0, waiting for transfers between devices: 228 us -> none  [on_device(): lax.psum(jnp.einsum('tkca,tkcb->kab', left_env, inner, preferred_element_...]
    ppermute x0 -> x48, starting transfers between devices: none -> 50.7 us  [the longest x16 16.4 us: gather(): return along + [other_blk(a) for a in along]]
    all_gather x1 -> x0, waiting for transfers between devices: 47.8 us -> none  [on_device(): right_full = lax.all_gather(right_env, 'env', axis=2, tiled=True)]
    ppermute x0 -> x48, waiting for transfers between devices: none -> 45.5 us  [the longest x1 30.8 us: _on_device(): lefts = [left_env, other_env(left_env)]]
    reduce_sum x9 -> x0, other arithmetic: 26.4 us -> none  [the longest x2 7.97 us: on_device(): back = reduce_means(jnp.stack([jnp.sum(other * trial) for other in basis]))]
    psum x8 -> x0, blocking collectives: 25.9 us -> none  [the longest x7 22.9 us: reduce_means(): return lax.psum(values, 'blk') / count]
    pallas_call x0 -> x4, Pallas kernels: none -> 25.7 us  [the longest x2 17.3 us: _on_device(): pl.pallas_call(functools.partial(_step_kernel, cfg_step, step, n_left, le...]
    unnamed x16 -> x101, local copies, waits for them, and re-layouts: 11.7 us -> 36 us
  transfers between devices with their start and end apart: 4 -> 48, of which waited for: 4 -> 12; matrix products, arithmetic and copies ran while one was open for 2% -> 8% of each run, Pallas kernels for 0% -> 3%
where the time goes in v1:
time: 175 us; the launch traced here: 173 us
  starting transfers between devices  50.7 us (29%)
  waiting for transfers between devices  45.5 us (26%)
  local copies, waits for them, and re-layouts  41.5 us (24%)
  Pallas kernels  25.7 us (15%)
  other arithmetic  8.55 us (5%)
    unnamed x101, local copies, waits for them, and re-layouts  36 us
    ppermute x1, waiting for transfers between devices, _on_device(): lefts = [left_env, other_env(left_env)]  30.8 us
    pallas_call x2, Pallas kernels, _on_device(): pl.pallas_call(functools.partial(_step_kernel, cfg_step, step, n_left, le...  17.3 us
    ppermute x16, starting transfers between devices, gather(): return along + [other_blk(a) for a in along]  16.4 us
    ppermute x6, waiting for transfers between devices, reduce(): got = [_xor('term', n_term, s)(pieces[s]) for s in range(1, n_term)]  8.27 us
    ppermute x6, starting transfers between devices, gather(): along = [shard] + [_xor('term', n_term, s)(shard) for s in range(1, n_term)]  7.49 us
    ppermute x6, starting transfers between devices, reduce(): got = [_xor('term', n_term, s)(pieces[s]) for s in range(1, n_term)]  7.16 us
    ppermute x8, starting transfers between devices, gather(): along = along + [other_env(a) for a in along]  5.96 us
  transfers between devices with their start and end apart: 48, of which 12 were waited for; matrix products, arithmetic and copies ran while one was open for 8% of the time, Pallas kernels for 3%

profile of v1, /device:TPU:1, one launch (start us, length us, event | category | flops | bytes accessed | tf_op | source)
XLA Modules:
  0.0 172.9 jit_solution(3062162027028962270)
XLA Ops:
  0.6 2.1 %collective-permute-start.2 = (bf16[8,4,128,256]{3,2,1,0:T(8,128)(2,1)}, bf16[8,4,128,256]{3,2,1,0:T(8,128)(2,1)}, u32[]{:S(2)}, u32[]{:S(2)}) collective-permute-start(bf16[8,4,128,256]{3,2,1,0:T(8,128)(2,1)} %refs_21_.1), channel_id=1, source_target_pairs={{0,2},{2,0},{1,3},{3,1},{4,6},{6,4},{5,7},{7,5},{8,10},{10,8},{9,1... | collective-permute-start | bytes 6291464 | tf_op jit(solution)/shard_map/ppermute | solution.py:289
  6.9 1.6 copy-done.1
  8.5 1.2 copy-done.13
  9.8 1.0 copy-done.14
  10.8 5.5 %start_vector.1 = (f32[8,256,256]{2,1,0:T(8,128)S(1)}, f32[8,256,256]{2,1,0:T(8,128)S(1)}, bf16[8,4,128,256]{3,2,1,0:T(8,128)(2,1)S(1)}) custom-call(s32[75]{0:T(128)S(1)} %concatenate.29.meta, bf16[4,256,256]{2,1,0:T(8,128)(2,1)S(1)} %copy-done.14, bf16[4,256,256]{2,1,0:T(8,128)(2,1)} %collective-permute-done.psi_o, f32[4,256,256]{2,1,0:T(8,128)S(1)} %copy-done.13, ...), custom_call_target="tpu_custom_call" | custom-call | tf_op jit(solution)/shard_map/start_vector/pallas_call | solution.py:302
  16.3 1.3 copy-done.4
  17.6 30.8 %collective-permute-done.2.rest_1_.refs_20_.refs_22_ = bf16[8,4,128,256]{3,2,1,0:T(8,128)(2,1)} collective-permute-done((bf16[8,4,128,256]{3,2,1,0:T(8,128)(2,1)}, bf16[8,4,128,256]{3,2,1,0:T(8,128)(2,1)}, u32[]{:S(2)}, u32[]{:S(2)}) %collective-permute-start.2) | collective-permute-done | bytes 2097184 | tf_op jit(solution)/shard_map/ppermute | solution.py:289
  48.4 2.9 %first_sigma.1 = (f32[4,32,256]{2,1,0:T(8,128)S(1)}, bf16[4,32,256]{2,1,0:T(8,128)(2,1)S(1)}, bf16[4,32,256]{2,1,0:T(8,128)(2,1)S(1)}, bf16[4,32,256]{2,1,0:T(8,128)(2,1)S(1)}) custom-call(s32[75]{0:T(128)S(1)} %concatenate.29.meta, bf16[8,4,128,256]{3,2,1,0:T(8,128)(2,1)S(1)} %get-tuple-element.22.inner, bf16[8,4,128,256]{3,2,1,0:T(8,128)(2,1)S(1)} %copy-done, ...), custom_call_target="tpu_custom_call" | custom-call | tf_op jit(solution)/shard_map/first_sigma/pallas_call | solution.py:316
  51.3 1.3 collective-permute-start.3
  52.6 2.3 %collective-permute-start.4 = (bf16[4,32,256]{2,1,0:T(8,128)(2,1)S(1)}, bf16[4,32,256]{2,1,0:T(8,128)(2,1)S(1)}, u32[]{:S(2)}, u32[]{:S(2)}) collective-permute-start(bf16[4,32,256]{2,1,0:T(8,128)(2,1)S(1)} %get-tuple-element.25), channel_id=1, source_target_pairs={{0,8},{4,12},{8,0},{12,4},{1,9},{5,13},{9,1},{13,5},{2,10},{6,14},... | collective-permute-start | bytes 196616 | tf_op jit(solution)/shard_map/ppermute | solution.py:330
  55.0 2.4 %collective-permute-done.4 = bf16[4,32,256]{2,1,0:T(8,128)(2,1)S(1)} collective-permute-done((bf16[4,32,256]{2,1,0:T(8,128)(2,1)S(1)}, bf16[4,32,256]{2,1,0:T(8,128)(2,1)S(1)}, u32[]{:S(2)}, u32[]{:S(2)}) %collective-permute-start.4) | collective-permute-done | bytes 65568 | tf_op jit(solution)/shard_map/ppermute | solution.py:330
  57.4 2.6 %collective-permute-done.5 = bf16[4,32,256]{2,1,0:T(8,128)(2,1)S(1)} collective-permute-done((bf16[4,32,256]{2,1,0:T(8,128)(2,1)S(1)}, bf16[4,32,256]{2,1,0:T(8,128)(2,1)S(1)}, u32[]{:S(2)}, u32[]{:S(2)}) %collective-permute-start.5) | collective-permute-done | bytes 65568 | tf_op jit(solution)/shard_map/ppermute | solution.py:330
  60.1 1.3 collective-permute-start.9
  61.4 1.0 collective-permute-start.8
  62.4 3.3 %collective-permute-start.13 = (bf16[4,32,256]{2,1,0:T(8,128)(2,1)S(1)}, bf16[4,32,256]{2,1,0:T(8,128)(2,1)S(1)}, u32[]{:S(2)}, u32[]{:S(2)}) collective-permute-start(bf16[4,32,256]{2,1,0:T(8,128)(2,1)S(1)} %select_convert_fusion.1.refs_0_), channel_id=1, source_target_pairs={{0,1},{1,0},{2,3},{3,2},{4,5},{5,4},{6,7},{7,6},{8,9},{9,8},{10,11... | collective-permute-start | bytes 196616 | tf_op jit(solution)/shard_map/ppermute | solution.py:344
  65.8 2.8 %collective-permute-start.6 = (bf16[4,32,256]{2,1,0:T(8,128)(2,1)S(1)}, bf16[4,32,256]{2,1,0:T(8,128)(2,1)S(1)}, u32[]{:S(2)}, u32[]{:S(2)}) collective-permute-start(bf16[4,32,256]{2,1,0:T(8,128)(2,1)S(1)} %select_convert_fusion.1.refs_0_), channel_id=1, source_target_pairs={{0,4},{4,0},{8,12},{12,8},{1,5},{5,1},{9,13},{13,9},{2,6},{6,2},{1... | collective-permute-start | bytes 196616 | tf_op jit(solution)/shard_map/ppermute | solution.py:342
  69.2 2.5 %collective-permute-start.16 = (bf16[4,32,256]{2,1,0:T(8,128)(2,1)S(1)}, bf16[4,32,256]{2,1,0:T(8,128)(2,1)S(1)}, u32[]{:S(2)}, u32[]{:S(2)}) collective-permute-start(bf16[4,32,256]{2,1,0:T(8,128)(2,1)S(1)} %collective-permute-done.8.refs_3_), channel_id=1, source_target_pairs={{0,1},{1,0},{2,3},{3,2},{4,5},{5,4},{6,7},{7,6},{8,9},{9,8},{10,11... | collective-permute-start | bytes 196616 | tf_op jit(solution)/shard_map/ppermute | solution.py:344
  74.4 1.5 collective-permute-start.15
  82.8 1.6 copy-done.2
  84.4 1.6 copy-done.5
  86.0 1.6 copy-done.8
  96.0 7.7 %vector_and_sigma_1.1 = (f32[8,256,256]{2,1,0:T(8,128)S(1)}, bf16[8,256,256]{2,1,0:T(8,128)(2,1)S(1)}, f32[16,128]{1,0:T(8,128)S(1)}, f32[4,32,256]{2,1,0:T(8,12...) custom-call(s32[75]{0:T(128)S(1)} %concatenate.29.meta, ...), custom_call_target="tpu_custom_call" | custom-call | tf_op jit(solution)/shard_map/vector_and_sigma_1/pallas_call | solution.py:369
  103.6 1.4 copy-done.10
  105.0 1.4 collective-permute-start.22
  106.4 2.2 %collective-permute-start.23 = (bf16[4,32,256]{2,1,0:T(8,128)(2,1)S(1)}, bf16[4,32,256]{2,1,0:T(8,128)(2,1)S(1)}, u32[]{:S(2)}, u32[]{:S(2)}) collective-permute-start(bf16[4,32,256]{2,1,0:T(8,128)(2,1)S(1)} %get-tuple-element.33), channel_id=1, source_target_pairs={{0,12},{4,8},{8,4},{12,0},{1,13},{5,9},{9,5},{13,1},{2,14},{6,10},... | collective-permute-start | bytes 196616 | tf_op jit(solution)/shard_map/ppermute | solution.py:330
  109.2 3.2 %collective-permute-done.23 = bf16[4,32,256]{2,1,0:T(8,128)(2,1)S(1)} collective-permute-done((bf16[4,32,256]{2,1,0:T(8,128)(2,1)S(1)}, bf16[4,32,256]{2,1,0:T(8,128)(2,1)S(1)}, u32[]{:S(2)}, u32[]{:S(2)}) %collective-permute-start.23) | collective-permute-done | bytes 65568 | tf_op jit(solution)/shard_map/ppermute | solution.py:330
  112.4 1.8 %collective-permute-start.31 = (bf16[4,32,256]{2,1,0:T(8,128)(2,1)S(1)}, bf16[4,32,256]{2,1,0:T(8,128)(2,1)S(1)}, u32[]{:S(2)}, u32[]{:S(2)}) collective-permute-start(bf16[4,32,256]{2,1,0:T(8,128)(2,1)S(1)} %select_convert_fusion.refs_0_), channel_id=1, source_target_pairs={{0,1},{1,0},{2,3},{3,2},{4,5},{5,4},{6,7},{7,6},{8,9},{9,8},{10,11... | collective-permute-start | bytes 196616 | tf_op jit(solution)/shard_map/ppermute | solution.py:344
  114.4 1.7 collective-permute-start.26
  116.6 1.4 collective-permute-start.24
  118.5 1.3 copy.12
  119.8 1.7 collective-permute-start.34
  121.5 1.3 collective-permute-start.30
  123.2 1.3 collective-permute-start.29
  124.7 1.6 convert_bitcast_fusion.1
  126.3 1.3 collective-permute-start.33
  130.7 1.6 copy-done.6
  132.3 1.6 copy-done.9
  133.9 1.6 copy-done.11
  137.2 9.6 %vector_and_sigma_2.1 = (f32[8,256,256]{2,1,0:T(8,128)}, bf16[8,256,256]{2,1,0:T(8,128)(2,1)S(1)}, f32[16,128]{1,0:T(8,128)S(1)}, f32[4,64,128]{2,1,0:T(8,128)S(...) custom-call(s32[75]{0:T(128)S(1)} %concatenate.29.meta, ...), custom_call_target="tpu_custom_call" | custom-call | tf_op jit(solution)/shard_map/vector_and_sigma_2/pallas_call | solution.py:369
  150.7 1.7 collective-permute-start.45
  152.4 1.5 copy.13
  155.0 1.1 collective-permute-done.44
  156.0 1.1 collective-permute-start.46
  157.7 1.9 %collective-permute-start.40 = (bf16[4,64,128]{2,1,0:T(8,128)(2,1)S(1)}, bf16[4,64,128]{2,1,0:T(8,128)(2,1)S(1)}, u32[]{:S(2)}, u32[]{:S(2)}) collective-permute-start(bf16[4,64,128]{2,1,0:T(8,128)(2,1)S(1)} %copy-done.42), channel_id=1, source_target_pairs={{0,8},{4,12},{8,0},{12,4},{1,9},{5,13},{9,1},{13,5},{2,10},{6,14},... | collective-permute-start | bytes 196616 | tf_op jit(solution)/shard_map/ppermute | solution.py:398
  159.6 1.6 collective-permute-start.41
  161.3 2.9 %collective-permute-start.47 = (f32[16,128]{1,0:T(8,128)S(1)}, f32[16,128]{1,0:T(8,128)S(1)}, u32[]{:S(2)}, u32[]{:S(2)}) collective-permute-start(f32[16,128]{1,0:T(8,128)S(1)} %add.136), channel_id=1, source_target_pairs={{0,1},{1,0},{2,3},{3,2},{4,5},{5,4},{6,7},{7,6},{8,9},{9,8},{10,11... | collective-permute-start | bytes 24584 | tf_op jit(solution)/shard_map/ppermute | solution.py:405
  164.2 3.8 %maximum_bitcast_fusion = (f32[1,3]{1,0:T(1,128)S(1)}, f32[1,3]{1,0:T(1,128)S(1)}) fusion(f32[1]{0:T(128)} %bitcast.22, f32[1]{0:T(128)} %bitcast.21, f32[1]{0:T(128)} %bitcast.20, f32[1]{0:T(128)} %bitcast.26, f32[1]{0:T(128)} %bitcast.25, f32[1]{0:T(128)} %bitcast.24), kind=kLoop, calls=%fused_computation.14 | loop fusion | flops 12 | bytes 48 | tf_op jit(solution)/shard_map/stack | solution.py:416
  169.3 2.6 %collective-permute-done.42 = bf16[4,64,128]{2,1,0:T(8,128)(2,1)S(1)} collective-permute-done((bf16[4,64,128]{2,1,0:T(8,128)(2,1)S(1)}, bf16[4,64,128]{2,1,0:T(8,128)(2,1)S(1)}, u32[]{:S(2)}, u32[]{:S(2)}) %collective-permute-start.42) | collective-permute-done | bytes 65568 | tf_op jit(solution)/shard_map/ppermute | solution.py:403
  (176 shorter events, 38.1 us)
Async XLA Ops:
  0.6 47.8 %collective-permute-start.2 = (bf16[8,4,128,256]{3,2,1,0:T(8,128)(2,1)}, bf16[8,4,128,256]{3,2,1,0:T(8,128)(2,1)}, u32[]{:S(2)}, u32[]{:S(2)}) collective-permute-start(bf16[8,4,128,256]{3,2,1,0:T(8,128)(2,1)} %refs_21_.1), channel_id=1, source_target_pairs={{0,2},{2,0},{1,3},{3,1},{4,6},{6,4},{5,7},{7,5},{8,10},{10,8},{9,1... | collective-permute-start | bytes 6291464 | tf_op jit(solution)/shard_map/ppermute | solution.py:289
  2.7 4.2 %collective-permute-start.1 = (f32[4,256,256]{2,1,0:T(8,128)}, f32[4,256,256]{2,1,0:T(8,128)S(1)}, u32[]{:S(2)}, u32[]{:S(2)}) collective-permute-start(f32[4,256,256]{2,1,0:T(8,128)} %pre.1), channel_id=1, source_target_pairs={{0,1},{1,0},{2,3},{3,2},{4,5},{5,4},{6,7},{7,6},{8,9},{9,8},{10,11... | collective-permute-start | bytes 3145736 | tf_op jit(solution)/shard_map/ppermute | solution.py:290
  3.7 3.2 %collective-permute-start = (bf16[4,256,256]{2,1,0:T(8,128)(2,1)}, bf16[4,256,256]{2,1,0:T(8,128)(2,1)}, u32[]{:S(2)}, u32[]{:S(2)}) collective-permute-start(bf16[4,256,256]{2,1,0:T(8,128)(2,1)} %psi.1), channel_id=1, source_target_pairs={{0,1},{1,0},{2,3},{3,2},{4,5},{5,4},{6,7},{7,6},{8,9},{9,8},{10,11... | collective-permute-start | bytes 1572872 | tf_op jit(solution)/shard_map/ppermute | solution.py:290
  51.3 3.6 %collective-permute-start.3 = (bf16[4,32,256]{2,1,0:T(8,128)(2,1)S(1)}, bf16[4,32,256]{2,1,0:T(8,128)(2,1)S(1)}, u32[]{:S(2)}, u32[]{:S(2)}) collective-permute-start(bf16[4,32,256]{2,1,0:T(8,128)(2,1)S(1)} %get-tuple-element.24), channel_id=1, source_target_pairs={{0,4},{4,0},{8,12},{12,8},{1,5},{5,1},{9,13},{13,9},{2,6},{6,2},{1... | collective-permute-start | bytes 196616 | tf_op jit(solution)/shard_map/ppermute | solution.py:330
  52.6 4.7 %collective-permute-start.4 = (bf16[4,32,256]{2,1,0:T(8,128)(2,1)S(1)}, bf16[4,32,256]{2,1,0:T(8,128)(2,1)S(1)}, u32[]{:S(2)}, u32[]{:S(2)}) collective-permute-start(bf16[4,32,256]{2,1,0:T(8,128)(2,1)S(1)} %get-tuple-element.25), channel_id=1, source_target_pairs={{0,8},{4,12},{8,0},{12,4},{1,9},{5,13},{9,1},{13,5},{2,10},{6,14},... | collective-permute-start | bytes 196616 | tf_op jit(solution)/shard_map/ppermute | solution.py:330
  55.0 5.0 %collective-permute-start.5 = (bf16[4,32,256]{2,1,0:T(8,128)(2,1)S(1)}, bf16[4,32,256]{2,1,0:T(8,128)(2,1)S(1)}, u32[]{:S(2)}, u32[]{:S(2)}) collective-permute-start(bf16[4,32,256]{2,1,0:T(8,128)(2,1)S(1)} %get-tuple-element.26), channel_id=1, source_target_pairs={{0,12},{4,8},{8,4},{12,0},{1,13},{5,9},{9,5},{13,1},{2,14},{6,10},... | collective-permute-start | bytes 196616 | tf_op jit(solution)/shard_map/ppermute | solution.py:330
  60.1 8.5 %collective-permute-start.9 = (bf16[4,32,256]{2,1,0:T(8,128)(2,1)S(1)}, bf16[4,32,256]{2,1,0:T(8,128)(2,1)S(1)}, u32[]{:S(2)}, u32[]{:S(2)}) collective-permute-start(bf16[4,32,256]{2,1,0:T(8,128)(2,1)S(1)} %select_convert_fusion.1.refs_0_), channel_id=1, source_target_pairs={{0,2},{2,0},{1,3},{3,1},{4,6},{6,4},{5,7},{7,5},{8,10},{10,8},{9,1... | collective-permute-start | bytes 196616 | tf_op jit(solution)/shard_map/ppermute | solution.py:343
  61.4 7.8 %collective-permute-start.8 = (bf16[4,32,256]{2,1,0:T(8,128)(2,1)S(1)}, bf16[4,32,256]{2,1,0:T(8,128)(2,1)S(1)}, u32[]{:S(2)}, u32[]{:S(2)}) collective-permute-start(bf16[4,32,256]{2,1,0:T(8,128)(2,1)S(1)} %select_convert_fusion.1.refs_0_), channel_id=1, source_target_pairs={{0,12},{4,8},{8,4},{12,0},{1,13},{5,9},{9,5},{13,1},{2,14},{6,10},... | collective-permute-start | bytes 196616 | tf_op jit(solution)/shard_map/ppermute | solution.py:342
  62.4 9.3 %collective-permute-start.13 = (bf16[4,32,256]{2,1,0:T(8,128)(2,1)S(1)}, bf16[4,32,256]{2,1,0:T(8,128)(2,1)S(1)}, u32[]{:S(2)}, u32[]{:S(2)}) collective-permute-start(bf16[4,32,256]{2,1,0:T(8,128)(2,1)S(1)} %select_convert_fusion.1.refs_0_), channel_id=1, source_target_pairs={{0,1},{1,0},{2,3},{3,2},{4,5},{5,4},{6,7},{7,6},{8,9},{9,8},{10,11... | collective-permute-start | bytes 196616 | tf_op jit(solution)/shard_map/ppermute | solution.py:344
  65.7 6.6 %collective-permute-start.7 = (bf16[4,32,256]{2,1,0:T(8,128)(2,1)S(1)}, bf16[4,32,256]{2,1,0:T(8,128)(2,1)S(1)}, u32[]{:S(2)}, u32[]{:S(2)}) collective-permute-start(bf16[4,32,256]{2,1,0:T(8,128)(2,1)S(1)} %select_convert_fusion.1.refs_0_), channel_id=1, source_target_pairs={{0,8},{4,12},{8,0},{12,4},{1,9},{5,13},{9,1},{13,5},{2,10},{6,14},... | collective-permute-start | bytes 196616 | tf_op jit(solution)/shard_map/ppermute | solution.py:342
  65.8 7.4 %collective-permute-start.6 = (bf16[4,32,256]{2,1,0:T(8,128)(2,1)S(1)}, bf16[4,32,256]{2,1,0:T(8,128)(2,1)S(1)}, u32[]{:S(2)}, u32[]{:S(2)}) collective-permute-start(bf16[4,32,256]{2,1,0:T(8,128)(2,1)S(1)} %select_convert_fusion.1.refs_0_), channel_id=1, source_target_pairs={{0,4},{4,0},{8,12},{12,8},{1,5},{5,1},{9,13},{13,9},{2,6},{6,2},{1... | collective-permute-start | bytes 196616 | tf_op jit(solution)/shard_map/ppermute | solution.py:342
  68.6 5.1 %collective-permute-start.17 = (bf16[4,32,256]{2,1,0:T(8,128)(2,1)S(1)}, bf16[4,32,256]{2,1,0:T(8,128)(2,1)S(1)}, u32[]{:S(2)}, u32[]{:S(2)}) collective-permute-start(bf16[4,32,256]{2,1,0:T(8,128)(2,1)S(1)} %collective-permute-done.9.refs_4_), channel_id=1, source_target_pairs={{0,1},{1,0},{2,3},{3,2},{4,5},{5,4},{6,7},{7,6},{8,9},{9,8},{10,11... | collective-permute-start | bytes 196616 | tf_op jit(solution)/shard_map/ppermute | solution.py:344
  69.2 6.7 %collective-permute-start.16 = (bf16[4,32,256]{2,1,0:T(8,128)(2,1)S(1)}, bf16[4,32,256]{2,1,0:T(8,128)(2,1)S(1)}, u32[]{:S(2)}, u32[]{:S(2)}) collective-permute-start(bf16[4,32,256]{2,1,0:T(8,128)(2,1)S(1)} %collective-permute-done.8.refs_3_), channel_id=1, source_target_pairs={{0,1},{1,0},{2,3},{3,2},{4,5},{5,4},{6,7},{7,6},{8,9},{9,8},{10,11... | collective-permute-start | bytes 196616 | tf_op jit(solution)/shard_map/ppermute | solution.py:344
  71.7 4.8 %collective-permute-start.12 = (bf16[4,32,256]{2,1,0:T(8,128)(2,1)S(1)}, bf16[4,32,256]{2,1,0:T(8,128)(2,1)S(1)}, u32[]{:S(2)}, u32[]{:S(2)}) collective-permute-start(bf16[4,32,256]{2,1,0:T(8,128)(2,1)S(1)} %collective-permute-done.8.refs_3_), channel_id=1, source_target_pairs={{0,2},{2,0},{1,3},{3,1},{4,6},{6,4},{5,7},{7,5},{8,10},{10,8},{9,1... | collective-permute-start | bytes 196616 | tf_op jit(solution)/shard_map/ppermute | solution.py:343
  72.3 5.4 %collective-permute-start.11 = (bf16[4,32,256]{2,1,0:T(8,128)(2,1)S(1)}, bf16[4,32,256]{2,1,0:T(8,128)(2,1)S(1)}, u32[]{:S(2)}, u32[]{:S(2)}) collective-permute-start(bf16[4,32,256]{2,1,0:T(8,128)(2,1)S(1)} %collective-permute-done.7.refs_2_), channel_id=1, source_target_pairs={{0,2},{2,0},{1,3},{3,1},{4,6},{6,4},{5,7},{7,5},{8,10},{10,8},{9,1... | collective-permute-start | bytes 196616 | tf_op jit(solution)/shard_map/ppermute | solution.py:343
  73.2 5.7 %collective-permute-start.10 = (bf16[4,32,256]{2,1,0:T(8,128)(2,1)S(1)}, bf16[4,32,256]{2,1,0:T(8,128)(2,1)S(1)}, u32[]{:S(2)}, u32[]{:S(2)}) collective-permute-start(bf16[4,32,256]{2,1,0:T(8,128)(2,1)S(1)} %collective-permute-done.6.refs_1_), channel_id=1, source_target_pairs={{0,2},{2,0},{1,3},{3,1},{4,6},{6,4},{5,7},{7,5},{8,10},{10,8},{9,1... | collective-permute-start | bytes 196616 | tf_op jit(solution)/shard_map/ppermute | solution.py:343
  74.4 5.3 %collective-permute-start.15 = (bf16[4,32,256]{2,1,0:T(8,128)(2,1)S(1)}, bf16[4,32,256]{2,1,0:T(8,128)(2,1)S(1)}, u32[]{:S(2)}, u32[]{:S(2)}) collective-permute-start(bf16[4,32,256]{2,1,0:T(8,128)(2,1)S(1)} %collective-permute-done.7.refs_2_), channel_id=1, source_target_pairs={{0,1},{1,0},{2,3},{3,2},{4,5},{5,4},{6,7},{7,6},{8,9},{9,8},{10,11... | collective-permute-start | bytes 196616 | tf_op jit(solution)/shard_map/ppermute | solution.py:344
  76.5 3.8 %collective-permute-start.14 = (bf16[4,32,256]{2,1,0:T(8,128)(2,1)S(1)}, bf16[4,32,256]{2,1,0:T(8,128)(2,1)S(1)}, u32[]{:S(2)}, u32[]{:S(2)}) collective-permute-start(bf16[4,32,256]{2,1,0:T(8,128)(2,1)S(1)} %collective-permute-done.6.refs_1_), channel_id=1, source_target_pairs={{0,1},{1,0},{2,3},{3,2},{4,5},{5,4},{6,7},{7,6},{8,9},{9,8},{10,11... | collective-permute-start | bytes 196616 | tf_op jit(solution)/shard_map/ppermute | solution.py:344
  76.5 4.4 %collective-permute-start.20 = (bf16[4,32,256]{2,1,0:T(8,128)(2,1)S(1)}, bf16[4,32,256]{2,1,0:T(8,128)(2,1)S(1)}, u32[]{:S(2)}, u32[]{:S(2)}) collective-permute-start(bf16[4,32,256]{2,1,0:T(8,128)(2,1)S(1)} %collective-permute-done.12.refs_7_), channel_id=1, source_target_pairs={{0,1},{1,0},{2,3},{3,2},{4,5},{5,4},{6,7},{7,6},{8,9},{9,8},{10,11... | collective-permute-start | bytes 196616 | tf_op jit(solution)/shard_map/ppermute | solution.py:344
  77.6 3.9 %collective-permute-start.19 = (bf16[4,32,256]{2,1,0:T(8,128)(2,1)S(1)}, bf16[4,32,256]{2,1,0:T(8,128)(2,1)S(1)}, u32[]{:S(2)}, u32[]{:S(2)}) collective-permute-start(bf16[4,32,256]{2,1,0:T(8,128)(2,1)S(1)} %collective-permute-done.11.refs_6_), channel_id=1, source_target_pairs={{0,1},{1,0},{2,3},{3,2},{4,5},{5,4},{6,7},{7,6},{8,9},{9,8},{10,11... | collective-permute-start | bytes 196616 | tf_op jit(solution)/shard_map/ppermute | solution.py:344
  78.9 3.3 %collective-permute-start.18 = (bf16[4,32,256]{2,1,0:T(8,128)(2,1)S(1)}, bf16[4,32,256]{2,1,0:T(8,128)(2,1)S(1)}, u32[]{:S(2)}, u32[]{:S(2)}) collective-permute-start(bf16[4,32,256]{2,1,0:T(8,128)(2,1)S(1)} %collective-permute-done.10.refs_5_), channel_id=1, source_target_pairs={{0,1},{1,0},{2,3},{3,2},{4,5},{5,4},{6,7},{7,6},{8,9},{9,8},{10,11... | collective-permute-start | bytes 196616 | tf_op jit(solution)/shard_map/ppermute | solution.py:344
  105.0 4.1 %collective-permute-start.21 = (bf16[4,32,256]{2,1,0:T(8,128)(2,1)S(1)}, bf16[4,32,256]{2,1,0:T(8,128)(2,1)S(1)}, u32[]{:S(2)}, u32[]{:S(2)}) collective-permute-start(bf16[4,32,256]{2,1,0:T(8,128)(2,1)S(1)} %get-tuple-element.31), channel_id=1, source_target_pairs={{0,4},{4,0},{8,12},{12,8},{1,5},{5,1},{9,13},{13,9},{2,6},{6,2},{1... | collective-permute-start | bytes 196616 | tf_op jit(solution)/shard_map/ppermute | solution.py:330
  105.0 4.1 %collective-permute-start.22 = (bf16[4,32,256]{2,1,0:T(8,128)(2,1)S(1)}, bf16[4,32,256]{2,1,0:T(8,128)(2,1)S(1)}, u32[]{:S(2)}, u32[]{:S(2)}) collective-permute-start(bf16[4,32,256]{2,1,0:T(8,128)(2,1)S(1)} %get-tuple-element.32), channel_id=1, source_target_pairs={{0,8},{4,12},{8,0},{12,4},{1,9},{5,13},{9,1},{13,5},{2,10},{6,14},... | collective-permute-start | bytes 196616 | tf_op jit(solution)/shard_map/ppermute | solution.py:330
  106.4 5.9 %collective-permute-start.23 = (bf16[4,32,256]{2,1,0:T(8,128)(2,1)S(1)}, bf16[4,32,256]{2,1,0:T(8,128)(2,1)S(1)}, u32[]{:S(2)}, u32[]{:S(2)}) collective-permute-start(bf16[4,32,256]{2,1,0:T(8,128)(2,1)S(1)} %get-tuple-element.33), channel_id=1, source_target_pairs={{0,12},{4,8},{8,4},{12,0},{1,13},{5,9},{9,5},{13,1},{2,14},{6,10},... | collective-permute-start | bytes 196616 | tf_op jit(solution)/shard_map/ppermute | solution.py:330
  112.4 9.1 %collective-permute-start.31 = (bf16[4,32,256]{2,1,0:T(8,128)(2,1)S(1)}, bf16[4,32,256]{2,1,0:T(8,128)(2,1)S(1)}, u32[]{:S(2)}, u32[]{:S(2)}) collective-permute-start(bf16[4,32,256]{2,1,0:T(8,128)(2,1)S(1)} %select_convert_fusion.refs_0_), channel_id=1, source_target_pairs={{0,1},{1,0},{2,3},{3,2},{4,5},{5,4},{6,7},{7,6},{8,9},{9,8},{10,11... | collective-permute-start | bytes 196616 | tf_op jit(solution)/shard_map/ppermute | solution.py:344
  114.2 8.6 %collective-permute-start.27 = (bf16[4,32,256]{2,1,0:T(8,128)(2,1)S(1)}, bf16[4,32,256]{2,1,0:T(8,128)(2,1)S(1)}, u32[]{:S(2)}, u32[]{:S(2)}) collective-permute-start(bf16[4,32,256]{2,1,0:T(8,128)(2,1)S(1)} %select_convert_fusion.refs_0_), channel_id=1, source_target_pairs={{0,2},{2,0},{1,3},{3,1},{4,6},{6,4},{5,7},{7,5},{8,10},{10,8},{9,1... | collective-permute-start | bytes 196616 | tf_op jit(solution)/shard_map/ppermute | solution.py:343
  114.4 5.5 %collective-permute-start.26 = (bf16[4,32,256]{2,1,0:T(8,128)(2,1)S(1)}, bf16[4,32,256]{2,1,0:T(8,128)(2,1)S(1)}, u32[]{:S(2)}, u32[]{:S(2)}) collective-permute-start(bf16[4,32,256]{2,1,0:T(8,128)(2,1)S(1)} %select_convert_fusion.refs_0_), channel_id=1, source_target_pairs={{0,12},{4,8},{8,4},{12,0},{1,13},{5,9},{9,5},{13,1},{2,14},{6,10},... | collective-permute-start | bytes 196616 | tf_op jit(solution)/shard_map/ppermute | solution.py:342
  116.1 7.1 %collective-permute-start.25 = (bf16[4,32,256]{2,1,0:T(8,128)(2,1)S(1)}, bf16[4,32,256]{2,1,0:T(8,128)(2,1)S(1)}, u32[]{:S(2)}, u32[]{:S(2)}) collective-permute-start(bf16[4,32,256]{2,1,0:T(8,128)(2,1)S(1)} %select_convert_fusion.refs_0_), channel_id=1, source_target_pairs={{0,8},{4,12},{8,0},{12,4},{1,9},{5,13},{9,1},{13,5},{2,10},{6,14},... | collective-permute-start | bytes 196616 | tf_op jit(solution)/shard_map/ppermute | solution.py:342
  116.6 7.9 %collective-permute-start.24 = (bf16[4,32,256]{2,1,0:T(8,128)(2,1)S(1)}, bf16[4,32,256]{2,1,0:T(8,128)(2,1)S(1)}, u32[]{:S(2)}, u32[]{:S(2)}) collective-permute-start(bf16[4,32,256]{2,1,0:T(8,128)(2,1)S(1)} %select_convert_fusion.refs_0_), channel_id=1, source_target_pairs={{0,4},{4,0},{8,12},{12,8},{1,5},{5,1},{9,13},{13,9},{2,6},{6,2},{1... | collective-permute-start | bytes 196616 | tf_op jit(solution)/shard_map/ppermute | solution.py:342
  119.8 7.7 %collective-permute-start.34 = (bf16[4,32,256]{2,1,0:T(8,128)(2,1)S(1)}, bf16[4,32,256]{2,1,0:T(8,128)(2,1)S(1)}, u32[]{:S(2)}, u32[]{:S(2)}) collective-permute-start(bf16[4,32,256]{2,1,0:T(8,128)(2,1)S(1)} %collective-permute-done.26.refs_3_), channel_id=1, source_target_pairs={{0,1},{1,0},{2,3},{3,2},{4,5},{5,4},{6,7},{7,6},{8,9},{9,8},{10,11... | collective-permute-start | bytes 196616 | tf_op jit(solution)/shard_map/ppermute | solution.py:344
  121.5 6.2 %collective-permute-start.30 = (bf16[4,32,256]{2,1,0:T(8,128)(2,1)S(1)}, bf16[4,32,256]{2,1,0:T(8,128)(2,1)S(1)}, u32[]{:S(2)}, u32[]{:S(2)}) collective-permute-start(bf16[4,32,256]{2,1,0:T(8,128)(2,1)S(1)} %collective-permute-done.26.refs_3_), channel_id=1, source_target_pairs={{0,2},{2,0},{1,3},{3,1},{4,6},{6,4},{5,7},{7,5},{8,10},{10,8},{9,1... | collective-permute-start | bytes 196616 | tf_op jit(solution)/shard_map/ppermute | solution.py:343
  122.8 3.5 %collective-permute-start.35 = (bf16[4,32,256]{2,1,0:T(8,128)(2,1)S(1)}, bf16[4,32,256]{2,1,0:T(8,128)(2,1)S(1)}, u32[]{:S(2)}, u32[]{:S(2)}) collective-permute-start(bf16[4,32,256]{2,1,0:T(8,128)(2,1)S(1)} %collective-permute-done.27.refs_4_), channel_id=1, source_target_pairs={{0,1},{1,0},{2,3},{3,2},{4,5},{5,4},{6,7},{7,6},{8,9},{9,8},{10,11... | collective-permute-start | bytes 196616 | tf_op jit(solution)/shard_map/ppermute | solution.py:344
  123.2 4.9 %collective-permute-start.29 = (bf16[4,32,256]{2,1,0:T(8,128)(2,1)S(1)}, bf16[4,32,256]{2,1,0:T(8,128)(2,1)S(1)}, u32[]{:S(2)}, u32[]{:S(2)}) collective-permute-start(bf16[4,32,256]{2,1,0:T(8,128)(2,1)S(1)} %collective-permute-done.25.refs_2_), channel_id=1, source_target_pairs={{0,2},{2,0},{1,3},{3,1},{4,6},{6,4},{5,7},{7,5},{8,10},{10,8},{9,1... | collective-permute-start | bytes 196616 | tf_op jit(solution)/shard_map/ppermute | solution.py:343
  124.5 4.3 %collective-permute-start.28 = (bf16[4,32,256]{2,1,0:T(8,128)(2,1)S(1)}, bf16[4,32,256]{2,1,0:T(8,128)(2,1)S(1)}, u32[]{:S(2)}, u32[]{:S(2)}) collective-permute-start(bf16[4,32,256]{2,1,0:T(8,128)(2,1)S(1)} %collective-permute-done.24.refs_1_), channel_id=1, source_target_pairs={{0,2},{2,0},{1,3},{3,1},{4,6},{6,4},{5,7},{7,5},{8,10},{10,8},{9,1... | collective-permute-start | bytes 196616 | tf_op jit(solution)/shard_map/ppermute | solution.py:343
  126.3 4.0 %collective-permute-start.33 = (bf16[4,32,256]{2,1,0:T(8,128)(2,1)S(1)}, bf16[4,32,256]{2,1,0:T(8,128)(2,1)S(1)}, u32[]{:S(2)}, u32[]{:S(2)}) collective-permute-start(bf16[4,32,256]{2,1,0:T(8,128)(2,1)S(1)} %collective-permute-done.25.refs_2_), channel_id=1, source_target_pairs={{0,1},{1,0},{2,3},{3,2},{4,5},{5,4},{6,7},{7,6},{8,9},{9,8},{10,11... | collective-permute-start | bytes 196616 | tf_op jit(solution)/shard_map/ppermute | solution.py:344
  127.6 2.7 %collective-permute-start.32 = (bf16[4,32,256]{2,1,0:T(8,128)(2,1)S(1)}, bf16[4,32,256]{2,1,0:T(8,128)(2,1)S(1)}, u32[]{:S(2)}, u32[]{:S(2)}) collective-permute-start(bf16[4,32,256]{2,1,0:T(8,128)(2,1)S(1)} %collective-permute-done.24.refs_1_), channel_id=1, source_target_pairs={{0,1},{1,0},{2,3},{3,2},{4,5},{5,4},{6,7},{7,6},{8,9},{9,8},{10,11... | collective-permute-start | bytes 196616 | tf_op jit(solution)/shard_map/ppermute | solution.py:344
  127.7 2.7 %collective-permute-start.38 = (bf16[4,32,256]{2,1,0:T(8,128)(2,1)S(1)}, bf16[4,32,256]{2,1,0:T(8,128)(2,1)S(1)}, u32[]{:S(2)}, u32[]{:S(2)}) collective-permute-start(bf16[4,32,256]{2,1,0:T(8,128)(2,1)S(1)} %collective-permute-done.30.refs_7_), channel_id=1, source_target_pairs={{0,1},{1,0},{2,3},{3,2},{4,5},{5,4},{6,7},{7,6},{8,9},{9,8},{10,11... | collective-permute-start | bytes 196616 | tf_op jit(solution)/shard_map/ppermute | solution.py:344
  128.1 2.2 %collective-permute-start.37 = (bf16[4,32,256]{2,1,0:T(8,128)(2,1)S(1)}, bf16[4,32,256]{2,1,0:T(8,128)(2,1)S(1)}, u32[]{:S(2)}, u32[]{:S(2)}) collective-permute-start(bf16[4,32,256]{2,1,0:T(8,128)(2,1)S(1)} %collective-permute-done.29.refs_6_), channel_id=1, source_target_pairs={{0,1},{1,0},{2,3},{3,2},{4,5},{5,4},{6,7},{7,6},{8,9},{9,8},{10,11... | collective-permute-start | bytes 196616 | tf_op jit(solution)/shard_map/ppermute | solution.py:344
  128.8 1.9 %collective-permute-start.36 = (bf16[4,32,256]{2,1,0:T(8,128)(2,1)S(1)}, bf16[4,32,256]{2,1,0:T(8,128)(2,1)S(1)}, u32[]{:S(2)}, u32[]{:S(2)}) collective-permute-start(bf16[4,32,256]{2,1,0:T(8,128)(2,1)S(1)} %collective-permute-done.28.refs_5_), channel_id=1, source_target_pairs={{0,1},{1,0},{2,3},{3,2},{4,5},{5,4},{6,7},{7,6},{8,9},{9,8},{10,11... | collective-permute-start | bytes 196616 | tf_op jit(solution)/shard_map/ppermute | solution.py:344
  149.7 4.2 %collective-permute-start.43 = (f32[16,128]{1,0:T(8,128)S(1)}, f32[16,128]{1,0:T(8,128)S(1)}, u32[]{:S(2)}, u32[]{:S(2)}) collective-permute-start(f32[16,128]{1,0:T(8,128)S(1)} %get-tuple-element.41), channel_id=1, source_target_pairs={{0,4},{4,0},{8,12},{12,8},{1,5},{5,1},{9,13},{13,9},{2,6},{6,2},{1... | collective-permute-start | bytes 24584 | tf_op jit(solution)/shard_map/ppermute | solution.py:399
  150.7 4.3 %collective-permute-start.45 = (f32[16,128]{1,0:T(8,128)S(1)}, f32[16,128]{1,0:T(8,128)S(1)}, u32[]{:S(2)}, u32[]{:S(2)}) collective-permute-start(f32[16,128]{1,0:T(8,128)S(1)} %get-tuple-element.41), channel_id=1, source_target_pairs={{0,12},{4,8},{8,4},{12,0},{1,13},{5,9},{9,5},{13,1},{2,14},{6,10},... | collective-permute-start | bytes 24584 | tf_op jit(solution)/shard_map/ppermute | solution.py:399
  152.3 3.7 %collective-permute-start.44 = (f32[16,128]{1,0:T(8,128)S(1)}, f32[16,128]{1,0:T(8,128)S(1)}, u32[]{:S(2)}, u32[]{:S(2)}) collective-permute-start(f32[16,128]{1,0:T(8,128)S(1)} %get-tuple-element.41), channel_id=1, source_target_pairs={{0,8},{4,12},{8,0},{12,4},{1,9},{5,13},{9,1},{13,5},{2,10},{6,14},... | collective-permute-start | bytes 24584 | tf_op jit(solution)/shard_map/ppermute | solution.py:399
  156.0 5.3 %collective-permute-start.46 = (f32[16,128]{1,0:T(8,128)S(1)}, f32[16,128]{1,0:T(8,128)S(1)}, u32[]{:S(2)}, u32[]{:S(2)}) collective-permute-start(f32[16,128]{1,0:T(8,128)S(1)} %add_add_fusion), channel_id=1, source_target_pairs={{0,2},{2,0},{1,3},{3,1},{4,6},{6,4},{5,7},{7,5},{8,10},{10,8},{9,1... | collective-permute-start | bytes 24584 | tf_op jit(solution)/shard_map/ppermute | solution.py:404
  157.7 10.4 %collective-permute-start.39 = (bf16[4,64,128]{2,1,0:T(8,128)(2,1)S(1)}, bf16[4,64,128]{2,1,0:T(8,128)(2,1)S(1)}, u32[]{:S(2)}, u32[]{:S(2)}) collective-permute-start(bf16[4,64,128]{2,1,0:T(8,128)(2,1)S(1)} %copy-done.44), channel_id=1, source_target_pairs={{0,4},{4,0},{8,12},{12,8},{1,5},{5,1},{9,13},{13,9},{2,6},{6,2},{1... | collective-permute-start | bytes 196616 | tf_op jit(solution)/shard_map/ppermute | solution.py:398
  157.7 10.4 %collective-permute-start.40 = (bf16[4,64,128]{2,1,0:T(8,128)(2,1)S(1)}, bf16[4,64,128]{2,1,0:T(8,128)(2,1)S(1)}, u32[]{:S(2)}, u32[]{:S(2)}) collective-permute-start(bf16[4,64,128]{2,1,0:T(8,128)(2,1)S(1)} %copy-done.42), channel_id=1, source_target_pairs={{0,8},{4,12},{8,0},{12,4},{1,9},{5,13},{9,1},{13,5},{2,10},{6,14},... | collective-permute-start | bytes 196616 | tf_op jit(solution)/shard_map/ppermute | solution.py:398
  159.6 8.5 %collective-permute-start.41 = (bf16[4,64,128]{2,1,0:T(8,128)(2,1)S(1)}, bf16[4,64,128]{2,1,0:T(8,128)(2,1)S(1)}, u32[]{:S(2)}, u32[]{:S(2)}) collective-permute-start(bf16[4,64,128]{2,1,0:T(8,128)(2,1)S(1)} %copy-done.40), channel_id=1, source_target_pairs={{0,12},{4,8},{8,4},{12,0},{1,13},{5,9},{9,5},{13,1},{2,14},{6,10},... | collective-permute-start | bytes 196616 | tf_op jit(solution)/shard_map/ppermute | solution.py:398
  161.3 6.7 %collective-permute-start.47 = (f32[16,128]{1,0:T(8,128)S(1)}, f32[16,128]{1,0:T(8,128)S(1)}, u32[]{:S(2)}, u32[]{:S(2)}) collective-permute-start(f32[16,128]{1,0:T(8,128)S(1)} %add.136), channel_id=1, source_target_pairs={{0,1},{1,0},{2,3},{3,2},{4,5},{5,4},{6,7},{7,6},{8,9},{9,8},{10,11... | collective-permute-start | bytes 24584 | tf_op jit(solution)/shard_map/ppermute | solution.py:405
  168.3 3.6 %collective-permute-start.42 = (bf16[4,64,128]{2,1,0:T(8,128)(2,1)S(1)}, bf16[4,64,128]{2,1,0:T(8,128)(2,1)S(1)}, u32[]{:S(2)}, u32[]{:S(2)}) collective-permute-start(bf16[4,64,128]{2,1,0:T(8,128)(2,1)S(1)} %get-tuple-element.43), channel_id=1, source_target_pairs={{0,2},{2,0},{1,3},{3,1},{4,6},{6,4},{5,7},{7,5},{8,10},{10,8},{9,1... | collective-permute-start | bytes 196616 | tf_op jit(solution)/shard_map/ppermute | solution.py:403
  (50 other events, 259.9 us)

commit v2 on v1

--- a/solution.py
+++ b/solution.py
@@ -18,7 +18,15 @@
     return [pl.BlockSpec(memory_space=s) for s in shapes]
 
 
-ANY, VM, SM = pl.ANY, pltpu.VMEM, pltpu.SMEM
+HB, VM, SM = pltpu.HBM, pltpu.VMEM, pltpu.SMEM
+
+
+def _hbm(*arrays):
+    return [pltpu.with_memory_space_constraint(x, pltpu.HBM) for x in arrays]
+
+
+def _vmem(*arrays):
+    return [pltpu.with_memory_space_constraint(x, pltpu.VMEM) for x in arrays]
 
 
 def _fold(x):
@@ -66,7 +74,10 @@
         outs[0][...] = acc[...]
 
 
-def _first_kernel(cfg, meta, psi, psi_o, pre, pre_o, right, v0, pret, inner, vb, work):
+def _first_kernel(cfg, meta, psi, psi_o, pre, pre_o, right, *refs):
+    held_h, held, (vb, work, sem) = refs[:3], refs[3:6], refs[6:]
+    v0, pret, inner = held
+    saves = [pltpu.make_async_copy(a, b, sem.at[i]) for i, (a, b) in enumerate(zip(held, held_h))]
     sec, states, width = psi.shape
     n_sec = sec * cfg["n_blk"]
     blk, env_pos = meta[2], meta[0]
@@ -90,6 +101,8 @@
         return ()
 
     _over(n_sec, states, width, 0, make)
+    saves[0].start()
+    saves[1].start()
     terms = right.shape[0]
 
     def one(i, carry):
@@ -99,22 +112,31 @@
         return carry
 
     lax.fori_loop(0, terms * sec, one, 0, unroll=4)
-
-
-def _second_kernel(cfg, n_left, meta, inner, *rest):
-    lefts, outs, acc = rest[:n_left], rest[n_left:-1], rest[-1]
-    terms, sec = inner.shape[:2]
-
-    def one(k, carry):
+    saves[2].start()
+    for c in saves:
+        c.wait()
+
+
+def _second_kernel(cfg, n_left, meta, *refs):
+    ins_h, outs, acc = refs[: 1 + n_left], refs[1 + n_left : -3 - n_left], refs[-3 - n_left]
+    ins, sem = refs[-2 - n_left : -1], refs[-1]
+    terms, sec = ins[0].shape[:2]
+    copies = [
+        [pltpu.make_async_copy(a.at[:, k], b.at[:, k], sem.at[i, k]) for i, (a, b) in enumerate(zip(ins_h, ins))]
+        for k in range(sec)
+    ]
+    for group in copies:
+        for c in group:
+            c.start()
+    for k in range(sec):
+        for c in copies[k]:
+            c.wait()
         total = None
         for t in range(terms):
-            left = jnp.concatenate([ref[t, k] for ref in lefts], axis=0)
-            got = jnp.dot(inner[t, k], left, preferred_element_type=F32)
+            left = jnp.concatenate([ref[t, k] for ref in ins[1:]], axis=0)
+            got = jnp.dot(ins[0][t, k], left, preferred_element_type=F32)
             total = got if total is None else total + got
         acc[k] = total
-        return carry
-
-    lax.fori_loop(0, sec, one, 0)
     _emit(cfg, meta, acc, outs)
 
 
@@ -210,11 +232,8 @@
 
             mine.append(jnp.sum(lax.fori_loop(0, sec, part, jnp.zeros((8, width), F32))) / count)
         scalars = scalars + mine
-        for k in range(sec):
-            acc[k, :, :] = acc[k, :, :]
         if cfg["direct"]:
             n, part = cfg["n_term"], width // cfg["n_term"]
-            turned = cfg["turned"]
             for k in range(sec):
                 outs[n][k] = acc[k].T
             z = meta[1]
@@ -266,7 +285,7 @@
     half = right_env.shape[2]
     direct = n_env == 2 and n_blk == 2 and n_term in (2, 4)
     part = half // n_term
-    cfg = dict(direct=direct, swap=direct, n_term=n_term, n_blk=n_blk, sec=sec, part=part, turned=None)
+    cfg = dict(direct=direct, swap=direct, n_term=n_term, n_blk=n_blk, sec=sec, part=part)
     env_pos, term_pos, blk_pos = (lax.axis_index(a) for a in ("env", "term", "blk"))
     other_env = _xor("env", 2, 1)
     other_blk = _xor("blk", 2, 1)
@@ -301,27 +320,39 @@
     params = pltpu.CompilerParams(vmem_limit_bytes=VMEM_LIMIT)
     v0, pret, inner = pl.pallas_call(
         functools.partial(_first_kernel, cfg),
-        out_shape=(sds(full, F32), sds(full, F32), sds((terms, sec, half, states), BF16)),
+        out_shape=(HB(full, F32), HB(full, F32), HB((terms, sec, half, states), BF16)),
         in_specs=_specs(SM, VM, VM, VM, VM, VM),
-        out_specs=_specs(VM, VM, VM),
-        scratch_shapes=[pltpu.VMEM(full, BF16), pltpu.VMEM(full, F32)],
+        out_specs=_specs(HB, HB, HB),
+        scratch_shapes=[
+            pltpu.VMEM(full, F32),
+            pltpu.VMEM(full, F32),
+            pltpu.VMEM((terms, sec, half, states), BF16),
+            pltpu.VMEM(full, BF16),
+            pltpu.VMEM(full, F32),
+            pltpu.SemaphoreType.DMA((3,)),
+        ],
         compiler_params=params,
         name="start_vector",
     )(meta, psi, psi_o, precond, pre_o, right_env)
 
     if direct:
-        piece_shapes = [sds((sec, part, width), F32)] + [sds((sec, part, width), BF16)] * (n_term - 1)
-    else:
-        piece_shapes = [sds((sec, half, width), F32)]
+        piece_shapes = [VM((sec, part, width), F32)] + [VM((sec, part, width), BF16)] * (n_term - 1)
+    else:
+        piece_shapes = [VM((sec, half, width), F32)]
     pieces = pl.pallas_call(
         functools.partial(_second_kernel, cfg, n_left),
         out_shape=tuple(piece_shapes),
-        in_specs=_specs(SM, *[VM] * (1 + n_left)),
+        in_specs=_specs(SM, *[HB] * (1 + n_left)),
         out_specs=tuple(_specs(*[VM] * len(piece_shapes))),
-        scratch_shapes=[pltpu.VMEM((sec, half, width), F32)],
+        scratch_shapes=[
+            pltpu.VMEM((sec, half, width), F32),
+            pltpu.VMEM(inner.shape, BF16),
+            *[pltpu.VMEM(x.shape, BF16) for x in lefts],
+            pltpu.SemaphoreType.DMA((1 + n_left, sec)),
+        ],
         compiler_params=params,
         name="first_sigma",
-    )(meta, inner, *lefts)
+    )(meta, *_hbm(inner, *lefts))
 
     live_own = lax.dynamic_slice_in_dim(sector_dims, blk_pos * sec, sec)[:, None, None]
 
@@ -357,10 +388,10 @@
         shards = gather(reduce(pieces))
         if last:
             if direct:
-                outs = [sds((sec, chunk, half), F32)] + [sds((sec, chunk, half), BF16)] * (n_term - 1)
-                outs.append(sds((sec, states, half), F32))
+                outs = [VM((sec, chunk, half), F32)] + [VM((sec, chunk, half), BF16)] * (n_term - 1)
+                outs.append(VM((sec, states, half), F32))
             else:
-                outs = [sds((sec, states, half), F32)]
+                outs = [VM((sec, states, half), F32)]
         else:
             outs = piece_shapes
         cfg_step = dict(cfg, n_out=len(outs))
@@ -368,9 +399,9 @@
         moved += [sds(right_env.shape, BF16)] + [sds(x.shape, BF16) for x in lefts]
         results = pl.pallas_call(
             functools.partial(_step_kernel, cfg_step, step, n_left, len(shards), last),
-            out_shape=(sds(full, F32), sds(full, BF16), sds((16, 128), F32), *outs),
-            in_specs=_specs(SM, *[VM] * len(shards), *[ANY] * len(moved)),
-            out_specs=tuple(_specs(ANY, ANY, VM, *[VM] * len(outs))),
+            out_shape=(HB(full, F32), HB(full, BF16), VM((16, 128), F32), *outs),
+            in_specs=_specs(SM, *[VM] * len(shards), *[HB] * len(moved)),
+            out_specs=tuple(_specs(HB, HB, VM, *[VM] * len(outs))),
             scratch_shapes=[pltpu.VMEM(m.shape, m.dtype) for m in moved]
             + [
                 pltpu.VMEM(full, F32),
@@ -381,7 +412,7 @@
             ],
             compiler_params=params,
             name=f"vector_and_sigma_{step}",
-        )(meta, *shards, *basis, pret, *olds, right_env, *lefts)
+        )(meta, *_vmem(*shards), *_hbm(*basis, pret, *olds, right_env, *lefts))
         vec, sig, dots = results[:3]
         pieces = results[3:]
         basis.append(vec)

time: 175 us -> 151 us (0.86)
  local copies, waits for them, and re-layouts: 41.5 us -> 10.2 us
  starting transfers between devices: 50.7 us -> 55.8 us
  Pallas kernels: 25.7 us -> 30.5 us
  other arithmetic: 8.55 us -> 5.86 us
    unnamed x101 -> x7, local copies, waits for them, and re-layouts: 36 us -> 4.61 us
    ppermute x16, starting transfers between devices: 16.4 us -> 21.4 us  [gather(): return along + [other_blk(a) for a in along]]
    pallas_call x2, Pallas kernels: 17.3 us -> 20.2 us  [_on_device(): pl.pallas_call(functools.partial(_step_kernel, cfg_step, step, n_left, le...]
  transfers between devices with their start and end apart: 48 -> 48, of which waited for: 12 -> 15; matrix products, arithmetic and copies ran while one was open for 8% -> 7% of each run, Pallas kernels for 3% -> 4%
where the time goes in v2:
time: 151 us; the launch traced here: 150 us
  starting transfers between devices  55.8 us (37%)
  waiting for transfers between devices  46.8 us (31%)
  Pallas kernels  30.5 us (20%)
  local copies, waits for them, and re-layouts  10.2 us (7%)
  other arithmetic  5.86 us (4%)
    ppermute x1, waiting for transfers between devices, _on_device(): lefts = [left_env, other_env(left_env)]  31.2 us
    ppermute x16, starting transfers between devices, gather(): return along + [other_blk(a) for a in along]  21.4 us
    pallas_call x2, Pallas kernels, _on_device(): pl.pallas_call(functools.partial(_step_kernel, cfg_step, step, n_left, le...  20.2 us
    ppermute x6, waiting for transfers between devices, reduce(): got = [_xor('term', n_term, s)(pieces[s]) for s in range(1, n_term)]  8.14 us
    ppermute x6, starting transfers between devices, gather(): along = [shard] + [_xor('term', n_term, s)(shard) for s in range(1, n_term)]  7.5 us
    ppermute x6, starting transfers between devices, reduce(): got = [_xor('term', n_term, s)(pieces[s]) for s in range(1, n_term)]  7.22 us
    pallas_call x1, Pallas kernels, _on_device(): pl.pallas_call(functools.partial(_first_kernel, cfg), out_shape=(HB(full,...  6.39 us
    ppermute x8, starting transfers between devices, gather(): along = along + [other_env(a) for a in along]  5.96 us
  transfers between devices with their start and end apart: 48, of which 15 were waited for; matrix products, arithmetic and copies ran while one was open for 7% of the time, Pallas kernels for 4%

profile of v2, /device:TPU:1, one launch (start us, length us, event | category | flops | bytes accessed | tf_op | source)
XLA Modules:
  0.0 150.1 jit_solution(9731041252540917160)
XLA Ops:
  0.6 2.1 %collective-permute-start.2 = (bf16[8,4,128,256]{3,2,1,0:T(8,128)(2,1)}, bf16[8,4,128,256]{3,2,1,0:T(8,128)(2,1)}, u32[]{:S(2)}, u32[]{:S(2)}) collective-permute-start(bf16[8,4,128,256]{3,2,1,0:T(8,128)(2,1)} %refs_21_.1), channel_id=1, source_target_pairs={{0,2},{2,0},{1,3},{3,1},{4,6},{6,4},{5,7},{7,5},{8,10},{10,8},{9,1... | collective-permute-start | bytes 6291464 | tf_op jit(solution)/shard_map/ppermute | solution.py:308
  2.7 1.0 collective-permute-start.1
  6.0 0.9 collective-permute-done.psi_o
  6.9 1.6 %copy-done = bf16[8,4,128,256]{3,2,1,0:T(8,128)(2,1)S(1)} copy-done((bf16[8,4,128,256]{3,2,1,0:T(8,128)(2,1)S(1)}, bf16[8,4,128,256]{3,2,1,0:T(8,128)(2,1)}, u32[]{:S(2)}) %copy-start) | copy-done | bytes 2097176
  8.5 1.2 copy-done.1
  9.8 1.0 copy-done.2
  10.8 6.4 %start_vector.1 = (f32[8,256,256]{2,1,0:T(8,128)}, f32[8,256,256]{2,1,0:T(8,128)}, bf16[8,4,128,256]{3,2,1,0:T(8,128)(2,1)}) custom-call(s32[75]{0:T(128)S(1)} %concatenate.29.meta, bf16[4,256,256]{2,1,0:T(8,128)(2,1)S(1)} %copy-done.2, bf16[4,256,256]{2,1,0:T(8,128)(2,1)S(1)} %collective-permute-done.psi_o, f32[4,256,256]{2,1,0:T(8,128)S(1)} %copy-done.1, ...), custom_call_target="tpu_custom_call" | custom-call | tf_op jit(solution)/shard_map/start_vector/pallas_call | solution.py:321
  17.2 31.2 %collective-permute-done.2.refs_2_.refs_20_.refs_22_ = bf16[8,4,128,256]{3,2,1,0:T(8,128)(2,1)} collective-permute-done((bf16[8,4,128,256]{3,2,1,0:T(8,128)(2,1)}, bf16[8,4,128,256]{3,2,1,0:T(8,128)(2,1)}, u32[]{:S(2)}, u32[]{:S(2)}) %collective-permute-start.2) | collective-permute-done | bytes 2097184 | tf_op jit(solution)/shard_map/ppermute | solution.py:308
  48.4 3.9 %first_sigma.1 = (f32[4,32,256]{2,1,0:T(8,128)S(1)}, bf16[4,32,256]{2,1,0:T(8,128)(2,1)S(1)}, bf16[4,32,256]{2,1,0:T(8,128)(2,1)S(1)}, bf16[4,32,256]{2,1,0:T(8,128)(2,1)S(1)}) custom-call(s32[75]{0:T(128)S(1)} %concatenate.29.meta, bf16[8,4,128,256]{3,2,1,0:T(8,128)(2,1)} %get-tuple-element.22.refs_0_, bf16[8,4,128,256]{3,2,1,0:T(8,128)(2,1)} %refs_21_.1, ...), custom_call_target="tpu_custom_call" | custom-call | tf_op jit(solution)/shard_map/first_sigma/pallas_call | solution.py:342
  52.3 1.3 collective-permute-start.3
  53.6 2.3 %collective-permute-start.4 = (bf16[4,32,256]{2,1,0:T(8,128)(2,1)S(1)}, bf16[4,32,256]{2,1,0:T(8,128)(2,1)S(1)}, u32[]{:S(2)}, u32[]{:S(2)}) collective-permute-start(bf16[4,32,256]{2,1,0:T(8,128)(2,1)S(1)} %get-tuple-element.25), channel_id=1, source_target_pairs={{0,8},{4,12},{8,0},{12,4},{1,9},{5,13},{9,1},{13,5},{2,10},{6,14},... | collective-permute-start | bytes 196616 | tf_op jit(solution)/shard_map/ppermute | solution.py:361
  55.9 2.4 %collective-permute-done.4 = bf16[4,32,256]{2,1,0:T(8,128)(2,1)S(1)} collective-permute-done((bf16[4,32,256]{2,1,0:T(8,128)(2,1)S(1)}, bf16[4,32,256]{2,1,0:T(8,128)(2,1)S(1)}, u32[]{:S(2)}, u32[]{:S(2)}) %collective-permute-start.4) | collective-permute-done | bytes 65568 | tf_op jit(solution)/shard_map/ppermute | solution.py:361
  58.3 2.6 %collective-permute-done.5 = bf16[4,32,256]{2,1,0:T(8,128)(2,1)S(1)} collective-permute-done((bf16[4,32,256]{2,1,0:T(8,128)(2,1)S(1)}, bf16[4,32,256]{2,1,0:T(8,128)(2,1)S(1)}, u32[]{:S(2)}, u32[]{:S(2)}) %collective-permute-start.5) | collective-permute-done | bytes 65568 | tf_op jit(solution)/shard_map/ppermute | solution.py:361
  61.0 1.3 collective-permute-start.9
  62.3 1.0 collective-permute-start.8
  63.3 3.3 %collective-permute-start.13 = (bf16[4,32,256]{2,1,0:T(8,128)(2,1)S(1)}, bf16[4,32,256]{2,1,0:T(8,128)(2,1)S(1)}, u32[]{:S(2)}, u32[]{:S(2)}) collective-permute-start(bf16[4,32,256]{2,1,0:T(8,128)(2,1)S(1)} %select_convert_fusion.1.refs_0_), channel_id=1, source_target_pairs={{0,1},{1,0},{2,3},{3,2},{4,5},{5,4},{6,7},{7,6},{8,9},{9,8},{10,11... | collective-permute-start | bytes 196616 | tf_op jit(solution)/shard_map/ppermute | solution.py:375
  66.8 2.8 %collective-permute-start.6 = (bf16[4,32,256]{2,1,0:T(8,128)(2,1)S(1)}, bf16[4,32,256]{2,1,0:T(8,128)(2,1)S(1)}, u32[]{:S(2)}, u32[]{:S(2)}) collective-permute-start(bf16[4,32,256]{2,1,0:T(8,128)(2,1)S(1)} %select_convert_fusion.1.refs_0_), channel_id=1, source_target_pairs={{0,4},{4,0},{8,12},{12,8},{1,5},{5,1},{9,13},{13,9},{2,6},{6,2},{1... | collective-permute-start | bytes 196616 | tf_op jit(solution)/shard_map/ppermute | solution.py:373
  70.1 2.5 %collective-permute-start.16 = (bf16[4,32,256]{2,1,0:T(8,128)(2,1)S(1)}, bf16[4,32,256]{2,1,0:T(8,128)(2,1)S(1)}, u32[]{:S(2)}, u32[]{:S(2)}) collective-permute-start(bf16[4,32,256]{2,1,0:T(8,128)(2,1)S(1)} %collective-permute-done.8.refs_3_), channel_id=1, source_target_pairs={{0,1},{1,0},{2,3},{3,2},{4,5},{5,4},{6,7},{7,6},{8,9},{9,8},{10,11... | collective-permute-start | bytes 196616 | tf_op jit(solution)/shard_map/ppermute | solution.py:375
  73.2 0.9 collective-permute-start.11
  74.7 1.5 %collective-permute-start.15 = (bf16[4,32,256]{2,1,0:T(8,128)(2,1)S(1)}, bf16[4,32,256]{2,1,0:T(8,128)(2,1)S(1)}, u32[]{:S(2)}, u32[]{:S(2)}) collective-permute-start(bf16[4,32,256]{2,1,0:T(8,128)(2,1)S(1)} %collective-permute-done.7.refs_2_), channel_id=1, source_target_pairs={{0,1},{1,0},{2,3},{3,2},{4,5},{5,4},{6,7},{7,6},{8,9},{9,8},{10,11... | collective-permute-start | bytes 196616 | tf_op jit(solution)/shard_map/ppermute | solution.py:375
  76.4 1.2 collective-permute-start.20
  77.5 1.6 %collective-permute-start.19 = (bf16[4,32,256]{2,1,0:T(8,128)(2,1)S(1)}, bf16[4,32,256]{2,1,0:T(8,128)(2,1)S(1)}, u32[]{:S(2)}, u32[]{:S(2)}) collective-permute-start(bf16[4,32,256]{2,1,0:T(8,128)(2,1)S(1)} %collective-permute-done.11.refs_6_), channel_id=1, source_target_pairs={{0,1},{1,0},{2,3},{3,2},{4,5},{5,4},{6,7},{7,6},{8,9},{9,8},{10,11... | collective-permute-start | bytes 196616 | tf_op jit(solution)/shard_map/ppermute | solution.py:375
  80.9 8.8 %vector_and_sigma_1.1 = (f32[8,256,256]{2,1,0:T(8,128)}, bf16[8,256,256]{2,1,0:T(8,128)(2,1)}, f32[16,128]{1,0:T(8,128)S(1)}, f32[4,32,256]{2,1,0:T(8,128)S(1)},...) custom-call(s32[75]{0:T(128)S(1)} %concatenate.29.meta, ...), custom_call_target="tpu_custom_call" | custom-call | tf_op jit(solution)/shard_map/vector_and_sigma_1/pallas_call | solution.py:400
  89.7 1.2 collective-permute-start.22
  90.9 2.3 %collective-permute-start.23 = (bf16[4,32,256]{2,1,0:T(8,128)(2,1)S(1)}, bf16[4,32,256]{2,1,0:T(8,128)(2,1)S(1)}, u32[]{:S(2)}, u32[]{:S(2)}) collective-permute-start(bf16[4,32,256]{2,1,0:T(8,128)(2,1)S(1)} %get-tuple-element.33), channel_id=1, source_target_pairs={{0,12},{4,8},{8,4},{12,0},{1,13},{5,9},{9,5},{13,1},{2,14},{6,10},... | collective-permute-start | bytes 196616 | tf_op jit(solution)/shard_map/ppermute | solution.py:361
  93.9 2.5 %collective-permute-done.23 = bf16[4,32,256]{2,1,0:T(8,128)(2,1)S(1)} collective-permute-done((bf16[4,32,256]{2,1,0:T(8,128)(2,1)S(1)}, bf16[4,32,256]{2,1,0:T(8,128)(2,1)S(1)}, u32[]{:S(2)}, u32[]{:S(2)}) %collective-permute-start.23) | collective-permute-done | bytes 65568 | tf_op jit(solution)/shard_map/ppermute | solution.py:361
  96.5 2.5 %collective-permute-start.31 = (bf16[4,32,256]{2,1,0:T(8,128)(2,1)S(1)}, bf16[4,32,256]{2,1,0:T(8,128)(2,1)S(1)}, u32[]{:S(2)}, u32[]{:S(2)}) collective-permute-start(bf16[4,32,256]{2,1,0:T(8,128)(2,1)S(1)} %select_convert_fusion.refs_0_), channel_id=1, source_target_pairs={{0,1},{1,0},{2,3},{3,2},{4,5},{5,4},{6,7},{7,6},{8,9},{9,8},{10,11... | collective-permute-start | bytes 196616 | tf_op jit(solution)/shard_map/ppermute | solution.py:375
  99.2 1.7 %collective-permute-start.26 = (bf16[4,32,256]{2,1,0:T(8,128)(2,1)S(1)}, bf16[4,32,256]{2,1,0:T(8,128)(2,1)S(1)}, u32[]{:S(2)}, u32[]{:S(2)}) collective-permute-start(bf16[4,32,256]{2,1,0:T(8,128)(2,1)S(1)} %select_convert_fusion.refs_0_), channel_id=1, source_target_pairs={{0,12},{4,8},{8,4},{12,0},{1,13},{5,9},{9,5},{13,1},{2,14},{6,10},... | collective-permute-start | bytes 196616 | tf_op jit(solution)/shard_map/ppermute | solution.py:373
  101.3 1.4 collective-permute-start.24
  102.7 1.5 copy.12
  104.2 2.1 %collective-permute-start.34 = (bf16[4,32,256]{2,1,0:T(8,128)(2,1)S(1)}, bf16[4,32,256]{2,1,0:T(8,128)(2,1)S(1)}, u32[]{:S(2)}, u32[]{:S(2)}) collective-permute-start(bf16[4,32,256]{2,1,0:T(8,128)(2,1)S(1)} %collective-permute-done.26.refs_3_), channel_id=1, source_target_pairs={{0,1},{1,0},{2,3},{3,2},{4,5},{5,4},{6,7},{7,6},{8,9},{9,8},{10,11... | collective-permute-start | bytes 196616 | tf_op jit(solution)/shard_map/ppermute | solution.py:375
  106.3 1.3 collective-permute-start.30
  108.0 1.3 collective-permute-start.29
  109.5 1.3 collective-permute-start.33
  111.3 2.2 %collective-permute-start.37 = (bf16[4,32,256]{2,1,0:T(8,128)(2,1)S(1)}, bf16[4,32,256]{2,1,0:T(8,128)(2,1)S(1)}, u32[]{:S(2)}, u32[]{:S(2)}) collective-permute-start(bf16[4,32,256]{2,1,0:T(8,128)(2,1)S(1)} %collective-permute-done.29.refs_6_), channel_id=1, source_target_pairs={{0,1},{1,0},{2,3},{3,2},{4,5},{5,4},{6,7},{7,6},{8,9},{9,8},{10,11... | collective-permute-start | bytes 196616 | tf_op jit(solution)/shard_map/ppermute | solution.py:375
  113.6 1.0 collective-permute-start.36
  115.4 11.4 %vector_and_sigma_2.1 = (f32[8,256,256]{2,1,0:T(8,128)}, bf16[8,256,256]{2,1,0:T(8,128)(2,1)}, f32[16,128]{1,0:T(8,128)S(1)}, f32[4,64,128]{2,1,0:T(8,128)S(1)},...) custom-call(s32[75]{0:T(128)S(1)} %concatenate.29.meta, ...), custom_call_target="tpu_custom_call" | custom-call | tf_op jit(solution)/shard_map/vector_and_sigma_2/pallas_call | solution.py:400
  127.7 1.7 %collective-permute-start.45 = (f32[16,128]{1,0:T(8,128)S(1)}, f32[16,128]{1,0:T(8,128)S(1)}, u32[]{:S(2)}, u32[]{:S(2)}) collective-permute-start(f32[16,128]{1,0:T(8,128)S(1)} %get-tuple-element.41), channel_id=1, source_target_pairs={{0,12},{4,8},{8,4},{12,0},{1,13},{5,9},{9,5},{13,1},{2,14},{6,10},... | collective-permute-start | bytes 24584 | tf_op jit(solution)/shard_map/ppermute | solution.py:430
  129.6 1.5 copy.13
  131.1 0.9 collective-permute-done.45
  132.0 1.1 collective-permute-done.44
  133.1 1.1 collective-permute-start.46
  134.8 1.5 %collective-permute-start.40 = (bf16[4,64,128]{2,1,0:T(8,128)(2,1)S(1)}, bf16[4,64,128]{2,1,0:T(8,128)(2,1)S(1)}, u32[]{:S(2)}, u32[]{:S(2)}) collective-permute-start(bf16[4,64,128]{2,1,0:T(8,128)(2,1)S(1)} %get-tuple-element.38), channel_id=1, source_target_pairs={{0,8},{4,12},{8,0},{12,4},{1,9},{5,13},{9,1},{13,5},{2,10},{6,14},... | collective-permute-start | bytes 196616 | tf_op jit(solution)/shard_map/ppermute | solution.py:429
  136.3 2.0 %collective-permute-start.41 = (bf16[4,64,128]{2,1,0:T(8,128)(2,1)S(1)}, bf16[4,64,128]{2,1,0:T(8,128)(2,1)S(1)}, u32[]{:S(2)}, u32[]{:S(2)}) collective-permute-start(bf16[4,64,128]{2,1,0:T(8,128)(2,1)S(1)} %get-tuple-element.39), channel_id=1, source_target_pairs={{0,12},{4,8},{8,4},{12,0},{1,13},{5,9},{9,5},{13,1},{2,14},{6,10},... | collective-permute-start | bytes 196616 | tf_op jit(solution)/shard_map/ppermute | solution.py:429
  138.4 2.9 %collective-permute-start.47 = (f32[16,128]{1,0:T(8,128)S(1)}, f32[16,128]{1,0:T(8,128)S(1)}, u32[]{:S(2)}, u32[]{:S(2)}) collective-permute-start(f32[16,128]{1,0:T(8,128)S(1)} %add.136), channel_id=1, source_target_pairs={{0,1},{1,0},{2,3},{3,2},{4,5},{5,4},{6,7},{7,6},{8,9},{9,8},{10,11... | collective-permute-start | bytes 24584 | tf_op jit(solution)/shard_map/ppermute | solution.py:436
  141.3 3.8 %maximum_bitcast_fusion = (f32[1,3]{1,0:T(1,128)S(1)}, f32[1,3]{1,0:T(1,128)S(1)}) fusion(f32[1]{0:T(128)} %bitcast.22, f32[1]{0:T(128)} %bitcast.21, f32[1]{0:T(128)} %bitcast.20, f32[1]{0:T(128)} %bitcast.26, f32[1]{0:T(128)} %bitcast.25, f32[1]{0:T(128)} %bitcast.24), kind=kLoop, calls=%fused_computation.14 | loop fusion | flops 12 | bytes 48 | tf_op jit(solution)/shard_map/stack | solution.py:447
  146.4 2.7 %collective-permute-done.42 = bf16[4,64,128]{2,1,0:T(8,128)(2,1)S(1)} collective-permute-done((bf16[4,64,128]{2,1,0:T(8,128)(2,1)S(1)}, bf16[4,64,128]{2,1,0:T(8,128)(2,1)S(1)}, u32[]{:S(2)}, u32[]{:S(2)}) %collective-permute-start.42) | collective-permute-done | bytes 65568 | tf_op jit(solution)/shard_map/ppermute | solution.py:434
  149.1 0.9 pad_maximum_fusion
  (82 shorter events, 12.5 us)
Async XLA Ops:
  0.6 47.8 %collective-permute-start.2 = (bf16[8,4,128,256]{3,2,1,0:T(8,128)(2,1)}, bf16[8,4,128,256]{3,2,1,0:T(8,128)(2,1)}, u32[]{:S(2)}, u32[]{:S(2)}) collective-permute-start(bf16[8,4,128,256]{3,2,1,0:T(8,128)(2,1)} %refs_21_.1), channel_id=1, source_target_pairs={{0,2},{2,0},{1,3},{3,1},{4,6},{6,4},{5,7},{7,5},{8,10},{10,8},{9,1... | collective-permute-start | bytes 6291464 | tf_op jit(solution)/shard_map/ppermute | solution.py:308
  2.7 4.2 %collective-permute-start.1 = (f32[4,256,256]{2,1,0:T(8,128)}, f32[4,256,256]{2,1,0:T(8,128)S(1)}, u32[]{:S(2)}, u32[]{:S(2)}) collective-permute-start(f32[4,256,256]{2,1,0:T(8,128)} %pre.1), channel_id=1, source_target_pairs={{0,1},{1,0},{2,3},{3,2},{4,5},{5,4},{6,7},{7,6},{8,9},{9,8},{10,11... | collective-permute-start | bytes 3145736 | tf_op jit(solution)/shard_map/ppermute | solution.py:309
  3.7 3.2 %collective-permute-start = (bf16[4,256,256]{2,1,0:T(8,128)(2,1)}, bf16[4,256,256]{2,1,0:T(8,128)(2,1)S(1)}, u32[]{:S(2)}, u32[]{:S(2)}) collective-permute-start(bf16[4,256,256]{2,1,0:T(8,128)(2,1)} %psi.1), channel_id=1, source_target_pairs={{0,1},{1,0},{2,3},{3,2},{4,5},{5,4},{6,7},{7,6},{8,9},{9,8},{10,11... | collective-permute-start | bytes 1572872 | tf_op jit(solution)/shard_map/ppermute | solution.py:309
  52.3 3.6 %collective-permute-start.3 = (bf16[4,32,256]{2,1,0:T(8,128)(2,1)S(1)}, bf16[4,32,256]{2,1,0:T(8,128)(2,1)S(1)}, u32[]{:S(2)}, u32[]{:S(2)}) collective-permute-start(bf16[4,32,256]{2,1,0:T(8,128)(2,1)S(1)} %get-tuple-element.24), channel_id=1, source_target_pairs={{0,4},{4,0},{8,12},{12,8},{1,5},{5,1},{9,13},{13,9},{2,6},{6,2},{1... | collective-permute-start | bytes 196616 | tf_op jit(solution)/shard_map/ppermute | solution.py:361
  53.6 4.7 %collective-permute-start.4 = (bf16[4,32,256]{2,1,0:T(8,128)(2,1)S(1)}, bf16[4,32,256]{2,1,0:T(8,128)(2,1)S(1)}, u32[]{:S(2)}, u32[]{:S(2)}) collective-permute-start(bf16[4,32,256]{2,1,0:T(8,128)(2,1)S(1)} %get-tuple-element.25), channel_id=1, source_target_pairs={{0,8},{4,12},{8,0},{12,4},{1,9},{5,13},{9,1},{13,5},{2,10},{6,14},... | collective-permute-start | bytes 196616 | tf_op jit(solution)/shard_map/ppermute | solution.py:361
  55.9 5.0 %collective-permute-start.5 = (bf16[4,32,256]{2,1,0:T(8,128)(2,1)S(1)}, bf16[4,32,256]{2,1,0:T(8,128)(2,1)S(1)}, u32[]{:S(2)}, u32[]{:S(2)}) collective-permute-start(bf16[4,32,256]{2,1,0:T(8,128)(2,1)S(1)} %get-tuple-element.26), channel_id=1, source_target_pairs={{0,12},{4,8},{8,4},{12,0},{1,13},{5,9},{9,5},{13,1},{2,14},{6,10},... | collective-permute-start | bytes 196616 | tf_op jit(solution)/shard_map/ppermute | solution.py:361
  61.0 8.5 %collective-permute-start.9 = (bf16[4,32,256]{2,1,0:T(8,128)(2,1)S(1)}, bf16[4,32,256]{2,1,0:T(8,128)(2,1)S(1)}, u32[]{:S(2)}, u32[]{:S(2)}) collective-permute-start(bf16[4,32,256]{2,1,0:T(8,128)(2,1)S(1)} %select_convert_fusion.1.refs_0_), channel_id=1, source_target_pairs={{0,2},{2,0},{1,3},{3,1},{4,6},{6,4},{5,7},{7,5},{8,10},{10,8},{9,1... | collective-permute-start | bytes 196616 | tf_op jit(solution)/shard_map/ppermute | solution.py:374
  62.3 7.8 %collective-permute-start.8 = (bf16[4,32,256]{2,1,0:T(8,128)(2,1)S(1)}, bf16[4,32,256]{2,1,0:T(8,128)(2,1)S(1)}, u32[]{:S(2)}, u32[]{:S(2)}) collective-permute-start(bf16[4,32,256]{2,1,0:T(8,128)(2,1)S(1)} %select_convert_fusion.1.refs_0_), channel_id=1, source_target_pairs={{0,12},{4,8},{8,4},{12,0},{1,13},{5,9},{9,5},{13,1},{2,14},{6,10},... | collective-permute-start | bytes 196616 | tf_op jit(solution)/shard_map/ppermute | solution.py:373
  63.3 9.3 %collective-permute-start.13 = (bf16[4,32,256]{2,1,0:T(8,128)(2,1)S(1)}, bf16[4,32,256]{2,1,0:T(8,128)(2,1)S(1)}, u32[]{:S(2)}, u32[]{:S(2)}) collective-permute-start(bf16[4,32,256]{2,1,0:T(8,128)(2,1)S(1)} %select_convert_fusion.1.refs_0_), channel_id=1, source_target_pairs={{0,1},{1,0},{2,3},{3,2},{4,5},{5,4},{6,7},{7,6},{8,9},{9,8},{10,11... | collective-permute-start | bytes 196616 | tf_op jit(solution)/shard_map/ppermute | solution.py:375
  66.6 6.6 %collective-permute-start.7 = (bf16[4,32,256]{2,1,0:T(8,128)(2,1)S(1)}, bf16[4,32,256]{2,1,0:T(8,128)(2,1)S(1)}, u32[]{:S(2)}, u32[]{:S(2)}) collective-permute-start(bf16[4,32,256]{2,1,0:T(8,128)(2,1)S(1)} %select_convert_fusion.1.refs_0_), channel_id=1, source_target_pairs={{0,8},{4,12},{8,0},{12,4},{1,9},{5,13},{9,1},{13,5},{2,10},{6,14},... | collective-permute-start | bytes 196616 | tf_op jit(solution)/shard_map/ppermute | solution.py:373
  66.8 7.4 %collective-permute-start.6 = (bf16[4,32,256]{2,1,0:T(8,128)(2,1)S(1)}, bf16[4,32,256]{2,1,0:T(8,128)(2,1)S(1)}, u32[]{:S(2)}, u32[]{:S(2)}) collective-permute-start(bf16[4,32,256]{2,1,0:T(8,128)(2,1)S(1)} %select_convert_fusion.1.refs_0_), channel_id=1, source_target_pairs={{0,4},{4,0},{8,12},{12,8},{1,5},{5,1},{9,13},{13,9},{2,6},{6,2},{1... | collective-permute-start | bytes 196616 | tf_op jit(solution)/shard_map/ppermute | solution.py:373
  69.6 5.1 %collective-permute-start.17 = (bf16[4,32,256]{2,1,0:T(8,128)(2,1)S(1)}, bf16[4,32,256]{2,1,0:T(8,128)(2,1)S(1)}, u32[]{:S(2)}, u32[]{:S(2)}) collective-permute-start(bf16[4,32,256]{2,1,0:T(8,128)(2,1)S(1)} %collective-permute-done.9.refs_4_), channel_id=1, source_target_pairs={{0,1},{1,0},{2,3},{3,2},{4,5},{5,4},{6,7},{7,6},{8,9},{9,8},{10,11... | collective-permute-start | bytes 196616 | tf_op jit(solution)/shard_map/ppermute | solution.py:375
  70.1 6.1 %collective-permute-start.16 = (bf16[4,32,256]{2,1,0:T(8,128)(2,1)S(1)}, bf16[4,32,256]{2,1,0:T(8,128)(2,1)S(1)}, u32[]{:S(2)}, u32[]{:S(2)}) collective-permute-start(bf16[4,32,256]{2,1,0:T(8,128)(2,1)S(1)} %collective-permute-done.8.refs_3_), channel_id=1, source_target_pairs={{0,1},{1,0},{2,3},{3,2},{4,5},{5,4},{6,7},{7,6},{8,9},{9,8},{10,11... | collective-permute-start | bytes 196616 | tf_op jit(solution)/shard_map/ppermute | solution.py:375
  72.7 3.7 %collective-permute-start.12 = (bf16[4,32,256]{2,1,0:T(8,128)(2,1)S(1)}, bf16[4,32,256]{2,1,0:T(8,128)(2,1)S(1)}, u32[]{:S(2)}, u32[]{:S(2)}) collective-permute-start(bf16[4,32,256]{2,1,0:T(8,128)(2,1)S(1)} %collective-permute-done.8.refs_3_), channel_id=1, source_target_pairs={{0,2},{2,0},{1,3},{3,1},{4,6},{6,4},{5,7},{7,5},{8,10},{10,8},{9,1... | collective-permute-start | bytes 196616 | tf_op jit(solution)/shard_map/ppermute | solution.py:374
  73.2 4.4 %collective-permute-start.11 = (bf16[4,32,256]{2,1,0:T(8,128)(2,1)S(1)}, bf16[4,32,256]{2,1,0:T(8,128)(2,1)S(1)}, u32[]{:S(2)}, u32[]{:S(2)}) collective-permute-start(bf16[4,32,256]{2,1,0:T(8,128)(2,1)S(1)} %collective-permute-done.7.refs_2_), channel_id=1, source_target_pairs={{0,2},{2,0},{1,3},{3,1},{4,6},{6,4},{5,7},{7,5},{8,10},{10,8},{9,1... | collective-permute-start | bytes 196616 | tf_op jit(solution)/shard_map/ppermute | solution.py:374
  74.1 5.1 %collective-permute-start.10 = (bf16[4,32,256]{2,1,0:T(8,128)(2,1)S(1)}, bf16[4,32,256]{2,1,0:T(8,128)(2,1)S(1)}, u32[]{:S(2)}, u32[]{:S(2)}) collective-permute-start(bf16[4,32,256]{2,1,0:T(8,128)(2,1)S(1)} %collective-permute-done.6.refs_1_), channel_id=1, source_target_pairs={{0,2},{2,0},{1,3},{3,1},{4,6},{6,4},{5,7},{7,5},{8,10},{10,8},{9,1... | collective-permute-start | bytes 196616 | tf_op jit(solution)/shard_map/ppermute | solution.py:374
  74.7 5.3 %collective-permute-start.15 = (bf16[4,32,256]{2,1,0:T(8,128)(2,1)S(1)}, bf16[4,32,256]{2,1,0:T(8,128)(2,1)S(1)}, u32[]{:S(2)}, u32[]{:S(2)}) collective-permute-start(bf16[4,32,256]{2,1,0:T(8,128)(2,1)S(1)} %collective-permute-done.7.refs_2_), channel_id=1, source_target_pairs={{0,1},{1,0},{2,3},{3,2},{4,5},{5,4},{6,7},{7,6},{8,9},{9,8},{10,11... | collective-permute-start | bytes 196616 | tf_op jit(solution)/shard_map/ppermute | solution.py:375
  76.2 3.8 %collective-permute-start.14 = (bf16[4,32,256]{2,1,0:T(8,128)(2,1)S(1)}, bf16[4,32,256]{2,1,0:T(8,128)(2,1)S(1)}, u32[]{:S(2)}, u32[]{:S(2)}) collective-permute-start(bf16[4,32,256]{2,1,0:T(8,128)(2,1)S(1)} %collective-permute-done.6.refs_1_), channel_id=1, source_target_pairs={{0,1},{1,0},{2,3},{3,2},{4,5},{5,4},{6,7},{7,6},{8,9},{9,8},{10,11... | collective-permute-start | bytes 196616 | tf_op jit(solution)/shard_map/ppermute | solution.py:375
  76.4 3.6 %collective-permute-start.20 = (bf16[4,32,256]{2,1,0:T(8,128)(2,1)S(1)}, bf16[4,32,256]{2,1,0:T(8,128)(2,1)S(1)}, u32[]{:S(2)}, u32[]{:S(2)}) collective-permute-start(bf16[4,32,256]{2,1,0:T(8,128)(2,1)S(1)} %collective-permute-done.12.refs_7_), channel_id=1, source_target_pairs={{0,1},{1,0},{2,3},{3,2},{4,5},{5,4},{6,7},{7,6},{8,9},{9,8},{10,11... | collective-permute-start | bytes 196616 | tf_op jit(solution)/shard_map/ppermute | solution.py:375
  77.5 2.5 %collective-permute-start.19 = (bf16[4,32,256]{2,1,0:T(8,128)(2,1)S(1)}, bf16[4,32,256]{2,1,0:T(8,128)(2,1)S(1)}, u32[]{:S(2)}, u32[]{:S(2)}) collective-permute-start(bf16[4,32,256]{2,1,0:T(8,128)(2,1)S(1)} %collective-permute-done.11.refs_6_), channel_id=1, source_target_pairs={{0,1},{1,0},{2,3},{3,2},{4,5},{5,4},{6,7},{7,6},{8,9},{9,8},{10,11... | collective-permute-start | bytes 196616 | tf_op jit(solution)/shard_map/ppermute | solution.py:375
  79.2 1.7 %collective-permute-start.18 = (bf16[4,32,256]{2,1,0:T(8,128)(2,1)S(1)}, bf16[4,32,256]{2,1,0:T(8,128)(2,1)S(1)}, u32[]{:S(2)}, u32[]{:S(2)}) collective-permute-start(bf16[4,32,256]{2,1,0:T(8,128)(2,1)S(1)} %collective-permute-done.10.refs_5_), channel_id=1, source_target_pairs={{0,1},{1,0},{2,3},{3,2},{4,5},{5,4},{6,7},{7,6},{8,9},{9,8},{10,11... | collective-permute-start | bytes 196616 | tf_op jit(solution)/shard_map/ppermute | solution.py:375
  89.7 3.6 %collective-permute-start.21 = (bf16[4,32,256]{2,1,0:T(8,128)(2,1)S(1)}, bf16[4,32,256]{2,1,0:T(8,128)(2,1)S(1)}, u32[]{:S(2)}, u32[]{:S(2)}) collective-permute-start(bf16[4,32,256]{2,1,0:T(8,128)(2,1)S(1)} %get-tuple-element.31), channel_id=1, source_target_pairs={{0,4},{4,0},{8,12},{12,8},{1,5},{5,1},{9,13},{13,9},{2,6},{6,2},{1... | collective-permute-start | bytes 196616 | tf_op jit(solution)/shard_map/ppermute | solution.py:361
  89.7 4.2 %collective-permute-start.22 = (bf16[4,32,256]{2,1,0:T(8,128)(2,1)S(1)}, bf16[4,32,256]{2,1,0:T(8,128)(2,1)S(1)}, u32[]{:S(2)}, u32[]{:S(2)}) collective-permute-start(bf16[4,32,256]{2,1,0:T(8,128)(2,1)S(1)} %get-tuple-element.32), channel_id=1, source_target_pairs={{0,8},{4,12},{8,0},{12,4},{1,9},{5,13},{9,1},{13,5},{2,10},{6,14},... | collective-permute-start | bytes 196616 | tf_op jit(solution)/shard_map/ppermute | solution.py:361
  90.9 5.5 %collective-permute-start.23 = (bf16[4,32,256]{2,1,0:T(8,128)(2,1)S(1)}, bf16[4,32,256]{2,1,0:T(8,128)(2,1)S(1)}, u32[]{:S(2)}, u32[]{:S(2)}) collective-permute-start(bf16[4,32,256]{2,1,0:T(8,128)(2,1)S(1)} %get-tuple-element.33), channel_id=1, source_target_pairs={{0,12},{4,8},{8,4},{12,0},{1,13},{5,9},{9,5},{13,1},{2,14},{6,10},... | collective-permute-start | bytes 196616 | tf_op jit(solution)/shard_map/ppermute | solution.py:361
  96.5 9.8 %collective-permute-start.31 = (bf16[4,32,256]{2,1,0:T(8,128)(2,1)S(1)}, bf16[4,32,256]{2,1,0:T(8,128)(2,1)S(1)}, u32[]{:S(2)}, u32[]{:S(2)}) collective-permute-start(bf16[4,32,256]{2,1,0:T(8,128)(2,1)S(1)} %select_convert_fusion.refs_0_), channel_id=1, source_target_pairs={{0,1},{1,0},{2,3},{3,2},{4,5},{5,4},{6,7},{7,6},{8,9},{9,8},{10,11... | collective-permute-start | bytes 196616 | tf_op jit(solution)/shard_map/ppermute | solution.py:375
  99.0 8.6 %collective-permute-start.27 = (bf16[4,32,256]{2,1,0:T(8,128)(2,1)S(1)}, bf16[4,32,256]{2,1,0:T(8,128)(2,1)S(1)}, u32[]{:S(2)}, u32[]{:S(2)}) collective-permute-start(bf16[4,32,256]{2,1,0:T(8,128)(2,1)S(1)} %select_convert_fusion.refs_0_), channel_id=1, source_target_pairs={{0,2},{2,0},{1,3},{3,1},{4,6},{6,4},{5,7},{7,5},{8,10},{10,8},{9,1... | collective-permute-start | bytes 196616 | tf_op jit(solution)/shard_map/ppermute | solution.py:374
  99.2 5.1 %collective-permute-start.26 = (bf16[4,32,256]{2,1,0:T(8,128)(2,1)S(1)}, bf16[4,32,256]{2,1,0:T(8,128)(2,1)S(1)}, u32[]{:S(2)}, u32[]{:S(2)}) collective-permute-start(bf16[4,32,256]{2,1,0:T(8,128)(2,1)S(1)} %select_convert_fusion.refs_0_), channel_id=1, source_target_pairs={{0,12},{4,8},{8,4},{12,0},{1,13},{5,9},{9,5},{13,1},{2,14},{6,10},... | collective-permute-start | bytes 196616 | tf_op jit(solution)/shard_map/ppermute | solution.py:373
  100.8 7.2 %collective-permute-start.25 = (bf16[4,32,256]{2,1,0:T(8,128)(2,1)S(1)}, bf16[4,32,256]{2,1,0:T(8,128)(2,1)S(1)}, u32[]{:S(2)}, u32[]{:S(2)}) collective-permute-start(bf16[4,32,256]{2,1,0:T(8,128)(2,1)S(1)} %select_convert_fusion.refs_0_), channel_id=1, source_target_pairs={{0,8},{4,12},{8,0},{12,4},{1,9},{5,13},{9,1},{13,5},{2,10},{6,14},... | collective-permute-start | bytes 196616 | tf_op jit(solution)/shard_map/ppermute | solution.py:373
  101.3 7.9 %collective-permute-start.24 = (bf16[4,32,256]{2,1,0:T(8,128)(2,1)S(1)}, bf16[4,32,256]{2,1,0:T(8,128)(2,1)S(1)}, u32[]{:S(2)}, u32[]{:S(2)}) collective-permute-start(bf16[4,32,256]{2,1,0:T(8,128)(2,1)S(1)} %select_convert_fusion.refs_0_), channel_id=1, source_target_pairs={{0,4},{4,0},{8,12},{12,8},{1,5},{5,1},{9,13},{13,9},{2,6},{6,2},{1... | collective-permute-start | bytes 196616 | tf_op jit(solution)/shard_map/ppermute | solution.py:373
  104.2 6.6 %collective-permute-start.34 = (bf16[4,32,256]{2,1,0:T(8,128)(2,1)S(1)}, bf16[4,32,256]{2,1,0:T(8,128)(2,1)S(1)}, u32[]{:S(2)}, u32[]{:S(2)}) collective-permute-start(bf16[4,32,256]{2,1,0:T(8,128)(2,1)S(1)} %collective-permute-done.26.refs_3_), channel_id=1, source_target_pairs={{0,1},{1,0},{2,3},{3,2},{4,5},{5,4},{6,7},{7,6},{8,9},{9,8},{10,11... | collective-permute-start | bytes 196616 | tf_op jit(solution)/shard_map/ppermute | solution.py:375
  106.3 4.6 %collective-permute-start.30 = (bf16[4,32,256]{2,1,0:T(8,128)(2,1)S(1)}, bf16[4,32,256]{2,1,0:T(8,128)(2,1)S(1)}, u32[]{:S(2)}, u32[]{:S(2)}) collective-permute-start(bf16[4,32,256]{2,1,0:T(8,128)(2,1)S(1)} %collective-permute-done.26.refs_3_), channel_id=1, source_target_pairs={{0,2},{2,0},{1,3},{3,1},{4,6},{6,4},{5,7},{7,5},{8,10},{10,8},{9,1... | collective-permute-start | bytes 196616 | tf_op jit(solution)/shard_map/ppermute | solution.py:374
  107.6 1.9 %collective-permute-start.35 = (bf16[4,32,256]{2,1,0:T(8,128)(2,1)S(1)}, bf16[4,32,256]{2,1,0:T(8,128)(2,1)S(1)}, u32[]{:S(2)}, u32[]{:S(2)}) collective-permute-start(bf16[4,32,256]{2,1,0:T(8,128)(2,1)S(1)} %collective-permute-done.27.refs_4_), channel_id=1, source_target_pairs={{0,1},{1,0},{2,3},{3,2},{4,5},{5,4},{6,7},{7,6},{8,9},{9,8},{10,11... | collective-permute-start | bytes 196616 | tf_op jit(solution)/shard_map/ppermute | solution.py:375
  108.0 3.4 %collective-permute-start.29 = (bf16[4,32,256]{2,1,0:T(8,128)(2,1)S(1)}, bf16[4,32,256]{2,1,0:T(8,128)(2,1)S(1)}, u32[]{:S(2)}, u32[]{:S(2)}) collective-permute-start(bf16[4,32,256]{2,1,0:T(8,128)(2,1)S(1)} %collective-permute-done.25.refs_2_), channel_id=1, source_target_pairs={{0,2},{2,0},{1,3},{3,1},{4,6},{6,4},{5,7},{7,5},{8,10},{10,8},{9,1... | collective-permute-start | bytes 196616 | tf_op jit(solution)/shard_map/ppermute | solution.py:374
  109.3 4.3 %collective-permute-start.28 = (bf16[4,32,256]{2,1,0:T(8,128)(2,1)S(1)}, bf16[4,32,256]{2,1,0:T(8,128)(2,1)S(1)}, u32[]{:S(2)}, u32[]{:S(2)}) collective-permute-start(bf16[4,32,256]{2,1,0:T(8,128)(2,1)S(1)} %collective-permute-done.24.refs_1_), channel_id=1, source_target_pairs={{0,2},{2,0},{1,3},{3,1},{4,6},{6,4},{5,7},{7,5},{8,10},{10,8},{9,1... | collective-permute-start | bytes 196616 | tf_op jit(solution)/shard_map/ppermute | solution.py:374
  109.5 5.6 %collective-permute-start.33 = (bf16[4,32,256]{2,1,0:T(8,128)(2,1)S(1)}, bf16[4,32,256]{2,1,0:T(8,128)(2,1)S(1)}, u32[]{:S(2)}, u32[]{:S(2)}) collective-permute-start(bf16[4,32,256]{2,1,0:T(8,128)(2,1)S(1)} %collective-permute-done.25.refs_2_), channel_id=1, source_target_pairs={{0,1},{1,0},{2,3},{3,2},{4,5},{5,4},{6,7},{7,6},{8,9},{9,8},{10,11... | collective-permute-start | bytes 196616 | tf_op jit(solution)/shard_map/ppermute | solution.py:375
  110.8 4.2 %collective-permute-start.32 = (bf16[4,32,256]{2,1,0:T(8,128)(2,1)S(1)}, bf16[4,32,256]{2,1,0:T(8,128)(2,1)S(1)}, u32[]{:S(2)}, u32[]{:S(2)}) collective-permute-start(bf16[4,32,256]{2,1,0:T(8,128)(2,1)S(1)} %collective-permute-done.24.refs_1_), channel_id=1, source_target_pairs={{0,1},{1,0},{2,3},{3,2},{4,5},{5,4},{6,7},{7,6},{8,9},{9,8},{10,11... | collective-permute-start | bytes 196616 | tf_op jit(solution)/shard_map/ppermute | solution.py:375
  110.9 4.1 %collective-permute-start.38 = (bf16[4,32,256]{2,1,0:T(8,128)(2,1)S(1)}, bf16[4,32,256]{2,1,0:T(8,128)(2,1)S(1)}, u32[]{:S(2)}, u32[]{:S(2)}) collective-permute-start(bf16[4,32,256]{2,1,0:T(8,128)(2,1)S(1)} %collective-permute-done.30.refs_7_), channel_id=1, source_target_pairs={{0,1},{1,0},{2,3},{3,2},{4,5},{5,4},{6,7},{7,6},{8,9},{9,8},{10,11... | collective-permute-start | bytes 196616 | tf_op jit(solution)/shard_map/ppermute | solution.py:375
  111.3 3.7 %collective-permute-start.37 = (bf16[4,32,256]{2,1,0:T(8,128)(2,1)S(1)}, bf16[4,32,256]{2,1,0:T(8,128)(2,1)S(1)}, u32[]{:S(2)}, u32[]{:S(2)}) collective-permute-start(bf16[4,32,256]{2,1,0:T(8,128)(2,1)S(1)} %collective-permute-done.29.refs_6_), channel_id=1, source_target_pairs={{0,1},{1,0},{2,3},{3,2},{4,5},{5,4},{6,7},{7,6},{8,9},{9,8},{10,11... | collective-permute-start | bytes 196616 | tf_op jit(solution)/shard_map/ppermute | solution.py:375
  113.6 1.9 %collective-permute-start.36 = (bf16[4,32,256]{2,1,0:T(8,128)(2,1)S(1)}, bf16[4,32,256]{2,1,0:T(8,128)(2,1)S(1)}, u32[]{:S(2)}, u32[]{:S(2)}) collective-permute-start(bf16[4,32,256]{2,1,0:T(8,128)(2,1)S(1)} %collective-permute-done.28.refs_5_), channel_id=1, source_target_pairs={{0,1},{1,0},{2,3},{3,2},{4,5},{5,4},{6,7},{7,6},{8,9},{9,8},{10,11... | collective-permute-start | bytes 196616 | tf_op jit(solution)/shard_map/ppermute | solution.py:375
  126.9 4.2 %collective-permute-start.43 = (f32[16,128]{1,0:T(8,128)S(1)}, f32[16,128]{1,0:T(8,128)S(1)}, u32[]{:S(2)}, u32[]{:S(2)}) collective-permute-start(f32[16,128]{1,0:T(8,128)S(1)} %get-tuple-element.41), channel_id=1, source_target_pairs={{0,4},{4,0},{8,12},{12,8},{1,5},{5,1},{9,13},{13,9},{2,6},{6,2},{1... | collective-permute-start | bytes 24584 | tf_op jit(solution)/shard_map/ppermute | solution.py:430
  127.7 4.3 %collective-permute-start.45 = (f32[16,128]{1,0:T(8,128)S(1)}, f32[16,128]{1,0:T(8,128)S(1)}, u32[]{:S(2)}, u32[]{:S(2)}) collective-permute-start(f32[16,128]{1,0:T(8,128)S(1)} %get-tuple-element.41), channel_id=1, source_target_pairs={{0,12},{4,8},{8,4},{12,0},{1,13},{5,9},{9,5},{13,1},{2,14},{6,10},... | collective-permute-start | bytes 24584 | tf_op jit(solution)/shard_map/ppermute | solution.py:430
  129.4 3.7 %collective-permute-start.44 = (f32[16,128]{1,0:T(8,128)S(1)}, f32[16,128]{1,0:T(8,128)S(1)}, u32[]{:S(2)}, u32[]{:S(2)}) collective-permute-start(f32[16,128]{1,0:T(8,128)S(1)} %get-tuple-element.41), channel_id=1, source_target_pairs={{0,8},{4,12},{8,0},{12,4},{1,9},{5,13},{9,1},{13,5},{2,10},{6,14},... | collective-permute-start | bytes 24584 | tf_op jit(solution)/shard_map/ppermute | solution.py:430
  133.1 5.3 %collective-permute-start.46 = (f32[16,128]{1,0:T(8,128)S(1)}, f32[16,128]{1,0:T(8,128)S(1)}, u32[]{:S(2)}, u32[]{:S(2)}) collective-permute-start(f32[16,128]{1,0:T(8,128)S(1)} %add_add_fusion), channel_id=1, source_target_pairs={{0,2},{2,0},{1,3},{3,1},{4,6},{6,4},{5,7},{7,5},{8,10},{10,8},{9,1... | collective-permute-start | bytes 24584 | tf_op jit(solution)/shard_map/ppermute | solution.py:435
  134.8 10.4 %collective-permute-start.39 = (bf16[4,64,128]{2,1,0:T(8,128)(2,1)S(1)}, bf16[4,64,128]{2,1,0:T(8,128)(2,1)S(1)}, u32[]{:S(2)}, u32[]{:S(2)}) collective-permute-start(bf16[4,64,128]{2,1,0:T(8,128)(2,1)S(1)} %get-tuple-element.37), channel_id=1, source_target_pairs={{0,4},{4,0},{8,12},{12,8},{1,5},{5,1},{9,13},{13,9},{2,6},{6,2},{1... | collective-permute-start | bytes 196616 | tf_op jit(solution)/shard_map/ppermute | solution.py:429
  134.8 10.4 %collective-permute-start.40 = (bf16[4,64,128]{2,1,0:T(8,128)(2,1)S(1)}, bf16[4,64,128]{2,1,0:T(8,128)(2,1)S(1)}, u32[]{:S(2)}, u32[]{:S(2)}) collective-permute-start(bf16[4,64,128]{2,1,0:T(8,128)(2,1)S(1)} %get-tuple-element.38), channel_id=1, source_target_pairs={{0,8},{4,12},{8,0},{12,4},{1,9},{5,13},{9,1},{13,5},{2,10},{6,14},... | collective-permute-start | bytes 196616 | tf_op jit(solution)/shard_map/ppermute | solution.py:429
  136.3 8.9 %collective-permute-start.41 = (bf16[4,64,128]{2,1,0:T(8,128)(2,1)S(1)}, bf16[4,64,128]{2,1,0:T(8,128)(2,1)S(1)}, u32[]{:S(2)}, u32[]{:S(2)}) collective-permute-start(bf16[4,64,128]{2,1,0:T(8,128)(2,1)S(1)} %get-tuple-element.39), channel_id=1, source_target_pairs={{0,12},{4,8},{8,4},{12,0},{1,13},{5,9},{9,5},{13,1},{2,14},{6,10},... | collective-permute-start | bytes 196616 | tf_op jit(solution)/shard_map/ppermute | solution.py:429
  138.4 6.7 %collective-permute-start.47 = (f32[16,128]{1,0:T(8,128)S(1)}, f32[16,128]{1,0:T(8,128)S(1)}, u32[]{:S(2)}, u32[]{:S(2)}) collective-permute-start(f32[16,128]{1,0:T(8,128)S(1)} %add.136), channel_id=1, source_target_pairs={{0,1},{1,0},{2,3},{3,2},{4,5},{5,4},{6,7},{7,6},{8,9},{9,8},{10,11... | collective-permute-start | bytes 24584 | tf_op jit(solution)/shard_map/ppermute | solution.py:436
  145.4 3.7 %collective-permute-start.42 = (bf16[4,64,128]{2,1,0:T(8,128)(2,1)S(1)}, bf16[4,64,128]{2,1,0:T(8,128)(2,1)S(1)}, u32[]{:S(2)}, u32[]{:S(2)}) collective-permute-start(bf16[4,64,128]{2,1,0:T(8,128)(2,1)S(1)} %get-tuple-element.43), channel_id=1, source_target_pairs={{0,2},{2,0},{1,3},{3,1},{4,6},{6,4},{5,7},{7,5},{8,10},{10,8},{9,1... | collective-permute-start | bytes 196616 | tf_op jit(solution)/shard_map/ppermute | solution.py:434
  (3 other events, 3.9 us)

commit v3 on v0

v3 whole, which is shorter than its diff:
```python
import functools

import jax
import jax.numpy as jnp
from jax import lax
from jax.experimental import pallas as pl
from jax.experimental.pallas import tpu as pltpu
from jax.sharding import PartitionSpec as P

ITERS = 3
EPS = 1e-06
F32, BF16 = jnp.float32, jnp.bfloat16
ROWS = 64
TAIL_ROWS = 16
VMEM_LIMIT = 32 * 1024 * 1024
HB, VM, SM = pltpu.HBM, pltpu.VMEM, pltpu.SMEM


def _specs(*shapes):
    return [pl.BlockSpec(memory_space=s) for s in shapes]


def _hbm(*arrays):
    return [pltpu.with_memory_space_constraint(x, HB) for x in arrays]


def _vmem(*arrays):
    return [pltpu.with_memory_space_constraint(x, VM) for x in arrays]


def _fold(x):
    return jnp.sum(x.reshape(x.shape[0] // 8, 8, x.shape[1]), axis=0)


def _over(n_sec, states, width, n_acc, body):
    blocks = states // ROWS

    def step(i, accs):
        for b in range(blocks):
            accs = tuple(x + y for x, y in zip(accs, body(i, slice(b * ROWS, (b + 1) * ROWS))))
        return accs

    zero = tuple(jnp.zeros((8, width), F32) for _ in range(n_acc))
    return tuple(jnp.sum(a) for a in lax.fori_loop(0, n_sec, step, zero))


def _low(cfg, value, env_pos):
    low = value.astype(BF16)
    if cfg["direct"]:
        half = value.shape[1] // 2
        turned = jnp.concatenate([value[:, half:], value[:, :half]], axis=1).astype(BF16)
        low = jnp.where(env_pos == 0, low, turned)
    return low


def _put_scalars(ref, values):
    shape = ref.shape
    row = lax.broadcasted_iota(jnp.int32, shape, 0)
    out = jnp.zeros(shape, F32)
    for index, value in enumerate(values):
        out = jnp.where(row == index, value, out)
    ref[...] = out


def _emit(cfg, meta, acc, outs):
    if cfg["direct"]:
        part, z = cfg["part"], meta[1]
        for s in range(cfg["n_term"]):
            rows = pl.ds(pl.multiple_of((z ^ s) * part, part), part)
            outs[s][...] = acc[:, rows, :].astype(outs[s].dtype)
    else:
        outs[0][...] = acc[...]


def _first_kernel(cfg, meta, psi, psi_o, pre, pre_o, right, start, pret, inner, scale_ref, vb):
    sec, states, width = psi.shape
    n_sec = sec * cfg["n_blk"]
    blk, env_pos = meta[2], meta[0]
    base = blk * sec
    for part, (p_ref, c_ref) in enumerate(((psi, pre), (psi_o, pre_o))):
        for k in range(p_ref.shape[0]):
            at = lax.rem(base + part * sec + k, n_sec)
            live = meta[cfg["dims_at"] + at]
            row = lax.broadcasted_iota(jnp.int32, (states, width), 0)
            col = lax.broadcasted_iota(jnp.int32, (states, width), 1)
            value = jnp.where((row < live) & (col < live), p_ref[k].astype(F32).T, 0.0)
            start[at] = value.astype(BF16)
            pret[at] = c_ref[k].T

    def square(s, r):
        value = start[s, r, :].astype(F32)
        return (_fold(value * value),)

    (total,) = _over(n_sec, states, width, 1, square)
    scale = lax.rsqrt(total / (n_sec * states * width) + EPS)
    _put_scalars(scale_ref, [scale] * 8)

    def make(s, r):
        vb[s, r, :] = _low(cfg, start[s, r, :].astype(F32) * scale, env_pos)
        return ()

    _over(n_sec, states, width, 0, make)
    for k in range(sec):
        for t in range(right.shape[0]):
            chosen = vb[meta[cfg["pair_at"] + t * sec + k]]
            inner[t, k] = jnp.dot(right[t, k], chosen, preferred_element_type=F32).astype(BF16)


def _second_kernel(cfg, k0, n_left, meta, inner, *refs):
    lefts, far_h, outs = refs[: n_left - 1], refs[n_left - 1], refs[n_left:-3]
    far, acc, sem = refs[-3:]
    terms, count = far.shape[:2]
    move = pltpu.make_async_copy(far_h, far, sem)
    move.start()
    move.wait()
    for k in range(count):
        total = None
        for t in range(terms):
            left = jnp.concatenate([ref[t, k0 + k] for ref in lefts] + [far[t, k]], axis=0)
            got = jnp.dot(inner[t, k0 + k], left, preferred_element_type=F32)
            total = got if total is None else total + got
        acc[k] = total
    _emit(cfg, meta, acc, outs)


def _step_kernel(cfg, step, places, chunks, n_near, last, meta, *refs):
    it = iter(refs)
    take = lambda n: [next(it) for _ in range(n)]
    shards = take(len(places))
    (start, scale_ref), vecs, (pre,) = take(2), take(step - 1), take(1)
    olds_h, (right_h,), near_h, far_h = take(step - 1), take(1), take(n_near), take(len(chunks))
    (sig_h,) = take(1)
    vnew, dots = (None, None) if last else take(2)
    outs = take(cfg["n_out"])
    if last:
        vnew, turned = take(2)
    olds, (right,), near, (far,) = take(step - 1), take(1), take(n_near), take(1)
    sig, vb, acc, sem = take(4)
    env_pos, z, blk = meta[0], meta[1], meta[2]
    n_sec, states, width = vnew.shape
    sec, half, part = cfg["sec"], right.shape[2], cfg["part"]
    count = n_sec * states * width
    moves = [*zip(olds_h, olds), (right_h, right), *zip(near_h, near)]
    moves += [(h, far.at[:, k0 : k0 + nk]) for (k0, nk), h in zip(chunks, far_h)]
    moves = [pltpu.make_async_copy(a, b, sem.at[i]) for i, (a, b) in enumerate(moves)]
    for c in moves:
        c.start()
    save = pltpu.make_async_copy(sig, sig_h, sem.at[len(moves)])
    scale0 = scale_ref[0, 0]
    basis = [lambda s, r: start[s, r, :].astype(F32) * scale0]
    basis += [lambda s, r, v=v: v[s, r, :] for v in vecs]

    pairs = [(j, l) for j in range(step) for l in range(j, step)]
    accs = [jnp.zeros((8, width), F32) for _ in range(2 * step + len(pairs))]
    blocks = []
    for ref, place in zip(shards, places):
        if place is None:
            for s in range(n_sec):
                for r in range(0, states, ROWS):
                    blocks.append((ref, (s, slice(r, r + ROWS)), s, slice(r, r + ROWS)))
            continue
        b, e, hops, k0 = place
        for m, s in enumerate(hops):
            rows = pl.ds(pl.multiple_of((env_pos ^ e) * half + (z ^ s) * part, part), part)
            for k in range(ref.shape[1]):
                blocks.append((ref, (m, k), (blk ^ b) * sec + k0 + k, rows))
    for ref, at, s, r in blocks:
        low = ref[at]
        sig[s, r, :] = low
        value, cond = low.astype(F32), pre[s, r, :]
        scaled = value * cond
        held = [b(s, r) for b in basis]
        terms_ = [_fold(h * value) for h in held] + [_fold(h * scaled) for h in held]
        condh = [h * cond for h in held]
        terms_ += [_fold(condh[j] * held[l]) for j, l in pairs]
        accs = [a + t for a, t in zip(accs, terms_)]
    save.start()
    sums = [jnp.sum(a) / count for a in accs]
    proj = sums[:step]
    gram = {}
    for (j, l), value in zip(pairs, sums[2 * step :]):
        gram[j, l] = gram[l, j] = value
    back = [sums[step + j] - sum(proj[l] * gram[j, l] for l in range(step)) for j in range(step)]

    over = functools.partial(_over, n_sec, states, width)
    for c in moves[: step - 1]:
        c.wait()

    def trial_pass(s, r):
        value = sig[s, r, :].astype(F32)
        held = [b(s, r) for b in basis]
        trial = value
        for h, b in zip(proj, held):
            trial = trial - h * b
        trial = trial * pre[s, r, :]
        for g, b in zip(back, held):
            trial = trial - g * b
        vnew[s, r, :] = trial
        crossed = [o[s, r, :].astype(F32) for o in olds] + [value]
        return (_fold(trial * trial), *[_fold(trial * o) for o in crossed])

    square, *cross = over(1 + step, trial_pass)
    scale = lax.rsqrt(square / count + EPS)
    cross = [x * scale / count for x in cross]

    def final_pass(s, r):
        value = vnew[s, r, :] * scale
        vnew[s, r, :] = value
        vb[s, r, :] = _low(cfg, value, env_pos)
        return ()

    over(0, final_pass)
    for c in moves[step - 1 :]:
        c.wait()
    for k in range(sec):
        total = None
        for t in range(right.shape[0]):
            chosen = vb[meta[cfg["pair_at"] + t * sec + k]]
            inner = jnp.dot(right[t, k], chosen, preferred_element_type=F32).astype(BF16)
            left = jnp.concatenate([ref[t, k] for ref in [*near, far]], axis=0)
            got = jnp.dot(inner, left, preferred_element_type=F32)
            total = got if total is None else total + got
        acc[k] = total
    scalars = proj + cross
    if not last:
        _emit(cfg, meta, acc, outs)
        _put_scalars(dots, scalars)
        save.wait()
        return

    rows = pl.ds(pl.multiple_of(env_pos * half, half), half)
    mine = []
    for b in [*basis, lambda s, r: vnew[s, r, :]]:
        total = jnp.zeros((8, width), F32)
        for k in range(sec):
            total = total + _fold(b(blk * sec + k, rows) * acc[k])
        mine.append(jnp.sum(total) / count)
    known, pieces = outs[0], outs[1:]
    _put_scalars(known, scalars)
    for k in range(sec):
        turned[k] = acc[k].T
    chunk = states // cfg["n_term"]
    if cfg["direct"]:
        for s in range(cfg["n_term"]):
            rows = pl.ds(pl.multiple_of((z ^ s) * chunk, chunk), chunk)
            for k in range(sec):
                pieces[s][k * chunk : (k + 1) * chunk, :] = turned[k, rows, :].astype(pieces[s].dtype)
            row = lax.broadcasted_iota(jnp.int32, (TAIL_ROWS, half), 0)
            tail = jnp.zeros((TAIL_ROWS, half), F32)
            for j, value in enumerate(mine):
                rest = jnp.full((TAIL_ROWS, half), value, F32)
                for p in range(3):
                    cut = rest.astype(BF16).astype(F32)
                    tail = jnp.where(row == 3 * j + p, cut, tail)
                    rest = rest - cut
            pieces[s][sec * chunk :, :] = tail.astype(pieces[s].dtype)
    else:
        pieces[0][...] = turned[...]
        _put_scalars(pieces[1], mine)
    save.wait()


def _rows_kernel(cfg, meta, sig_a, sig_b, out_h, sig, turned, rows, sem):
    chunk = rows.shape[2]
    first = pl.ds(pl.multiple_of(meta[1] * chunk, chunk), chunk)
    own = pl.ds(meta[2] * cfg["sec"], cfg["sec"])
    loads = [pltpu.make_async_copy(ref.at[own], sig.at[i], sem.at[i]) for i, ref in enumerate((sig_a, sig_b))]
    for c in loads:
        c.start()
    for i, c in enumerate(loads):
        c.wait()
        for k in range(rows.shape[1]):
            turned[i, k] = sig[i, k].astype(F32).T
            rows[i, k] = turned[i, k, first, :]
    save = pltpu.make_async_copy(rows, out_h.at[0 : rows.shape[0]], sem.at[2])
    save.start()
    save.wait()


def _final_kernel(cfg, meta, first, known, sums, own, theirs, held_h, out_h, sub, last_rows, sem):
    del held_h
    mine, other = own[...], theirs[...].astype(F32)
    swapped = jnp.where(meta[0] == 0, mine, other), jnp.where(meta[0] == 0, other, mine)
    last_rows[0] = jnp.concatenate(swapped, axis=2)
    save = pltpu.make_async_copy(last_rows, out_h.at[ITERS - 1 : ITERS], sem)
    save.start()
    row = lax.broadcasted_iota(jnp.int32, sub.shape, 0)
    col = lax.broadcasted_iota(jnp.int32, sub.shape, 1)
    out = jnp.zeros(sub.shape, F32)
    for i, j, ref, at in ((0, 0, first, 0), (0, 1, first, 1), (0, 2, known, 2),
                          (1, 0, known, 0), (1, 1, known, 1), (1, 2, known, 3)):
        out = jnp.where((row == i) & (col == j), ref[at : at + 1, 0:1], out)
    for j in range(ITERS):
        value = sum(ref[j : j + 1, 0:1] for ref in sums)
        out = jnp.where((row == ITERS - 1) & (col == j), value, out)
    sub[...] = out
    save.wait()


def solution(mesh):
    n_env, n_term, n_blk = (mesh.shape[a] for a in ("env", "term", "blk"))

    def on_device(psi, left_env, right_env, pairing, sector_dims, precond):
        return _on_device(n_env, n_term, n_blk, psi, left_env, right_env, pairing, sector_dims, precond)

    placed = (
        P(("parts", "blk"), None, None),
        P(("parts", "term"), "blk", "env", None),
        P(("parts", "term"), "blk", "env", None),
        P(("parts", "term"), "blk"),
        P("parts"),
        P(("parts", "blk"), None, None),
    )
    return jax.shard_map(
        on_device,
        mesh=mesh,
        in_specs=placed,
        out_specs=(P(None, ("parts", "blk"), "term", None), P("parts", None)),
        check_vma=False,
    )


def _xor(axis, n, s):
    return functools.partial(lax.ppermute, axis_name=axis, perm=[(i, i ^ s) for i in range(n)])


def _on_device(n_env, n_term, n_blk, psi, left_env, right_env, pairing, sector_dims, precond):
    sec, states, width = psi.shape
    terms = left_env.shape[0]
    n_sec = sec * n_blk
    half = right_env.shape[2]
    direct = n_env == 2 and n_blk == 2 and n_term in (2, 4)
    part, chunk = half // n_term, states // n_term
    cfg = dict(direct=direct, n_term=n_term, n_blk=n_blk, sec=sec, part=part)
    env_pos, term_pos, blk_pos = (lax.axis_index(a) for a in ("env", "term", "blk"))
    other_env = _xor("env", 2, 1)
    other_blk = _xor("blk", 2, 1)
    flat = jnp.stack([x.astype(jnp.int32) for x in (env_pos, term_pos, blk_pos)])
    meta = jnp.concatenate([flat, pairing.reshape(-1), sector_dims.reshape(-1)])
    cfg["pair_at"] = 3
    cfg["dims_at"] = 3 + terms * sec
    chunks = [(0, sec)]
    if direct:
        near = [left_env]
        far = [other_env(left_env[:, k0 : k0 + nk]) for k0, nk in chunks]
        psi_o, pre_o = other_blk(psi), other_blk(precond)
    else:
        near = []
        far = [lax.all_gather(left_env, "env", axis=2, tiled=True)]
        psi_o, pre_o = (
            lax.dynamic_slice_in_dim(
                jnp.concatenate([lax.all_gather(x, "blk", axis=0, tiled=True)] * 2, axis=0),
                (blk_pos + 1) * sec,
                sec * (n_blk - 1),
                0,
            )
            for x in (psi, precond)
        )
    n_near = len(near)

    full = (n_sec, states, width)
    params = pltpu.CompilerParams(vmem_limit_bytes=VMEM_LIMIT)
    start, pret, inner, scale0 = pl.pallas_call(
        functools.partial(_first_kernel, cfg),
        out_shape=(VM(full, BF16), VM(full, F32), VM((terms, sec, half, states), BF16), VM((8, 128), F32)),
        in_specs=_specs(SM, VM, VM, VM, VM, VM),
        out_specs=_specs(VM, VM, VM, VM),
        scratch_shapes=[pltpu.VMEM(full, BF16)],
        compiler_params=params,
        name="start_vector",
    )(meta, psi, psi_o, precond, pre_o, right_env)

    def piece_shapes(nk):
        if direct:
            return [VM((nk, part, width), F32)] + [VM((nk, part, width), BF16)] * (n_term - 1)
        return [VM((nk, half, width), F32)]

    live_own = lax.dynamic_slice_in_dim(sector_dims, blk_pos * sec, sec)

    def reduce(pieces, k0=0):
        if not direct:
            flat_sum = pieces[0].reshape(sec * half, width)
            return lax.psum_scatter(flat_sum, "term", scatter_dimension=0, tiled=True)
        got = [_xor("term", n_term, s)(pieces[s]) for s in range(1, n_term)]
        total = pieces[0]
        for g in got:
            total = total + g.astype(F32)
        live = live_own[k0 : k0 + total.shape[0], None, None]
        row = env_pos * half + term_pos * part + lax.broadcasted_iota(jnp.int32, total.shape, 1)
        col = lax.broadcasted_iota(jnp.int32, total.shape, 2)
        return jnp.where((row < live) & (col < live), total, 0.0).astype(BF16)[None]

    def gather(shard, k0=0):
        if direct:
            hops = range(n_term)
            along = [shard] + [_xor("term", n_term, s)(shard) for s in hops[1:]]
            across = [other_env(a) for a in along]
            here = along + across
            there = [other_blk(a) for a in here]
            places = [(b, e, [s], k0) for b in range(2) for e in range(2) for s in hops]
            return here + there, places
        whole = lax.all_gather(shard, "term", axis=0, tiled=True).reshape(sec, half, width)
        whole = lax.all_gather(whole, "env", axis=1, tiled=True)
        row = lax.broadcasted_iota(jnp.int32, whole.shape, 1)
        col = lax.broadcasted_iota(jnp.int32, whole.shape, 2)
        live = live_own[:, None, None]
        whole = jnp.where((row < live) & (col < live), whole, 0.0).astype(BF16)
        return [lax.all_gather(whole, "blk", axis=0, tiled=True)], [None]

    shards, places = [], []
    for (k0, nk), moved in zip(chunks, far):
        pieces = pl.pallas_call(
            functools.partial(_second_kernel, cfg, k0, n_near + 1),
            out_shape=tuple(piece_shapes(nk)),
            in_specs=_specs(SM, VM, *[VM] * n_near, HB),
            out_specs=tuple(_specs(*[VM] * len(piece_shapes(nk)))),
            scratch_shapes=[
                pltpu.VMEM(moved.shape, BF16),
                pltpu.VMEM((nk, half, width), F32),
                pltpu.SemaphoreType.DMA,
            ],
            compiler_params=params,
            name=f"first_sigma_{k0}",
        )(meta, *_vmem(inner, *near), *_hbm(moved))
        more, at = gather(reduce(pieces, k0), k0)
        shards, places = shards + more, places + at

    vecs, olds = [], []
    far_shape = (terms, sec, *far[0].shape[2:])
    for step in range(1, ITERS):
        last = step + 1 == ITERS
        if step > 1:
            shards, places = gather(reduce(pieces))
        if last:
            if direct:
                size = (sec * chunk + TAIL_ROWS, half)
                outs = [VM((8, 128), F32), VM(size, F32)] + [VM(size, BF16)] * (n_term - 1)
            else:
                outs = [VM((8, 128), F32), VM((sec, states, half), F32), VM((8, 128), F32)]
            made = (HB(full, BF16),)
        else:
            outs = piece_shapes(sec)
            made = (HB(full, BF16), VM(full, F32), VM((8, 128), F32))
        n_fixed = 2 + (step - 1) + 1
        n_moved = (step - 1) + 1 + n_near + len(chunks)
        results = pl.pallas_call(
            functools.partial(_step_kernel, dict(cfg, n_out=len(outs)), step, places, chunks, n_near, last),
            out_shape=(*made, *outs),
            in_specs=_specs(SM, *[VM] * (len(shards) + n_fixed), *[HB] * n_moved),
            out_specs=tuple(_specs(HB, *[VM] * (len(made) - 1 + len(outs)))),
            scratch_shapes=[pltpu.VMEM(full, F32), pltpu.VMEM((sec, states, half), F32)] * last
            + [pltpu.VMEM(full, BF16)] * (step - 1)
            + [
                pltpu.VMEM(right_env.shape, BF16),
                *[pltpu.VMEM(x.shape, BF16) for x in near],
                pltpu.VMEM(far_shape, BF16),
                pltpu.VMEM(full, BF16),
                pltpu.VMEM(full, BF16),
                pltpu.VMEM((sec, half, width), F32),
                pltpu.SemaphoreType.DMA((n_moved + 1,)),
            ],
            compiler_params=params,
            name=f"vector_and_sigma_{step}",
        )(
            meta,
            *_vmem(*shards, start, scale0, *vecs, pret),
            *_hbm(*olds, right_env, *near, *far),
        )
        olds.append(results[0])
        if last:
            known, pieces = results[1], results[2:]
        else:
            vecs.append(results[1])
            first = results[2]
            pieces = results[3:]

    out_shape = (ITERS, sec, chunk, states)
    held = None
    if direct:
        held = pl.pallas_call(
            functools.partial(_rows_kernel, cfg),
            out_shape=HB(out_shape, F32),
            in_specs=_specs(SM, HB, HB),
            out_specs=_specs(HB)[0],
            scratch_shapes=[
                pltpu.VMEM((ITERS - 1, sec, states, states), BF16),
                pltpu.VMEM((ITERS - 1, sec, states, states), F32),
                pltpu.VMEM((ITERS - 1, sec, chunk, states), F32),
                pltpu.SemaphoreType.DMA((3,)),
            ],
            compiler_params=params,
            cost_estimate=pl.CostEstimate(flops=1 << 20, bytes_accessed=1 << 22, transcendentals=0),
            name="first_rows",
        )(meta, *_hbm(*olds))
    live = live_own[:, None, None]
    if direct:
        total = pieces[0]
        for s in range(1, n_term):
            total = total + _xor("term", n_term, s)(pieces[s]).astype(F32)
        cut = total[sec * chunk : sec * chunk + 3 * ITERS, :]
        sent = cut.reshape(ITERS, 3, half).sum(axis=1)
        mine = total[: sec * chunk].reshape(sec, chunk, half)
        row = term_pos * chunk + lax.broadcasted_iota(jnp.int32, mine.shape, 1)
        col = env_pos * half + lax.broadcasted_iota(jnp.int32, mine.shape, 2)
        own = jnp.where((row < live) & (col < live), mine, 0.0)
        theirs = other_env(own.astype(BF16))
        corners = [(i, i ^ 3) for i in range(4)]
        sums = [sent, other_blk(sent), other_env(sent), lax.ppermute(sent, ("env", "blk"), corners)]
        return pl.pallas_call(
            lambda meta, first, known, a, b, c, d, *refs: _final_kernel(cfg, meta, first, known, (a, b, c, d), *refs),
            out_shape=(HB(out_shape, F32), jax.ShapeDtypeStruct((ITERS, ITERS), F32)),
            in_specs=_specs(SM, *[VM] * 8, HB),
            out_specs=tuple(_specs(HB, VM)),
            scratch_shapes=[pltpu.VMEM((1, sec, chunk, states), F32), pltpu.SemaphoreType.DMA],
            input_output_aliases={9: 0},
            compiler_params=params,
            name="last_rows",
        )(meta, *_vmem(first, known, *sums, own, theirs), *_hbm(held))
    own = lax.psum_scatter(pieces[0], "term", scatter_dimension=1, tiled=True)
    both = lax.all_gather(own, "env", axis=2, tiled=True)
    row = term_pos * chunk + lax.broadcasted_iota(jnp.int32, both.shape, 1)
    col = lax.broadcasted_iota(jnp.int32, both.shape, 2)
    both = jnp.where((row < live) & (col < live), both, 0.0)
    scal = lax.psum(pieces[1], ("term", "env", "blk"))[:ITERS, 0]
    rows_out = []
    for sig in olds:
        mine = lax.dynamic_slice(sig, (blk_pos * sec, 0, term_pos * chunk), (sec, states, chunk))
        rows_out.append(jnp.swapaxes(mine, 1, 2).astype(F32))
    rows_out.append(both)
    first, second = first[:, 0], known[:, 0]
    subspace = jnp.stack([
        jnp.stack([first[0], first[1], second[2]]),
        jnp.stack([second[0], second[1], second[3]]),
        scal,
    ])
    return jnp.stack(rows_out), subspace
```

time: 409 us -> 139 us (0.34)
  waiting for transfers between devices: 276 us -> 48 us
  starting transfers between devices: 0.16 us -> 54.2 us
  other arithmetic: 37.6 us -> 0.34 us
  blocking collectives: 32.7 us -> 0 us
  Pallas kernels: 0 us -> 25.1 us
  matrix products: 17.7 us -> 0 us
  between operations: 17.3 us -> 0.84 us
  local copies, waits for them, and re-layouts: 26 us -> 9.99 us
    psum x3 -> x0, waiting for transfers between devices: 228 us -> none  [on_device(): lax.psum(jnp.einsum('tkca,tkcb->kab', left_env, inner, preferred_element_...]
    ppermute x0 -> x46, starting transfers between devices: none -> 54.2 us  [the longest x16 21.7 us: gather(): there = [other_blk(a) for a in here]]
    ppermute x0 -> x46, waiting for transfers between devices: none -> 48 us  [the longest x1 32.1 us: _on_device(): far = [other_env(left_env[:, k0:k0 + nk]) for k0, nk in chunks]]
    all_gather x1 -> x0, waiting for transfers between devices: 47.8 us -> none  [on_device(): right_full = lax.all_gather(right_env, 'env', axis=2, tiled=True)]
    reduce_sum x9 -> x1, other arithmetic: 26.4 us -> 0.02 us  [_on_device(): sent = cut.reshape(ITERS, 3, half).sum(axis=1)]
    psum x8 -> x0, blocking collectives: 25.9 us -> none  [the longest x7 22.9 us: reduce_means(): return lax.psum(values, 'blk') / count]
    pallas_call x0 -> x6, Pallas kernels: none -> 25.1 us  [the longest x2 14.2 us: _on_device(): pl.pallas_call(functools.partial(_step_kernel, dict(cfg, n_out=len(outs))...]
    dot_general x3 -> x0, matrix products: 17.7 us -> none  [on_device(): jnp.einsum('tkca,tkcb->kab', left_env, inner, preferred_element_type=jnp....]
  transfers between devices with their start and end apart: 4 -> 46, of which waited for: 4 -> 15; matrix products, arithmetic and copies ran while one was open for 2% -> 2% of each run, Pallas kernels for 0% -> 4%
where the time goes in v3:
time: 139 us; the launch traced here: 138 us
  starting transfers between devices  54.2 us (39%)
  waiting for transfers between devices  48 us (35%)
  Pallas kernels  25.1 us (18%)
  local copies, waits for them, and re-layouts  9.99 us (7%)
    ppermute x1, waiting for transfers between devices, _on_device(): far = [other_env(left_env[:, k0:k0 + nk]) for k0, nk in chunks]  32.1 us
    ppermute x16, starting transfers between devices, gather(): there = [other_blk(a) for a in here]  21.7 us
    pallas_call x2, Pallas kernels, _on_device(): pl.pallas_call(functools.partial(_step_kernel, dict(cfg, n_out=len(outs))...  14.2 us
    unnamed x21, local copies, waits for them, and re-layouts  8.42 us
    ppermute x6, waiting for transfers between devices, reduce(): got = [_xor('term', n_term, s)(pieces[s]) for s in range(1, n_term)]  8.15 us
    ppermute x6, starting transfers between devices, gather(): along = [shard] + [_xor('term', n_term, s)(shard) for s in hops[1:]]  7.3 us
    ppermute x6, starting transfers between devices, reduce(): got = [_xor('term', n_term, s)(pieces[s]) for s in range(1, n_term)]  7.22 us
    ppermute x8, starting transfers between devices, gather(): across = [other_env(a) for a in along]  6.42 us
  transfers between devices with their start and end apart: 46, of which 15 were waited for; matrix products, arithmetic and copies ran while one was open for 2% of the time, Pallas kernels for 4%

profile of v3, /device:TPU:1, one launch (start us, length us, event | category | flops | bytes accessed | tf_op | source)
XLA Modules:
  0.0 138.5 jit_solution(9554542665076896010)
XLA Ops:
  0.6 2.1 %collective-permute-start.2 = (bf16[8,4,128,256]{3,2,1,0:T(8,128)(2,1)}, bf16[8,4,128,256]{3,2,1,0:T(8,128)(2,1)}, u32[]{:S(2)}, u32[]{:S(2)}) collective-permute-start(bf16[8,4,128,256]{3,2,1,0:T(8,128)(2,1)} %refs_22_.1), channel_id=1, source_target_pairs={{0,2},{2,0},{1,3},{3,1},{4,6},{6,4},{5,7},{7,5},{8,10},{10,8},{9,1... | collective-permute-start | bytes 6291464 | tf_op jit(solution)/shard_map/ppermute | solution.py:345
  2.7 1.0 collective-permute-start.1
  6.0 0.9 collective-permute-done.psi_o
  6.9 1.0 copy-done.5
  7.9 1.6 %copy-done.1 = bf16[8,4,128,256]{3,2,1,0:T(8,128)(2,1)S(1)} copy-done((bf16[8,4,128,256]{3,2,1,0:T(8,128)(2,1)S(1)}, bf16[8,4,128,256]{3,2,1,0:T(8,128)(2,1)}, u32[]{:S(2)}) %copy-start.1) | copy-done | bytes 2097176
  9.5 1.2 copy-done.4
  10.7 1.2 copy-done.6
  12.0 1.0 copy-done.7
  13.0 3.2 %start_vector.1 = (bf16[8,256,256]{2,1,0:T(8,128)(2,1)S(1)}, f32[8,256,256]{2,1,0:T(8,128)S(1)}, bf16[8,4,128,256]{3,2,1,0:T(8,128)(2,1)S(1)}, f32[8,128]{1,0:T(8,128)S(1)}) custom-call(s32[43]{0:T(128)S(1)} %concatenate.3.meta, bf16[4,256,256]{2,1,0:T(8,128)(2,1)S(1)} %copy-done.7, bf16[4,256,256]{2,1,0:T(8,128)(2,1)} %collective-permute-done.psi_o, ...), custom_call_target="tpu_custom_call" | custom-call | tf_op jit(solution)/shard_map/start_vector/pallas_call | solution.py:363
  16.3 32.1 %collective-permute-done.2.refs_1_.refs_21_.refs_23_ = bf16[8,4,128,256]{3,2,1,0:T(8,128)(2,1)} collective-permute-done((bf16[8,4,128,256]{3,2,1,0:T(8,128)(2,1)}, bf16[8,4,128,256]{3,2,1,0:T(8,128)(2,1)}, u32[]{:S(2)}, u32[]{:S(2)}) %collective-permute-start.2) | collective-permute-done | bytes 2097184 | tf_op jit(solution)/shard_map/ppermute | solution.py:345
  48.4 3.0 %first_sigma_0.1 = (f32[4,32,256]{2,1,0:T(8,128)S(1)}, bf16[4,32,256]{2,1,0:T(8,128)(2,1)S(1)}, bf16[4,32,256]{2,1,0:T(8,128)(2,1)S(1)}, bf16[4,32,256]{2,1,0:T(8,128)(2,1)S(1)}) custom-call(s32[43]{0:T(128)S(1)} %concatenate.3.meta, bf16[8,4,128,256]{3,2,1,0:T(8,128)(2,1)S(1)} %get-tuple-element.23.inner, bf16[8,4,128,256]{3,2,1,0:T(8,128)(2,1)S(1)} %copy-done, ...), custom_call_target="tpu_custom_call" | custom-call | tf_op jit(solution)/shard_map/first_sigma_0/pallas_call | solution.py:412
  51.4 1.3 collective-permute-start.3
  52.7 2.3 %collective-permute-start.4 = (bf16[4,32,256]{2,1,0:T(8,128)(2,1)S(1)}, bf16[4,32,256]{2,1,0:T(8,128)(2,1)S(1)}, u32[]{:S(2)}, u32[]{:S(2)}) collective-permute-start(bf16[4,32,256]{2,1,0:T(8,128)(2,1)S(1)} %get-tuple-element.26), channel_id=1, source_target_pairs={{0,8},{4,12},{8,0},{12,4},{1,9},{5,13},{9,1},{13,5},{2,10},{6,14},... | collective-permute-start | bytes 196616 | tf_op jit(solution)/shard_map/ppermute | solution.py:384
  55.0 2.4 %collective-permute-done.4 = bf16[4,32,256]{2,1,0:T(8,128)(2,1)S(1)} collective-permute-done((bf16[4,32,256]{2,1,0:T(8,128)(2,1)S(1)}, bf16[4,32,256]{2,1,0:T(8,128)(2,1)S(1)}, u32[]{:S(2)}, u32[]{:S(2)}) %collective-permute-start.4) | collective-permute-done | bytes 65568 | tf_op jit(solution)/shard_map/ppermute | solution.py:384
  57.4 2.6 %collective-permute-done.5 = bf16[4,32,256]{2,1,0:T(8,128)(2,1)S(1)} collective-permute-done((bf16[4,32,256]{2,1,0:T(8,128)(2,1)S(1)}, bf16[4,32,256]{2,1,0:T(8,128)(2,1)S(1)}, u32[]{:S(2)}, u32[]{:S(2)}) %collective-permute-start.5) | collective-permute-done | bytes 65568 | tf_op jit(solution)/shard_map/ppermute | solution.py:384
  60.1 1.3 collective-permute-start.9
  61.4 1.0 collective-permute-start.8
  62.4 3.3 %collective-permute-start.13 = (bf16[1,4,32,256]{3,2,1,0:T(8,128)(2,1)S(1)}, bf16[1,4,32,256]{3,2,1,0:T(8,128)(2,1)S(1)}, u32[]{:S(2)}, u32[]{:S(2)}) collective-permute-start(bf16[1,4,32,256]{3,2,1,0:T(8,128)(2,1)S(1)} %fusion.1.refs_0_), channel_id=1, source_target_pairs={{0,1},{1,0},{2,3},{3,2},{4,5},{5,4},{6,7},{7,6},{8,9},{9,8},{10,11... | collective-permute-start | bytes 196616 | tf_op jit(solution)/shard_map/ppermute | solution.py:399
  65.8 2.8 %collective-permute-start.6 = (bf16[1,4,32,256]{3,2,1,0:T(8,128)(2,1)S(1)}, bf16[1,4,32,256]{3,2,1,0:T(8,128)(2,1)S(1)}, u32[]{:S(2)}, u32[]{:S(2)}) collective-permute-start(bf16[1,4,32,256]{3,2,1,0:T(8,128)(2,1)S(1)} %fusion.1.refs_0_), channel_id=1, source_target_pairs={{0,4},{4,0},{8,12},{12,8},{1,5},{5,1},{9,13},{13,9},{2,6},{6,2},{1... | collective-permute-start | bytes 196616 | tf_op jit(solution)/shard_map/ppermute | solution.py:396
  69.2 2.5 %collective-permute-start.16 = (bf16[1,4,32,256]{3,2,1,0:T(8,128)(2,1)S(1)}, bf16[1,4,32,256]{3,2,1,0:T(8,128)(2,1)S(1)}, u32[]{:S(2)}, u32[]{:S(2)}) collective-permute-start(bf16[1,4,32,256]{3,2,1,0:T(8,128)(2,1)S(1)} %collective-permute-done.8.refs_3_), channel_id=1, source_target_pairs={{0,1},{1,0},{2,3},{3,2},{4,5},{5,4},{6,7},{7,6},{8,9},{9,8},{10,11... | collective-permute-start | bytes 196616 | tf_op jit(solution)/shard_map/ppermute | solution.py:399
  72.3 0.9 collective-permute-start.11
  73.7 1.5 %collective-permute-start.15 = (bf16[1,4,32,256]{3,2,1,0:T(8,128)(2,1)S(1)}, bf16[1,4,32,256]{3,2,1,0:T(8,128)(2,1)S(1)}, u32[]{:S(2)}, u32[]{:S(2)}) collective-permute-start(bf16[1,4,32,256]{3,2,1,0:T(8,128)(2,1)S(1)} %collective-permute-done.7.refs_2_), channel_id=1, source_target_pairs={{0,1},{1,0},{2,3},{3,2},{4,5},{5,4},{6,7},{7,6},{8,9},{9,8},{10,11... | collective-permute-start | bytes 196616 | tf_op jit(solution)/shard_map/ppermute | solution.py:399
  75.5 1.2 collective-permute-start.20
  76.6 1.7 %collective-permute-start.19 = (bf16[1,4,32,256]{3,2,1,0:T(8,128)(2,1)S(1)}, bf16[1,4,32,256]{3,2,1,0:T(8,128)(2,1)S(1)}, u32[]{:S(2)}, u32[]{:S(2)}) collective-permute-start(bf16[1,4,32,256]{3,2,1,0:T(8,128)(2,1)S(1)} %collective-permute-done.11.refs_6_), channel_id=1, source_target_pairs={{0,1},{1,0},{2,3},{3,2},{4,5},{5,4},{6,7},{7,6},{8,9},{9,8},{10,11... | collective-permute-start | bytes 196616 | tf_op jit(solution)/shard_map/ppermute | solution.py:399
  80.0 6.2 %vector_and_sigma_1.1 = (bf16[8,256,256]{2,1,0:T(8,128)(2,1)}, f32[8,256,256]{2,1,0:T(8,128)S(1)}, f32[8,128]{1,0:T(8,128)S(1)}, f32[4,32,256]{2,1,0:T(8,128)S(1...) custom-call(s32[43]{0:T(128)S(1)} %concatenate.3.meta, ...), custom_call_target="tpu_custom_call" | custom-call | tf_op jit(solution)/shard_map/vector_and_sigma_1/pallas_call | solution.py:446
  86.2 1.2 collective-permute-start.22
  87.4 2.3 %collective-permute-start.23 = (bf16[4,32,256]{2,1,0:T(8,128)(2,1)S(1)}, bf16[4,32,256]{2,1,0:T(8,128)(2,1)S(1)}, u32[]{:S(2)}, u32[]{:S(2)}) collective-permute-start(bf16[4,32,256]{2,1,0:T(8,128)(2,1)S(1)} %get-tuple-element.35), channel_id=1, source_target_pairs={{0,12},{4,8},{8,4},{12,0},{1,13},{5,9},{9,5},{13,1},{2,14},{6,10},... | collective-permute-start | bytes 196616 | tf_op jit(solution)/shard_map/ppermute | solution.py:384
  90.4 2.5 %collective-permute-done.23 = bf16[4,32,256]{2,1,0:T(8,128)(2,1)S(1)} collective-permute-done((bf16[4,32,256]{2,1,0:T(8,128)(2,1)S(1)}, bf16[4,32,256]{2,1,0:T(8,128)(2,1)S(1)}, u32[]{:S(2)}, u32[]{:S(2)}) %collective-permute-start.23) | collective-permute-done | bytes 65568 | tf_op jit(solution)/shard_map/ppermute | solution.py:384
  93.7 1.5 %collective-permute-start.26 = (bf16[1,4,32,256]{3,2,1,0:T(8,128)(2,1)S(1)}, bf16[1,4,32,256]{3,2,1,0:T(8,128)(2,1)S(1)}, u32[]{:S(2)}, u32[]{:S(2)}) collective-permute-start(bf16[1,4,32,256]{3,2,1,0:T(8,128)(2,1)S(1)} %fusion.2.refs_0_), channel_id=1, source_target_pairs={{0,12},{4,8},{8,4},{12,0},{1,13},{5,9},{9,5},{13,1},{2,14},{6,10},... | collective-permute-start | bytes 196616 | tf_op jit(solution)/shard_map/ppermute | solution.py:396
  95.1 2.8 %collective-permute-start.31 = (bf16[1,4,32,256]{3,2,1,0:T(8,128)(2,1)S(1)}, bf16[1,4,32,256]{3,2,1,0:T(8,128)(2,1)S(1)}, u32[]{:S(2)}, u32[]{:S(2)}) collective-permute-start(bf16[1,4,32,256]{3,2,1,0:T(8,128)(2,1)S(1)} %fusion.2.refs_0_), channel_id=1, source_target_pairs={{0,1},{1,0},{2,3},{3,2},{4,5},{5,4},{6,7},{7,6},{8,9},{9,8},{10,11... | collective-permute-start | bytes 196616 | tf_op jit(solution)/shard_map/ppermute | solution.py:399
  98.4 1.4 collective-permute-start.24
  100.3 2.1 %collective-permute-start.34 = (bf16[1,4,32,256]{3,2,1,0:T(8,128)(2,1)S(1)}, bf16[1,4,32,256]{3,2,1,0:T(8,128)(2,1)}, u32[]{:S(2)}, u32[]{:S(2)}) collective-permute-start(bf16[1,4,32,256]{3,2,1,0:T(8,128)(2,1)S(1)} %collective-permute-done.26.refs_3_), channel_id=1, source_target_pairs={{0,1},{1,0},{2,3},{3,2},{4,5},{5,4},{6,7},{7,6},{8,9},{9,8},{10,11... | collective-permute-start | bytes 196616 | tf_op jit(solution)/shard_map/ppermute | solution.py:399
  102.5 1.3 collective-permute-start.30
  104.4 1.3 collective-permute-start.29
  105.9 1.0 collective-permute-start.33
  107.6 2.0 %collective-permute-start.37 = (bf16[1,4,32,256]{3,2,1,0:T(8,128)(2,1)}, bf16[1,4,32,256]{3,2,1,0:T(8,128)(2,1)S(1)}, u32[]{:S(2)}, u32[]{:S(2)}) collective-permute-start(bf16[1,4,32,256]{3,2,1,0:T(8,128)(2,1)} %collective-permute-done.29.refs_6_), channel_id=1, source_target_pairs={{0,1},{1,0},{2,3},{3,2},{4,5},{5,4},{6,7},{7,6},{8,9},{9,8},{10,11... | collective-permute-start | bytes 196616 | tf_op jit(solution)/shard_map/ppermute | solution.py:399
  109.6 1.1 collective-permute-start.36
  110.8 1.1 collective-permute-done.36.refs_13_
  111.9 1.6 %copy-done.3 = f32[8,256,256]{2,1,0:T(8,128)S(1)} copy-done((f32[8,256,256]{2,1,0:T(8,128)S(1)}, f32[8,256,256]{2,1,0:T(8,128)}, u32[]{:S(2)}) %copy-start.3) | copy-done | bytes 2097176
  113.5 8.0 %vector_and_sigma_2.1 = (bf16[8,256,256]{2,1,0:T(8,128)(2,1)}, f32[8,128]{1,0:T(8,128)S(1)}, f32[272,128]{1,0:T(8,128)S(1)}, bf16[272,128]{1,0:T(8,128)(2,1)S(1)...) custom-call(s32[43]{0:T(128)S(1)} %concatenate.3.meta, bf16[1,4,32,256]{3,2,1,0:T(8,128)(2,1)S(1)} %fusion.2.refs_0_, ...), custom_call_target="tpu_custom_call" | custom-call | tf_op jit(solution)/shard_map/vector_and_sigma_2/pallas_call | solution.py:446
  121.5 1.8 %collective-permute-start.40 = (bf16[272,128]{1,0:T(8,128)(2,1)S(1)}, bf16[272,128]{1,0:T(8,128)(2,1)S(1)}, u32[]{:S(2)}, u32[]{:S(2)}) collective-permute-start(bf16[272,128]{1,0:T(8,128)(2,1)S(1)} %get-tuple-element.41), channel_id=1, source_target_pairs={{0,8},{4,12},{8,0},{12,4},{1,9},{5,13},{9,1},{13,5},{2,10},{6,14},... | collective-permute-start | bytes 208904 | tf_op jit(solution)/shard_map/ppermute | solution.py:499
  123.4 1.7 %collective-permute-start.41 = (bf16[272,128]{1,0:T(8,128)(2,1)S(1)}, bf16[272,128]{1,0:T(8,128)(2,1)S(1)}, u32[]{:S(2)}, u32[]{:S(2)}) collective-permute-start(bf16[272,128]{1,0:T(8,128)(2,1)S(1)} %get-tuple-element.42), channel_id=1, source_target_pairs={{0,12},{4,8},{8,4},{12,0},{1,13},{5,9},{9,5},{13,1},{2,14},{6,10},... | collective-permute-start | bytes 208904 | tf_op jit(solution)/shard_map/ppermute | solution.py:499
  125.8 2.8 %collective-permute-done.41 = bf16[272,128]{1,0:T(8,128)(2,1)S(1)} collective-permute-done((bf16[272,128]{1,0:T(8,128)(2,1)S(1)}, bf16[272,128]{1,0:T(8,128)(2,1)S(1)}, u32[]{:S(2)}, u32[]{:S(2)}) %collective-permute-start.41) | collective-permute-done | bytes 69664 | tf_op jit(solution)/shard_map/ppermute | solution.py:499
  128.8 1.0 collective-permute-start.45
  129.8 3.0 %collective-permute-start.44 = (f32[3,128]{1,0:T(4,128)S(1)}, f32[3,128]{1,0:T(4,128)S(1)}, u32[]{:S(2)}, u32[]{:S(2)}) collective-permute-start(f32[3,128]{1,0:T(4,128)S(1)} %reduce_sum.9.a), channel_id=1, source_target_pairs={{0,3},{1,2},{2,1},{3,0},{4,7},{5,6},{6,5},{7,4},{8,11},{9,10},{10,... | collective-permute-start | bytes 4616 | tf_op jit(solution)/shard_map/ppermute | solution.py:508
  132.8 0.9 collective-permute-start.43
  133.7 2.8 %first_rows.1.refs_2_ = f32[3,4,64,256]{3,2,1,0:T(8,128)} custom-call(s32[43]{0:T(128)S(1)} %concatenate.3.meta, bf16[8,256,256]{2,1,0:T(8,128)(2,1)} %get-tuple-element.37.refs_20_.sig_a, bf16[8,256,256]{2,1,0:T(8,128)(2,1)} %get-tuple-element.43.sig_b), custom_call_target="tpu_custom_call" | custom-call | flops 1048576 | bytes 4194304 | tf_op jit(solution)/shard_map/first_rows/pallas_call | solution.py:480
  136.6 1.9 %last_rows.1 = (f32[3,4,64,256]{3,2,1,0:T(8,128)}, f32[3,3]{1,0:T(4,128)}) custom-call(s32[43]{0:T(128)S(1)} %concatenate.3.meta, f32[8,128]{1,0:T(8,128)S(1)} %get-tuple-element.31.first, f32[8,128]{1,0:T(8,128)S(1)} %get-tuple-element.38.known, f32[3,128]{1,0:T(4,128)S(1)} %reduce_sum.9.a, ...), custom_call_target="tpu_custom_call", output_to_operand_aliasing={{0}: (9, {})} | custom-call | tf_op jit(solution)/shard_map/last_rows/pallas_call | solution.py:509
  (85 shorter events, 11.2 us)
Async XLA Ops:
  0.6 47.8 %collective-permute-start.2 = (bf16[8,4,128,256]{3,2,1,0:T(8,128)(2,1)}, bf16[8,4,128,256]{3,2,1,0:T(8,128)(2,1)}, u32[]{:S(2)}, u32[]{:S(2)}) collective-permute-start(bf16[8,4,128,256]{3,2,1,0:T(8,128)(2,1)} %refs_22_.1), channel_id=1, source_target_pairs={{0,2},{2,0},{1,3},{3,1},{4,6},{6,4},{5,7},{7,5},{8,10},{10,8},{9,1... | collective-permute-start | bytes 6291464 | tf_op jit(solution)/shard_map/ppermute | solution.py:345
  2.7 4.2 %collective-permute-start.1 = (f32[4,256,256]{2,1,0:T(8,128)}, f32[4,256,256]{2,1,0:T(8,128)S(1)}, u32[]{:S(2)}, u32[]{:S(2)}) collective-permute-start(f32[4,256,256]{2,1,0:T(8,128)} %pre.1), channel_id=1, source_target_pairs={{0,1},{1,0},{2,3},{3,2},{4,5},{5,4},{6,7},{7,6},{8,9},{9,8},{10,11... | collective-permute-start | bytes 3145736 | tf_op jit(solution)/shard_map/ppermute | solution.py:346
  3.7 3.2 %collective-permute-start = (bf16[4,256,256]{2,1,0:T(8,128)(2,1)}, bf16[4,256,256]{2,1,0:T(8,128)(2,1)}, u32[]{:S(2)}, u32[]{:S(2)}) collective-permute-start(bf16[4,256,256]{2,1,0:T(8,128)(2,1)} %psi.1), channel_id=1, source_target_pairs={{0,1},{1,0},{2,3},{3,2},{4,5},{5,4},{6,7},{7,6},{8,9},{9,8},{10,11... | collective-permute-start | bytes 1572872 | tf_op jit(solution)/shard_map/ppermute | solution.py:346
  5.3 87.6 %copy-start.8 = (s32[4]{0:T(128)}, s32[4]{0:T(128)S(1)}, u32[]{:S(2)}) copy-start(s32[4]{0:T(128)S(1)} %dynamic_slice.3) | copy-start | bytes 52
  16.3 63.7 %copy-start.2 = (f32[8,256,256]{2,1,0:T(8,128)}, f32[8,256,256]{2,1,0:T(8,128)S(1)}, u32[]{:S(2)}) copy-start(f32[8,256,256]{2,1,0:T(8,128)S(1)} %get-tuple-element.30.refs_18_.refs_19_) | copy-start | bytes 6291460
  51.4 3.6 %collective-permute-start.3 = (bf16[4,32,256]{2,1,0:T(8,128)(2,1)S(1)}, bf16[4,32,256]{2,1,0:T(8,128)(2,1)S(1)}, u32[]{:S(2)}, u32[]{:S(2)}) collective-permute-start(bf16[4,32,256]{2,1,0:T(8,128)(2,1)S(1)} %get-tuple-element.25), channel_id=1, source_target_pairs={{0,4},{4,0},{8,12},{12,8},{1,5},{5,1},{9,13},{13,9},{2,6},{6,2},{1... | collective-permute-start | bytes 196616 | tf_op jit(solution)/shard_map/ppermute | solution.py:384
  52.7 4.7 %collective-permute-start.4 = (bf16[4,32,256]{2,1,0:T(8,128)(2,1)S(1)}, bf16[4,32,256]{2,1,0:T(8,128)(2,1)S(1)}, u32[]{:S(2)}, u32[]{:S(2)}) collective-permute-start(bf16[4,32,256]{2,1,0:T(8,128)(2,1)S(1)} %get-tuple-element.26), channel_id=1, source_target_pairs={{0,8},{4,12},{8,0},{12,4},{1,9},{5,13},{9,1},{13,5},{2,10},{6,14},... | collective-permute-start | bytes 196616 | tf_op jit(solution)/shard_map/ppermute | solution.py:384
  55.0 5.0 %collective-permute-start.5 = (bf16[4,32,256]{2,1,0:T(8,128)(2,1)S(1)}, bf16[4,32,256]{2,1,0:T(8,128)(2,1)S(1)}, u32[]{:S(2)}, u32[]{:S(2)}) collective-permute-start(bf16[4,32,256]{2,1,0:T(8,128)(2,1)S(1)} %get-tuple-element.27), channel_id=1, source_target_pairs={{0,12},{4,8},{8,4},{12,0},{1,13},{5,9},{9,5},{13,1},{2,14},{6,10},... | collective-permute-start | bytes 196616 | tf_op jit(solution)/shard_map/ppermute | solution.py:384
  60.1 8.5 %collective-permute-start.9 = (bf16[1,4,32,256]{3,2,1,0:T(8,128)(2,1)S(1)}, bf16[1,4,32,256]{3,2,1,0:T(8,128)(2,1)S(1)}, u32[]{:S(2)}, u32[]{:S(2)}) collective-permute-start(bf16[1,4,32,256]{3,2,1,0:T(8,128)(2,1)S(1)} %fusion.1.refs_0_), channel_id=1, source_target_pairs={{0,2},{2,0},{1,3},{3,1},{4,6},{6,4},{5,7},{7,5},{8,10},{10,8},{9,1... | collective-permute-start | bytes 196616 | tf_op jit(solution)/shard_map/ppermute | solution.py:397
  61.4 7.8 %collective-permute-start.8 = (bf16[1,4,32,256]{3,2,1,0:T(8,128)(2,1)S(1)}, bf16[1,4,32,256]{3,2,1,0:T(8,128)(2,1)S(1)}, u32[]{:S(2)}, u32[]{:S(2)}) collective-permute-start(bf16[1,4,32,256]{3,2,1,0:T(8,128)(2,1)S(1)} %fusion.1.refs_0_), channel_id=1, source_target_pairs={{0,12},{4,8},{8,4},{12,0},{1,13},{5,9},{9,5},{13,1},{2,14},{6,10},... | collective-permute-start | bytes 196616 | tf_op jit(solution)/shard_map/ppermute | solution.py:396
  62.4 9.3 %collective-permute-start.13 = (bf16[1,4,32,256]{3,2,1,0:T(8,128)(2,1)S(1)}, bf16[1,4,32,256]{3,2,1,0:T(8,128)(2,1)S(1)}, u32[]{:S(2)}, u32[]{:S(2)}) collective-permute-start(bf16[1,4,32,256]{3,2,1,0:T(8,128)(2,1)S(1)} %fusion.1.refs_0_), channel_id=1, source_target_pairs={{0,1},{1,0},{2,3},{3,2},{4,5},{5,4},{6,7},{7,6},{8,9},{9,8},{10,11... | collective-permute-start | bytes 196616 | tf_op jit(solution)/shard_map/ppermute | solution.py:399
  65.7 6.6 %collective-permute-start.7 = (bf16[1,4,32,256]{3,2,1,0:T(8,128)(2,1)S(1)}, bf16[1,4,32,256]{3,2,1,0:T(8,128)(2,1)S(1)}, u32[]{:S(2)}, u32[]{:S(2)}) collective-permute-start(bf16[1,4,32,256]{3,2,1,0:T(8,128)(2,1)S(1)} %fusion.1.refs_0_), channel_id=1, source_target_pairs={{0,8},{4,12},{8,0},{12,4},{1,9},{5,13},{9,1},{13,5},{2,10},{6,14},... | collective-permute-start | bytes 196616 | tf_op jit(solution)/shard_map/ppermute | solution.py:396
  65.8 7.4 %collective-permute-start.6 = (bf16[1,4,32,256]{3,2,1,0:T(8,128)(2,1)S(1)}, bf16[1,4,32,256]{3,2,1,0:T(8,128)(2,1)S(1)}, u32[]{:S(2)}, u32[]{:S(2)}) collective-permute-start(bf16[1,4,32,256]{3,2,1,0:T(8,128)(2,1)S(1)} %fusion.1.refs_0_), channel_id=1, source_target_pairs={{0,4},{4,0},{8,12},{12,8},{1,5},{5,1},{9,13},{13,9},{2,6},{6,2},{1... | collective-permute-start | bytes 196616 | tf_op jit(solution)/shard_map/ppermute | solution.py:396
  68.6 5.1 %collective-permute-start.17 = (bf16[1,4,32,256]{3,2,1,0:T(8,128)(2,1)S(1)}, bf16[1,4,32,256]{3,2,1,0:T(8,128)(2,1)S(1)}, u32[]{:S(2)}, u32[]{:S(2)}) collective-permute-start(bf16[1,4,32,256]{3,2,1,0:T(8,128)(2,1)S(1)} %collective-permute-done.9.refs_4_), channel_id=1, source_target_pairs={{0,1},{1,0},{2,3},{3,2},{4,5},{5,4},{6,7},{7,6},{8,9},{9,8},{10,11... | collective-permute-start | bytes 196616 | tf_op jit(solution)/shard_map/ppermute | solution.py:399
  69.2 6.1 %collective-permute-start.16 = (bf16[1,4,32,256]{3,2,1,0:T(8,128)(2,1)S(1)}, bf16[1,4,32,256]{3,2,1,0:T(8,128)(2,1)S(1)}, u32[]{:S(2)}, u32[]{:S(2)}) collective-permute-start(bf16[1,4,32,256]{3,2,1,0:T(8,128)(2,1)S(1)} %collective-permute-done.8.refs_3_), channel_id=1, source_target_pairs={{0,1},{1,0},{2,3},{3,2},{4,5},{5,4},{6,7},{7,6},{8,9},{9,8},{10,11... | collective-permute-start | bytes 196616 | tf_op jit(solution)/shard_map/ppermute | solution.py:399
  71.7 3.7 %collective-permute-start.12 = (bf16[1,4,32,256]{3,2,1,0:T(8,128)(2,1)S(1)}, bf16[1,4,32,256]{3,2,1,0:T(8,128)(2,1)S(1)}, u32[]{:S(2)}, u32[]{:S(2)}) collective-permute-start(bf16[1,4,32,256]{3,2,1,0:T(8,128)(2,1)S(1)} %collective-permute-done.8.refs_3_), channel_id=1, source_target_pairs={{0,2},{2,0},{1,3},{3,1},{4,6},{6,4},{5,7},{7,5},{8,10},{10,8},{9,1... | collective-permute-start | bytes 196616 | tf_op jit(solution)/shard_map/ppermute | solution.py:397
  72.3 4.4 %collective-permute-start.11 = (bf16[1,4,32,256]{3,2,1,0:T(8,128)(2,1)S(1)}, bf16[1,4,32,256]{3,2,1,0:T(8,128)(2,1)S(1)}, u32[]{:S(2)}, u32[]{:S(2)}) collective-permute-start(bf16[1,4,32,256]{3,2,1,0:T(8,128)(2,1)S(1)} %collective-permute-done.7.refs_2_), channel_id=1, source_target_pairs={{0,2},{2,0},{1,3},{3,1},{4,6},{6,4},{5,7},{7,5},{8,10},{10,8},{9,1... | collective-permute-start | bytes 196616 | tf_op jit(solution)/shard_map/ppermute | solution.py:397
  73.2 5.1 %collective-permute-start.10 = (bf16[1,4,32,256]{3,2,1,0:T(8,128)(2,1)S(1)}, bf16[1,4,32,256]{3,2,1,0:T(8,128)(2,1)S(1)}, u32[]{:S(2)}, u32[]{:S(2)}) collective-permute-start(bf16[1,4,32,256]{3,2,1,0:T(8,128)(2,1)S(1)} %collective-permute-done.6.refs_1_), channel_id=1, source_target_pairs={{0,2},{2,0},{1,3},{3,1},{4,6},{6,4},{5,7},{7,5},{8,10},{10,8},{9,1... | collective-permute-start | bytes 196616 | tf_op jit(solution)/shard_map/ppermute | solution.py:397
  73.7 5.3 %collective-permute-start.15 = (bf16[1,4,32,256]{3,2,1,0:T(8,128)(2,1)S(1)}, bf16[1,4,32,256]{3,2,1,0:T(8,128)(2,1)S(1)}, u32[]{:S(2)}, u32[]{:S(2)}) collective-permute-start(bf16[1,4,32,256]{3,2,1,0:T(8,128)(2,1)S(1)} %collective-permute-done.7.refs_2_), channel_id=1, source_target_pairs={{0,1},{1,0},{2,3},{3,2},{4,5},{5,4},{6,7},{7,6},{8,9},{9,8},{10,11... | collective-permute-start | bytes 196616 | tf_op jit(solution)/shard_map/ppermute | solution.py:399
  75.3 3.8 %collective-permute-start.14 = (bf16[1,4,32,256]{3,2,1,0:T(8,128)(2,1)S(1)}, bf16[1,4,32,256]{3,2,1,0:T(8,128)(2,1)S(1)}, u32[]{:S(2)}, u32[]{:S(2)}) collective-permute-start(bf16[1,4,32,256]{3,2,1,0:T(8,128)(2,1)S(1)} %collective-permute-done.6.refs_1_), channel_id=1, source_target_pairs={{0,1},{1,0},{2,3},{3,2},{4,5},{5,4},{6,7},{7,6},{8,9},{9,8},{10,11... | collective-permute-start | bytes 196616 | tf_op jit(solution)/shard_map/ppermute | solution.py:399
  75.5 3.6 %collective-permute-start.20 = (bf16[1,4,32,256]{3,2,1,0:T(8,128)(2,1)S(1)}, bf16[1,4,32,256]{3,2,1,0:T(8,128)(2,1)S(1)}, u32[]{:S(2)}, u32[]{:S(2)}) collective-permute-start(bf16[1,4,32,256]{3,2,1,0:T(8,128)(2,1)S(1)} %collective-permute-done.12.refs_7_), channel_id=1, source_target_pairs={{0,1},{1,0},{2,3},{3,2},{4,5},{5,4},{6,7},{7,6},{8,9},{9,8},{10,11... | collective-permute-start | bytes 196616 | tf_op jit(solution)/shard_map/ppermute | solution.py:399
  76.6 2.6 %collective-permute-start.19 = (bf16[1,4,32,256]{3,2,1,0:T(8,128)(2,1)S(1)}, bf16[1,4,32,256]{3,2,1,0:T(8,128)(2,1)S(1)}, u32[]{:S(2)}, u32[]{:S(2)}) collective-permute-start(bf16[1,4,32,256]{3,2,1,0:T(8,128)(2,1)S(1)} %collective-permute-done.11.refs_6_), channel_id=1, source_target_pairs={{0,1},{1,0},{2,3},{3,2},{4,5},{5,4},{6,7},{7,6},{8,9},{9,8},{10,11... | collective-permute-start | bytes 196616 | tf_op jit(solution)/shard_map/ppermute | solution.py:399
  78.3 1.7 %collective-permute-start.18 = (bf16[1,4,32,256]{3,2,1,0:T(8,128)(2,1)S(1)}, bf16[1,4,32,256]{3,2,1,0:T(8,128)(2,1)S(1)}, u32[]{:S(2)}, u32[]{:S(2)}) collective-permute-start(bf16[1,4,32,256]{3,2,1,0:T(8,128)(2,1)S(1)} %collective-permute-done.10.refs_5_), channel_id=1, source_target_pairs={{0,1},{1,0},{2,3},{3,2},{4,5},{5,4},{6,7},{7,6},{8,9},{9,8},{10,11... | collective-permute-start | bytes 196616 | tf_op jit(solution)/shard_map/ppermute | solution.py:399
  86.2 3.6 %collective-permute-start.21 = (bf16[4,32,256]{2,1,0:T(8,128)(2,1)S(1)}, bf16[4,32,256]{2,1,0:T(8,128)(2,1)S(1)}, u32[]{:S(2)}, u32[]{:S(2)}) collective-permute-start(bf16[4,32,256]{2,1,0:T(8,128)(2,1)S(1)} %get-tuple-element.33), channel_id=1, source_target_pairs={{0,4},{4,0},{8,12},{12,8},{1,5},{5,1},{9,13},{13,9},{2,6},{6,2},{1... | collective-permute-start | bytes 196616 | tf_op jit(solution)/shard_map/ppermute | solution.py:384
  86.2 4.2 %collective-permute-start.22 = (bf16[4,32,256]{2,1,0:T(8,128)(2,1)S(1)}, bf16[4,32,256]{2,1,0:T(8,128)(2,1)S(1)}, u32[]{:S(2)}, u32[]{:S(2)}) collective-permute-start(bf16[4,32,256]{2,1,0:T(8,128)(2,1)S(1)} %get-tuple-element.34), channel_id=1, source_target_pairs={{0,8},{4,12},{8,0},{12,4},{1,9},{5,13},{9,1},{13,5},{2,10},{6,14},... | collective-permute-start | bytes 196616 | tf_op jit(solution)/shard_map/ppermute | solution.py:384
  87.4 5.5 %collective-permute-start.23 = (bf16[4,32,256]{2,1,0:T(8,128)(2,1)S(1)}, bf16[4,32,256]{2,1,0:T(8,128)(2,1)S(1)}, u32[]{:S(2)}, u32[]{:S(2)}) collective-permute-start(bf16[4,32,256]{2,1,0:T(8,128)(2,1)S(1)} %get-tuple-element.35), channel_id=1, source_target_pairs={{0,12},{4,8},{8,4},{12,0},{1,13},{5,9},{9,5},{13,1},{2,14},{6,10},... | collective-permute-start | bytes 196616 | tf_op jit(solution)/shard_map/ppermute | solution.py:384
  93.0 6.8 %collective-permute-start.27 = (bf16[1,4,32,256]{3,2,1,0:T(8,128)(2,1)S(1)}, bf16[1,4,32,256]{3,2,1,0:T(8,128)(2,1)S(1)}, u32[]{:S(2)}, u32[]{:S(2)}) collective-permute-start(bf16[1,4,32,256]{3,2,1,0:T(8,128)(2,1)S(1)} %fusion.2.refs_0_), channel_id=1, source_target_pairs={{0,2},{2,0},{1,3},{3,1},{4,6},{6,4},{5,7},{7,5},{8,10},{10,8},{9,1... | collective-permute-start | bytes 196616 | tf_op jit(solution)/shard_map/ppermute | solution.py:397
  93.7 6.7 %collective-permute-start.26 = (bf16[1,4,32,256]{3,2,1,0:T(8,128)(2,1)S(1)}, bf16[1,4,32,256]{3,2,1,0:T(8,128)(2,1)S(1)}, u32[]{:S(2)}, u32[]{:S(2)}) collective-permute-start(bf16[1,4,32,256]{3,2,1,0:T(8,128)(2,1)S(1)} %fusion.2.refs_0_), channel_id=1, source_target_pairs={{0,12},{4,8},{8,4},{12,0},{1,13},{5,9},{9,5},{13,1},{2,14},{6,10},... | collective-permute-start | bytes 196616 | tf_op jit(solution)/shard_map/ppermute | solution.py:396
  95.1 7.3 %collective-permute-start.31 = (bf16[1,4,32,256]{3,2,1,0:T(8,128)(2,1)S(1)}, bf16[1,4,32,256]{3,2,1,0:T(8,128)(2,1)S(1)}, u32[]{:S(2)}, u32[]{:S(2)}) collective-permute-start(bf16[1,4,32,256]{3,2,1,0:T(8,128)(2,1)S(1)} %fusion.2.refs_0_), channel_id=1, source_target_pairs={{0,1},{1,0},{2,3},{3,2},{4,5},{5,4},{6,7},{7,6},{8,9},{9,8},{10,11... | collective-permute-start | bytes 196616 | tf_op jit(solution)/shard_map/ppermute | solution.py:399
  97.9 6.5 %collective-permute-start.25 = (bf16[1,4,32,256]{3,2,1,0:T(8,128)(2,1)S(1)}, bf16[1,4,32,256]{3,2,1,0:T(8,128)(2,1)S(1)}, u32[]{:S(2)}, u32[]{:S(2)}) collective-permute-start(bf16[1,4,32,256]{3,2,1,0:T(8,128)(2,1)S(1)} %fusion.2.refs_0_), channel_id=1, source_target_pairs={{0,8},{4,12},{8,0},{12,4},{1,9},{5,13},{9,1},{13,5},{2,10},{6,14},... | collective-permute-start | bytes 196616 | tf_op jit(solution)/shard_map/ppermute | solution.py:396
  98.4 7.3 %collective-permute-start.24 = (bf16[1,4,32,256]{3,2,1,0:T(8,128)(2,1)S(1)}, bf16[1,4,32,256]{3,2,1,0:T(8,128)(2,1)S(1)}, u32[]{:S(2)}, u32[]{:S(2)}) collective-permute-start(bf16[1,4,32,256]{3,2,1,0:T(8,128)(2,1)S(1)} %fusion.2.refs_0_), channel_id=1, source_target_pairs={{0,4},{4,0},{8,12},{12,8},{1,5},{5,1},{9,13},{13,9},{2,6},{6,2},{1... | collective-permute-start | bytes 196616 | tf_op jit(solution)/shard_map/ppermute | solution.py:396
  99.8 6.1 %collective-permute-start.35 = (bf16[1,4,32,256]{3,2,1,0:T(8,128)(2,1)S(1)}, bf16[1,4,32,256]{3,2,1,0:T(8,128)(2,1)}, u32[]{:S(2)}, u32[]{:S(2)}) collective-permute-start(bf16[1,4,32,256]{3,2,1,0:T(8,128)(2,1)S(1)} %collective-permute-done.27.refs_4_), channel_id=1, source_target_pairs={{0,1},{1,0},{2,3},{3,2},{4,5},{5,4},{6,7},{7,6},{8,9},{9,8},{10,11... | collective-permute-start | bytes 196616 | tf_op jit(solution)/shard_map/ppermute | solution.py:399
  100.3 6.5 %collective-permute-start.34 = (bf16[1,4,32,256]{3,2,1,0:T(8,128)(2,1)S(1)}, bf16[1,4,32,256]{3,2,1,0:T(8,128)(2,1)}, u32[]{:S(2)}, u32[]{:S(2)}) collective-permute-start(bf16[1,4,32,256]{3,2,1,0:T(8,128)(2,1)S(1)} %collective-permute-done.26.refs_3_), channel_id=1, source_target_pairs={{0,1},{1,0},{2,3},{3,2},{4,5},{5,4},{6,7},{7,6},{8,9},{9,8},{10,11... | collective-permute-start | bytes 196616 | tf_op jit(solution)/shard_map/ppermute | solution.py:399
  102.5 4.5 %collective-permute-start.30 = (bf16[1,4,32,256]{3,2,1,0:T(8,128)(2,1)S(1)}, bf16[1,4,32,256]{3,2,1,0:T(8,128)(2,1)}, u32[]{:S(2)}, u32[]{:S(2)}) collective-permute-start(bf16[1,4,32,256]{3,2,1,0:T(8,128)(2,1)S(1)} %collective-permute-done.26.refs_3_), channel_id=1, source_target_pairs={{0,2},{2,0},{1,3},{3,1},{4,6},{6,4},{5,7},{7,5},{8,10},{10,8},{9,1... | collective-permute-start | bytes 196616 | tf_op jit(solution)/shard_map/ppermute | solution.py:397
  104.4 3.2 %collective-permute-start.29 = (bf16[1,4,32,256]{3,2,1,0:T(8,128)(2,1)S(1)}, bf16[1,4,32,256]{3,2,1,0:T(8,128)(2,1)}, u32[]{:S(2)}, u32[]{:S(2)}) collective-permute-start(bf16[1,4,32,256]{3,2,1,0:T(8,128)(2,1)S(1)} %collective-permute-done.25.refs_2_), channel_id=1, source_target_pairs={{0,2},{2,0},{1,3},{3,1},{4,6},{6,4},{5,7},{7,5},{8,10},{10,8},{9,1... | collective-permute-start | bytes 196616 | tf_op jit(solution)/shard_map/ppermute | solution.py:397
  105.7 4.0 %collective-permute-start.28 = (bf16[1,4,32,256]{3,2,1,0:T(8,128)(2,1)S(1)}, bf16[1,4,32,256]{3,2,1,0:T(8,128)(2,1)}, u32[]{:S(2)}, u32[]{:S(2)}) collective-permute-start(bf16[1,4,32,256]{3,2,1,0:T(8,128)(2,1)S(1)} %collective-permute-done.24.refs_1_), channel_id=1, source_target_pairs={{0,2},{2,0},{1,3},{3,1},{4,6},{6,4},{5,7},{7,5},{8,10},{10,8},{9,1... | collective-permute-start | bytes 196616 | tf_op jit(solution)/shard_map/ppermute | solution.py:397
  105.9 4.9 %collective-permute-start.33 = (bf16[1,4,32,256]{3,2,1,0:T(8,128)(2,1)S(1)}, bf16[1,4,32,256]{3,2,1,0:T(8,128)(2,1)S(1)}, u32[]{:S(2)}, u32[]{:S(2)}) collective-permute-start(bf16[1,4,32,256]{3,2,1,0:T(8,128)(2,1)S(1)} %collective-permute-done.25.refs_2_), channel_id=1, source_target_pairs={{0,1},{1,0},{2,3},{3,2},{4,5},{5,4},{6,7},{7,6},{8,9},{9,8},{10,11... | collective-permute-start | bytes 196616 | tf_op jit(solution)/shard_map/ppermute | solution.py:399
  106.9 3.9 %collective-permute-start.32 = (bf16[1,4,32,256]{3,2,1,0:T(8,128)(2,1)S(1)}, bf16[1,4,32,256]{3,2,1,0:T(8,128)(2,1)S(1)}, u32[]{:S(2)}, u32[]{:S(2)}) collective-permute-start(bf16[1,4,32,256]{3,2,1,0:T(8,128)(2,1)S(1)} %collective-permute-done.24.refs_1_), channel_id=1, source_target_pairs={{0,1},{1,0},{2,3},{3,2},{4,5},{5,4},{6,7},{7,6},{8,9},{9,8},{10,11... | collective-permute-start | bytes 196616 | tf_op jit(solution)/shard_map/ppermute | solution.py:399
  106.9 3.8 %collective-permute-start.38 = (bf16[1,4,32,256]{3,2,1,0:T(8,128)(2,1)}, bf16[1,4,32,256]{3,2,1,0:T(8,128)(2,1)S(1)}, u32[]{:S(2)}, u32[]{:S(2)}) collective-permute-start(bf16[1,4,32,256]{3,2,1,0:T(8,128)(2,1)} %collective-permute-done.30.refs_7_), channel_id=1, source_target_pairs={{0,1},{1,0},{2,3},{3,2},{4,5},{5,4},{6,7},{7,6},{8,9},{9,8},{10,11... | collective-permute-start | bytes 196616 | tf_op jit(solution)/shard_map/ppermute | solution.py:399
  107.6 3.2 %collective-permute-start.37 = (bf16[1,4,32,256]{3,2,1,0:T(8,128)(2,1)}, bf16[1,4,32,256]{3,2,1,0:T(8,128)(2,1)S(1)}, u32[]{:S(2)}, u32[]{:S(2)}) collective-permute-start(bf16[1,4,32,256]{3,2,1,0:T(8,128)(2,1)} %collective-permute-done.29.refs_6_), channel_id=1, source_target_pairs={{0,1},{1,0},{2,3},{3,2},{4,5},{5,4},{6,7},{7,6},{8,9},{9,8},{10,11... | collective-permute-start | bytes 196616 | tf_op jit(solution)/shard_map/ppermute | solution.py:399
  109.6 2.2 %collective-permute-start.36 = (bf16[1,4,32,256]{3,2,1,0:T(8,128)(2,1)}, bf16[1,4,32,256]{3,2,1,0:T(8,128)(2,1)S(1)}, u32[]{:S(2)}, u32[]{:S(2)}) collective-permute-start(bf16[1,4,32,256]{3,2,1,0:T(8,128)(2,1)} %collective-permute-done.28.refs_5_), channel_id=1, source_target_pairs={{0,1},{1,0},{2,3},{3,2},{4,5},{5,4},{6,7},{7,6},{8,9},{9,8},{10,11... | collective-permute-start | bytes 196616 | tf_op jit(solution)/shard_map/ppermute | solution.py:399
  121.5 3.6 %collective-permute-start.39 = (bf16[272,128]{1,0:T(8,128)(2,1)S(1)}, bf16[272,128]{1,0:T(8,128)(2,1)S(1)}, u32[]{:S(2)}, u32[]{:S(2)}) collective-permute-start(bf16[272,128]{1,0:T(8,128)(2,1)S(1)} %get-tuple-element.40), channel_id=1, source_target_pairs={{0,4},{4,0},{8,12},{12,8},{1,5},{5,1},{9,13},{13,9},{2,6},{6,2},{1... | collective-permute-start | bytes 208904 | tf_op jit(solution)/shard_map/ppermute | solution.py:499
  121.5 4.2 %collective-permute-start.40 = (bf16[272,128]{1,0:T(8,128)(2,1)S(1)}, bf16[272,128]{1,0:T(8,128)(2,1)S(1)}, u32[]{:S(2)}, u32[]{:S(2)}) collective-permute-start(bf16[272,128]{1,0:T(8,128)(2,1)S(1)} %get-tuple-element.41), channel_id=1, source_target_pairs={{0,8},{4,12},{8,0},{12,4},{1,9},{5,13},{9,1},{13,5},{2,10},{6,14},... | collective-permute-start | bytes 208904 | tf_op jit(solution)/shard_map/ppermute | solution.py:499
  123.4 5.2 %collective-permute-start.41 = (bf16[272,128]{1,0:T(8,128)(2,1)S(1)}, bf16[272,128]{1,0:T(8,128)(2,1)S(1)}, u32[]{:S(2)}, u32[]{:S(2)}) collective-permute-start(bf16[272,128]{1,0:T(8,128)(2,1)S(1)} %get-tuple-element.42), channel_id=1, source_target_pairs={{0,12},{4,8},{8,4},{12,0},{1,13},{5,9},{9,5},{13,1},{2,14},{6,10},... | collective-permute-start | bytes 208904 | tf_op jit(solution)/shard_map/ppermute | solution.py:499
  128.8 7.8 %collective-permute-start.45 = (bf16[4,64,128]{2,1,0:T(8,128)(2,1)S(1)}, bf16[4,64,128]{2,1,0:T(8,128)(2,1)S(1)}, u32[]{:S(2)}, u32[]{:S(2)}) collective-permute-start(bf16[4,64,128]{2,1,0:T(8,128)(2,1)S(1)} %get-tuple-element.44), channel_id=1, source_target_pairs={{0,2},{2,0},{1,3},{3,1},{4,6},{6,4},{5,7},{7,5},{8,10},{10,8},{9,1... | collective-permute-start | bytes 196616 | tf_op jit(solution)/shard_map/ppermute | solution.py:506
  129.8 6.7 %collective-permute-start.44 = (f32[3,128]{1,0:T(4,128)S(1)}, f32[3,128]{1,0:T(4,128)S(1)}, u32[]{:S(2)}, u32[]{:S(2)}) collective-permute-start(f32[3,128]{1,0:T(4,128)S(1)} %reduce_sum.9.a), channel_id=1, source_target_pairs={{0,3},{1,2},{2,1},{3,0},{4,7},{5,6},{6,5},{7,4},{8,11},{9,10},{10,... | collective-permute-start | bytes 4616 | tf_op jit(solution)/shard_map/ppermute | solution.py:508
  132.8 3.8 %collective-permute-start.43 = (f32[3,128]{1,0:T(4,128)S(1)}, f32[3,128]{1,0:T(4,128)S(1)}, u32[]{:S(2)}, u32[]{:S(2)}) collective-permute-start(f32[3,128]{1,0:T(4,128)S(1)} %reduce_sum.9.a), channel_id=1, source_target_pairs={{0,2},{2,0},{1,3},{3,1},{4,6},{6,4},{5,7},{7,5},{8,10},{10,8},{9,1... | collective-permute-start | bytes 4616 | tf_op jit(solution)/shard_map/ppermute | solution.py:508
  133.7 2.9 %collective-permute-start.42 = (f32[3,128]{1,0:T(4,128)S(1)}, f32[3,128]{1,0:T(4,128)S(1)}, u32[]{:S(2)}, u32[]{:S(2)}) collective-permute-start(f32[3,128]{1,0:T(4,128)S(1)} %reduce_sum.9.a), channel_id=1, source_target_pairs={{0,1},{1,0},{2,3},{3,2},{4,5},{5,4},{6,7},{7,6},{8,9},{9,8},{10,11... | collective-permute-start | bytes 4616 | tf_op jit(solution)/shard_map/ppermute | solution.py:508
  (8 other events, 65.3 us)

commit v4 on v3

v4 whole, which is shorter than its diff:
```python
import functools

import jax
import jax.numpy as jnp
from jax import lax
from jax.experimental import pallas as pl
from jax.experimental.pallas import tpu as pltpu
from jax.sharding import PartitionSpec as P

ITERS = 3
EPS = 1e-06
F32, BF16 = jnp.float32, jnp.bfloat16
ROWS = 64
TAIL_ROWS = 16
SPLIT = 4
VMEM_LIMIT = 32 * 1024 * 1024
HB, VM, SM = pltpu.HBM, pltpu.VMEM, pltpu.SMEM


def _specs(*shapes):
    return [pl.BlockSpec(memory_space=s) for s in shapes]


def _hbm(*arrays):
    return [pltpu.with_memory_space_constraint(x, HB) for x in arrays]


def _vmem(*arrays):
    return [pltpu.with_memory_space_constraint(x, VM) for x in arrays]


def _fold(x):
    return jnp.sum(x.reshape(x.shape[0] // 8, 8, x.shape[1]), axis=0)


def _over(n_sec, states, width, n_acc, body):
    blocks = states // ROWS

    def step(i, accs):
        for b in range(blocks):
            accs = tuple(x + y for x, y in zip(accs, body(i, slice(b * ROWS, (b + 1) * ROWS))))
        return accs

    zero = tuple(jnp.zeros((8, width), F32) for _ in range(n_acc))
    return tuple(jnp.sum(a) for a in lax.fori_loop(0, n_sec, step, zero))


def _low(cfg, value, env_pos):
    low = value.astype(BF16)
    if cfg["direct"]:
        half = value.shape[1] // 2
        turned = jnp.concatenate([value[:, half:], value[:, :half]], axis=1).astype(BF16)
        low = jnp.where(env_pos == 0, low, turned)
    return low


def _put_scalars(ref, values):
    shape = ref.shape
    row = lax.broadcasted_iota(jnp.int32, shape, 0)
    out = jnp.zeros(shape, F32)
    for index, value in enumerate(values):
        out = jnp.where(row == index, value, out)
    ref[...] = out


def _first_kernel(cfg, meta, psi, psi_o, pre, pre_o, right_h, start, pret_h, inner, scale_ref, vb, right, pret, sem):
    sec, states, width = psi.shape
    n_sec = sec * cfg["n_blk"]
    blk, env_pos = meta[2], meta[0]
    base = blk * sec
    load = pltpu.make_async_copy(_group(cfg, meta, right_h), right, sem.at[0])
    load.start()
    for part, (p_ref, c_ref) in enumerate(((psi, pre), (psi_o, pre_o))):
        for k in range(p_ref.shape[0]):
            at = lax.rem(base + part * sec + k, n_sec)
            live = meta[cfg["dims_at"] + at]
            row = lax.broadcasted_iota(jnp.int32, (states, width), 0)
            col = lax.broadcasted_iota(jnp.int32, (states, width), 1)
            value = jnp.where((row < live) & (col < live), p_ref[k].astype(F32).T, 0.0)
            start[at] = value.astype(BF16)
            pret[at] = c_ref[k].T
    save = pltpu.make_async_copy(pret, pret_h, sem.at[1])
    save.start()

    def square(s, r):
        value = start[s, r, :].astype(F32)
        return (_fold(value * value),)

    (total,) = _over(n_sec, states, width, 1, square)
    scale = lax.rsqrt(total / (n_sec * states * width) + EPS)
    _put_scalars(scale_ref, [scale] * 8)

    def make(s, r):
        vb[s, r, :] = _low(cfg, start[s, r, :].astype(F32) * scale, env_pos)
        return ()

    _over(n_sec, states, width, 0, make)
    load.wait()
    terms, held = right.shape[:2]
    for k in range(held):
        for t in range(terms):
            chosen = vb[meta[cfg["pair_at"] + t * held + k]]
            inner[t, k] = jnp.dot(right[t, k], chosen, preferred_element_type=F32).astype(BF16)
    save.wait()


def _group(cfg, meta, ref):
    return ref.at[:, pl.ds(meta[3] * cfg["held"], cfg["held"])]


def _env_moves(cfg, meta, places, refs, right, left, sem, first=0):
    moves = []
    for ref, (kind, t0, r0, own) in zip(refs, places):
        src = _group(cfg, meta, ref) if own else ref
        step = ref.shape[0] // SPLIT
        for i in range(SPLIT):
            t = pl.ds(t0 + i * step, step)
            dst = right.at[t] if kind == "right" else left.at[t, :, pl.ds(r0, ref.shape[2]), :]
            moves.append(pltpu.make_async_copy(src.at[pl.ds(i * step, step)], dst, sem.at[first + len(moves)]))
            moves[-1].start()
    return moves


def _own_sigma_kernel(cfg, places, meta, inner, *refs):
    lefts, acc, left, sem = refs[: len(places)], refs[-3], refs[-2], refs[-1]
    for c in _env_moves(cfg, meta, places, lefts, None, left, sem):
        c.wait()
    for k in range(inner.shape[1]):
        total = None
        for t in range(inner.shape[0]):
            got = jnp.dot(inner[t, k], left[t, k], preferred_element_type=F32)
            total = got if total is None else total + got
        acc[k] = total


def _far_sigma_kernel(cfg, places, t0, meta, vb, acc, *refs):
    envs, out, right, left, sem = refs[: len(places)], refs[-4], refs[-3], refs[-2], refs[-1]
    terms, held = right.shape[:2]
    moves = _env_moves(cfg, meta, places, envs, right, left, sem)
    for c in moves[:SPLIT]:
        c.wait()
    inner = []
    for k in range(held):
        for t in range(terms):
            chosen = vb[meta[cfg["pair_at"] + (t0 + t) * held + k]]
            inner.append(jnp.dot(right[t, k], chosen, preferred_element_type=F32).astype(BF16))
    for c in moves[SPLIT:]:
        c.wait()
    for k in range(held):
        total = acc[k]
        for t in range(terms):
            total = total + jnp.dot(inner[k * terms + t], left[t, k], preferred_element_type=F32)
        out[k] = total.astype(out.dtype)


def _step_kernel(cfg, step, places, env_places, last, meta, *refs):
    it = iter(refs)
    take = lambda n: [next(it) for _ in range(n)]
    shards = take(len(places))
    (start, scale_ref), vecs, (pre_h,) = take(2), take(step - 1), take(1)
    olds_h, envs_h, (sig_h,) = take(step - 1), take(len(env_places)), take(1)
    vnew, dots = (None, None) if last else take(2)
    outs = take(cfg["n_out"])
    if last:
        vnew, turned = take(2)
    olds = take(step - 1)
    right, left, pre, sig, vb, acc, sem = take(7)
    env_pos, z, blk, mine_at = meta[0], meta[1], meta[2], meta[3]
    n_sec, states, width = vnew.shape
    sec, held_sec, half = cfg["sec"], cfg["held"], right.shape[2]
    count = n_sec * states * width
    n_held = sec // held_sec

    def sector(b, h, k):
        if not cfg["direct"]:
            return b * sec + k
        return (blk ^ b) * sec + (mine_at ^ h) * held_sec + k

    order = [(b, h, k) for b in range(cfg["n_blk"]) for h in range(n_held) for k in range(held_sec)]
    pre_moves = [pltpu.make_async_copy(pre_h.at[sector(*o)], pre.at[sector(*o)], sem.at[i]) for i, o in enumerate(order)]
    old_moves = [pltpu.make_async_copy(a, b, sem.at[n_sec + i]) for i, (a, b) in enumerate(zip(olds_h, olds))]
    for c in pre_moves + old_moves:
        c.start()
    env_moves = _env_moves(cfg, meta, env_places, envs_h, right, left, sem, n_sec + step)
    save = pltpu.make_async_copy(sig, sig_h, sem.at[n_sec + step - 1])
    scale0 = scale_ref[0, 0]
    basis = [lambda s, r: start[s, r, :].astype(F32) * scale0]
    basis += [lambda s, r, v=v: v[s, r, :] for v in vecs]

    pairs = [(j, l) for j in range(step) for l in range(j, step)]
    accs = [jnp.zeros((8, width), F32) for _ in range(2 * step + len(pairs))]
    blocks = {o: [] for o in order}
    for ref, place in zip(shards, places):
        if place is None:
            for b, h, k in order:
                for r in range(0, states, ROWS):
                    at = b * sec + k
                    blocks[b, h, k].append((ref, at, slice(r, r + ROWS), at, slice(r, r + ROWS)))
            continue
        b, e, h = place
        for k in range(held_sec):
            for r in range(0, half, ROWS):
                rows = pl.ds(pl.multiple_of((env_pos ^ e) * half + r, ROWS), ROWS)
                blocks[b, h, k].append((ref, k, slice(r, r + ROWS), sector(b, h, k), rows))
    for ready, o in zip(pre_moves, order):
        ready.wait()
        for ref, k, r, s, rows in blocks[o]:
            low = ref[k, r, :]
            sig[s, rows, :] = low
            value, cond = low.astype(F32), pre[s, rows, :]
            scaled = value * cond
            held = [b(s, rows) for b in basis]
            found = [_fold(h * value) for h in held] + [_fold(h * scaled) for h in held]
            condh = [h * cond for h in held]
            found += [_fold(condh[j] * held[l]) for j, l in pairs]
            accs = [a + t for a, t in zip(accs, found)]
    save.start()
    sums = [jnp.sum(a) / count for a in accs]
    proj = sums[:step]
    gram = {}
    for (j, l), value in zip(pairs, sums[2 * step :]):
        gram[j, l] = gram[l, j] = value
    back = [sums[step + j] - sum(proj[l] * gram[j, l] for l in range(step)) for j in range(step)]

    over = functools.partial(_over, n_sec, states, width)
    for c in old_moves:
        c.wait()

    def trial_pass(s, r):
        value = sig[s, r, :].astype(F32)
        held = [b(s, r) for b in basis]
        trial = value
        for h, b in zip(proj, held):
            trial = trial - h * b
        trial = trial * pre[s, r, :]
        for g, b in zip(back, held):
            trial = trial - g * b
        vnew[s, r, :] = trial
        crossed = [o[s, r, :].astype(F32) for o in olds] + [value]
        return (_fold(trial * trial), *[_fold(trial * o) for o in crossed])

    square, *cross = over(1 + step, trial_pass)
    scale = lax.rsqrt(square / count + EPS)
    cross = [x * scale / count for x in cross]

    def final_pass(s, r):
        value = vnew[s, r, :] * scale
        vnew[s, r, :] = value
        vb[s, r, :] = _low(cfg, value, env_pos)
        return ()

    over(0, final_pass)
    for c in env_moves:
        c.wait()
    for k in range(held_sec):
        total = None
        for t in range(right.shape[0]):
            chosen = vb[meta[cfg["pair_at"] + t * held_sec + k]]
            inner = jnp.dot(right[t, k], chosen, preferred_element_type=F32).astype(BF16)
            got = jnp.dot(inner, left[t, k], preferred_element_type=F32)
            total = got if total is None else total + got
        acc[k] = total
    scalars = proj + cross
    if not last:
        outs[0][...] = acc[...].astype(outs[0].dtype)
        _put_scalars(dots, scalars)
        save.wait()
        return

    rows = pl.ds(pl.multiple_of(env_pos * half, half), half)
    mine = []
    for b in [*basis, lambda s, r: vnew[s, r, :]]:
        total = jnp.zeros((8, width), F32)
        for k in range(held_sec):
            total = total + _fold(b(sector(0, 0, k) if cfg["direct"] else blk * sec + k, rows) * acc[k])
        mine.append(jnp.sum(total) / count)
    _put_scalars(outs[0], scalars)
    if cfg["direct"]:
        for k in range(held_sec):
            turned[k] = acc[k].T
        span = states // 2
        side = lax.div(z, 2)
        tail = _addends(mine, half)
        for out, at in ((outs[1], side), (outs[2], 1 - side)):
            for k in range(held_sec):
                rows = pl.ds(pl.multiple_of(at * span, span), span)
                out[k * span : (k + 1) * span, :] = turned[k, rows, :].astype(out.dtype)
            out[held_sec * span :, :] = tail.astype(out.dtype)
    else:
        _put_scalars(outs[1], mine)
        for k in range(held_sec):
            outs[2][k] = acc[k].T
    save.wait()


def _addends(values, width):
    row = lax.broadcasted_iota(jnp.int32, (TAIL_ROWS, width), 0)
    tail = jnp.zeros((TAIL_ROWS, width), F32)
    for j, value in enumerate(values):
        rest = jnp.broadcast_to(value, (TAIL_ROWS, width))
        for p in range(3):
            cut = rest.astype(BF16).astype(F32)
            tail = jnp.where(row == 3 * j + p, cut, tail)
            rest = rest - cut
    return tail


def _added(*tails):
    return [
        sum(tail[3 * j + p : 3 * j + p + 1, 0:1].astype(F32) for tail in tails for p in range(3)) for j in range(ITERS)
    ]


def _rows_kernel(cfg, meta, sig_a, sig_b, out_h, sig, turned, rows, sem):
    chunk = rows.shape[2]
    first = pl.ds(pl.multiple_of(meta[1] * chunk, chunk), chunk)
    own = pl.ds(meta[2] * cfg["sec"], cfg["sec"])
    loads = [pltpu.make_async_copy(ref.at[own], sig.at[i], sem.at[i]) for i, ref in enumerate((sig_a, sig_b))]
    for c in loads:
        c.start()
    for i, c in enumerate(loads):
        c.wait()
        for k in range(rows.shape[1]):
            turned[i, k] = sig[i, k].astype(F32).T
            rows[i, k] = turned[i, k, first, :]
    save = pltpu.make_async_copy(rows, out_h.at[0 : rows.shape[0]], sem.at[2])
    save.start()
    save.wait()


def _merge_kernel(cfg, meta, kept, got, own, keep_out, give_out):
    held, chunk, half = own.shape
    span = 2 * chunk
    z = meta[1]
    at_tail = slice(held * span, held * span + TAIL_ROWS)
    tail = _addends(_added(kept[at_tail, :], got[at_tail, :]), half)
    side = lax.rem(z, 2)
    for which, out in ((side, keep_out), (1 - side, give_out)):
        first = pl.multiple_of(which * chunk, chunk)
        for k in range(held):
            rows = pl.ds(pl.multiple_of(k * span + first, chunk), chunk)
            live = meta[cfg["dims_at"] + meta[2] * cfg["sec"] + meta[3] * held + k]
            at_row = lax.div(z, 2) * span + first + lax.broadcasted_iota(jnp.int32, (chunk, half), 0)
            at_col = meta[0] * half + lax.broadcasted_iota(jnp.int32, (chunk, half), 1)
            value = kept[rows, :] + got[rows, :].astype(F32)
            value = jnp.where((at_row < live) & (at_col < live), value, 0.0)
            out[k * chunk : (k + 1) * chunk, :] = value.astype(BF16)
            if out is keep_out:
                own[k] = value
        out[held * chunk :, :] = tail.astype(BF16)


def _final_kernel(cfg, meta, own, by_env, by_term, by_both, held_h, out_h, rows, sem):
    del held_h
    held, chunk, half = own.shape
    for k in range(held):
        at = slice(k * chunk, (k + 1) * chunk)
        pairs = (own[k], by_env[at, :].astype(F32)), (by_term[at, :].astype(F32), by_both[at, :].astype(F32))
        for h, (mine, other) in enumerate(pairs):
            both = jnp.where(meta[0] == 0, mine, other), jnp.where(meta[0] == 0, other, mine)
            rows[0, (meta[3] ^ h) * held + k] = jnp.concatenate(both, axis=1)
    save = pltpu.make_async_copy(rows, out_h.at[ITERS - 1 : ITERS], sem)
    save.start()
    save.wait()


def _dots_kernel(at, own, by_env, by_term, by_both, out):
    found = _added(*(ref[at : at + TAIL_ROWS, :] for ref in (own, by_env, by_term, by_both)))
    _put_scalars(out, found)


def _subspace_kernel(first, known, dots, other, sub):
    row = lax.broadcasted_iota(jnp.int32, sub.shape, 0)
    col = lax.broadcasted_iota(jnp.int32, sub.shape, 1)
    out = jnp.zeros(sub.shape, F32)
    for i, j, ref, at in ((0, 0, first, 0), (0, 1, first, 1), (0, 2, known, 2),
                          (1, 0, known, 0), (1, 1, known, 1), (1, 2, known, 3)):
        out = jnp.where((row == i) & (col == j), ref[at : at + 1, 0:1], out)
    for j in range(ITERS):
        value = dots[j : j + 1, 0:1] + other[j : j + 1, 0:1]
        out = jnp.where((row == ITERS - 1) & (col == j), value, out)
    sub[...] = out


def solution(mesh):
    n_env, n_term, n_blk = (mesh.shape[a] for a in ("env", "term", "blk"))

    def on_device(psi, left_env, right_env, pairing, sector_dims, precond):
        return _on_device(n_env, n_term, n_blk, psi, left_env, right_env, pairing, sector_dims, precond)

    placed = (
        P(("parts", "blk"), None, None),
        P(("parts", "term"), "blk", "env", None),
        P(("parts", "term"), "blk", "env", None),
        P(("parts", "term"), "blk"),
        P("parts"),
        P(("parts", "blk"), None, None),
    )
    return jax.shard_map(
        on_device,
        mesh=mesh,
        in_specs=placed,
        out_specs=(P(None, ("parts", "blk"), "term", None), P("parts", None)),
        check_vma=False,
    )


def _xor(axis, n, s):
    return functools.partial(lax.ppermute, axis_name=axis, perm=[(i, i ^ s) for i in range(n)])


def _cut_kernel(held, which, env_h, *refs):
    count = (len(refs) - 1) // 2
    outs, bufs, sem = refs[:count], refs[count:-1], refs[-1]
    loads, saves = [], []
    for i, (out, buf) in enumerate(zip(outs, bufs)):
        at = (1 - which[0] if i == 0 else which[0]) * held
        loads.append(pltpu.make_async_copy(env_h.at[:, pl.ds(at, held)], buf, sem.at[0, i]))
        saves.append(pltpu.make_async_copy(buf, out, sem.at[1, i]))
        loads[-1].start()
    for load, save in zip(loads, saves):
        load.wait()
        save.start()
    for save in saves:
        save.wait()


def _cut(env, mine, held, count):
    shape = (env.shape[0], held, *env.shape[2:])
    return pl.pallas_call(
        functools.partial(_cut_kernel, held),
        out_shape=tuple(HB(shape, BF16) for _ in range(count)),
        in_specs=_specs(SM, HB),
        out_specs=tuple(_specs(*[HB] * count)),
        scratch_shapes=[pltpu.VMEM(shape, BF16) for _ in range(count)] + [pltpu.SemaphoreType.DMA((2, count))],
        compiler_params=pltpu.CompilerParams(vmem_limit_bytes=VMEM_LIMIT),
        name="sectors_to_send",
    )(mine.astype(jnp.int32).reshape(1), *_hbm(env))


def _on_device(n_env, n_term, n_blk, psi, left_env, right_env, pairing, sector_dims, precond):
    sec, states, width = psi.shape
    terms = left_env.shape[0]
    n_sec = sec * n_blk
    half = right_env.shape[2]
    direct = n_env == 2 and n_blk == 2 and n_term == 4 and sec % 2 == 0 and terms % 2 == 0
    chunk = states // n_term
    held = sec // 2 if direct else sec
    cfg = dict(direct=direct, n_blk=n_blk, sec=sec, held=held)
    env_pos, term_pos, blk_pos = (lax.axis_index(a) for a in ("env", "term", "blk"))
    mine = (term_pos ^ (term_pos >> 1)) & 1 if direct else jnp.zeros_like(term_pos)
    next_term, far_term = _xor("term", 4, 1), _xor("term", 4, 3)
    other_env, other_blk = _xor("env", 2, 1), _xor("blk", 2, 1)
    corners = functools.partial(
        lax.ppermute, axis_name=("term", "env"), perm=[(2 * t + e, 2 * (t ^ 1) + (e ^ 1)) for t in range(4) for e in range(2)]
    )
    group = lambda x, which: lax.dynamic_slice_in_dim(x, which * held, held, 1)

    if direct:
        to_next, to_env = _cut(left_env, mine, held, 2)
        (right_to_next,) = _cut(right_env, mine, held, 1)
        psi_o, pre_o = other_blk(psi), other_blk(precond)
        next_left = next_term(to_next)
        far_left = other_env(to_env)
        next_right = next_term(right_to_next)
        next_far_left = other_env(next_left)
        own_table = group(pairing, mine)
        own_places = [("left", 0, 0, True), ("left", 0, half, False)]
        next_places = [("right", 0, 0, False), ("left", 0, 0, False), ("left", 0, half, False)]
        own_envs, next_envs = [left_env, far_left], [next_right, next_left, next_far_left]
        n_terms = 2 * terms
        shift = lambda place: (place[0], place[1] + terms, *place[2:])
        env_places = [("right", 0, 0, True), *own_places, *map(shift, next_places)]
        envs = [right_env, *own_envs, *next_envs]
    else:
        own_envs = [lax.all_gather(left_env, "env", axis=2, tiled=True)]
        own_places = [("left", 0, 0, False)]
        own_table = pairing
        n_terms = terms
        env_places, envs = [("right", 0, 0, True), *own_places], [right_env, *own_envs]
        psi_o, pre_o = (
            lax.dynamic_slice_in_dim(
                jnp.concatenate([lax.all_gather(x, "blk", axis=0, tiled=True)] * 2, axis=0),
                (blk_pos + 1) * sec,
                sec * (n_blk - 1),
                0,
            )
            for x in (psi, precond)
        )
    flat = jnp.stack([x.astype(jnp.int32) for x in (env_pos, term_pos, blk_pos, mine)])
    own_meta = jnp.concatenate([flat, sector_dims.reshape(-1), own_table.reshape(-1)])
    cfg["dims_at"] = 4
    cfg["pair_at"] = 4 + n_sec

    full = (n_sec, states, width)
    params = pltpu.CompilerParams(vmem_limit_bytes=VMEM_LIMIT)
    dma = pltpu.SemaphoreType.DMA
    start, pret, inner, scale0, vb0 = pl.pallas_call(
        functools.partial(_first_kernel, cfg),
        out_shape=(
            VM(full, BF16),
            HB(full, F32),
            VM((terms, held, half, states), BF16),
            VM((8, 128), F32),
            VM(full, BF16),
        ),
        in_specs=_specs(SM, VM, VM, VM, VM, HB),
        out_specs=_specs(VM, HB, VM, VM, VM),
        scratch_shapes=[pltpu.VMEM((terms, held, half, states), BF16), pltpu.VMEM(full, F32), dma((2,))],
        compiler_params=params,
        name="start_vector",
    )(own_meta, psi, psi_o, precond, pre_o, *_hbm(right_env))

    partial = pl.pallas_call(
        functools.partial(_own_sigma_kernel, cfg, own_places),
        out_shape=VM((held, half, width), F32),
        in_specs=_specs(SM, VM, *[HB] * len(own_envs)),
        out_specs=_specs(VM)[0],
        scratch_shapes=[pltpu.VMEM((terms, held, states, width), BF16), dma((SPLIT * len(own_envs),))],
        compiler_params=params,
        name="first_sigma_own_terms",
    )(own_meta, *_vmem(inner), *_hbm(*own_envs))
    meta = own_meta
    if direct:
        next_pairing = next_term(lax.optimization_barrier((pairing, partial))[0])
        meta = jnp.concatenate([own_meta, group(next_pairing, mine).reshape(-1)])
        partial = pl.pallas_call(
            functools.partial(_far_sigma_kernel, cfg, next_places, terms),
            out_shape=VM((held, half, width), BF16),
            in_specs=_specs(SM, VM, VM, *[HB] * len(next_envs)),
            out_specs=_specs(VM)[0],
            scratch_shapes=[
                pltpu.VMEM((terms, held, half, states), BF16),
                pltpu.VMEM((terms, held, states, width), BF16),
                dma((SPLIT * len(next_envs),)),
            ],
            compiler_params=params,
            name="first_sigma_next_terms",
        )(meta, *_vmem(vb0, partial), *_hbm(*next_envs))

    live_own = lax.dynamic_slice_in_dim(sector_dims, blk_pos * sec, sec)

    def masked(value, row0, live):
        row = row0 + lax.broadcasted_iota(jnp.int32, value.shape, 1)
        col = lax.broadcasted_iota(jnp.int32, value.shape, 2)
        live = live[:, None, None]
        return jnp.where((row < live) & (col < live), value, 0.0).astype(BF16)

    def combine(partial):
        if direct:
            total = partial.astype(F32) + far_term(partial).astype(F32)
            shard = masked(total, env_pos * half, lax.dynamic_slice_in_dim(live_own, mine * held, held))
            here = [shard, next_term(shard), other_env(shard), corners(shard)]
            there = [other_blk(x) for x in here]
            return here + there, [(b, e, h) for b in range(2) for e, h in ((0, 0), (0, 1), (1, 0), (1, 1))]
        flat_sum = lax.psum_scatter(partial.reshape(sec * half, width), "term", scatter_dimension=0, tiled=True)
        whole = lax.all_gather(flat_sum, "term", axis=0, tiled=True).reshape(sec, half, width)
        whole = masked(lax.all_gather(whole, "env", axis=1, tiled=True), 0, live_own)
        return [lax.all_gather(whole, "blk", axis=0, tiled=True)], [None]

    vecs, olds = [], []
    for step in range(1, ITERS):
        last = step + 1 == ITERS
        shards, places = combine(partial)
        if last:
            outs = [VM((8, 128), F32)]
            if direct:
                size = (held * states // 2 + TAIL_ROWS, half)
                outs += [VM(size, F32), VM(size, BF16)]
            else:
                outs += [VM((8, 128), F32), VM((sec, states, half), F32)]
            made = (HB(full, BF16),)
        else:
            outs = [VM((held, half, width), BF16 if direct else F32)]
            made = (HB(full, BF16), VM(full, F32), VM((8, 128), F32))
        n_hbm = 1 + (step - 1) + len(envs)
        results = pl.pallas_call(
            functools.partial(_step_kernel, dict(cfg, n_out=len(outs)), step, places, env_places, last),
            out_shape=(*made, *outs),
            in_specs=_specs(SM, *[VM] * (len(shards) + 2 + len(vecs)), *[HB] * n_hbm),
            out_specs=tuple(_specs(HB, *[VM] * (len(made) - 1 + len(outs)))),
            scratch_shapes=[pltpu.VMEM(full, F32), pltpu.VMEM((held, states, half), F32)] * last
            + [pltpu.VMEM(full, BF16)] * (step - 1)
            + [
                pltpu.VMEM((n_terms, held, half, states), BF16),
                pltpu.VMEM((n_terms, held, states, width), BF16),
                pltpu.VMEM(full, F32),
                pltpu.VMEM(full, BF16),
                pltpu.VMEM(full, BF16),
                pltpu.VMEM((held, half, width), F32),
                dma((n_sec + step + SPLIT * len(envs),)),
            ],
            compiler_params=params,
            name=f"vector_and_sigma_{step}",
        )(
            meta,
            *_vmem(*shards, start, scale0, *vecs),
            *_hbm(pret, *olds, *envs),
        )
        olds.append(results[0])
        if last:
            known, *pieces = results[1:]
        else:
            vecs.append(results[1])
            first, partial = results[2:]

    out_shape = (ITERS, sec, chunk, states)
    if direct:
        rows01 = pl.pallas_call(
            functools.partial(_rows_kernel, cfg),
            out_shape=HB(out_shape, F32),
            in_specs=_specs(SM, HB, HB),
            out_specs=_specs(HB)[0],
            scratch_shapes=[
                pltpu.VMEM((ITERS - 1, sec, states, states), BF16),
                pltpu.VMEM((ITERS - 1, sec, states, states), F32),
                pltpu.VMEM((ITERS - 1, sec, chunk, states), F32),
                dma((3,)),
            ],
            compiler_params=params,
            cost_estimate=pl.CostEstimate(flops=1 << 20, bytes_accessed=1 << 22, transcendentals=0),
            name="first_rows",
        )(meta, *_hbm(*olds))
        kept, given = pieces
        got = far_term(given)
        size = (held * chunk + TAIL_ROWS, half)
        own, keep, give = pl.pallas_call(
            functools.partial(_merge_kernel, cfg),
            out_shape=(VM((held, chunk, half), F32), VM(size, BF16), VM(size, BF16)),
            in_specs=_specs(SM, VM, VM),
            out_specs=tuple(_specs(VM, VM, VM)),
            compiler_params=params,
            name="last_sums",
        )(meta, *_vmem(lax.optimization_barrier((kept, rows01))[0], got))
        parts = [other_env(keep), next_term(give), corners(give)]
        dots = pl.pallas_call(
            functools.partial(_dots_kernel, held * chunk),
            out_shape=VM((8, 128), F32),
            in_specs=_specs(*[VM] * 4),
            out_specs=_specs(VM)[0],
            compiler_params=params,
            name="last_dots",
        )(*_vmem(keep, *parts))
        other_dots = other_blk(dots)
        sigmas = pl.pallas_call(
            functools.partial(_final_kernel, cfg),
            out_shape=HB(out_shape, F32),
            in_specs=_specs(SM, *[VM] * 4, HB),
            out_specs=_specs(HB)[0],
            scratch_shapes=[pltpu.VMEM((1, sec, chunk, states), F32), dma],
            input_output_aliases={5: 0},
            compiler_params=params,
            name="last_rows",
        )(meta, *_vmem(own, *parts), *_hbm(rows01))
        subspace = pl.pallas_call(
            _subspace_kernel,
            out_shape=jax.ShapeDtypeStruct((ITERS, ITERS), F32),
            in_specs=_specs(*[VM] * 4),
            out_specs=_specs(VM)[0],
            compiler_params=params,
            name="subspace",
        )(*_vmem(first, known, dots, other_dots))
        return sigmas, subspace
    dots = pieces.pop(0)
    own = lax.psum_scatter(pieces[0], "term", scatter_dimension=1, tiled=True)
    both = lax.all_gather(own, "env", axis=2, tiled=True)
    row = term_pos * chunk + lax.broadcasted_iota(jnp.int32, both.shape, 1)
    col = lax.broadcasted_iota(jnp.int32, both.shape, 2)
    live = live_own[:, None, None]
    both = jnp.where((row < live) & (col < live), both, 0.0)
    rows_out = []
    for sig in olds:
        part = lax.dynamic_slice(sig, (blk_pos * sec, 0, term_pos * chunk), (sec, states, chunk))
        rows_out.append(jnp.swapaxes(part, 1, 2).astype(F32))
    rows_out.append(both)
    scal = lax.psum(dots, ("term", "env", "blk"))[:ITERS, 0]
    first, second = first[:, 0], known[:, 0]
    subspace = jnp.stack([
        jnp.stack([first[0], first[1], second[2]]),
        jnp.stack([second[0], second[1], second[3]]),
        scal,
    ])
    return jnp.stack(rows_out), subspace
```

time: 139 us -> 122 us (0.88)
  starting transfers between devices: 54.2 us -> 42.5 us
  waiting for transfers between devices: 48 us -> 40.5 us
  Pallas kernels: 25.1 us -> 32.2 us
  local copies, waits for them, and re-layouts: 9.99 us -> 5.69 us
    ppermute x44 -> x26, starting transfers between devices: 53.2 us -> 38.5 us  [the longest x8 11.8 us: combine(): there = [other_blk(x) for x in here]]
    pallas_call x2 -> x8, Pallas kernels: 4.82 us -> 13 us  [the longest x2 4.99 us: _cut(): pl.pallas_call(functools.partial(_cut_kernel, held), out_shape=tuple((HB(...]
    ppermute x44 -> x26, waiting for transfers between devices: 47.1 us -> 39.2 us  [the longest x1 18.5 us: _on_device(): next_left = next_term(to_next)]
    unnamed x21 -> x18, local copies, waits for them, and re-layouts: 8.42 us -> 5.11 us
    ppermute x2, starting transfers between devices: 0.96 us -> 3.93 us  [_on_device(): psi_o, pre_o = (other_blk(psi), other_blk(precond))]
  transfers between devices with their start and end apart: 46 -> 28, of which waited for: 15 -> 16; matrix products, arithmetic and copies ran while one was open for 2% -> 0% of each run, Pallas kernels for 4% -> 10%
where the time goes in v4:
time: 122 us
  starting transfers between devices  42.5 us (35%)
  waiting for transfers between devices  40.5 us (33%)
  Pallas kernels  32.2 us (26%)
  local copies, waits for them, and re-layouts  5.69 us (5%)
    ppermute x1, waiting for transfers between devices, _on_device(): next_left = next_term(to_next)  18.5 us
    pallas_call x2, Pallas kernels, _on_device(): pl.pallas_call(functools.partial(_step_kernel, dict(cfg, n_out=len(outs))...  12.9 us
    ppermute x8, starting transfers between devices, combine(): there = [other_blk(x) for x in here]  11.8 us
    ppermute x6, starting transfers between devices, combine(): here = [shard, next_term(shard), other_env(shard), corners(shard)]  7.14 us
    ppermute x2, waiting for transfers between devices, combine(): total = partial.astype(F32) + far_term(partial).astype(F32)  6.5 us
    ppermute x2, starting transfers between devices, combine(): total = partial.astype(F32) + far_term(partial).astype(F32)  6.02 us
    unnamed x18, local copies, waits for them, and re-layouts  5.11 us
    pallas_call x2, Pallas kernels, _cut(): pl.pallas_call(functools.partial(_cut_kernel, held), out_shape=tuple((HB(...  4.99 us
  transfers between devices with their start and end apart: 28, of which 16 were waited for; matrix products, arithmetic and copies ran while one was open for 0% of the time, Pallas kernels for 10%

profile of v4, /device:TPU:1, one launch (start us, length us, event | category | flops | bytes accessed | tf_op | source)
XLA Modules:
  0.0 121.9 jit_solution(17332059910454612120)
XLA Ops:
  0.6 2.7 %sectors_to_send.2 = (bf16[8,2,128,256]{3,2,1,0:T(8,128)(2,1)}, bf16[8,2,128,256]{3,2,1,0:T(8,128)(2,1)}) custom-call(s32[1]{0:T(128)} %bitcast.3.which, bf16[8,4,128,256]{3,2,1,0:T(8,128)(2,1)} %refs_14_.1), custom_call_target="tpu_custom_call" | custom-call | tf_op jit(solution)/shard_map/sectors_to_send/pallas_call | solution.py:430
  3.4 2.2 %collective-permute-start.5 = (bf16[8,2,128,256]{3,2,1,0:T(8,128)(2,1)}, bf16[8,2,128,256]{3,2,1,0:T(8,128)(2,1)}, u32[]{:S(2)}, u32[]{:S(2)}) collective-permute-start(bf16[8,2,128,256]{3,2,1,0:T(8,128)(2,1)} %get-tuple-element.26), channel_id=1, source_target_pairs={{0,4},{4,0},{8,12},{12,8},{1,5},{5,1},{9,13},{13,9},{2,6},{6,2},{1... | collective-permute-start | bytes 3145736 | tf_op jit(solution)/shard_map/ppermute | solution.py:463
  5.6 1.0 collective-permute-start.1
  6.5 1.2 collective-permute-start.2
  7.7 2.3 %sectors_to_send.3 = bf16[8,2,128,256]{3,2,1,0:T(8,128)(2,1)} custom-call(s32[1]{0:T(128)} %bitcast.3.which, bf16[8,4,128,256]{3,2,1,0:T(8,128)(2,1)} %refs_13_.1), custom_call_target="tpu_custom_call" | custom-call | tf_op jit(solution)/shard_map/sectors_to_send/pallas_call | solution.py:430
  10.3 18.5 %collective-permute-done.5.refs_1_.refs_15_.refs_17_ = bf16[8,2,128,256]{3,2,1,0:T(8,128)(2,1)} collective-permute-done((bf16[8,2,128,256]{3,2,1,0:T(8,128)(2,1)}, bf16[8,2,128,256]{3,2,1,0:T(8,128)(2,1)}, u32[]{:S(2)}, u32[]{:S(2)}) %collective-permute-start.5) | collective-permute-done | bytes 1048608 | tf_op jit(solution)/shard_map/ppermute | solution.py:463
  28.8 1.1 collective-permute-start.6
  29.8 3.0 %collective-permute-start = (bf16[4,256,256]{2,1,0:T(8,128)(2,1)S(1)}, bf16[4,256,256]{2,1,0:T(8,128)(2,1)S(1)}, u32[]{:S(2)}, u32[]{:S(2)}) collective-permute-start(bf16[4,256,256]{2,1,0:T(8,128)(2,1)S(1)} %copy-done.3), channel_id=1, source_target_pairs={{0,1},{1,0},{2,3},{3,2},{4,5},{5,4},{6,7},{7,6},{8,9},{9,8},{10,11... | collective-permute-start | bytes 1572872 | tf_op jit(solution)/shard_map/ppermute | solution.py:462
  33.0 1.3 %collective-permute-done.psi_o = bf16[4,256,256]{2,1,0:T(8,128)(2,1)S(1)} collective-permute-done((bf16[4,256,256]{2,1,0:T(8,128)(2,1)S(1)}, bf16[4,256,256]{2,1,0:T(8,128)(2,1)S(1)}, u32[]{:S(2)}, u32[]{:S(2)}) %collective-permute-start) | collective-permute-done | bytes 524320 | tf_op jit(solution)/shard_map/ppermute | solution.py:462
  34.3 0.8 copy-done.5
  35.1 1.0 copy-done.1
  36.1 1.2 %copy-done.2 = f32[4,256,256]{2,1,0:T(8,128)S(1)} copy-done((f32[4,256,256]{2,1,0:T(8,128)S(1)}, f32[4,256,256]{2,1,0:T(8,128)}, u32[]{:S(2)}) %copy-start.2) | copy-done | bytes 1048600
  37.3 1.0 copy-done.4
  38.4 1.0 copy-done.6
  39.4 3.5 %start_vector.1 = (bf16[8,256,256]{2,1,0:T(8,128)(2,1)S(1)}, f32[8,256,256]{2,1,0:T(8,128)}, bf16[8,2,128,256]{3,2,1,0:T(8,128)(2,1)S(1)}, f32[8,128]{1,0:T(8,128)S(1)}, bf16[8,256,256]{2,1,0:T(8,128)(2,1)S(1)}) custom-call(s32[28]{0:T(128)S(1)} %concatenate.7.meta, bf16[4,256,256]{2,1,0:T(8,128)(2,1)S(1)} %copy-done.4, bf16[4,256,256]{2,1,0:T(8,128)(2,1)S(1)} %copy-done.6, ...), custom_call_target="tpu_custom_call" | custom-call | tf_op jit(solution)/shard_map/start_vector/pallas_call | solution.py:498
  42.9 2.6 %first_sigma_own_terms.1.acc = f32[2,128,256]{2,1,0:T(8,128)S(1)} custom-call(s32[28]{0:T(128)S(1)} %concatenate.7.meta, bf16[8,2,128,256]{3,2,1,0:T(8,128)(2,1)S(1)} %get-tuple-element.22.inner, bf16[8,4,128,256]{3,2,1,0:T(8,128)(2,1)} %refs_14_.1, bf16[8,2,128,256]{3,2,1,0:T(8,128)(2,1)} %collective-permute-done.2.refs_1_.refs_13_.refs_15_), custom_call_target="tpu_custom_call" | custom-call | tf_op jit(solution)/shard_map/first_sigma_own_terms/pallas_call | solution.py:514
  45.5 1.4 %collective-permute-start.3 = (s32[8,4]{0,1:T(4,128)S(1)}, s32[8,4]{0,1:T(4,128)S(1)}, u32[]{:S(2)}, u32[]{:S(2)}) collective-permute-start(s32[8,4]{0,1:T(4,128)S(1)} %copy-done.8), channel_id=1, source_target_pairs={{0,4},{4,0},{8,12},{12,8},{1,5},{5,1},{9,13},{13,9},{2,6},{6,2},{1... | collective-permute-start | bytes 392 | tf_op jit(solution)/shard_map/ppermute | solution.py:525
  46.9 4.4 %collective-permute-done.3 = s32[8,4]{0,1:T(4,128)S(1)} collective-permute-done((s32[8,4]{0,1:T(4,128)S(1)}, s32[8,4]{0,1:T(4,128)S(1)}, u32[]{:S(2)}, u32[]{:S(2)}) %collective-permute-start.3) | collective-permute-done | bytes 160 | tf_op jit(solution)/shard_map/ppermute | solution.py:525
  52.1 2.9 %first_sigma_next_terms.1 = bf16[2,128,256]{2,1,0:T(8,128)(2,1)S(1)} custom-call(s32[44]{0:T(128)S(1)} %concatenate.8.meta, bf16[8,256,256]{2,1,0:T(8,128)(2,1)S(1)} %get-tuple-element.25.vb, f32[2,128,256]{2,1,0:T(8,128)S(1)} %first_sigma_own_terms.1.acc, bf16[8,2,128,256]{3,2,1,0:T(8,128)(2,1)} %collective-permute-done.4.refs_0_.refs_14_.refs_16_, ...), custom_call_target="tpu_custom_call" | custom-call | tf_op jit(solution)/shard_map/first_sigma_next_terms/pallas_call | solution.py:527
  55.0 2.7 %collective-permute-start.7 = (bf16[2,128,256]{2,1,0:T(8,128)(2,1)S(1)}, bf16[2,128,256]{2,1,0:T(8,128)(2,1)S(1)}, u32[]{:S(2)}, u32[]{:S(2)}) collective-permute-start(bf16[2,128,256]{2,1,0:T(8,128)(2,1)S(1)} %first_sigma_next_terms.1), channel_id=1, source_target_pairs={{0,12},{4,8},{8,4},{12,0},{1,13},{5,9},{9,5},{13,1},{2,14},{6,10},... | collective-permute-start | bytes 393224 | tf_op jit(solution)/shard_map/ppermute | solution.py:551
  57.8 2.9 %collective-permute-done.7 = bf16[2,128,256]{2,1,0:T(8,128)(2,1)S(1)} collective-permute-done((bf16[2,128,256]{2,1,0:T(8,128)(2,1)S(1)}, bf16[2,128,256]{2,1,0:T(8,128)(2,1)S(1)}, u32[]{:S(2)}, u32[]{:S(2)}) %collective-permute-start.7) | collective-permute-done | bytes 131104 | tf_op jit(solution)/shard_map/ppermute | solution.py:551
  60.8 1.3 %collective-permute-start.10 = (bf16[2,128,256]{2,1,0:T(8,128)(2,1)S(1)}, bf16[2,128,256]{2,1,0:T(8,128)(2,1)S(1)}, u32[]{:S(2)}, u32[]{:S(2)}) collective-permute-start(bf16[2,128,256]{2,1,0:T(8,128)(2,1)S(1)} %select_convert_fusion.1.refs_0_), channel_id=1, source_target_pairs={{0,6},{2,4},{4,2},{6,0},{8,14},{10,12},{12,10},{14,8},{1,7},{3,5},... | collective-permute-start | bytes 393224 | tf_op jit(solution)/shard_map/ppermute | solution.py:553
  62.1 1.5 %collective-permute-start.8 = (bf16[2,128,256]{2,1,0:T(8,128)(2,1)S(1)}, bf16[2,128,256]{2,1,0:T(8,128)(2,1)S(1)}, u32[]{:S(2)}, u32[]{:S(2)}) collective-permute-start(bf16[2,128,256]{2,1,0:T(8,128)(2,1)S(1)} %select_convert_fusion.1.refs_0_), channel_id=1, source_target_pairs={{0,4},{4,0},{8,12},{12,8},{1,5},{5,1},{9,13},{13,9},{2,6},{6,2},{1... | collective-permute-start | bytes 393224 | tf_op jit(solution)/shard_map/ppermute | solution.py:553
  63.5 4.9 %collective-permute-start.11 = (bf16[2,128,256]{2,1,0:T(8,128)(2,1)S(1)}, bf16[2,128,256]{2,1,0:T(8,128)(2,1)S(1)}, u32[]{:S(2)}, u32[]{:S(2)}) collective-permute-start(bf16[2,128,256]{2,1,0:T(8,128)(2,1)S(1)} %select_convert_fusion.1.refs_0_), channel_id=1, source_target_pairs={{0,1},{1,0},{2,3},{3,2},{4,5},{5,4},{6,7},{7,6},{8,9},{9,8},{10,11... | collective-permute-start | bytes 393224 | tf_op jit(solution)/shard_map/ppermute | solution.py:554
  68.4 2.4 %collective-permute-start.14 = (bf16[2,128,256]{2,1,0:T(8,128)(2,1)S(1)}, bf16[2,128,256]{2,1,0:T(8,128)(2,1)S(1)}, u32[]{:S(2)}, u32[]{:S(2)}) collective-permute-start(bf16[2,128,256]{2,1,0:T(8,128)(2,1)S(1)} %collective-permute-done.10.refs_3_), channel_id=1, source_target_pairs={{0,1},{1,0},{2,3},{3,2},{4,5},{5,4},{6,7},{7,6},{8,9},{9,8},{10,11... | collective-permute-start | bytes 393224 | tf_op jit(solution)/shard_map/ppermute | solution.py:554
  70.8 1.3 %collective-permute-start.13 = (bf16[2,128,256]{2,1,0:T(8,128)(2,1)S(1)}, bf16[2,128,256]{2,1,0:T(8,128)(2,1)S(1)}, u32[]{:S(2)}, u32[]{:S(2)}) collective-permute-start(bf16[2,128,256]{2,1,0:T(8,128)(2,1)S(1)} %collective-permute-done.9.refs_2_), channel_id=1, source_target_pairs={{0,1},{1,0},{2,3},{3,2},{4,5},{5,4},{6,7},{7,6},{8,9},{9,8},{10,11... | collective-permute-start | bytes 393224 | tf_op jit(solution)/shard_map/ppermute | solution.py:554
  72.3 0.8 collective-permute-done.13.refs_6_
  73.5 6.0 %vector_and_sigma_1.1 = (bf16[8,256,256]{2,1,0:T(8,128)(2,1)}, f32[8,256,256]{2,1,0:T(8,128)S(1)}, f32[8,128]{1,0:T(8,128)S(1)}, bf16[2,128,256]{2,1,0:T(8,128)(2,1)S(1)}) custom-call(s32[44]{0:T(128)S(1)} %concatenate.8.meta, bf16[2,128,256]{2,1,0:T(8,128)(2,1)S(1)} %select_convert_fusion.1.refs_0_, ...), custom_call_target="tpu_custom_call" | custom-call | tf_op jit(solution)/shard_map/vector_and_sigma_1/pallas_call | solution.py:577
  79.5 3.4 %collective-permute-start.15 = (bf16[2,128,256]{2,1,0:T(8,128)(2,1)S(1)}, bf16[2,128,256]{2,1,0:T(8,128)(2,1)S(1)}, u32[]{:S(2)}, u32[]{:S(2)}) collective-permute-start(bf16[2,128,256]{2,1,0:T(8,128)(2,1)S(1)} %get-tuple-element.30), channel_id=1, source_target_pairs={{0,12},{4,8},{8,4},{12,0},{1,13},{5,9},{9,5},{13,1},{2,14},{6,10},... | collective-permute-start | bytes 393224 | tf_op jit(solution)/shard_map/ppermute | solution.py:551
  82.9 3.6 %collective-permute-done.15 = bf16[2,128,256]{2,1,0:T(8,128)(2,1)S(1)} collective-permute-done((bf16[2,128,256]{2,1,0:T(8,128)(2,1)S(1)}, bf16[2,128,256]{2,1,0:T(8,128)(2,1)S(1)}, u32[]{:S(2)}, u32[]{:S(2)}) %collective-permute-start.15) | collective-permute-done | bytes 131104 | tf_op jit(solution)/shard_map/ppermute | solution.py:551
  86.5 4.1 %collective-permute-start.18 = (bf16[2,128,256]{2,1,0:T(8,128)(2,1)S(1)}, bf16[2,128,256]{2,1,0:T(8,128)(2,1)S(1)}, u32[]{:S(2)}, u32[]{:S(2)}) collective-permute-start(bf16[2,128,256]{2,1,0:T(8,128)(2,1)S(1)} %select_convert_fusion.refs_0_), channel_id=1, source_target_pairs={{0,6},{2,4},{4,2},{6,0},{8,14},{10,12},{12,10},{14,8},{1,7},{3,5},... | collective-permute-start | bytes 393224 | tf_op jit(solution)/shard_map/ppermute | solution.py:553
  91.0 1.1 collective-permute-start.19
  92.1 1.9 %collective-permute-done.18.refs_3_ = bf16[2,128,256]{2,1,0:T(8,128)(2,1)S(1)} collective-permute-done((bf16[2,128,256]{2,1,0:T(8,128)(2,1)S(1)}, bf16[2,128,256]{2,1,0:T(8,128)(2,1)S(1)}, u32[]{:S(2)}, u32[]{:S(2)}) %collective-permute-start.18) | collective-permute-done | bytes 131104 | tf_op jit(solution)/shard_map/ppermute | solution.py:553
  94.0 1.4 %collective-permute-start.22 = (bf16[2,128,256]{2,1,0:T(8,128)(2,1)S(1)}, bf16[2,128,256]{2,1,0:T(8,128)(2,1)S(1)}, u32[]{:S(2)}, u32[]{:S(2)}) collective-permute-start(bf16[2,128,256]{2,1,0:T(8,128)(2,1)S(1)} %collective-permute-done.18.refs_3_), channel_id=1, source_target_pairs={{0,1},{1,0},{2,3},{3,2},{4,5},{5,4},{6,7},{7,6},{8,9},{9,8},{10,11... | collective-permute-start | bytes 393224 | tf_op jit(solution)/shard_map/ppermute | solution.py:554
  95.3 2.0 %collective-permute-done.17.refs_2_ = bf16[2,128,256]{2,1,0:T(8,128)(2,1)S(1)} collective-permute-done((bf16[2,128,256]{2,1,0:T(8,128)(2,1)S(1)}, bf16[2,128,256]{2,1,0:T(8,128)(2,1)S(1)}, u32[]{:S(2)}, u32[]{:S(2)}) %collective-permute-start.17) | collective-permute-done | bytes 131104 | tf_op jit(solution)/shard_map/ppermute | solution.py:553
  97.9 1.0 collective-permute-done.21.refs_6_
  99.2 6.9 %vector_and_sigma_2.1 = (bf16[8,256,256]{2,1,0:T(8,128)(2,1)}, f32[8,128]{1,0:T(8,128)S(1)}, f32[272,128]{1,0:T(8,128)S(1)}, bf16[272,128]{1,0:T(8,128)(2,1)S(1)}) custom-call(s32[44]{0:T(128)S(1)} %concatenate.8.meta, bf16[2,128,256]{2,1,0:T(8,128)(2,1)S(1)} %select_convert_fusion.refs_0_, bf16[2,128,256]{2,1,0:T(8,128)(2,1)S(1)} %collective-permute-done.16.refs_1_, ...), custom_call_target="tpu_custom_call" | custom-call | tf_op jit(solution)/shard_map/vector_and_sigma_2/pallas_call | solution.py:577
  106.1 1.8 %collective-permute-start.23 = (bf16[272,128]{1,0:T(8,128)(2,1)S(1)}, bf16[272,128]{1,0:T(8,128)(2,1)S(1)}, u32[]{:S(2)}, u32[]{:S(2)}) collective-permute-start(bf16[272,128]{1,0:T(8,128)(2,1)S(1)} %get-tuple-element.36), channel_id=1, source_target_pairs={{0,12},{4,8},{8,4},{12,0},{1,13},{5,9},{9,5},{13,1},{2,14},{6,10},... | collective-permute-start | bytes 208904 | tf_op jit(solution)/shard_map/ppermute | solution.py:625
  107.9 2.8 %first_rows.1.held_h = f32[3,4,64,256]{3,2,1,0:T(8,128)} custom-call(s32[44]{0:T(128)S(1)} %concatenate.8.meta, bf16[8,256,256]{2,1,0:T(8,128)(2,1)} %get-tuple-element.32.refs_12_.sig_a, bf16[8,256,256]{2,1,0:T(8,128)(2,1)} %get-tuple-element.34.sig_b), custom_call_target="tpu_custom_call" | custom-call | flops 1048576 | bytes 4194304 | tf_op jit(solution)/shard_map/first_rows/pallas_call | solution.py:609
  110.8 0.8 collective-permute-done.23.got
  111.6 0.6 last_sums.1
  112.3 1.6 %collective-permute-start.26 = (bf16[144,128]{1,0:T(8,128)(2,1)S(1)}, bf16[144,128]{1,0:T(8,128)(2,1)S(1)}, u32[]{:S(2)}, u32[]{:S(2)}) collective-permute-start(bf16[144,128]{1,0:T(8,128)(2,1)S(1)} %get-tuple-element.39), channel_id=1, source_target_pairs={{0,6},{2,4},{4,2},{6,0},{8,14},{10,12},{12,10},{14,8},{1,7},{3,5},... | collective-permute-start | bytes 110600 | tf_op jit(solution)/shard_map/ppermute | solution.py:635
  113.9 1.0 collective-permute-start.25
  115.1 1.0 collective-permute-done.26.by_both
  116.1 0.9 collective-permute-done.25.by_term
  117.0 3.0 %collective-permute-start.27 = (f32[8,128]{1,0:T(8,128)S(1)}, f32[8,128]{1,0:T(8,128)S(1)}, u32[]{:S(2)}, u32[]{:S(2)}) collective-permute-start(f32[8,128]{1,0:T(8,128)S(1)} %last_dots.1.dots), channel_id=1, source_target_pairs={{0,1},{1,0},{2,3},{3,2},{4,5},{5,4},{6,7},{7,6},{8,9},{9,8},{10,11... | collective-permute-start | bytes 12296 | tf_op jit(solution)/shard_map/ppermute | solution.py:644
  120.0 1.3 %last_rows.1 = f32[3,4,64,256]{3,2,1,0:T(8,128)} custom-call(s32[44]{0:T(128)S(1)} %concatenate.8.meta, f32[2,64,128]{2,1,0:T(8,128)S(1)} %get-tuple-element.37.own, bf16[144,128]{1,0:T(8,128)(2,1)S(1)} %collective-permute-done.24.by_env, bf16[144,128]{1,0:T(8,128)(2,1)S(1)} %collective-permute-done.25.by_term, ...), custom_call_target="tpu_custom_call", output_to_operand_aliasing={{}: (5, {})} | custom-call | tf_op jit(solution)/shard_map/last_rows/pallas_call | solution.py:645
  121.3 0.6 subspace.1
  (50 shorter events, 3.7 us)
Async XLA Ops:
  0.6 4.9 %copy-start = (f32[4,256,256]{2,1,0:T(8,128)S(1)}, f32[4,256,256]{2,1,0:T(8,128)}, u32[]{:S(2)}) copy-start(f32[4,256,256]{2,1,0:T(8,128)} %pre.1) | copy-start | bytes 3145732
  3.3 26.5 %copy-start.3 = (bf16[4,256,256]{2,1,0:T(8,128)(2,1)S(1)}, bf16[4,256,256]{2,1,0:T(8,128)(2,1)}, u32[]{:S(2)}) copy-start(bf16[4,256,256]{2,1,0:T(8,128)(2,1)} %psi.1) | copy-start | bytes 1572868
  3.3 29.5 %copy-start.8 = (s32[8,4]{0,1:T(4,128)S(1)}, s32[8,4]{0,1:T(4,128)}, u32[]{:S(2)}) copy-start(s32[8,4]{0,1:T(4,128)} %param.9) | copy-start | bytes 388
  3.3 29.6 %copy-start.7 = (s32[8]{0:T(128)S(1)}, s32[8]{0:T(128)}, u32[]{:S(2)}) copy-start(s32[8]{0:T(128)} %param.10) | copy-start | bytes 100
  3.4 25.4 %collective-permute-start.5 = (bf16[8,2,128,256]{3,2,1,0:T(8,128)(2,1)}, bf16[8,2,128,256]{3,2,1,0:T(8,128)(2,1)}, u32[]{:S(2)}, u32[]{:S(2)}) collective-permute-start(bf16[8,2,128,256]{3,2,1,0:T(8,128)(2,1)} %get-tuple-element.26), channel_id=1, source_target_pairs={{0,4},{4,0},{8,12},{12,8},{1,5},{5,1},{9,13},{13,9},{2,6},{6,2},{1... | collective-permute-start | bytes 3145736 | tf_op jit(solution)/shard_map/ppermute | solution.py:463
  5.6 29.6 %collective-permute-start.1 = (f32[4,256,256]{2,1,0:T(8,128)S(1)}, f32[4,256,256]{2,1,0:T(8,128)S(1)}, u32[]{:S(2)}, u32[]{:S(2)}) collective-permute-start(f32[4,256,256]{2,1,0:T(8,128)S(1)} %copy-done), channel_id=1, source_target_pairs={{0,1},{1,0},{2,3},{3,2},{4,5},{5,4},{6,7},{7,6},{8,9},{9,8},{10,11... | collective-permute-start | bytes 3145736 | tf_op jit(solution)/shard_map/ppermute | solution.py:462
  6.5 36.4 %collective-permute-start.2 = (bf16[8,2,128,256]{3,2,1,0:T(8,128)(2,1)}, bf16[8,2,128,256]{3,2,1,0:T(8,128)(2,1)}, u32[]{:S(2)}, u32[]{:S(2)}) collective-permute-start(bf16[8,2,128,256]{3,2,1,0:T(8,128)(2,1)} %get-tuple-element.23), channel_id=1, source_target_pairs={{0,2},{2,0},{1,3},{3,1},{4,6},{6,4},{5,7},{7,5},{8,10},{10,8},{9,1... | collective-permute-start | bytes 3145736 | tf_op jit(solution)/shard_map/ppermute | solution.py:464
  10.1 41.5 %collective-permute-start.4 = (bf16[8,2,128,256]{3,2,1,0:T(8,128)(2,1)}, bf16[8,2,128,256]{3,2,1,0:T(8,128)(2,1)}, u32[]{:S(2)}, u32[]{:S(2)}) collective-permute-start(bf16[8,2,128,256]{3,2,1,0:T(8,128)(2,1)} %sectors_to_send.3), channel_id=1, source_target_pairs={{0,4},{4,0},{8,12},{12,8},{1,5},{5,1},{9,13},{13,9},{2,6},{6,2},{1... | collective-permute-start | bytes 3145736 | tf_op jit(solution)/shard_map/ppermute | solution.py:465
  28.8 23.4 %collective-permute-start.6 = (bf16[8,2,128,256]{3,2,1,0:T(8,128)(2,1)}, bf16[8,2,128,256]{3,2,1,0:T(8,128)(2,1)}, u32[]{:S(2)}, u32[]{:S(2)}) collective-permute-start(bf16[8,2,128,256]{3,2,1,0:T(8,128)(2,1)} %collective-permute-done.5.refs_1_.refs_15_.refs_17_), channel_id=1, source_target_pairs={{0,2},{2,0},{1,3},{3,1},{4,6},{6,4},{5,7},{7,5},{8,10},{10,8},{9,1... | collective-permute-start | bytes 3145736 | tf_op jit(solution)/shard_map/ppermute | solution.py:466
  29.8 4.5 %collective-permute-start = (bf16[4,256,256]{2,1,0:T(8,128)(2,1)S(1)}, bf16[4,256,256]{2,1,0:T(8,128)(2,1)S(1)}, u32[]{:S(2)}, u32[]{:S(2)}) collective-permute-start(bf16[4,256,256]{2,1,0:T(8,128)(2,1)S(1)} %copy-done.3), channel_id=1, source_target_pairs={{0,1},{1,0},{2,3},{3,2},{4,5},{5,4},{6,7},{7,6},{8,9},{9,8},{10,11... | collective-permute-start | bytes 1572872 | tf_op jit(solution)/shard_map/ppermute | solution.py:462
  34.3 0.8 copy-start.5
  35.1 1.0 copy-start.1
  36.1 1.2 %copy-start.2 = (f32[4,256,256]{2,1,0:T(8,128)S(1)}, f32[4,256,256]{2,1,0:T(8,128)}, u32[]{:S(2)}) copy-start(f32[4,256,256]{2,1,0:T(8,128)} %copy-done.1) | copy-start | bytes 3145732
  37.3 1.0 copy-start.4
  38.4 1.0 copy-start.6
  45.5 5.8 %collective-permute-start.3 = (s32[8,4]{0,1:T(4,128)S(1)}, s32[8,4]{0,1:T(4,128)S(1)}, u32[]{:S(2)}, u32[]{:S(2)}) collective-permute-start(s32[8,4]{0,1:T(4,128)S(1)} %copy-done.8), channel_id=1, source_target_pairs={{0,4},{4,0},{8,12},{12,8},{1,5},{5,1},{9,13},{13,9},{2,6},{6,2},{1... | collective-permute-start | bytes 392 | tf_op jit(solution)/shard_map/ppermute | solution.py:525
  55.0 5.7 %collective-permute-start.7 = (bf16[2,128,256]{2,1,0:T(8,128)(2,1)S(1)}, bf16[2,128,256]{2,1,0:T(8,128)(2,1)S(1)}, u32[]{:S(2)}, u32[]{:S(2)}) collective-permute-start(bf16[2,128,256]{2,1,0:T(8,128)(2,1)S(1)} %first_sigma_next_terms.1), channel_id=1, source_target_pairs={{0,12},{4,8},{8,4},{12,0},{1,13},{5,9},{9,5},{13,1},{2,14},{6,10},... | collective-permute-start | bytes 393224 | tf_op jit(solution)/shard_map/ppermute | solution.py:551
  60.8 7.6 %collective-permute-start.10 = (bf16[2,128,256]{2,1,0:T(8,128)(2,1)S(1)}, bf16[2,128,256]{2,1,0:T(8,128)(2,1)S(1)}, u32[]{:S(2)}, u32[]{:S(2)}) collective-permute-start(bf16[2,128,256]{2,1,0:T(8,128)(2,1)S(1)} %select_convert_fusion.1.refs_0_), channel_id=1, source_target_pairs={{0,6},{2,4},{4,2},{6,0},{8,14},{10,12},{12,10},{14,8},{1,7},{3,5},... | collective-permute-start | bytes 393224 | tf_op jit(solution)/shard_map/ppermute | solution.py:553
  62.1 8.8 %collective-permute-start.9 = (bf16[2,128,256]{2,1,0:T(8,128)(2,1)S(1)}, bf16[2,128,256]{2,1,0:T(8,128)(2,1)S(1)}, u32[]{:S(2)}, u32[]{:S(2)}) collective-permute-start(bf16[2,128,256]{2,1,0:T(8,128)(2,1)S(1)} %select_convert_fusion.1.refs_0_), channel_id=1, source_target_pairs={{0,2},{2,0},{1,3},{3,1},{4,6},{6,4},{5,7},{7,5},{8,10},{10,8},{9,1... | collective-permute-start | bytes 393224 | tf_op jit(solution)/shard_map/ppermute | solution.py:553
  62.1 10.1 %collective-permute-start.8 = (bf16[2,128,256]{2,1,0:T(8,128)(2,1)S(1)}, bf16[2,128,256]{2,1,0:T(8,128)(2,1)S(1)}, u32[]{:S(2)}, u32[]{:S(2)}) collective-permute-start(bf16[2,128,256]{2,1,0:T(8,128)(2,1)S(1)} %select_convert_fusion.1.refs_0_), channel_id=1, source_target_pairs={{0,4},{4,0},{8,12},{12,8},{1,5},{5,1},{9,13},{13,9},{2,6},{6,2},{1... | collective-permute-start | bytes 393224 | tf_op jit(solution)/shard_map/ppermute | solution.py:553
  63.5 8.8 %collective-permute-start.11 = (bf16[2,128,256]{2,1,0:T(8,128)(2,1)S(1)}, bf16[2,128,256]{2,1,0:T(8,128)(2,1)S(1)}, u32[]{:S(2)}, u32[]{:S(2)}) collective-permute-start(bf16[2,128,256]{2,1,0:T(8,128)(2,1)S(1)} %select_convert_fusion.1.refs_0_), channel_id=1, source_target_pairs={{0,1},{1,0},{2,3},{3,2},{4,5},{5,4},{6,7},{7,6},{8,9},{9,8},{10,11... | collective-permute-start | bytes 393224 | tf_op jit(solution)/shard_map/ppermute | solution.py:554
  68.4 3.9 %collective-permute-start.14 = (bf16[2,128,256]{2,1,0:T(8,128)(2,1)S(1)}, bf16[2,128,256]{2,1,0:T(8,128)(2,1)S(1)}, u32[]{:S(2)}, u32[]{:S(2)}) collective-permute-start(bf16[2,128,256]{2,1,0:T(8,128)(2,1)S(1)} %collective-permute-done.10.refs_3_), channel_id=1, source_target_pairs={{0,1},{1,0},{2,3},{3,2},{4,5},{5,4},{6,7},{7,6},{8,9},{9,8},{10,11... | collective-permute-start | bytes 393224 | tf_op jit(solution)/shard_map/ppermute | solution.py:554
  70.8 2.3 %collective-permute-start.13 = (bf16[2,128,256]{2,1,0:T(8,128)(2,1)S(1)}, bf16[2,128,256]{2,1,0:T(8,128)(2,1)S(1)}, u32[]{:S(2)}, u32[]{:S(2)}) collective-permute-start(bf16[2,128,256]{2,1,0:T(8,128)(2,1)S(1)} %collective-permute-done.9.refs_2_), channel_id=1, source_target_pairs={{0,1},{1,0},{2,3},{3,2},{4,5},{5,4},{6,7},{7,6},{8,9},{9,8},{10,11... | collective-permute-start | bytes 393224 | tf_op jit(solution)/shard_map/ppermute | solution.py:554
  72.2 1.3 %collective-permute-start.12 = (bf16[2,128,256]{2,1,0:T(8,128)(2,1)S(1)}, bf16[2,128,256]{2,1,0:T(8,128)(2,1)S(1)}, u32[]{:S(2)}, u32[]{:S(2)}) collective-permute-start(bf16[2,128,256]{2,1,0:T(8,128)(2,1)S(1)} %collective-permute-done.8.refs_1_), channel_id=1, source_target_pairs={{0,1},{1,0},{2,3},{3,2},{4,5},{5,4},{6,7},{7,6},{8,9},{9,8},{10,11... | collective-permute-start | bytes 393224 | tf_op jit(solution)/shard_map/ppermute | solution.py:554
  79.5 6.9 %collective-permute-start.15 = (bf16[2,128,256]{2,1,0:T(8,128)(2,1)S(1)}, bf16[2,128,256]{2,1,0:T(8,128)(2,1)S(1)}, u32[]{:S(2)}, u32[]{:S(2)}) collective-permute-start(bf16[2,128,256]{2,1,0:T(8,128)(2,1)S(1)} %get-tuple-element.30), channel_id=1, source_target_pairs={{0,12},{4,8},{8,4},{12,0},{1,13},{5,9},{9,5},{13,1},{2,14},{6,10},... | collective-permute-start | bytes 393224 | tf_op jit(solution)/shard_map/ppermute | solution.py:551
  86.5 7.4 %collective-permute-start.18 = (bf16[2,128,256]{2,1,0:T(8,128)(2,1)S(1)}, bf16[2,128,256]{2,1,0:T(8,128)(2,1)S(1)}, u32[]{:S(2)}, u32[]{:S(2)}) collective-permute-start(bf16[2,128,256]{2,1,0:T(8,128)(2,1)S(1)} %select_convert_fusion.refs_0_), channel_id=1, source_target_pairs={{0,6},{2,4},{4,2},{6,0},{8,14},{10,12},{12,10},{14,8},{1,7},{3,5},... | collective-permute-start | bytes 393224 | tf_op jit(solution)/shard_map/ppermute | solution.py:553
  90.6 6.8 %collective-permute-start.17 = (bf16[2,128,256]{2,1,0:T(8,128)(2,1)S(1)}, bf16[2,128,256]{2,1,0:T(8,128)(2,1)S(1)}, u32[]{:S(2)}, u32[]{:S(2)}) collective-permute-start(bf16[2,128,256]{2,1,0:T(8,128)(2,1)S(1)} %select_convert_fusion.refs_0_), channel_id=1, source_target_pairs={{0,2},{2,0},{1,3},{3,1},{4,6},{6,4},{5,7},{7,5},{8,10},{10,8},{9,1... | collective-permute-start | bytes 393224 | tf_op jit(solution)/shard_map/ppermute | solution.py:553
  90.6 7.3 %collective-permute-start.16 = (bf16[2,128,256]{2,1,0:T(8,128)(2,1)S(1)}, bf16[2,128,256]{2,1,0:T(8,128)(2,1)S(1)}, u32[]{:S(2)}, u32[]{:S(2)}) collective-permute-start(bf16[2,128,256]{2,1,0:T(8,128)(2,1)S(1)} %select_convert_fusion.refs_0_), channel_id=1, source_target_pairs={{0,4},{4,0},{8,12},{12,8},{1,5},{5,1},{9,13},{13,9},{2,6},{6,2},{1... | collective-permute-start | bytes 393224 | tf_op jit(solution)/shard_map/ppermute | solution.py:553
  91.0 6.9 %collective-permute-start.19 = (bf16[2,128,256]{2,1,0:T(8,128)(2,1)S(1)}, bf16[2,128,256]{2,1,0:T(8,128)(2,1)S(1)}, u32[]{:S(2)}, u32[]{:S(2)}) collective-permute-start(bf16[2,128,256]{2,1,0:T(8,128)(2,1)S(1)} %select_convert_fusion.refs_0_), channel_id=1, source_target_pairs={{0,1},{1,0},{2,3},{3,2},{4,5},{5,4},{6,7},{7,6},{8,9},{9,8},{10,11... | collective-permute-start | bytes 393224 | tf_op jit(solution)/shard_map/ppermute | solution.py:554
  94.0 3.9 %collective-permute-start.22 = (bf16[2,128,256]{2,1,0:T(8,128)(2,1)S(1)}, bf16[2,128,256]{2,1,0:T(8,128)(2,1)S(1)}, u32[]{:S(2)}, u32[]{:S(2)}) collective-permute-start(bf16[2,128,256]{2,1,0:T(8,128)(2,1)S(1)} %collective-permute-done.18.refs_3_), channel_id=1, source_target_pairs={{0,1},{1,0},{2,3},{3,2},{4,5},{5,4},{6,7},{7,6},{8,9},{9,8},{10,11... | collective-permute-start | bytes 393224 | tf_op jit(solution)/shard_map/ppermute | solution.py:554
  97.4 1.5 %collective-permute-start.21 = (bf16[2,128,256]{2,1,0:T(8,128)(2,1)S(1)}, bf16[2,128,256]{2,1,0:T(8,128)(2,1)S(1)}, u32[]{:S(2)}, u32[]{:S(2)}) collective-permute-start(bf16[2,128,256]{2,1,0:T(8,128)(2,1)S(1)} %collective-permute-done.17.refs_2_), channel_id=1, source_target_pairs={{0,1},{1,0},{2,3},{3,2},{4,5},{5,4},{6,7},{7,6},{8,9},{9,8},{10,11... | collective-permute-start | bytes 393224 | tf_op jit(solution)/shard_map/ppermute | solution.py:554
  97.9 1.3 %collective-permute-start.20 = (bf16[2,128,256]{2,1,0:T(8,128)(2,1)S(1)}, bf16[2,128,256]{2,1,0:T(8,128)(2,1)S(1)}, u32[]{:S(2)}, u32[]{:S(2)}) collective-permute-start(bf16[2,128,256]{2,1,0:T(8,128)(2,1)S(1)} %collective-permute-done.16.refs_1_), channel_id=1, source_target_pairs={{0,1},{1,0},{2,3},{3,2},{4,5},{5,4},{6,7},{7,6},{8,9},{9,8},{10,11... | collective-permute-start | bytes 393224 | tf_op jit(solution)/shard_map/ppermute | solution.py:554
  106.1 5.5 %collective-permute-start.23 = (bf16[272,128]{1,0:T(8,128)(2,1)S(1)}, bf16[272,128]{1,0:T(8,128)(2,1)S(1)}, u32[]{:S(2)}, u32[]{:S(2)}) collective-permute-start(bf16[272,128]{1,0:T(8,128)(2,1)S(1)} %get-tuple-element.36), channel_id=1, source_target_pairs={{0,12},{4,8},{8,4},{12,0},{1,13},{5,9},{9,5},{13,1},{2,14},{6,10},... | collective-permute-start | bytes 208904 | tf_op jit(solution)/shard_map/ppermute | solution.py:625
  112.2 2.9 %collective-permute-start.24 = (bf16[144,128]{1,0:T(8,128)(2,1)S(1)}, bf16[144,128]{1,0:T(8,128)(2,1)S(1)}, u32[]{:S(2)}, u32[]{:S(2)}) collective-permute-start(bf16[144,128]{1,0:T(8,128)(2,1)S(1)} %get-tuple-element.38.own), channel_id=1, source_target_pairs={{0,2},{2,0},{1,3},{3,1},{4,6},{6,4},{5,7},{7,5},{8,10},{10,8},{9,1... | collective-permute-start | bytes 110600 | tf_op jit(solution)/shard_map/ppermute | solution.py:635
  112.3 3.8 %collective-permute-start.26 = (bf16[144,128]{1,0:T(8,128)(2,1)S(1)}, bf16[144,128]{1,0:T(8,128)(2,1)S(1)}, u32[]{:S(2)}, u32[]{:S(2)}) collective-permute-start(bf16[144,128]{1,0:T(8,128)(2,1)S(1)} %get-tuple-element.39), channel_id=1, source_target_pairs={{0,6},{2,4},{4,2},{6,0},{8,14},{10,12},{12,10},{14,8},{1,7},{3,5},... | collective-permute-start | bytes 110600 | tf_op jit(solution)/shard_map/ppermute | solution.py:635
  113.9 3.0 %collective-permute-start.25 = (bf16[144,128]{1,0:T(8,128)(2,1)S(1)}, bf16[144,128]{1,0:T(8,128)(2,1)S(1)}, u32[]{:S(2)}, u32[]{:S(2)}) collective-permute-start(bf16[144,128]{1,0:T(8,128)(2,1)S(1)} %get-tuple-element.39), channel_id=1, source_target_pairs={{0,4},{4,0},{8,12},{12,8},{1,5},{5,1},{9,13},{13,9},{2,6},{6,2},{1... | collective-permute-start | bytes 110600 | tf_op jit(solution)/shard_map/ppermute | solution.py:635
  117.0 4.3 %collective-permute-start.27 = (f32[8,128]{1,0:T(8,128)S(1)}, f32[8,128]{1,0:T(8,128)S(1)}, u32[]{:S(2)}, u32[]{:S(2)}) collective-permute-start(f32[8,128]{1,0:T(8,128)S(1)} %last_dots.1.dots), channel_id=1, source_target_pairs={{0,1},{1,0},{2,3},{3,2},{4,5},{5,4},{6,7},{7,6},{8,9},{9,8},{10,11... | collective-permute-start | bytes 12296 | tf_op jit(solution)/shard_map/ppermute | solution.py:644

commit v5 on v4

--- a/solution.py
+++ b/solution.py
@@ -12,8 +12,8 @@
 F32, BF16 = jnp.float32, jnp.bfloat16
 ROWS = 64
 TAIL_ROWS = 16
-SPLIT = 4
-VMEM_LIMIT = 32 * 1024 * 1024
+SPAN = 8
+VMEM_LIMIT = 16 * 1024 * 1024
 HB, VM, SM = pltpu.HBM, pltpu.VMEM, pltpu.SMEM
 
 
@@ -43,15 +43,6 @@
 
     zero = tuple(jnp.zeros((8, width), F32) for _ in range(n_acc))
     return tuple(jnp.sum(a) for a in lax.fori_loop(0, n_sec, step, zero))
-
-
-def _low(cfg, value, env_pos):
-    low = value.astype(BF16)
-    if cfg["direct"]:
-        half = value.shape[1] // 2
-        turned = jnp.concatenate([value[:, half:], value[:, :half]], axis=1).astype(BF16)
-        low = jnp.where(env_pos == 0, low, turned)
-    return low
 
 
 def _put_scalars(ref, values):
@@ -63,13 +54,12 @@
     ref[...] = out
 
 
-def _first_kernel(cfg, meta, psi, psi_o, pre, pre_o, right_h, start, pret_h, inner, scale_ref, vb, right, pret, sem):
+def _first_kernel(cfg, places, meta, psi, psi_o, pre, pre_o, *refs):
+    envs, (start, pret, scale_ref, vb_h, acc, vb, right, left, sem) = refs[: len(places)], refs[len(places) :]
     sec, states, width = psi.shape
     n_sec = sec * cfg["n_blk"]
-    blk, env_pos = meta[2], meta[0]
-    base = blk * sec
-    load = pltpu.make_async_copy(_group(cfg, meta, right_h), right, sem.at[0])
-    load.start()
+    base = meta[2] * sec
+    moves = _env_moves(cfg, meta, places, envs, right, left, sem)
     for part, (p_ref, c_ref) in enumerate(((psi, pre), (psi_o, pre_o))):
         for k in range(p_ref.shape[0]):
             at = lax.rem(base + part * sec + k, n_sec)
@@ -79,28 +69,38 @@
             value = jnp.where((row < live) & (col < live), p_ref[k].astype(F32).T, 0.0)
             start[at] = value.astype(BF16)
             pret[at] = c_ref[k].T
-    save = pltpu.make_async_copy(pret, pret_h, sem.at[1])
-    save.start()
-
     def square(s, r):
         value = start[s, r, :].astype(F32)
         return (_fold(value * value),)
 
     (total,) = _over(n_sec, states, width, 1, square)
     scale = lax.rsqrt(total / (n_sec * states * width) + EPS)
-    _put_scalars(scale_ref, [scale] * 8)
+    count = n_sec * states * width
+
+    def cond(s, r):
+        value = start[s, r, :].astype(F32)
+        return (_fold(value * value * pret[s, r, :]),)
+
+    (damped,) = _over(n_sec, states, width, 1, cond)
+    _put_scalars(scale_ref, [scale, damped * scale * scale / count])
 
     def make(s, r):
-        vb[s, r, :] = _low(cfg, start[s, r, :].astype(F32) * scale, env_pos)
+        vb[s, r, :] = (start[s, r, :].astype(F32) * scale).astype(BF16)
         return ()
 
     _over(n_sec, states, width, 0, make)
-    load.wait()
-    terms, held = right.shape[:2]
-    for k in range(held):
-        for t in range(terms):
-            chosen = vb[meta[cfg["pair_at"] + t * held + k]]
-            inner[t, k] = jnp.dot(right[t, k], chosen, preferred_element_type=F32).astype(BF16)
+    save = pltpu.make_async_copy(vb, vb_h, sem.at[len(moves)])
+    save.start()
+    for _, c in moves:
+        c.wait()
+    for k in range(acc.shape[0]):
+        total = None
+        for t in range(right.shape[0]):
+            chosen = vb[meta[cfg["pair_at"] + t * acc.shape[0] + k]]
+            inner = jnp.dot(right[t, k], chosen, preferred_element_type=F32).astype(BF16)
+            got = jnp.dot(inner, left[t, k], preferred_element_type=F32)
+            total = got if total is None else total + got
+        acc[k] = total
     save.wait()
 
 
@@ -110,46 +110,54 @@
 
 def _env_moves(cfg, meta, places, refs, right, left, sem, first=0):
     moves = []
-    for ref, (kind, t0, r0, own) in zip(refs, places):
+    for ref, (kind, t0, far, own) in zip(refs, places):
         src = _group(cfg, meta, ref) if own else ref
-        step = ref.shape[0] // SPLIT
-        for i in range(SPLIT):
-            t = pl.ds(t0 + i * step, step)
-            dst = right.at[t] if kind == "right" else left.at[t, :, pl.ds(r0, ref.shape[2]), :]
-            moves.append(pltpu.make_async_copy(src.at[pl.ds(i * step, step)], dst, sem.at[first + len(moves)]))
-            moves[-1].start()
+        step = cfg["span"]
+        for i in range(0, ref.shape[0], step):
+            t = pl.ds(t0 + i, step)
+            side = meta[0] ^ far if cfg["direct"] else 0
+            rows = pl.ds(pl.multiple_of(side * ref.shape[2], ref.shape[2]), ref.shape[2])
+            dst = right.at[t] if kind == "right" else left.at[t, :, rows, :]
+            moves.append((t0 + i, src.at[pl.ds(i, step)], dst))
+    moves.sort(key=lambda m: m[0])
+    moves = [(t, pltpu.make_async_copy(a, b, sem.at[first + i])) for i, (t, a, b) in enumerate(moves)]
+    for _, c in moves:
+        c.start()
     return moves
 
 
-def _own_sigma_kernel(cfg, places, meta, inner, *refs):
-    lefts, acc, left, sem = refs[: len(places)], refs[-3], refs[-2], refs[-1]
-    for c in _env_moves(cfg, meta, places, lefts, None, left, sem):
-        c.wait()
-    for k in range(inner.shape[1]):
-        total = None
-        for t in range(inner.shape[0]):
-            got = jnp.dot(inner[t, k], left[t, k], preferred_element_type=F32)
-            total = got if total is None else total + got
-        acc[k] = total
-
-
-def _far_sigma_kernel(cfg, places, t0, meta, vb, acc, *refs):
-    envs, out, right, left, sem = refs[: len(places)], refs[-4], refs[-3], refs[-2], refs[-1]
-    terms, held = right.shape[:2]
-    moves = _env_moves(cfg, meta, places, envs, right, left, sem)
-    for c in moves[:SPLIT]:
-        c.wait()
-    inner = []
+def _near_sigma_kernel(cfg, t0, meta, acc, vb_h, right_h, near_h, out, inner_far, vb, right, near, inner, sem):
+    moves = [(vb_h, vb), (right_h, right), (near_h, near)]
+    moves = [pltpu.make_async_copy(a, b, sem.at[i]) for i, (a, b) in enumerate(moves)]
+    for c in moves:
+        c.start()
+    moves[0].wait()
+    moves[1].wait()
+    terms, held, half = right.shape[:3]
     for k in range(held):
         for t in range(terms):
             chosen = vb[meta[cfg["pair_at"] + (t0 + t) * held + k]]
-            inner.append(jnp.dot(right[t, k], chosen, preferred_element_type=F32).astype(BF16))
-    for c in moves[SPLIT:]:
-        c.wait()
+            inner[t, k] = jnp.dot(right[t, k], chosen, preferred_element_type=F32).astype(BF16)
+    moves[2].wait()
+    own, other = (pl.ds(pl.multiple_of(side * half, half), half) for side in (meta[0], 1 - meta[0]))
     for k in range(held):
         total = acc[k]
         for t in range(terms):
-            total = total + jnp.dot(inner[k * terms + t], left[t, k], preferred_element_type=F32)
+            total = total + jnp.dot(inner[t, k, :, own], near[t, k], preferred_element_type=F32)
+            inner_far[t, k] = inner[t, k, :, other]
+        out[k] = total
+
+
+def _far_sigma_kernel(acc, inner, far_h, out, far, sem):
+    held = far.shape[1]
+    moves = [pltpu.make_async_copy(far_h.at[:, k], far.at[:, k], sem.at[k]) for k in range(held)]
+    for c in moves:
+        c.start()
+    for k in range(held):
+        moves[k].wait()
+        total = acc[k]
+        for t in range(far.shape[0]):
+            total = total + jnp.dot(inner[t, k], far[t, k], preferred_element_type=F32)
         out[k] = total.astype(out.dtype)
 
 
@@ -157,14 +165,15 @@
     it = iter(refs)
     take = lambda n: [next(it) for _ in range(n)]
     shards = take(len(places))
-    (start, scale_ref), vecs, (pre_h,) = take(2), take(step - 1), take(1)
+    (start, scale_ref), vecs, (pre,) = take(2), take(step - 1), take(1)
     olds_h, envs_h, (sig_h,) = take(step - 1), take(len(env_places)), take(1)
     vnew, dots = (None, None) if last else take(2)
     outs = take(cfg["n_out"])
     if last:
         vnew, turned = take(2)
     olds = take(step - 1)
-    right, left, pre, sig, vb, acc, sem = take(7)
+    right, left, sig, vb, acc, sem = take(6)
+    by_rows = take(2) if last and cfg["direct"] else None
     env_pos, z, blk, mine_at = meta[0], meta[1], meta[2], meta[3]
     n_sec, states, width = vnew.shape
     sec, held_sec, half = cfg["sec"], cfg["held"], right.shape[2]
@@ -177,17 +186,19 @@
         return (blk ^ b) * sec + (mine_at ^ h) * held_sec + k
 
     order = [(b, h, k) for b in range(cfg["n_blk"]) for h in range(n_held) for k in range(held_sec)]
-    pre_moves = [pltpu.make_async_copy(pre_h.at[sector(*o)], pre.at[sector(*o)], sem.at[i]) for i, o in enumerate(order)]
-    old_moves = [pltpu.make_async_copy(a, b, sem.at[n_sec + i]) for i, (a, b) in enumerate(zip(olds_h, olds))]
-    for c in pre_moves + old_moves:
+    old_moves = [pltpu.make_async_copy(a, b, sem.at[i]) for i, (a, b) in enumerate(zip(olds_h, olds))]
+    for c in old_moves:
         c.start()
-    env_moves = _env_moves(cfg, meta, env_places, envs_h, right, left, sem, n_sec + step)
-    save = pltpu.make_async_copy(sig, sig_h, sem.at[n_sec + step - 1])
-    scale0 = scale_ref[0, 0]
-    basis = [lambda s, r: start[s, r, :].astype(F32) * scale0]
+    env_moves = _env_moves(cfg, meta, env_places, envs_h, right, left, sem, step)
+    if by_rows:
+        save = pltpu.make_async_copy(by_rows[1], sig_h.at[0 : ITERS - 1], sem.at[step - 1])
+    else:
+        save = pltpu.make_async_copy(sig, sig_h, sem.at[step - 1])
+    scales = [scale_ref[0, 0]] + [1.0] * (step - 1)
+    basis = [lambda s, r: start[s, r, :].astype(F32)]
     basis += [lambda s, r, v=v: v[s, r, :] for v in vecs]
 
-    pairs = [(j, l) for j in range(step) for l in range(j, step)]
+    pairs = [(j, l) for l in range(1, step) for j in range(l + 1)]
     accs = [jnp.zeros((8, width), F32) for _ in range(2 * step + len(pairs))]
     blocks = {o: [] for o in order}
     for ref, place in zip(shards, places):
@@ -202,8 +213,7 @@
             for r in range(0, half, ROWS):
                 rows = pl.ds(pl.multiple_of((env_pos ^ e) * half + r, ROWS), ROWS)
                 blocks[b, h, k].append((ref, k, slice(r, r + ROWS), sector(b, h, k), rows))
-    for ready, o in zip(pre_moves, order):
-        ready.wait()
+    for o in order:
         for ref, k, r, s, rows in blocks[o]:
             low = ref[k, r, :]
             sig[s, rows, :] = low
@@ -211,16 +221,19 @@
             scaled = value * cond
             held = [b(s, rows) for b in basis]
             found = [_fold(h * value) for h in held] + [_fold(h * scaled) for h in held]
-            condh = [h * cond for h in held]
-            found += [_fold(condh[j] * held[l]) for j, l in pairs]
+            condh = [h * cond for h in held[1:]]
+            found += [_fold(held[j] * condh[l - 1]) for j, l in pairs]
             accs = [a + t for a, t in zip(accs, found)]
-    save.start()
+    if not by_rows:
+        save.start()
     sums = [jnp.sum(a) / count for a in accs]
-    proj = sums[:step]
-    gram = {}
+    proj = [sums[j] * scales[j] for j in range(step)]
+    gram = {(0, 0): scale_ref[1, 0]}
     for (j, l), value in zip(pairs, sums[2 * step :]):
-        gram[j, l] = gram[l, j] = value
-    back = [sums[step + j] - sum(proj[l] * gram[j, l] for l in range(step)) for j in range(step)]
+        gram[j, l] = gram[l, j] = value * scales[j] * scales[l]
+    back = [sums[step + j] * scales[j] - sum(proj[l] * gram[j, l] for l in range(step)) for j in range(step)]
+    proj_scaled = [h * x for h, x in zip(proj, scales)]
+    back_scaled = [g * x for g, x in zip(back, scales)]
 
     over = functools.partial(_over, n_sec, states, width)
     for c in old_moves:
@@ -230,10 +243,10 @@
         value = sig[s, r, :].astype(F32)
         held = [b(s, r) for b in basis]
         trial = value
-        for h, b in zip(proj, held):
+        for h, b in zip(proj_scaled, held):
             trial = trial - h * b
         trial = trial * pre[s, r, :]
-        for g, b in zip(back, held):
+        for g, b in zip(back_scaled, held):
             trial = trial - g * b
         vnew[s, r, :] = trial
         crossed = [o[s, r, :].astype(F32) for o in olds] + [value]
@@ -246,20 +259,33 @@
     def final_pass(s, r):
         value = vnew[s, r, :] * scale
         vnew[s, r, :] = value
-        vb[s, r, :] = _low(cfg, value, env_pos)
+        vb[s, r, :] = value.astype(BF16)
         return ()
 
     over(0, final_pass)
-    for c in env_moves:
-        c.wait()
-    for k in range(held_sec):
-        total = None
-        for t in range(right.shape[0]):
-            chosen = vb[meta[cfg["pair_at"] + t * held_sec + k]]
-            inner = jnp.dot(right[t, k], chosen, preferred_element_type=F32).astype(BF16)
-            got = jnp.dot(inner, left[t, k], preferred_element_type=F32)
-            total = got if total is None else total + got
-        acc[k] = total
+    if by_rows:
+        turned_sig, sig_rows = by_rows
+        chunk, lanes = sig_rows.shape[2], turned_sig.shape[2]
+        side = pl.ds(pl.multiple_of(lax.div(z * chunk, lanes) * lanes, lanes), lanes)
+        first = pl.ds(pl.multiple_of(lax.rem(z * chunk, lanes), chunk), chunk)
+        for i, ref in enumerate([*olds, sig]):
+            for k in range(sec):
+                turned_sig[i, k] = ref[blk * sec + k, :, side].astype(F32).T
+                sig_rows[i, k] = turned_sig[i, k, first, :]
+        save.start()
+    span = cfg["span"]
+    for t0 in range(0, right.shape[0], span):
+        for t_move, c in env_moves:
+            if t0 <= t_move < t0 + span:
+                c.wait()
+        for k in range(held_sec):
+            total = None if t0 == 0 else acc[k]
+            for t in range(t0, t0 + span):
+                chosen = vb[meta[cfg["pair_at"] + t * held_sec + k]]
+                inner = jnp.dot(right[t, k], chosen, preferred_element_type=F32).astype(BF16)
+                got = jnp.dot(inner, left[t, k], preferred_element_type=F32)
+                total = got if total is None else total + got
+            acc[k] = total
     scalars = proj + cross
     if not last:
         outs[0][...] = acc[...].astype(outs[0].dtype)
@@ -269,11 +295,11 @@
 
     rows = pl.ds(pl.multiple_of(env_pos * half, half), half)
     mine = []
-    for b in [*basis, lambda s, r: vnew[s, r, :]]:
+    for b, scaled in zip([*basis, lambda s, r: vnew[s, r, :]], [*scales, 1.0]):
         total = jnp.zeros((8, width), F32)
         for k in range(held_sec):
             total = total + _fold(b(sector(0, 0, k) if cfg["direct"] else blk * sec + k, rows) * acc[k])
-        mine.append(jnp.sum(total) / count)
+        mine.append(jnp.sum(total) * scaled / count)
     _put_scalars(outs[0], scalars)
     if cfg["direct"]:
         for k in range(held_sec):
@@ -309,23 +335,6 @@
     return [
         sum(tail[3 * j + p : 3 * j + p + 1, 0:1].astype(F32) for tail in tails for p in range(3)) for j in range(ITERS)
     ]
-
-
-def _rows_kernel(cfg, meta, sig_a, sig_b, out_h, sig, turned, rows, sem):
-    chunk = rows.shape[2]
-    first = pl.ds(pl.multiple_of(meta[1] * chunk, chunk), chunk)
-    own = pl.ds(meta[2] * cfg["sec"], cfg["sec"])
-    loads = [pltpu.make_async_copy(ref.at[own], sig.at[i], sem.at[i]) for i, ref in enumerate((sig_a, sig_b))]
-    for c in loads:
-        c.start()
-    for i, c in enumerate(loads):
-        c.wait()
-        for k in range(rows.shape[1]):
-            turned[i, k] = sig[i, k].astype(F32).T
-            rows[i, k] = turned[i, k, first, :]
-    save = pltpu.make_async_copy(rows, out_h.at[0 : rows.shape[0]], sem.at[2])
-    save.start()
-    save.wait()
 
 
 def _merge_kernel(cfg, meta, kept, got, own, keep_out, give_out):
@@ -446,7 +455,8 @@
     direct = n_env == 2 and n_blk == 2 and n_term == 4 and sec % 2 == 0 and terms % 2 == 0
     chunk = states // n_term
     held = sec // 2 if direct else sec
-    cfg = dict(direct=direct, n_blk=n_blk, sec=sec, held=held)
+    span = SPAN if terms % SPAN == 0 else 1
+    cfg = dict(direct=direct, n_blk=n_blk, sec=sec, held=held, span=span)
     env_pos, term_pos, blk_pos = (lax.axis_index(a) for a in ("env", "term", "blk"))
     mine = (term_pos ^ (term_pos >> 1)) & 1 if direct else jnp.zeros_like(term_pos)
     next_term, far_term = _xor("term", 4, 1), _xor("term", 4, 3)
@@ -465,8 +475,8 @@
         next_right = next_term(right_to_next)
         next_far_left = other_env(next_left)
         own_table = group(pairing, mine)
-        own_places = [("left", 0, 0, True), ("left", 0, half, False)]
-        next_places = [("right", 0, 0, False), ("left", 0, 0, False), ("left", 0, half, False)]
+        own_places = [("left", 0, 0, True), ("left", 0, 1, False)]
+        next_places = [("right", 0, 0, False), ("left", 0, 0, False), ("left", 0, 1, False)]
         own_envs, next_envs = [left_env, far_left], [next_right, next_left, next_far_left]
         n_terms = 2 * terms
         shift = lambda place: (place[0], place[1] + terms, *place[2:])
@@ -495,48 +505,46 @@
     full = (n_sec, states, width)
     params = pltpu.CompilerParams(vmem_limit_bytes=VMEM_LIMIT)
     dma = pltpu.SemaphoreType.DMA
-    start, pret, inner, scale0, vb0 = pl.pallas_call(
-        functools.partial(_first_kernel, cfg),
-        out_shape=(
-            VM(full, BF16),
-            HB(full, F32),
-            VM((terms, held, half, states), BF16),
-            VM((8, 128), F32),
-            VM(full, BF16),
-        ),
-        in_specs=_specs(SM, VM, VM, VM, VM, HB),
-        out_specs=_specs(VM, HB, VM, VM, VM),
-        scratch_shapes=[pltpu.VMEM((terms, held, half, states), BF16), pltpu.VMEM(full, F32), dma((2,))],
+    n_moves = 3 * terms // span
+    first_places, first_envs = [("right", 0, 0, True), *own_places], [right_env, *own_envs]
+    start, pret, scale0, vb0, partial = pl.pallas_call(
+        functools.partial(_first_kernel, cfg, first_places),
+        out_shape=(VM(full, BF16), VM(full, F32), VM((8, 128), F32), HB(full, BF16), VM((held, half, width), F32)),
+        in_specs=_specs(SM, VM, VM, VM, VM, *[HB] * len(first_envs)),
+        out_specs=_specs(VM, VM, VM, HB, VM),
+        scratch_shapes=[
+            pltpu.VMEM(full, BF16),
+            pltpu.VMEM((terms, held, half, states), BF16),
+            pltpu.VMEM((terms, held, states, width), BF16),
+            dma((n_moves + 1,)),
+        ],
         compiler_params=params,
         name="start_vector",
-    )(own_meta, psi, psi_o, precond, pre_o, *_hbm(right_env))
-
-    partial = pl.pallas_call(
-        functools.partial(_own_sigma_kernel, cfg, own_places),
-        out_shape=VM((held, half, width), F32),
-        in_specs=_specs(SM, VM, *[HB] * len(own_envs)),
-        out_specs=_specs(VM)[0],
-        scratch_shapes=[pltpu.VMEM((terms, held, states, width), BF16), dma((SPLIT * len(own_envs),))],
-        compiler_params=params,
-        name="first_sigma_own_terms",
-    )(own_meta, *_vmem(inner), *_hbm(*own_envs))
+    )(own_meta, psi, psi_o, precond, pre_o, *_hbm(*first_envs))
+
     meta = own_meta
     if direct:
         next_pairing = next_term(lax.optimization_barrier((pairing, partial))[0])
         meta = jnp.concatenate([own_meta, group(next_pairing, mine).reshape(-1)])
-        partial = pl.pallas_call(
-            functools.partial(_far_sigma_kernel, cfg, next_places, terms),
-            out_shape=VM((held, half, width), BF16),
-            in_specs=_specs(SM, VM, VM, *[HB] * len(next_envs)),
-            out_specs=_specs(VM)[0],
-            scratch_shapes=[
-                pltpu.VMEM((terms, held, half, states), BF16),
-                pltpu.VMEM((terms, held, states, width), BF16),
-                dma((SPLIT * len(next_envs),)),
-            ],
+        piece = (terms, held, half, states)
+        partial, inner_far = pl.pallas_call(
+            functools.partial(_near_sigma_kernel, cfg, terms),
+            out_shape=(VM((held, half, width), F32), VM((terms, held, half, half), BF16)),
+            in_specs=_specs(SM, VM, HB, HB, HB),
+            out_specs=tuple(_specs(VM, VM)),
+            scratch_shapes=[pltpu.VMEM(full, BF16), *[pltpu.VMEM(piece, BF16)] * 3, dma((3,))],
             compiler_params=params,
             name="first_sigma_next_terms",
-        )(meta, *_vmem(vb0, partial), *_hbm(*next_envs))
+        )(meta, *_vmem(partial), *_hbm(vb0, next_right, next_left))
+        partial = pl.pallas_call(
+            _far_sigma_kernel,
+            out_shape=VM((held, half, width), BF16),
+            in_specs=_specs(VM, VM, HB),
+            out_specs=_specs(VM)[0],
+            scratch_shapes=[pltpu.VMEM(piece, BF16), dma((held,))],
+            compiler_params=params,
+            name="first_sigma_far_rows",
+        )(*_vmem(partial, inner_far), *_hbm(next_far_left))
 
     live_own = lax.dynamic_slice_in_dim(sector_dims, blk_pos * sec, sec)
 
@@ -558,6 +566,7 @@
         whole = masked(lax.all_gather(whole, "env", axis=1, tiled=True), 0, live_own)
         return [lax.all_gather(whole, "blk", axis=0, tiled=True)], [None]
 
+    out_shape = (ITERS, sec, chunk, states)
     vecs, olds = [], []
     for step in range(1, ITERS):
         last = step + 1 == ITERS
@@ -569,33 +578,33 @@
                 outs += [VM(size, F32), VM(size, BF16)]
             else:
                 outs += [VM((8, 128), F32), VM((sec, states, half), F32)]
-            made = (HB(full, BF16),)
+            made = (HB(out_shape, F32) if direct else HB(full, BF16),)
         else:
             outs = [VM((held, half, width), BF16 if direct else F32)]
             made = (HB(full, BF16), VM(full, F32), VM((8, 128), F32))
-        n_hbm = 1 + (step - 1) + len(envs)
+        n_hbm = (step - 1) + len(envs)
         results = pl.pallas_call(
             functools.partial(_step_kernel, dict(cfg, n_out=len(outs)), step, places, env_places, last),
             out_shape=(*made, *outs),
-            in_specs=_specs(SM, *[VM] * (len(shards) + 2 + len(vecs)), *[HB] * n_hbm),
+            in_specs=_specs(SM, *[VM] * (len(shards) + 3 + len(vecs)), *[HB] * n_hbm),
             out_specs=tuple(_specs(HB, *[VM] * (len(made) - 1 + len(outs)))),
             scratch_shapes=[pltpu.VMEM(full, F32), pltpu.VMEM((held, states, half), F32)] * last
             + [pltpu.VMEM(full, BF16)] * (step - 1)
             + [
                 pltpu.VMEM((n_terms, held, half, states), BF16),
                 pltpu.VMEM((n_terms, held, states, width), BF16),
-                pltpu.VMEM(full, F32),
                 pltpu.VMEM(full, BF16),
                 pltpu.VMEM(full, BF16),
                 pltpu.VMEM((held, half, width), F32),
-                dma((n_sec + step + SPLIT * len(envs),)),
-            ],
+                dma((step + len(envs) * n_moves,)),
+            ]
+            + [pltpu.VMEM((step, sec, 2 * chunk, states), F32), pltpu.VMEM((step, sec, chunk, states), F32)] * (last and direct),
             compiler_params=params,
             name=f"vector_and_sigma_{step}",
         )(
             meta,
-            *_vmem(*shards, start, scale0, *vecs),
-            *_hbm(pret, *olds, *envs),
+            *_vmem(*shards, start, scale0, *vecs, pret),
+            *_hbm(*olds, *envs),
         )
         olds.append(results[0])
         if last:
@@ -604,23 +613,7 @@
             vecs.append(results[1])
             first, partial = results[2:]
 
-    out_shape = (ITERS, sec, chunk, states)
     if direct:
-        rows01 = pl.pallas_call(
-            functools.partial(_rows_kernel, cfg),
-            out_shape=HB(out_shape, F32),
-            in_specs=_specs(SM, HB, HB),
-            out_specs=_specs(HB)[0],
-            scratch_shapes=[
-                pltpu.VMEM((ITERS - 1, sec, states, states), BF16),
-                pltpu.VMEM((ITERS - 1, sec, states, states), F32),
-                pltpu.VMEM((ITERS - 1, sec, chunk, states), F32),
-                dma((3,)),
-            ],
-            compiler_params=params,
-            cost_estimate=pl.CostEstimate(flops=1 << 20, bytes_accessed=1 << 22, transcendentals=0),
-            name="first_rows",
-        )(meta, *_hbm(*olds))
         kept, given = pieces
         got = far_term(given)
         size = (held * chunk + TAIL_ROWS, half)
@@ -631,7 +624,7 @@
             out_specs=tuple(_specs(VM, VM, VM)),
             compiler_params=params,
             name="last_sums",
-        )(meta, *_vmem(lax.optimization_barrier((kept, rows01))[0], got))
+        )(meta, *_vmem(kept, got))
         parts = [other_env(keep), next_term(give), corners(give)]
         dots = pl.pallas_call(
             functools.partial(_dots_kernel, held * chunk),
@@ -651,7 +644,7 @@
             input_output_aliases={5: 0},
             compiler_params=params,
             name="last_rows",
-        )(meta, *_vmem(own, *parts), *_hbm(rows01))
+        )(meta, *_vmem(own, *parts), *_hbm(olds[-1]))
         subspace = pl.pallas_call(
             _subspace_kernel,
             out_shape=jax.ShapeDtypeStruct((ITERS, ITERS), F32),

time: 122 us -> 120 us (0.984)
  Pallas kernels: 32.2 us -> 26.4 us
  waiting for transfers between devices: 40.5 us -> 42.5 us
    pallas_call x4 -> x3, Pallas kernels: 11.8 us -> 8.57 us  [the longest x1 3.62 us: _on_device(): pl.pallas_call(functools.partial(_first_kernel, cfg, first_places), out_s...]
    pallas_call x2, Pallas kernels: 12.9 us -> 10.4 us  [_on_device(): pl.pallas_call(functools.partial(_step_kernel, dict(cfg, n_out=len(outs))...]
    ppermute x1, waiting for transfers between devices: 0.83 us -> 3.07 us  [_on_device(): got = far_term(given)]
    ppermute x6, waiting for transfers between devices: 3.9 us -> 2.3 us  [combine(): here = [shard, next_term(shard), other_env(shard), corners(shard)]]
    ppermute x1, waiting for transfers between devices: 4.39 us -> 5.63 us  [_on_device(): next_pairing = next_term(lax.optimization_barrier((pairing, partial))[0])]
    unnamed x18 -> x20, local copies, waits for them, and re-layouts: 5.11 us -> 6.33 us
  transfers between devices with their start and end apart: 28 -> 28, of which waited for: 16 -> 16; matrix products, arithmetic and copies ran while one was open for 0% -> 0% of each run, Pallas kernels for 10% -> 9%
where the time goes in v5:
time: 120 us; the launch traced here: 119 us
  waiting for transfers between devices  42.5 us (35%)
  starting transfers between devices  42.3 us (35%)
  Pallas kernels  26.4 us (22%)
  local copies, waits for them, and re-layouts  6.9 us (6%)
    ppermute x1, waiting for transfers between devices, _on_device(): next_left = next_term(to_next)  18.6 us
    ppermute x8, starting transfers between devices, combine(): there = [other_blk(x) for x in here]  11.5 us
    pallas_call x2, Pallas kernels, _on_device(): pl.pallas_call(functools.partial(_step_kernel, dict(cfg, n_out=len(outs))...  10.4 us
    ppermute x6, starting transfers between devices, combine(): here = [shard, next_term(shard), other_env(shard), corners(shard)]  7.2 us
    ppermute x2, waiting for transfers between devices, combine(): total = partial.astype(F32) + far_term(partial).astype(F32)  7.05 us
    unnamed x20, local copies, waits for them, and re-layouts  6.33 us
    ppermute x1, waiting for transfers between devices, _on_device(): next_pairing = next_term(lax.optimization_barrier((pairing, partial))[0])  5.63 us
    ppermute x2, starting transfers between devices, combine(): total = partial.astype(F32) + far_term(partial).astype(F32)  5.49 us
  transfers between devices with their start and end apart: 28, of which 16 were waited for; matrix products, arithmetic and copies ran while one was open for 0% of the time, Pallas kernels for 9%

profile of v5, /device:TPU:1, one launch (start us, length us, event | category | flops | bytes accessed | tf_op | source)
XLA Modules:
  0.0 119.1 jit_solution(9718107908229244098)
XLA Ops:
  0.6 2.7 %sectors_to_send.2 = (bf16[8,2,128,256]{3,2,1,0:T(8,128)(2,1)}, bf16[8,2,128,256]{3,2,1,0:T(8,128)(2,1)}) custom-call(s32[1]{0:T(128)} %bitcast.3.which, bf16[8,4,128,256]{3,2,1,0:T(8,128)(2,1)} %refs_14_.1), custom_call_target="tpu_custom_call" | custom-call | tf_op jit(solution)/shard_map/sectors_to_send/pallas_call | solution.py:439
  3.4 2.2 %collective-permute-start.5 = (bf16[8,2,128,256]{3,2,1,0:T(8,128)(2,1)}, bf16[8,2,128,256]{3,2,1,0:T(8,128)(2,1)}, u32[]{:S(2)}, u32[]{:S(2)}) collective-permute-start(bf16[8,2,128,256]{3,2,1,0:T(8,128)(2,1)} %get-tuple-element.27), channel_id=1, source_target_pairs={{0,4},{4,0},{8,12},{12,8},{1,5},{5,1},{9,13},{13,9},{2,6},{6,2},{1... | collective-permute-start | bytes 3145736 | tf_op jit(solution)/shard_map/ppermute | solution.py:473
  5.5 1.0 collective-permute-start.1
  6.5 1.2 %collective-permute-start.2 = (bf16[8,2,128,256]{3,2,1,0:T(8,128)(2,1)}, bf16[8,2,128,256]{3,2,1,0:T(8,128)(2,1)}, u32[]{:S(2)}, u32[]{:S(2)}) collective-permute-start(bf16[8,2,128,256]{3,2,1,0:T(8,128)(2,1)} %get-tuple-element.23), channel_id=1, source_target_pairs={{0,2},{2,0},{1,3},{3,1},{4,6},{6,4},{5,7},{7,5},{8,10},{10,8},{9,1... | collective-permute-start | bytes 3145736 | tf_op jit(solution)/shard_map/ppermute | solution.py:474
  7.7 2.2 %sectors_to_send.3 = bf16[8,2,128,256]{3,2,1,0:T(8,128)(2,1)} custom-call(s32[1]{0:T(128)} %bitcast.3.which, bf16[8,4,128,256]{3,2,1,0:T(8,128)(2,1)} %refs_13_.1), custom_call_target="tpu_custom_call" | custom-call | tf_op jit(solution)/shard_map/sectors_to_send/pallas_call | solution.py:439
  10.2 18.6 %collective-permute-done.5.near_h.refs_15_.refs_17_ = bf16[8,2,128,256]{3,2,1,0:T(8,128)(2,1)} collective-permute-done((bf16[8,2,128,256]{3,2,1,0:T(8,128)(2,1)}, bf16[8,2,128,256]{3,2,1,0:T(8,128)(2,1)}, u32[]{:S(2)}, u32[]{:S(2)}) %collective-permute-start.5) | collective-permute-done | bytes 1048608 | tf_op jit(solution)/shard_map/ppermute | solution.py:473
  28.7 1.1 collective-permute-start.6
  29.8 3.0 %collective-permute-start = (bf16[4,256,256]{2,1,0:T(8,128)(2,1)S(1)}, bf16[4,256,256]{2,1,0:T(8,128)(2,1)S(1)}, u32[]{:S(2)}, u32[]{:S(2)}) collective-permute-start(bf16[4,256,256]{2,1,0:T(8,128)(2,1)S(1)} %copy-done.4), channel_id=1, source_target_pairs={{0,1},{1,0},{2,3},{3,2},{4,5},{5,4},{6,7},{7,6},{8,9},{9,8},{10,11... | collective-permute-start | bytes 1572872 | tf_op jit(solution)/shard_map/ppermute | solution.py:472
  33.0 1.3 %collective-permute-done.psi_o = bf16[4,256,256]{2,1,0:T(8,128)(2,1)S(1)} collective-permute-done((bf16[4,256,256]{2,1,0:T(8,128)(2,1)S(1)}, bf16[4,256,256]{2,1,0:T(8,128)(2,1)S(1)}, u32[]{:S(2)}, u32[]{:S(2)}) %collective-permute-start) | collective-permute-done | bytes 524320 | tf_op jit(solution)/shard_map/ppermute | solution.py:472
  34.3 0.8 copy-done.6
  35.1 1.0 copy-done.2
  36.1 1.2 %copy-done.1 = f32[4,256,256]{2,1,0:T(8,128)S(1)} copy-done((f32[4,256,256]{2,1,0:T(8,128)S(1)}, f32[4,256,256]{2,1,0:T(8,128)}, u32[]{:S(2)}) %copy-start.1) | copy-done | bytes 1048600
  37.3 1.2 %copy-done.3 = f32[4,256,256]{2,1,0:T(8,128)S(1)} copy-done((f32[4,256,256]{2,1,0:T(8,128)S(1)}, f32[4,256,256]{2,1,0:T(8,128)}, u32[]{:S(2)}) %copy-start.3) | copy-done | bytes 1048600
  38.6 1.0 copy-done.5
  39.6 1.0 copy-done.7
  40.6 3.6 %start_vector.1 = (bf16[8,256,256]{2,1,0:T(8,128)(2,1)S(1)}, f32[8,256,256]{2,1,0:T(8,128)S(1)}, f32[8,128]{1,0:T(8,128)S(1)}, bf16[8,256,256]{2,1,0:T(8,128)(2,1)}, f32[2,128,256]{2,1,0:T(8,128)S(1)}) custom-call(s32[28]{0:T(128)S(1)} %concatenate.7.meta, bf16[4,256,256]{2,1,0:T(8,128)(2,1)S(1)} %copy-done.5, bf16[4,256,256]{2,1,0:T(8,128)(2,1)S(1)} %copy-done.7, ...), custom_call_target="tpu_custom_call" | custom-call | tf_op jit(solution)/shard_map/start_vector/pallas_call | solution.py:510
  44.3 1.4 %collective-permute-start.3 = (s32[8,4]{0,1:T(4,128)S(1)}, s32[8,4]{0,1:T(4,128)S(1)}, u32[]{:S(2)}, u32[]{:S(2)}) collective-permute-start(s32[8,4]{0,1:T(4,128)S(1)} %copy-done.9), channel_id=1, source_target_pairs={{0,4},{4,0},{8,12},{12,8},{1,5},{5,1},{9,13},{13,9},{2,6},{6,2},{1... | collective-permute-start | bytes 392 | tf_op jit(solution)/shard_map/ppermute | solution.py:527
  45.6 5.6 %collective-permute-done.3 = s32[8,4]{0,1:T(4,128)S(1)} collective-permute-done((s32[8,4]{0,1:T(4,128)S(1)}, s32[8,4]{0,1:T(4,128)S(1)}, u32[]{:S(2)}, u32[]{:S(2)}) %collective-permute-start.3) | collective-permute-done | bytes 160 | tf_op jit(solution)/shard_map/ppermute | solution.py:527
  51.5 3.1 %first_sigma_next_terms.1 = (f32[2,128,256]{2,1,0:T(8,128)S(1)}, bf16[8,2,128,128]{3,2,1,0:T(8,128)(2,1)S(1)}) custom-call(s32[44]{0:T(128)S(1)} %concatenate.8.meta, f32[2,128,256]{2,1,0:T(8,128)S(1)} %get-tuple-element.24.acc, bf16[8,256,256]{2,1,0:T(8,128)(2,1)} %get-tuple-element.26.vb_h, ...), custom_call_target="tpu_custom_call" | custom-call | tf_op jit(solution)/shard_map/first_sigma_next_terms/pallas_call | solution.py:530
  54.6 1.9 %first_sigma_far_rows.1 = bf16[2,128,256]{2,1,0:T(8,128)(2,1)S(1)} custom-call(f32[2,128,256]{2,1,0:T(8,128)S(1)} %get-tuple-element.28.acc, bf16[8,2,128,128]{3,2,1,0:T(8,128)(2,1)S(1)} %get-tuple-element.29.inner, bf16[8,2,128,256]{3,2,1,0:T(8,128)(2,1)} %collective-permute-done.6.far_h.refs_16_.refs_18_), custom_call_target="tpu_custom_call" | custom-call | tf_op jit(solution)/shard_map/first_sigma_far_rows/pallas_call | solution.py:539
  56.5 3.2 %collective-permute-start.7 = (bf16[2,128,256]{2,1,0:T(8,128)(2,1)S(1)}, bf16[2,128,256]{2,1,0:T(8,128)(2,1)S(1)}, u32[]{:S(2)}, u32[]{:S(2)}) collective-permute-start(bf16[2,128,256]{2,1,0:T(8,128)(2,1)S(1)} %first_sigma_far_rows.1), channel_id=1, source_target_pairs={{0,12},{4,8},{8,4},{12,0},{1,13},{5,9},{9,5},{13,1},{2,14},{6,10},... | collective-permute-start | bytes 393224 | tf_op jit(solution)/shard_map/ppermute | solution.py:559
  59.8 2.5 %collective-permute-done.7 = bf16[2,128,256]{2,1,0:T(8,128)(2,1)S(1)} collective-permute-done((bf16[2,128,256]{2,1,0:T(8,128)(2,1)S(1)}, bf16[2,128,256]{2,1,0:T(8,128)(2,1)S(1)}, u32[]{:S(2)}, u32[]{:S(2)}) %collective-permute-start.7) | collective-permute-done | bytes 131104 | tf_op jit(solution)/shard_map/ppermute | solution.py:559
  62.4 3.7 %collective-permute-start.10 = (bf16[2,128,256]{2,1,0:T(8,128)(2,1)S(1)}, bf16[2,128,256]{2,1,0:T(8,128)(2,1)S(1)}, u32[]{:S(2)}, u32[]{:S(2)}) collective-permute-start(bf16[2,128,256]{2,1,0:T(8,128)(2,1)S(1)} %select_convert_fusion.1.refs_0_), channel_id=1, source_target_pairs={{0,6},{2,4},{4,2},{6,0},{8,14},{10,12},{12,10},{14,8},{1,7},{3,5},... | collective-permute-start | bytes 393224 | tf_op jit(solution)/shard_map/ppermute | solution.py:561
  66.5 2.0 %collective-permute-start.11 = (bf16[2,128,256]{2,1,0:T(8,128)(2,1)S(1)}, bf16[2,128,256]{2,1,0:T(8,128)(2,1)S(1)}, u32[]{:S(2)}, u32[]{:S(2)}) collective-permute-start(bf16[2,128,256]{2,1,0:T(8,128)(2,1)S(1)} %select_convert_fusion.1.refs_0_), channel_id=1, source_target_pairs={{0,1},{1,0},{2,3},{3,2},{4,5},{5,4},{6,7},{7,6},{8,9},{9,8},{10,11... | collective-permute-start | bytes 393224 | tf_op jit(solution)/shard_map/ppermute | solution.py:562
  68.5 2.8 %collective-permute-start.14 = (bf16[2,128,256]{2,1,0:T(8,128)(2,1)S(1)}, bf16[2,128,256]{2,1,0:T(8,128)(2,1)S(1)}, u32[]{:S(2)}, u32[]{:S(2)}) collective-permute-start(bf16[2,128,256]{2,1,0:T(8,128)(2,1)S(1)} %collective-permute-done.10.refs_3_), channel_id=1, source_target_pairs={{0,1},{1,0},{2,3},{3,2},{4,5},{5,4},{6,7},{7,6},{8,9},{9,8},{10,11... | collective-permute-start | bytes 393224 | tf_op jit(solution)/shard_map/ppermute | solution.py:562
  71.3 1.0 collective-permute-done.9.refs_2_
  72.2 1.2 %collective-permute-start.13 = (bf16[2,128,256]{2,1,0:T(8,128)(2,1)S(1)}, bf16[2,128,256]{2,1,0:T(8,128)(2,1)S(1)}, u32[]{:S(2)}, u32[]{:S(2)}) collective-permute-start(bf16[2,128,256]{2,1,0:T(8,128)(2,1)S(1)} %collective-permute-done.9.refs_2_), channel_id=1, source_target_pairs={{0,1},{1,0},{2,3},{3,2},{4,5},{5,4},{6,7},{7,6},{8,9},{9,8},{10,11... | collective-permute-start | bytes 393224 | tf_op jit(solution)/shard_map/ppermute | solution.py:562
  73.6 0.8 collective-permute-done.13.refs_6_
  74.8 4.8 %vector_and_sigma_1.1 = (bf16[8,256,256]{2,1,0:T(8,128)(2,1)}, f32[8,256,256]{2,1,0:T(8,128)S(1)}, f32[8,128]{1,0:T(8,128)S(1)}, bf16[2,128,256]{2,1,0:T(8,128)(2,1)S(1)}) custom-call(s32[44]{0:T(128)S(1)} %concatenate.8.meta, bf16[2,128,256]{2,1,0:T(8,128)(2,1)S(1)} %select_convert_fusion.1.refs_0_, ...), custom_call_target="tpu_custom_call" | custom-call | tf_op jit(solution)/shard_map/vector_and_sigma_1/pallas_call | solution.py:586
  79.6 2.3 %collective-permute-start.15 = (bf16[2,128,256]{2,1,0:T(8,128)(2,1)S(1)}, bf16[2,128,256]{2,1,0:T(8,128)(2,1)S(1)}, u32[]{:S(2)}, u32[]{:S(2)}) collective-permute-start(bf16[2,128,256]{2,1,0:T(8,128)(2,1)S(1)} %get-tuple-element.33), channel_id=1, source_target_pairs={{0,12},{4,8},{8,4},{12,0},{1,13},{5,9},{9,5},{13,1},{2,14},{6,10},... | collective-permute-start | bytes 393224 | tf_op jit(solution)/shard_map/ppermute | solution.py:559
  81.9 4.6 %collective-permute-done.15 = bf16[2,128,256]{2,1,0:T(8,128)(2,1)S(1)} collective-permute-done((bf16[2,128,256]{2,1,0:T(8,128)(2,1)S(1)}, bf16[2,128,256]{2,1,0:T(8,128)(2,1)S(1)}, u32[]{:S(2)}, u32[]{:S(2)}) %collective-permute-start.15) | collective-permute-done | bytes 131104 | tf_op jit(solution)/shard_map/ppermute | solution.py:559
  86.6 2.6 %collective-permute-start.18 = (bf16[2,128,256]{2,1,0:T(8,128)(2,1)S(1)}, bf16[2,128,256]{2,1,0:T(8,128)(2,1)S(1)}, u32[]{:S(2)}, u32[]{:S(2)}) collective-permute-start(bf16[2,128,256]{2,1,0:T(8,128)(2,1)S(1)} %select_convert_fusion.refs_0_), channel_id=1, source_target_pairs={{0,6},{2,4},{4,2},{6,0},{8,14},{10,12},{12,10},{14,8},{1,7},{3,5},... | collective-permute-start | bytes 393224 | tf_op jit(solution)/shard_map/ppermute | solution.py:561
  89.1 0.5 collective-permute-start.17
  89.7 1.8 %collective-permute-start.19 = (bf16[2,128,256]{2,1,0:T(8,128)(2,1)S(1)}, bf16[2,128,256]{2,1,0:T(8,128)(2,1)S(1)}, u32[]{:S(2)}, u32[]{:S(2)}) collective-permute-start(bf16[2,128,256]{2,1,0:T(8,128)(2,1)S(1)} %select_convert_fusion.refs_0_), channel_id=1, source_target_pairs={{0,1},{1,0},{2,3},{3,2},{4,5},{5,4},{6,7},{7,6},{8,9},{9,8},{10,11... | collective-permute-start | bytes 393224 | tf_op jit(solution)/shard_map/ppermute | solution.py:562
  91.5 2.8 %collective-permute-start.22 = (bf16[2,128,256]{2,1,0:T(8,128)(2,1)S(1)}, bf16[2,128,256]{2,1,0:T(8,128)(2,1)S(1)}, u32[]{:S(2)}, u32[]{:S(2)}) collective-permute-start(bf16[2,128,256]{2,1,0:T(8,128)(2,1)S(1)} %collective-permute-done.18.refs_3_), channel_id=1, source_target_pairs={{0,1},{1,0},{2,3},{3,2},{4,5},{5,4},{6,7},{7,6},{8,9},{9,8},{10,11... | collective-permute-start | bytes 393224 | tf_op jit(solution)/shard_map/ppermute | solution.py:562
  94.3 1.2 %collective-permute-done.17.refs_2_ = bf16[2,128,256]{2,1,0:T(8,128)(2,1)S(1)} collective-permute-done((bf16[2,128,256]{2,1,0:T(8,128)(2,1)S(1)}, bf16[2,128,256]{2,1,0:T(8,128)(2,1)S(1)}, u32[]{:S(2)}, u32[]{:S(2)}) %collective-permute-start.17) | collective-permute-done | bytes 131104 | tf_op jit(solution)/shard_map/ppermute | solution.py:561
  95.5 0.8 collective-permute-start.21
  96.4 1.0 collective-permute-done.21.refs_6_
  97.7 5.6 %vector_and_sigma_2.1 = (f32[3,4,64,256]{3,2,1,0:T(8,128)}, f32[8,128]{1,0:T(8,128)S(1)}, f32[272,128]{1,0:T(8,128)S(1)}, bf16[272,128]{1,0:T(8,128)(2,1)S(1)}) custom-call(s32[44]{0:T(128)S(1)} %concatenate.8.meta, bf16[2,128,256]{2,1,0:T(8,128)(2,1)S(1)} %select_convert_fusion.refs_0_, bf16[2,128,256]{2,1,0:T(8,128)(2,1)S(1)} %collective-permute-done.16.refs_1_, ...), custom_call_target="tpu_custom_call" | custom-call | tf_op jit(solution)/shard_map/vector_and_sigma_2/pallas_call | solution.py:586
  103.3 2.4 %collective-permute-start.23 = (bf16[272,128]{1,0:T(8,128)(2,1)S(1)}, bf16[272,128]{1,0:T(8,128)(2,1)S(1)}, u32[]{:S(2)}, u32[]{:S(2)}) collective-permute-start(bf16[272,128]{1,0:T(8,128)(2,1)S(1)} %get-tuple-element.37), channel_id=1, source_target_pairs={{0,12},{4,8},{8,4},{12,0},{1,13},{5,9},{9,5},{13,1},{2,14},{6,10},... | collective-permute-start | bytes 208904 | tf_op jit(solution)/shard_map/ppermute | solution.py:618
  105.7 3.1 %collective-permute-done.23.got = bf16[272,128]{1,0:T(8,128)(2,1)S(1)} collective-permute-done((bf16[272,128]{1,0:T(8,128)(2,1)S(1)}, bf16[272,128]{1,0:T(8,128)(2,1)S(1)}, u32[]{:S(2)}, u32[]{:S(2)}) %collective-permute-start.23) | collective-permute-done | bytes 69664 | tf_op jit(solution)/shard_map/ppermute | solution.py:618
  108.8 0.6 last_sums.1
  109.4 0.7 collective-permute-start.24
  110.1 2.1 %collective-permute-start.25 = (bf16[144,128]{1,0:T(8,128)(2,1)S(1)}, bf16[144,128]{1,0:T(8,128)(2,1)S(1)}, u32[]{:S(2)}, u32[]{:S(2)}) collective-permute-start(bf16[144,128]{1,0:T(8,128)(2,1)S(1)} %get-tuple-element.40), channel_id=1, source_target_pairs={{0,4},{4,0},{8,12},{12,8},{1,5},{5,1},{9,13},{13,9},{2,6},{6,2},{1... | collective-permute-start | bytes 110600 | tf_op jit(solution)/shard_map/ppermute | solution.py:628
  112.3 1.5 %collective-permute-done.26.by_both = bf16[144,128]{1,0:T(8,128)(2,1)S(1)} collective-permute-done((bf16[144,128]{1,0:T(8,128)(2,1)S(1)}, bf16[144,128]{1,0:T(8,128)(2,1)S(1)}, u32[]{:S(2)}, u32[]{:S(2)}) %collective-permute-start.26) | collective-permute-done | bytes 36896 | tf_op jit(solution)/shard_map/ppermute | solution.py:628
  114.2 3.0 %collective-permute-start.27 = (f32[8,128]{1,0:T(8,128)S(1)}, f32[8,128]{1,0:T(8,128)S(1)}, u32[]{:S(2)}, u32[]{:S(2)}) collective-permute-start(f32[8,128]{1,0:T(8,128)S(1)} %last_dots.1.dots), channel_id=1, source_target_pairs={{0,1},{1,0},{2,3},{3,2},{4,5},{5,4},{6,7},{7,6},{8,9},{9,8},{10,11... | collective-permute-start | bytes 12296 | tf_op jit(solution)/shard_map/ppermute | solution.py:637
  117.2 1.3 %last_rows.1 = f32[3,4,64,256]{3,2,1,0:T(8,128)} custom-call(s32[44]{0:T(128)S(1)} %concatenate.8.meta, f32[2,64,128]{2,1,0:T(8,128)S(1)} %get-tuple-element.38.own, bf16[144,128]{1,0:T(8,128)(2,1)S(1)} %collective-permute-done.24.by_env, bf16[144,128]{1,0:T(8,128)(2,1)S(1)} %collective-permute-done.25.by_term, ...), custom_call_target="tpu_custom_call", output_to_operand_aliasing={{}: (5, {})} | custom-call | tf_op jit(solution)/shard_map/last_rows/pallas_call | solution.py:638
  118.5 0.6 subspace.1
  (51 shorter events, 3.0 us)
Async XLA Ops:
  0.6 4.9 %copy-start = (f32[4,256,256]{2,1,0:T(8,128)S(1)}, f32[4,256,256]{2,1,0:T(8,128)}, u32[]{:S(2)}) copy-start(f32[4,256,256]{2,1,0:T(8,128)} %pre.1) | copy-start | bytes 3145732
  3.3 26.5 %copy-start.4 = (bf16[4,256,256]{2,1,0:T(8,128)(2,1)S(1)}, bf16[4,256,256]{2,1,0:T(8,128)(2,1)}, u32[]{:S(2)}) copy-start(bf16[4,256,256]{2,1,0:T(8,128)(2,1)} %psi.1) | copy-start | bytes 1572868
  3.3 29.5 %copy-start.9 = (s32[8,4]{0,1:T(4,128)S(1)}, s32[8,4]{0,1:T(4,128)}, u32[]{:S(2)}) copy-start(s32[8,4]{0,1:T(4,128)} %param.9) | copy-start | bytes 388
  3.3 29.6 %copy-start.8 = (s32[8]{0:T(128)S(1)}, s32[8]{0:T(128)}, u32[]{:S(2)}) copy-start(s32[8]{0:T(128)} %param.10) | copy-start | bytes 100
  3.4 25.4 %collective-permute-start.5 = (bf16[8,2,128,256]{3,2,1,0:T(8,128)(2,1)}, bf16[8,2,128,256]{3,2,1,0:T(8,128)(2,1)}, u32[]{:S(2)}, u32[]{:S(2)}) collective-permute-start(bf16[8,2,128,256]{3,2,1,0:T(8,128)(2,1)} %get-tuple-element.27), channel_id=1, source_target_pairs={{0,4},{4,0},{8,12},{12,8},{1,5},{5,1},{9,13},{13,9},{2,6},{6,2},{1... | collective-permute-start | bytes 3145736 | tf_op jit(solution)/shard_map/ppermute | solution.py:473
  5.5 29.6 %collective-permute-start.1 = (f32[4,256,256]{2,1,0:T(8,128)S(1)}, f32[4,256,256]{2,1,0:T(8,128)S(1)}, u32[]{:S(2)}, u32[]{:S(2)}) collective-permute-start(f32[4,256,256]{2,1,0:T(8,128)S(1)} %copy-done), channel_id=1, source_target_pairs={{0,1},{1,0},{2,3},{3,2},{4,5},{5,4},{6,7},{7,6},{8,9},{9,8},{10,11... | collective-permute-start | bytes 3145736 | tf_op jit(solution)/shard_map/ppermute | solution.py:472
  6.5 29.6 %collective-permute-start.2 = (bf16[8,2,128,256]{3,2,1,0:T(8,128)(2,1)}, bf16[8,2,128,256]{3,2,1,0:T(8,128)(2,1)}, u32[]{:S(2)}, u32[]{:S(2)}) collective-permute-start(bf16[8,2,128,256]{3,2,1,0:T(8,128)(2,1)} %get-tuple-element.23), channel_id=1, source_target_pairs={{0,2},{2,0},{1,3},{3,1},{4,6},{6,4},{5,7},{7,5},{8,10},{10,8},{9,1... | collective-permute-start | bytes 3145736 | tf_op jit(solution)/shard_map/ppermute | solution.py:474
  10.0 41.6 %collective-permute-start.4 = (bf16[8,2,128,256]{3,2,1,0:T(8,128)(2,1)}, bf16[8,2,128,256]{3,2,1,0:T(8,128)(2,1)}, u32[]{:S(2)}, u32[]{:S(2)}) collective-permute-start(bf16[8,2,128,256]{3,2,1,0:T(8,128)(2,1)} %sectors_to_send.3), channel_id=1, source_target_pairs={{0,4},{4,0},{8,12},{12,8},{1,5},{5,1},{9,13},{13,9},{2,6},{6,2},{1... | collective-permute-start | bytes 3145736 | tf_op jit(solution)/shard_map/ppermute | solution.py:475
  28.7 25.8 %collective-permute-start.6 = (bf16[8,2,128,256]{3,2,1,0:T(8,128)(2,1)}, bf16[8,2,128,256]{3,2,1,0:T(8,128)(2,1)}, u32[]{:S(2)}, u32[]{:S(2)}) collective-permute-start(bf16[8,2,128,256]{3,2,1,0:T(8,128)(2,1)} %collective-permute-done.5.near_h.refs_15_.refs_17_), channel_id=1, source_target_pairs={{0,2},{2,0},{1,3},{3,1},{4,6},{6,4},{5,7},{7,5},{8,10},{10,8},{9,1... | collective-permute-start | bytes 3145736 | tf_op jit(solution)/shard_map/ppermute | solution.py:476
  29.8 4.5 %collective-permute-start = (bf16[4,256,256]{2,1,0:T(8,128)(2,1)S(1)}, bf16[4,256,256]{2,1,0:T(8,128)(2,1)S(1)}, u32[]{:S(2)}, u32[]{:S(2)}) collective-permute-start(bf16[4,256,256]{2,1,0:T(8,128)(2,1)S(1)} %copy-done.4), channel_id=1, source_target_pairs={{0,1},{1,0},{2,3},{3,2},{4,5},{5,4},{6,7},{7,6},{8,9},{9,8},{10,11... | collective-permute-start | bytes 1572872 | tf_op jit(solution)/shard_map/ppermute | solution.py:472
  34.3 0.8 copy-start.6
  35.1 1.0 copy-start.2
  36.1 1.2 %copy-start.1 = (f32[4,256,256]{2,1,0:T(8,128)S(1)}, f32[4,256,256]{2,1,0:T(8,128)}, u32[]{:S(2)}) copy-start(f32[4,256,256]{2,1,0:T(8,128)} %pre.1) | copy-start | bytes 3145732
  37.3 1.2 %copy-start.3 = (f32[4,256,256]{2,1,0:T(8,128)S(1)}, f32[4,256,256]{2,1,0:T(8,128)}, u32[]{:S(2)}) copy-start(f32[4,256,256]{2,1,0:T(8,128)} %copy-done.2) | copy-start | bytes 3145732
  38.6 1.0 copy-start.5
  39.6 1.0 copy-start.7
  44.3 7.0 %collective-permute-start.3 = (s32[8,4]{0,1:T(4,128)S(1)}, s32[8,4]{0,1:T(4,128)S(1)}, u32[]{:S(2)}, u32[]{:S(2)}) collective-permute-start(s32[8,4]{0,1:T(4,128)S(1)} %copy-done.9), channel_id=1, source_target_pairs={{0,4},{4,0},{8,12},{12,8},{1,5},{5,1},{9,13},{13,9},{2,6},{6,2},{1... | collective-permute-start | bytes 392 | tf_op jit(solution)/shard_map/ppermute | solution.py:527
  56.5 5.8 %collective-permute-start.7 = (bf16[2,128,256]{2,1,0:T(8,128)(2,1)S(1)}, bf16[2,128,256]{2,1,0:T(8,128)(2,1)S(1)}, u32[]{:S(2)}, u32[]{:S(2)}) collective-permute-start(bf16[2,128,256]{2,1,0:T(8,128)(2,1)S(1)} %first_sigma_far_rows.1), channel_id=1, source_target_pairs={{0,12},{4,8},{8,4},{12,0},{1,13},{5,9},{9,5},{13,1},{2,14},{6,10},... | collective-permute-start | bytes 393224 | tf_op jit(solution)/shard_map/ppermute | solution.py:559
  62.4 6.1 %collective-permute-start.10 = (bf16[2,128,256]{2,1,0:T(8,128)(2,1)S(1)}, bf16[2,128,256]{2,1,0:T(8,128)(2,1)S(1)}, u32[]{:S(2)}, u32[]{:S(2)}) collective-permute-start(bf16[2,128,256]{2,1,0:T(8,128)(2,1)S(1)} %select_convert_fusion.1.refs_0_), channel_id=1, source_target_pairs={{0,6},{2,4},{4,2},{6,0},{8,14},{10,12},{12,10},{14,8},{1,7},{3,5},... | collective-permute-start | bytes 393224 | tf_op jit(solution)/shard_map/ppermute | solution.py:561
  66.1 6.1 %collective-permute-start.9 = (bf16[2,128,256]{2,1,0:T(8,128)(2,1)S(1)}, bf16[2,128,256]{2,1,0:T(8,128)(2,1)S(1)}, u32[]{:S(2)}, u32[]{:S(2)}) collective-permute-start(bf16[2,128,256]{2,1,0:T(8,128)(2,1)S(1)} %select_convert_fusion.1.refs_0_), channel_id=1, source_target_pairs={{0,2},{2,0},{1,3},{3,1},{4,6},{6,4},{5,7},{7,5},{8,10},{10,8},{9,1... | collective-permute-start | bytes 393224 | tf_op jit(solution)/shard_map/ppermute | solution.py:561
  66.3 7.2 %collective-permute-start.8 = (bf16[2,128,256]{2,1,0:T(8,128)(2,1)S(1)}, bf16[2,128,256]{2,1,0:T(8,128)(2,1)S(1)}, u32[]{:S(2)}, u32[]{:S(2)}) collective-permute-start(bf16[2,128,256]{2,1,0:T(8,128)(2,1)S(1)} %select_convert_fusion.1.refs_0_), channel_id=1, source_target_pairs={{0,4},{4,0},{8,12},{12,8},{1,5},{5,1},{9,13},{13,9},{2,6},{6,2},{1... | collective-permute-start | bytes 393224 | tf_op jit(solution)/shard_map/ppermute | solution.py:561
  66.5 7.1 %collective-permute-start.11 = (bf16[2,128,256]{2,1,0:T(8,128)(2,1)S(1)}, bf16[2,128,256]{2,1,0:T(8,128)(2,1)S(1)}, u32[]{:S(2)}, u32[]{:S(2)}) collective-permute-start(bf16[2,128,256]{2,1,0:T(8,128)(2,1)S(1)} %select_convert_fusion.1.refs_0_), channel_id=1, source_target_pairs={{0,1},{1,0},{2,3},{3,2},{4,5},{5,4},{6,7},{7,6},{8,9},{9,8},{10,11... | collective-permute-start | bytes 393224 | tf_op jit(solution)/shard_map/ppermute | solution.py:562
  68.5 5.1 %collective-permute-start.14 = (bf16[2,128,256]{2,1,0:T(8,128)(2,1)S(1)}, bf16[2,128,256]{2,1,0:T(8,128)(2,1)S(1)}, u32[]{:S(2)}, u32[]{:S(2)}) collective-permute-start(bf16[2,128,256]{2,1,0:T(8,128)(2,1)S(1)} %collective-permute-done.10.refs_3_), channel_id=1, source_target_pairs={{0,1},{1,0},{2,3},{3,2},{4,5},{5,4},{6,7},{7,6},{8,9},{9,8},{10,11... | collective-permute-start | bytes 393224 | tf_op jit(solution)/shard_map/ppermute | solution.py:562
  72.2 2.2 %collective-permute-start.13 = (bf16[2,128,256]{2,1,0:T(8,128)(2,1)S(1)}, bf16[2,128,256]{2,1,0:T(8,128)(2,1)S(1)}, u32[]{:S(2)}, u32[]{:S(2)}) collective-permute-start(bf16[2,128,256]{2,1,0:T(8,128)(2,1)S(1)} %collective-permute-done.9.refs_2_), channel_id=1, source_target_pairs={{0,1},{1,0},{2,3},{3,2},{4,5},{5,4},{6,7},{7,6},{8,9},{9,8},{10,11... | collective-permute-start | bytes 393224 | tf_op jit(solution)/shard_map/ppermute | solution.py:562
  73.4 1.3 %collective-permute-start.12 = (bf16[2,128,256]{2,1,0:T(8,128)(2,1)S(1)}, bf16[2,128,256]{2,1,0:T(8,128)(2,1)S(1)}, u32[]{:S(2)}, u32[]{:S(2)}) collective-permute-start(bf16[2,128,256]{2,1,0:T(8,128)(2,1)S(1)} %collective-permute-done.8.refs_1_), channel_id=1, source_target_pairs={{0,1},{1,0},{2,3},{3,2},{4,5},{5,4},{6,7},{7,6},{8,9},{9,8},{10,11... | collective-permute-start | bytes 393224 | tf_op jit(solution)/shard_map/ppermute | solution.py:562
  79.6 6.8 %collective-permute-start.15 = (bf16[2,128,256]{2,1,0:T(8,128)(2,1)S(1)}, bf16[2,128,256]{2,1,0:T(8,128)(2,1)S(1)}, u32[]{:S(2)}, u32[]{:S(2)}) collective-permute-start(bf16[2,128,256]{2,1,0:T(8,128)(2,1)S(1)} %get-tuple-element.33), channel_id=1, source_target_pairs={{0,12},{4,8},{8,4},{12,0},{1,13},{5,9},{9,5},{13,1},{2,14},{6,10},... | collective-permute-start | bytes 393224 | tf_op jit(solution)/shard_map/ppermute | solution.py:559
  86.6 4.9 %collective-permute-start.18 = (bf16[2,128,256]{2,1,0:T(8,128)(2,1)S(1)}, bf16[2,128,256]{2,1,0:T(8,128)(2,1)S(1)}, u32[]{:S(2)}, u32[]{:S(2)}) collective-permute-start(bf16[2,128,256]{2,1,0:T(8,128)(2,1)S(1)} %select_convert_fusion.refs_0_), channel_id=1, source_target_pairs={{0,6},{2,4},{4,2},{6,0},{8,14},{10,12},{12,10},{14,8},{1,7},{3,5},... | collective-permute-start | bytes 393224 | tf_op jit(solution)/shard_map/ppermute | solution.py:561
  89.1 6.4 %collective-permute-start.17 = (bf16[2,128,256]{2,1,0:T(8,128)(2,1)S(1)}, bf16[2,128,256]{2,1,0:T(8,128)(2,1)S(1)}, u32[]{:S(2)}, u32[]{:S(2)}) collective-permute-start(bf16[2,128,256]{2,1,0:T(8,128)(2,1)S(1)} %select_convert_fusion.refs_0_), channel_id=1, source_target_pairs={{0,2},{2,0},{1,3},{3,1},{4,6},{6,4},{5,7},{7,5},{8,10},{10,8},{9,1... | collective-permute-start | bytes 393224 | tf_op jit(solution)/shard_map/ppermute | solution.py:561
  89.6 6.7 %collective-permute-start.16 = (bf16[2,128,256]{2,1,0:T(8,128)(2,1)S(1)}, bf16[2,128,256]{2,1,0:T(8,128)(2,1)S(1)}, u32[]{:S(2)}, u32[]{:S(2)}) collective-permute-start(bf16[2,128,256]{2,1,0:T(8,128)(2,1)S(1)} %select_convert_fusion.refs_0_), channel_id=1, source_target_pairs={{0,4},{4,0},{8,12},{12,8},{1,5},{5,1},{9,13},{13,9},{2,6},{6,2},{1... | collective-permute-start | bytes 393224 | tf_op jit(solution)/shard_map/ppermute | solution.py:561
  89.7 6.7 %collective-permute-start.19 = (bf16[2,128,256]{2,1,0:T(8,128)(2,1)S(1)}, bf16[2,128,256]{2,1,0:T(8,128)(2,1)S(1)}, u32[]{:S(2)}, u32[]{:S(2)}) collective-permute-start(bf16[2,128,256]{2,1,0:T(8,128)(2,1)S(1)} %select_convert_fusion.refs_0_), channel_id=1, source_target_pairs={{0,1},{1,0},{2,3},{3,2},{4,5},{5,4},{6,7},{7,6},{8,9},{9,8},{10,11... | collective-permute-start | bytes 393224 | tf_op jit(solution)/shard_map/ppermute | solution.py:562
  91.5 4.9 %collective-permute-start.22 = (bf16[2,128,256]{2,1,0:T(8,128)(2,1)S(1)}, bf16[2,128,256]{2,1,0:T(8,128)(2,1)S(1)}, u32[]{:S(2)}, u32[]{:S(2)}) collective-permute-start(bf16[2,128,256]{2,1,0:T(8,128)(2,1)S(1)} %collective-permute-done.18.refs_3_), channel_id=1, source_target_pairs={{0,1},{1,0},{2,3},{3,2},{4,5},{5,4},{6,7},{7,6},{8,9},{9,8},{10,11... | collective-permute-start | bytes 393224 | tf_op jit(solution)/shard_map/ppermute | solution.py:562
  95.5 1.8 %collective-permute-start.21 = (bf16[2,128,256]{2,1,0:T(8,128)(2,1)S(1)}, bf16[2,128,256]{2,1,0:T(8,128)(2,1)S(1)}, u32[]{:S(2)}, u32[]{:S(2)}) collective-permute-start(bf16[2,128,256]{2,1,0:T(8,128)(2,1)S(1)} %collective-permute-done.17.refs_2_), channel_id=1, source_target_pairs={{0,1},{1,0},{2,3},{3,2},{4,5},{5,4},{6,7},{7,6},{8,9},{9,8},{10,11... | collective-permute-start | bytes 393224 | tf_op jit(solution)/shard_map/ppermute | solution.py:562
  96.4 1.3 %collective-permute-start.20 = (bf16[2,128,256]{2,1,0:T(8,128)(2,1)S(1)}, bf16[2,128,256]{2,1,0:T(8,128)(2,1)S(1)}, u32[]{:S(2)}, u32[]{:S(2)}) collective-permute-start(bf16[2,128,256]{2,1,0:T(8,128)(2,1)S(1)} %collective-permute-done.16.refs_1_), channel_id=1, source_target_pairs={{0,1},{1,0},{2,3},{3,2},{4,5},{5,4},{6,7},{7,6},{8,9},{9,8},{10,11... | collective-permute-start | bytes 393224 | tf_op jit(solution)/shard_map/ppermute | solution.py:562
  103.3 5.5 %collective-permute-start.23 = (bf16[272,128]{1,0:T(8,128)(2,1)S(1)}, bf16[272,128]{1,0:T(8,128)(2,1)S(1)}, u32[]{:S(2)}, u32[]{:S(2)}) collective-permute-start(bf16[272,128]{1,0:T(8,128)(2,1)S(1)} %get-tuple-element.37), channel_id=1, source_target_pairs={{0,12},{4,8},{8,4},{12,0},{1,13},{5,9},{9,5},{13,1},{2,14},{6,10},... | collective-permute-start | bytes 208904 | tf_op jit(solution)/shard_map/ppermute | solution.py:618
  109.4 2.9 %collective-permute-start.24 = (bf16[144,128]{1,0:T(8,128)(2,1)S(1)}, bf16[144,128]{1,0:T(8,128)(2,1)S(1)}, u32[]{:S(2)}, u32[]{:S(2)}) collective-permute-start(bf16[144,128]{1,0:T(8,128)(2,1)S(1)} %get-tuple-element.39.own), channel_id=1, source_target_pairs={{0,2},{2,0},{1,3},{3,1},{4,6},{6,4},{5,7},{7,5},{8,10},{10,8},{9,1... | collective-permute-start | bytes 110600 | tf_op jit(solution)/shard_map/ppermute | solution.py:628
  110.1 3.7 %collective-permute-start.26 = (bf16[144,128]{1,0:T(8,128)(2,1)S(1)}, bf16[144,128]{1,0:T(8,128)(2,1)S(1)}, u32[]{:S(2)}, u32[]{:S(2)}) collective-permute-start(bf16[144,128]{1,0:T(8,128)(2,1)S(1)} %get-tuple-element.40), channel_id=1, source_target_pairs={{0,6},{2,4},{4,2},{6,0},{8,14},{10,12},{12,10},{14,8},{1,7},{3,5},... | collective-permute-start | bytes 110600 | tf_op jit(solution)/shard_map/ppermute | solution.py:628
  110.1 4.1 %collective-permute-start.25 = (bf16[144,128]{1,0:T(8,128)(2,1)S(1)}, bf16[144,128]{1,0:T(8,128)(2,1)S(1)}, u32[]{:S(2)}, u32[]{:S(2)}) collective-permute-start(bf16[144,128]{1,0:T(8,128)(2,1)S(1)} %get-tuple-element.40), channel_id=1, source_target_pairs={{0,4},{4,0},{8,12},{12,8},{1,5},{5,1},{9,13},{13,9},{2,6},{6,2},{1... | collective-permute-start | bytes 110600 | tf_op jit(solution)/shard_map/ppermute | solution.py:628
  114.2 4.3 %collective-permute-start.27 = (f32[8,128]{1,0:T(8,128)S(1)}, f32[8,128]{1,0:T(8,128)S(1)}, u32[]{:S(2)}, u32[]{:S(2)}) collective-permute-start(f32[8,128]{1,0:T(8,128)S(1)} %last_dots.1.dots), channel_id=1, source_target_pairs={{0,1},{1,0},{2,3},{3,2},{4,5},{5,4},{6,7},{7,6},{8,9},{9,8},{10,11... | collective-permute-start | bytes 12296 | tf_op jit(solution)/shard_map/ppermute | solution.py:637

commit v6 on v5

--- a/solution.py
+++ b/solution.py
@@ -10,7 +10,7 @@
 ITERS = 3
 EPS = 1e-06
 F32, BF16 = jnp.float32, jnp.bfloat16
-ROWS = 64
+ROWS = 128
 TAIL_ROWS = 16
 SPAN = 8
 VMEM_LIMIT = 16 * 1024 * 1024
@@ -55,7 +55,7 @@
 
 
 def _first_kernel(cfg, places, meta, psi, psi_o, pre, pre_o, *refs):
-    envs, (start, pret, scale_ref, vb_h, acc, vb, right, left, sem) = refs[: len(places)], refs[len(places) :]
+    envs, (start, pret, scale_ref, acc, vb, right, left, sem) = refs[: len(places)], refs[len(places) :]
     sec, states, width = psi.shape
     n_sec = sec * cfg["n_blk"]
     base = meta[2] * sec
@@ -89,8 +89,6 @@
         return ()
 
     _over(n_sec, states, width, 0, make)
-    save = pltpu.make_async_copy(vb, vb_h, sem.at[len(moves)])
-    save.start()
     for _, c in moves:
         c.wait()
     for k in range(acc.shape[0]):
@@ -101,7 +99,6 @@
             got = jnp.dot(inner, left[t, k], preferred_element_type=F32)
             total = got if total is None else total + got
         acc[k] = total
-    save.wait()
 
 
 def _group(cfg, meta, ref):
@@ -126,19 +123,25 @@
     return moves
 
 
-def _near_sigma_kernel(cfg, t0, meta, acc, vb_h, right_h, near_h, out, inner_far, vb, right, near, inner, sem):
-    moves = [(vb_h, vb), (right_h, right), (near_h, near)]
+def _near_sigma_kernel(cfg, t0, meta, acc, start, scale_ref, right_h, near_h, out, inner_far, vb, right, near, inner, sem):
+    moves = [(right_h, right), (near_h, near)]
     moves = [pltpu.make_async_copy(a, b, sem.at[i]) for i, (a, b) in enumerate(moves)]
     for c in moves:
         c.start()
+    scale = scale_ref[0, 0]
+
+    def make(s, r):
+        vb[s, r, :] = (start[s, r, :].astype(F32) * scale).astype(BF16)
+        return ()
+
+    _over(*vb.shape, 0, make)
     moves[0].wait()
-    moves[1].wait()
     terms, held, half = right.shape[:3]
     for k in range(held):
         for t in range(terms):
             chosen = vb[meta[cfg["pair_at"] + (t0 + t) * held + k]]
             inner[t, k] = jnp.dot(right[t, k], chosen, preferred_element_type=F32).astype(BF16)
-    moves[2].wait()
+    moves[1].wait()
     own, other = (pl.ds(pl.multiple_of(side * half, half), half) for side in (meta[0], 1 - meta[0]))
     for k in range(held):
         total = acc[k]
@@ -507,16 +510,16 @@
     dma = pltpu.SemaphoreType.DMA
     n_moves = 3 * terms // span
     first_places, first_envs = [("right", 0, 0, True), *own_places], [right_env, *own_envs]
-    start, pret, scale0, vb0, partial = pl.pallas_call(
+    start, pret, scale0, partial = pl.pallas_call(
         functools.partial(_first_kernel, cfg, first_places),
-        out_shape=(VM(full, BF16), VM(full, F32), VM((8, 128), F32), HB(full, BF16), VM((held, half, width), F32)),
+        out_shape=(VM(full, BF16), VM(full, F32), VM((8, 128), F32), VM((held, half, width), F32)),
         in_specs=_specs(SM, VM, VM, VM, VM, *[HB] * len(first_envs)),
-        out_specs=_specs(VM, VM, VM, HB, VM),
+        out_specs=_specs(VM, VM, VM, VM),
         scratch_shapes=[
             pltpu.VMEM(full, BF16),
             pltpu.VMEM((terms, held, half, states), BF16),
             pltpu.VMEM((terms, held, states, width), BF16),
-            dma((n_moves + 1,)),
+            dma((n_moves,)),
         ],
         compiler_params=params,
         name="start_vector",
@@ -530,12 +533,12 @@
         partial, inner_far = pl.pallas_call(
             functools.partial(_near_sigma_kernel, cfg, terms),
             out_shape=(VM((held, half, width), F32), VM((terms, held, half, half), BF16)),
-            in_specs=_specs(SM, VM, HB, HB, HB),
+            in_specs=_specs(SM, VM, VM, VM, HB, HB),
             out_specs=tuple(_specs(VM, VM)),
-            scratch_shapes=[pltpu.VMEM(full, BF16), *[pltpu.VMEM(piece, BF16)] * 3, dma((3,))],
+            scratch_shapes=[pltpu.VMEM(full, BF16), *[pltpu.VMEM(piece, BF16)] * 3, dma((2,))],
             compiler_params=params,
             name="first_sigma_next_terms",
-        )(meta, *_vmem(partial), *_hbm(vb0, next_right, next_left))
+        )(meta, *_vmem(partial, start, scale0), *_hbm(next_right, next_left))
         partial = pl.pallas_call(
             _far_sigma_kernel,
             out_shape=VM((held, half, width), BF16),

time: 120 us -> 119 us (level)
  transfers between devices with their start and end apart: 28 -> 28, of which waited for: 16 -> 16; matrix products, arithmetic and copies ran while one was open for 0% -> 0% of each run, Pallas kernels for 9% -> 8%
where the time goes in v6:
time: 119 us
  waiting for transfers between devices  42.9 us (36%)
  starting transfers between devices  41.9 us (35%)
  Pallas kernels  26.1 us (22%)
  local copies, waits for them, and re-layouts  6.9 us (6%)
    ppermute x1, waiting for transfers between devices, _on_device(): next_left = next_term(to_next)  18.6 us
    ppermute x8, starting transfers between devices, combine(): there = [other_blk(x) for x in here]  11.1 us
    pallas_call x2, Pallas kernels, _on_device(): pl.pallas_call(functools.partial(_step_kernel, dict(cfg, n_out=len(outs))...  10.4 us
    ppermute x6, starting transfers between devices, combine(): here = [shard, next_term(shard), other_env(shard), corners(shard)]  7.18 us
    ppermute x2, waiting for transfers between devices, combine(): total = partial.astype(F32) + far_term(partial).astype(F32)  7.04 us
    unnamed x20, local copies, waits for them, and re-layouts  6.33 us
    ppermute x1, waiting for transfers between devices, _on_device(): next_pairing = next_term(lax.optimization_barrier((pairing, partial))[0])  5.64 us
    ppermute x2, starting transfers between devices, combine(): total = partial.astype(F32) + far_term(partial).astype(F32)  5.51 us
  transfers between devices with their start and end apart: 28, of which 16 were waited for; matrix products, arithmetic and copies ran while one was open for 0% of the time, Pallas kernels for 8%

profile of v6, /device:TPU:1, one launch (start us, length us, event | category | flops | bytes accessed | tf_op | source)
XLA Modules:
  0.0 118.8 jit_solution(3184386480935303671)
XLA Ops:
  0.6 2.7 %sectors_to_send.2 = (bf16[8,2,128,256]{3,2,1,0:T(8,128)(2,1)}, bf16[8,2,128,256]{3,2,1,0:T(8,128)(2,1)}) custom-call(s32[1]{0:T(128)} %bitcast.3.which, bf16[8,4,128,256]{3,2,1,0:T(8,128)(2,1)} %refs_14_.1), custom_call_target="tpu_custom_call" | custom-call | tf_op jit(solution)/shard_map/sectors_to_send/pallas_call | solution.py:442
  3.4 2.2 %collective-permute-start.5 = (bf16[8,2,128,256]{3,2,1,0:T(8,128)(2,1)}, bf16[8,2,128,256]{3,2,1,0:T(8,128)(2,1)}, u32[]{:S(2)}, u32[]{:S(2)}) collective-permute-start(bf16[8,2,128,256]{3,2,1,0:T(8,128)(2,1)} %get-tuple-element.27), channel_id=1, source_target_pairs={{0,4},{4,0},{8,12},{12,8},{1,5},{5,1},{9,13},{13,9},{2,6},{6,2},{1... | collective-permute-start | bytes 3145736 | tf_op jit(solution)/shard_map/ppermute | solution.py:476
  5.5 1.0 collective-permute-start.1
  6.5 1.2 %collective-permute-start.2 = (bf16[8,2,128,256]{3,2,1,0:T(8,128)(2,1)}, bf16[8,2,128,256]{3,2,1,0:T(8,128)(2,1)}, u32[]{:S(2)}, u32[]{:S(2)}) collective-permute-start(bf16[8,2,128,256]{3,2,1,0:T(8,128)(2,1)} %get-tuple-element.22), channel_id=1, source_target_pairs={{0,2},{2,0},{1,3},{3,1},{4,6},{6,4},{5,7},{7,5},{8,10},{10,8},{9,1... | collective-permute-start | bytes 3145736 | tf_op jit(solution)/shard_map/ppermute | solution.py:477
  7.7 2.2 %sectors_to_send.3 = bf16[8,2,128,256]{3,2,1,0:T(8,128)(2,1)} custom-call(s32[1]{0:T(128)} %bitcast.3.which, bf16[8,4,128,256]{3,2,1,0:T(8,128)(2,1)} %refs_13_.1), custom_call_target="tpu_custom_call" | custom-call | tf_op jit(solution)/shard_map/sectors_to_send/pallas_call | solution.py:442
  10.2 18.6 %collective-permute-done.5.near_h.refs_15_.refs_17_ = bf16[8,2,128,256]{3,2,1,0:T(8,128)(2,1)} collective-permute-done((bf16[8,2,128,256]{3,2,1,0:T(8,128)(2,1)}, bf16[8,2,128,256]{3,2,1,0:T(8,128)(2,1)}, u32[]{:S(2)}, u32[]{:S(2)}) %collective-permute-start.5) | collective-permute-done | bytes 1048608 | tf_op jit(solution)/shard_map/ppermute | solution.py:476
  28.7 1.1 collective-permute-start.6
  29.8 3.0 %collective-permute-start = (bf16[4,256,256]{2,1,0:T(8,128)(2,1)S(1)}, bf16[4,256,256]{2,1,0:T(8,128)(2,1)S(1)}, u32[]{:S(2)}, u32[]{:S(2)}) collective-permute-start(bf16[4,256,256]{2,1,0:T(8,128)(2,1)S(1)} %copy-done.4), channel_id=1, source_target_pairs={{0,1},{1,0},{2,3},{3,2},{4,5},{5,4},{6,7},{7,6},{8,9},{9,8},{10,11... | collective-permute-start | bytes 1572872 | tf_op jit(solution)/shard_map/ppermute | solution.py:475
  33.0 1.3 %collective-permute-done.psi_o = bf16[4,256,256]{2,1,0:T(8,128)(2,1)S(1)} collective-permute-done((bf16[4,256,256]{2,1,0:T(8,128)(2,1)S(1)}, bf16[4,256,256]{2,1,0:T(8,128)(2,1)S(1)}, u32[]{:S(2)}, u32[]{:S(2)}) %collective-permute-start) | collective-permute-done | bytes 524320 | tf_op jit(solution)/shard_map/ppermute | solution.py:475
  34.3 0.8 copy-done.6
  35.1 1.0 copy-done.2
  36.1 1.2 %copy-done.1 = f32[4,256,256]{2,1,0:T(8,128)S(1)} copy-done((f32[4,256,256]{2,1,0:T(8,128)S(1)}, f32[4,256,256]{2,1,0:T(8,128)}, u32[]{:S(2)}) %copy-start.1) | copy-done | bytes 1048600
  37.3 1.2 %copy-done.3 = f32[4,256,256]{2,1,0:T(8,128)S(1)} copy-done((f32[4,256,256]{2,1,0:T(8,128)S(1)}, f32[4,256,256]{2,1,0:T(8,128)}, u32[]{:S(2)}) %copy-start.3) | copy-done | bytes 1048600
  38.6 1.0 copy-done.5
  39.6 1.0 copy-done.7
  40.6 3.6 %start_vector.1 = (bf16[8,256,256]{2,1,0:T(8,128)(2,1)S(1)}, f32[8,256,256]{2,1,0:T(8,128)S(1)}, f32[8,128]{1,0:T(8,128)S(1)}, f32[2,128,256]{2,1,0:T(8,128)S(1)}) custom-call(s32[28]{0:T(128)S(1)} %concatenate.7.meta, bf16[4,256,256]{2,1,0:T(8,128)(2,1)S(1)} %copy-done.5, bf16[4,256,256]{2,1,0:T(8,128)(2,1)S(1)} %copy-done.7, f32[4,256,256]{2,1,0:T(8,128)S(1)} %copy-done.1, ...), custom_call_target="tpu_custom_call" | custom-call | tf_op jit(solution)/shard_map/start_vector/pallas_call | solution.py:513
  44.3 1.4 %collective-permute-start.3 = (s32[8,4]{0,1:T(4,128)S(1)}, s32[8,4]{0,1:T(4,128)S(1)}, u32[]{:S(2)}, u32[]{:S(2)}) collective-permute-start(s32[8,4]{0,1:T(4,128)S(1)} %copy-done.9), channel_id=1, source_target_pairs={{0,4},{4,0},{8,12},{12,8},{1,5},{5,1},{9,13},{13,9},{2,6},{6,2},{1... | collective-permute-start | bytes 392 | tf_op jit(solution)/shard_map/ppermute | solution.py:530
  45.6 5.6 %collective-permute-done.3 = s32[8,4]{0,1:T(4,128)S(1)} collective-permute-done((s32[8,4]{0,1:T(4,128)S(1)}, s32[8,4]{0,1:T(4,128)S(1)}, u32[]{:S(2)}, u32[]{:S(2)}) %collective-permute-start.3) | collective-permute-done | bytes 160 | tf_op jit(solution)/shard_map/ppermute | solution.py:530
  51.5 2.8 %first_sigma_next_terms.1 = (f32[2,128,256]{2,1,0:T(8,128)S(1)}, bf16[8,2,128,128]{3,2,1,0:T(8,128)(2,1)S(1)}) custom-call(s32[44]{0:T(128)S(1)} %concatenate.8.meta, f32[2,128,256]{2,1,0:T(8,128)S(1)} %get-tuple-element.23.acc, bf16[8,256,256]{2,1,0:T(8,128)(2,1)S(1)} %get-tuple-element.25.start.refs_8_, f32[8,128]{1,0:T(8,128)S(1)} %get-tuple-element.26.scale_ref.refs_9_, ...), custom_call_target="tpu_custom_call" | custom-call | tf_op jit(solution)/shard_map/first_sigma_next_terms/pallas_call | solution.py:533
  54.3 1.9 %first_sigma_far_rows.1 = bf16[2,128,256]{2,1,0:T(8,128)(2,1)S(1)} custom-call(f32[2,128,256]{2,1,0:T(8,128)S(1)} %get-tuple-element.28.acc, bf16[8,2,128,128]{3,2,1,0:T(8,128)(2,1)S(1)} %get-tuple-element.29.inner, bf16[8,2,128,256]{3,2,1,0:T(8,128)(2,1)} %collective-permute-done.6.far_h.refs_16_.refs_18_), custom_call_target="tpu_custom_call" | custom-call | tf_op jit(solution)/shard_map/first_sigma_far_rows/pallas_call | solution.py:542
  56.2 3.2 %collective-permute-start.7 = (bf16[2,128,256]{2,1,0:T(8,128)(2,1)S(1)}, bf16[2,128,256]{2,1,0:T(8,128)(2,1)S(1)}, u32[]{:S(2)}, u32[]{:S(2)}) collective-permute-start(bf16[2,128,256]{2,1,0:T(8,128)(2,1)S(1)} %first_sigma_far_rows.1), channel_id=1, source_target_pairs={{0,12},{4,8},{8,4},{12,0},{1,13},{5,9},{9,5},{13,1},{2,14},{6,10},... | collective-permute-start | bytes 393224 | tf_op jit(solution)/shard_map/ppermute | solution.py:562
  59.5 2.5 %collective-permute-done.7 = bf16[2,128,256]{2,1,0:T(8,128)(2,1)S(1)} collective-permute-done((bf16[2,128,256]{2,1,0:T(8,128)(2,1)S(1)}, bf16[2,128,256]{2,1,0:T(8,128)(2,1)S(1)}, u32[]{:S(2)}, u32[]{:S(2)}) %collective-permute-start.7) | collective-permute-done | bytes 131104 | tf_op jit(solution)/shard_map/ppermute | solution.py:562
  62.1 3.7 %collective-permute-start.10 = (bf16[2,128,256]{2,1,0:T(8,128)(2,1)S(1)}, bf16[2,128,256]{2,1,0:T(8,128)(2,1)S(1)}, u32[]{:S(2)}, u32[]{:S(2)}) collective-permute-start(bf16[2,128,256]{2,1,0:T(8,128)(2,1)S(1)} %select_convert_fusion.1.refs_0_), channel_id=1, source_target_pairs={{0,6},{2,4},{4,2},{6,0},{8,14},{10,12},{12,10},{14,8},{1,7},{3,5},... | collective-permute-start | bytes 393224 | tf_op jit(solution)/shard_map/ppermute | solution.py:564
  66.1 2.0 %collective-permute-start.11 = (bf16[2,128,256]{2,1,0:T(8,128)(2,1)S(1)}, bf16[2,128,256]{2,1,0:T(8,128)(2,1)S(1)}, u32[]{:S(2)}, u32[]{:S(2)}) collective-permute-start(bf16[2,128,256]{2,1,0:T(8,128)(2,1)S(1)} %select_convert_fusion.1.refs_0_), channel_id=1, source_target_pairs={{0,1},{1,0},{2,3},{3,2},{4,5},{5,4},{6,7},{7,6},{8,9},{9,8},{10,11... | collective-permute-start | bytes 393224 | tf_op jit(solution)/shard_map/ppermute | solution.py:565
  68.1 2.8 %collective-permute-start.14 = (bf16[2,128,256]{2,1,0:T(8,128)(2,1)S(1)}, bf16[2,128,256]{2,1,0:T(8,128)(2,1)S(1)}, u32[]{:S(2)}, u32[]{:S(2)}) collective-permute-start(bf16[2,128,256]{2,1,0:T(8,128)(2,1)S(1)} %collective-permute-done.10.refs_3_), channel_id=1, source_target_pairs={{0,1},{1,0},{2,3},{3,2},{4,5},{5,4},{6,7},{7,6},{8,9},{9,8},{10,11... | collective-permute-start | bytes 393224 | tf_op jit(solution)/shard_map/ppermute | solution.py:565
  70.9 0.9 collective-permute-done.9.refs_2_
  71.9 1.2 %collective-permute-start.13 = (bf16[2,128,256]{2,1,0:T(8,128)(2,1)S(1)}, bf16[2,128,256]{2,1,0:T(8,128)(2,1)S(1)}, u32[]{:S(2)}, u32[]{:S(2)}) collective-permute-start(bf16[2,128,256]{2,1,0:T(8,128)(2,1)S(1)} %collective-permute-done.9.refs_2_), channel_id=1, source_target_pairs={{0,1},{1,0},{2,3},{3,2},{4,5},{5,4},{6,7},{7,6},{8,9},{9,8},{10,11... | collective-permute-start | bytes 393224 | tf_op jit(solution)/shard_map/ppermute | solution.py:565
  73.2 0.8 collective-permute-done.13.refs_6_
  74.4 4.8 %vector_and_sigma_1.1 = (bf16[8,256,256]{2,1,0:T(8,128)(2,1)}, f32[8,256,256]{2,1,0:T(8,128)S(1)}, f32[8,128]{1,0:T(8,128)S(1)}, bf16[2,128,256]{2,1,0:T(8,128)(2,1)S(1)}) custom-call(s32[44]{0:T(128)S(1)} %concatenate.8.meta, bf16[2,128,256]{2,1,0:T(8,128)(2,1)S(1)} %select_convert_fusion.1.refs_0_, ...), custom_call_target="tpu_custom_call" | custom-call | tf_op jit(solution)/shard_map/vector_and_sigma_1/pallas_call | solution.py:589
  79.3 2.3 %collective-permute-start.15 = (bf16[2,128,256]{2,1,0:T(8,128)(2,1)S(1)}, bf16[2,128,256]{2,1,0:T(8,128)(2,1)S(1)}, u32[]{:S(2)}, u32[]{:S(2)}) collective-permute-start(bf16[2,128,256]{2,1,0:T(8,128)(2,1)S(1)} %get-tuple-element.31), channel_id=1, source_target_pairs={{0,12},{4,8},{8,4},{12,0},{1,13},{5,9},{9,5},{13,1},{2,14},{6,10},... | collective-permute-start | bytes 393224 | tf_op jit(solution)/shard_map/ppermute | solution.py:562
  81.6 4.6 %collective-permute-done.15 = bf16[2,128,256]{2,1,0:T(8,128)(2,1)S(1)} collective-permute-done((bf16[2,128,256]{2,1,0:T(8,128)(2,1)S(1)}, bf16[2,128,256]{2,1,0:T(8,128)(2,1)S(1)}, u32[]{:S(2)}, u32[]{:S(2)}) %collective-permute-start.15) | collective-permute-done | bytes 131104 | tf_op jit(solution)/shard_map/ppermute | solution.py:562
  86.2 2.6 %collective-permute-start.18 = (bf16[2,128,256]{2,1,0:T(8,128)(2,1)S(1)}, bf16[2,128,256]{2,1,0:T(8,128)(2,1)S(1)}, u32[]{:S(2)}, u32[]{:S(2)}) collective-permute-start(bf16[2,128,256]{2,1,0:T(8,128)(2,1)S(1)} %select_convert_fusion.refs_0_), channel_id=1, source_target_pairs={{0,6},{2,4},{4,2},{6,0},{8,14},{10,12},{12,10},{14,8},{1,7},{3,5},... | collective-permute-start | bytes 393224 | tf_op jit(solution)/shard_map/ppermute | solution.py:564
  88.8 0.5 collective-permute-start.17
  89.3 1.8 %collective-permute-start.19 = (bf16[2,128,256]{2,1,0:T(8,128)(2,1)S(1)}, bf16[2,128,256]{2,1,0:T(8,128)(2,1)S(1)}, u32[]{:S(2)}, u32[]{:S(2)}) collective-permute-start(bf16[2,128,256]{2,1,0:T(8,128)(2,1)S(1)} %select_convert_fusion.refs_0_), channel_id=1, source_target_pairs={{0,1},{1,0},{2,3},{3,2},{4,5},{5,4},{6,7},{7,6},{8,9},{9,8},{10,11... | collective-permute-start | bytes 393224 | tf_op jit(solution)/shard_map/ppermute | solution.py:565
  91.5 2.5 %collective-permute-start.22 = (bf16[2,128,256]{2,1,0:T(8,128)(2,1)S(1)}, bf16[2,128,256]{2,1,0:T(8,128)(2,1)S(1)}, u32[]{:S(2)}, u32[]{:S(2)}) collective-permute-start(bf16[2,128,256]{2,1,0:T(8,128)(2,1)S(1)} %collective-permute-done.18.refs_3_), channel_id=1, source_target_pairs={{0,1},{1,0},{2,3},{3,2},{4,5},{5,4},{6,7},{7,6},{8,9},{9,8},{10,11... | collective-permute-start | bytes 393224 | tf_op jit(solution)/shard_map/ppermute | solution.py:565
  94.0 1.4 %collective-permute-done.17.refs_2_ = bf16[2,128,256]{2,1,0:T(8,128)(2,1)S(1)} collective-permute-done((bf16[2,128,256]{2,1,0:T(8,128)(2,1)S(1)}, bf16[2,128,256]{2,1,0:T(8,128)(2,1)S(1)}, u32[]{:S(2)}, u32[]{:S(2)}) %collective-permute-start.17) | collective-permute-done | bytes 131104 | tf_op jit(solution)/shard_map/ppermute | solution.py:564
  95.3 0.7 collective-permute-start.21
  96.1 1.0 collective-permute-done.21.refs_6_
  97.4 5.6 %vector_and_sigma_2.1 = (f32[3,4,64,256]{3,2,1,0:T(8,128)}, f32[8,128]{1,0:T(8,128)S(1)}, f32[272,128]{1,0:T(8,128)S(1)}, bf16[272,128]{1,0:T(8,128)(2,1)S(1)}) custom-call(s32[44]{0:T(128)S(1)} %concatenate.8.meta, bf16[2,128,256]{2,1,0:T(8,128)(2,1)S(1)} %select_convert_fusion.refs_0_, bf16[2,128,256]{2,1,0:T(8,128)(2,1)S(1)} %collective-permute-done.16.refs_1_, ...), custom_call_target="tpu_custom_call" | custom-call | tf_op jit(solution)/shard_map/vector_and_sigma_2/pallas_call | solution.py:589
  103.0 2.4 %collective-permute-start.23 = (bf16[272,128]{1,0:T(8,128)(2,1)S(1)}, bf16[272,128]{1,0:T(8,128)(2,1)S(1)}, u32[]{:S(2)}, u32[]{:S(2)}) collective-permute-start(bf16[272,128]{1,0:T(8,128)(2,1)S(1)} %get-tuple-element.35), channel_id=1, source_target_pairs={{0,12},{4,8},{8,4},{12,0},{1,13},{5,9},{9,5},{13,1},{2,14},{6,10},... | collective-permute-start | bytes 208904 | tf_op jit(solution)/shard_map/ppermute | solution.py:621
  105.4 3.1 %collective-permute-done.23.got = bf16[272,128]{1,0:T(8,128)(2,1)S(1)} collective-permute-done((bf16[272,128]{1,0:T(8,128)(2,1)S(1)}, bf16[272,128]{1,0:T(8,128)(2,1)S(1)}, u32[]{:S(2)}, u32[]{:S(2)}) %collective-permute-start.23) | collective-permute-done | bytes 69664 | tf_op jit(solution)/shard_map/ppermute | solution.py:621
  108.5 0.6 last_sums.1
  109.1 0.6 collective-permute-start.24
  109.7 2.1 %collective-permute-start.25 = (bf16[144,128]{1,0:T(8,128)(2,1)S(1)}, bf16[144,128]{1,0:T(8,128)(2,1)S(1)}, u32[]{:S(2)}, u32[]{:S(2)}) collective-permute-start(bf16[144,128]{1,0:T(8,128)(2,1)S(1)} %get-tuple-element.38), channel_id=1, source_target_pairs={{0,4},{4,0},{8,12},{12,8},{1,5},{5,1},{9,13},{13,9},{2,6},{6,2},{1... | collective-permute-start | bytes 110600 | tf_op jit(solution)/shard_map/ppermute | solution.py:631
  112.0 1.5 %collective-permute-done.26.by_both = bf16[144,128]{1,0:T(8,128)(2,1)S(1)} collective-permute-done((bf16[144,128]{1,0:T(8,128)(2,1)S(1)}, bf16[144,128]{1,0:T(8,128)(2,1)S(1)}, u32[]{:S(2)}, u32[]{:S(2)}) %collective-permute-start.26) | collective-permute-done | bytes 36896 | tf_op jit(solution)/shard_map/ppermute | solution.py:631
  113.9 3.0 %collective-permute-start.27 = (f32[8,128]{1,0:T(8,128)S(1)}, f32[8,128]{1,0:T(8,128)S(1)}, u32[]{:S(2)}, u32[]{:S(2)}) collective-permute-start(f32[8,128]{1,0:T(8,128)S(1)} %last_dots.1.dots), channel_id=1, source_target_pairs={{0,1},{1,0},{2,3},{3,2},{4,5},{5,4},{6,7},{7,6},{8,9},{9,8},{10,11... | collective-permute-start | bytes 12296 | tf_op jit(solution)/shard_map/ppermute | solution.py:640
  116.9 1.3 %last_rows.1 = f32[3,4,64,256]{3,2,1,0:T(8,128)} custom-call(s32[44]{0:T(128)S(1)} %concatenate.8.meta, f32[2,64,128]{2,1,0:T(8,128)S(1)} %get-tuple-element.36.own, bf16[144,128]{1,0:T(8,128)(2,1)S(1)} %collective-permute-done.24.by_env, bf16[144,128]{1,0:T(8,128)(2,1)S(1)} %collective-permute-done.25.by_term, ...), custom_call_target="tpu_custom_call", output_to_operand_aliasing={{}: (5, {})} | custom-call | tf_op jit(solution)/shard_map/last_rows/pallas_call | solution.py:641
  118.2 0.6 subspace.1
  (51 shorter events, 3.4 us)
Async XLA Ops:
  0.6 4.9 %copy-start = (f32[4,256,256]{2,1,0:T(8,128)S(1)}, f32[4,256,256]{2,1,0:T(8,128)}, u32[]{:S(2)}) copy-start(f32[4,256,256]{2,1,0:T(8,128)} %pre.1) | copy-start | bytes 3145732
  3.3 26.5 %copy-start.4 = (bf16[4,256,256]{2,1,0:T(8,128)(2,1)S(1)}, bf16[4,256,256]{2,1,0:T(8,128)(2,1)}, u32[]{:S(2)}) copy-start(bf16[4,256,256]{2,1,0:T(8,128)(2,1)} %psi.1) | copy-start | bytes 1572868
  3.3 29.5 %copy-start.9 = (s32[8,4]{0,1:T(4,128)S(1)}, s32[8,4]{0,1:T(4,128)}, u32[]{:S(2)}) copy-start(s32[8,4]{0,1:T(4,128)} %param.9) | copy-start | bytes 388
  3.3 29.6 %copy-start.8 = (s32[8]{0:T(128)S(1)}, s32[8]{0:T(128)}, u32[]{:S(2)}) copy-start(s32[8]{0:T(128)} %param.10) | copy-start | bytes 100
  3.4 25.4 %collective-permute-start.5 = (bf16[8,2,128,256]{3,2,1,0:T(8,128)(2,1)}, bf16[8,2,128,256]{3,2,1,0:T(8,128)(2,1)}, u32[]{:S(2)}, u32[]{:S(2)}) collective-permute-start(bf16[8,2,128,256]{3,2,1,0:T(8,128)(2,1)} %get-tuple-element.27), channel_id=1, source_target_pairs={{0,4},{4,0},{8,12},{12,8},{1,5},{5,1},{9,13},{13,9},{2,6},{6,2},{1... | collective-permute-start | bytes 3145736 | tf_op jit(solution)/shard_map/ppermute | solution.py:476
  5.5 29.6 %collective-permute-start.1 = (f32[4,256,256]{2,1,0:T(8,128)S(1)}, f32[4,256,256]{2,1,0:T(8,128)S(1)}, u32[]{:S(2)}, u32[]{:S(2)}) collective-permute-start(f32[4,256,256]{2,1,0:T(8,128)S(1)} %copy-done), channel_id=1, source_target_pairs={{0,1},{1,0},{2,3},{3,2},{4,5},{5,4},{6,7},{7,6},{8,9},{9,8},{10,11... | collective-permute-start | bytes 3145736 | tf_op jit(solution)/shard_map/ppermute | solution.py:475
  6.5 29.6 %collective-permute-start.2 = (bf16[8,2,128,256]{3,2,1,0:T(8,128)(2,1)}, bf16[8,2,128,256]{3,2,1,0:T(8,128)(2,1)}, u32[]{:S(2)}, u32[]{:S(2)}) collective-permute-start(bf16[8,2,128,256]{3,2,1,0:T(8,128)(2,1)} %get-tuple-element.22), channel_id=1, source_target_pairs={{0,2},{2,0},{1,3},{3,1},{4,6},{6,4},{5,7},{7,5},{8,10},{10,8},{9,1... | collective-permute-start | bytes 3145736 | tf_op jit(solution)/shard_map/ppermute | solution.py:477
  10.0 41.6 %collective-permute-start.4 = (bf16[8,2,128,256]{3,2,1,0:T(8,128)(2,1)}, bf16[8,2,128,256]{3,2,1,0:T(8,128)(2,1)}, u32[]{:S(2)}, u32[]{:S(2)}) collective-permute-start(bf16[8,2,128,256]{3,2,1,0:T(8,128)(2,1)} %sectors_to_send.3), channel_id=1, source_target_pairs={{0,4},{4,0},{8,12},{12,8},{1,5},{5,1},{9,13},{13,9},{2,6},{6,2},{1... | collective-permute-start | bytes 3145736 | tf_op jit(solution)/shard_map/ppermute | solution.py:478
  28.7 25.5 %collective-permute-start.6 = (bf16[8,2,128,256]{3,2,1,0:T(8,128)(2,1)}, bf16[8,2,128,256]{3,2,1,0:T(8,128)(2,1)}, u32[]{:S(2)}, u32[]{:S(2)}) collective-permute-start(bf16[8,2,128,256]{3,2,1,0:T(8,128)(2,1)} %collective-permute-done.5.near_h.refs_15_.refs_17_), channel_id=1, source_target_pairs={{0,2},{2,0},{1,3},{3,1},{4,6},{6,4},{5,7},{7,5},{8,10},{10,8},{9,1... | collective-permute-start | bytes 3145736 | tf_op jit(solution)/shard_map/ppermute | solution.py:479
  29.8 4.5 %collective-permute-start = (bf16[4,256,256]{2,1,0:T(8,128)(2,1)S(1)}, bf16[4,256,256]{2,1,0:T(8,128)(2,1)S(1)}, u32[]{:S(2)}, u32[]{:S(2)}) collective-permute-start(bf16[4,256,256]{2,1,0:T(8,128)(2,1)S(1)} %copy-done.4), channel_id=1, source_target_pairs={{0,1},{1,0},{2,3},{3,2},{4,5},{5,4},{6,7},{7,6},{8,9},{9,8},{10,11... | collective-permute-start | bytes 1572872 | tf_op jit(solution)/shard_map/ppermute | solution.py:475
  34.3 0.8 copy-start.6
  35.1 1.0 copy-start.2
  36.1 1.2 %copy-start.1 = (f32[4,256,256]{2,1,0:T(8,128)S(1)}, f32[4,256,256]{2,1,0:T(8,128)}, u32[]{:S(2)}) copy-start(f32[4,256,256]{2,1,0:T(8,128)} %pre.1) | copy-start | bytes 3145732
  37.3 1.2 %copy-start.3 = (f32[4,256,256]{2,1,0:T(8,128)S(1)}, f32[4,256,256]{2,1,0:T(8,128)}, u32[]{:S(2)}) copy-start(f32[4,256,256]{2,1,0:T(8,128)} %copy-done.2) | copy-start | bytes 3145732
  38.6 1.0 copy-start.5
  39.6 1.0 copy-start.7
  44.3 7.0 %collective-permute-start.3 = (s32[8,4]{0,1:T(4,128)S(1)}, s32[8,4]{0,1:T(4,128)S(1)}, u32[]{:S(2)}, u32[]{:S(2)}) collective-permute-start(s32[8,4]{0,1:T(4,128)S(1)} %copy-done.9), channel_id=1, source_target_pairs={{0,4},{4,0},{8,12},{12,8},{1,5},{5,1},{9,13},{13,9},{2,6},{6,2},{1... | collective-permute-start | bytes 392 | tf_op jit(solution)/shard_map/ppermute | solution.py:530
  56.2 5.8 %collective-permute-start.7 = (bf16[2,128,256]{2,1,0:T(8,128)(2,1)S(1)}, bf16[2,128,256]{2,1,0:T(8,128)(2,1)S(1)}, u32[]{:S(2)}, u32[]{:S(2)}) collective-permute-start(bf16[2,128,256]{2,1,0:T(8,128)(2,1)S(1)} %first_sigma_far_rows.1), channel_id=1, source_target_pairs={{0,12},{4,8},{8,4},{12,0},{1,13},{5,9},{9,5},{13,1},{2,14},{6,10},... | collective-permute-start | bytes 393224 | tf_op jit(solution)/shard_map/ppermute | solution.py:562
  62.1 6.1 %collective-permute-start.10 = (bf16[2,128,256]{2,1,0:T(8,128)(2,1)S(1)}, bf16[2,128,256]{2,1,0:T(8,128)(2,1)S(1)}, u32[]{:S(2)}, u32[]{:S(2)}) collective-permute-start(bf16[2,128,256]{2,1,0:T(8,128)(2,1)S(1)} %select_convert_fusion.1.refs_0_), channel_id=1, source_target_pairs={{0,6},{2,4},{4,2},{6,0},{8,14},{10,12},{12,10},{14,8},{1,7},{3,5},... | collective-permute-start | bytes 393224 | tf_op jit(solution)/shard_map/ppermute | solution.py:564
  65.8 6.1 %collective-permute-start.9 = (bf16[2,128,256]{2,1,0:T(8,128)(2,1)S(1)}, bf16[2,128,256]{2,1,0:T(8,128)(2,1)S(1)}, u32[]{:S(2)}, u32[]{:S(2)}) collective-permute-start(bf16[2,128,256]{2,1,0:T(8,128)(2,1)S(1)} %select_convert_fusion.1.refs_0_), channel_id=1, source_target_pairs={{0,2},{2,0},{1,3},{3,1},{4,6},{6,4},{5,7},{7,5},{8,10},{10,8},{9,1... | collective-permute-start | bytes 393224 | tf_op jit(solution)/shard_map/ppermute | solution.py:564
  65.9 7.2 %collective-permute-start.8 = (bf16[2,128,256]{2,1,0:T(8,128)(2,1)S(1)}, bf16[2,128,256]{2,1,0:T(8,128)(2,1)S(1)}, u32[]{:S(2)}, u32[]{:S(2)}) collective-permute-start(bf16[2,128,256]{2,1,0:T(8,128)(2,1)S(1)} %select_convert_fusion.1.refs_0_), channel_id=1, source_target_pairs={{0,4},{4,0},{8,12},{12,8},{1,5},{5,1},{9,13},{13,9},{2,6},{6,2},{1... | collective-permute-start | bytes 393224 | tf_op jit(solution)/shard_map/ppermute | solution.py:564
  66.1 7.1 %collective-permute-start.11 = (bf16[2,128,256]{2,1,0:T(8,128)(2,1)S(1)}, bf16[2,128,256]{2,1,0:T(8,128)(2,1)S(1)}, u32[]{:S(2)}, u32[]{:S(2)}) collective-permute-start(bf16[2,128,256]{2,1,0:T(8,128)(2,1)S(1)} %select_convert_fusion.1.refs_0_), channel_id=1, source_target_pairs={{0,1},{1,0},{2,3},{3,2},{4,5},{5,4},{6,7},{7,6},{8,9},{9,8},{10,11... | collective-permute-start | bytes 393224 | tf_op jit(solution)/shard_map/ppermute | solution.py:565
  68.1 5.1 %collective-permute-start.14 = (bf16[2,128,256]{2,1,0:T(8,128)(2,1)S(1)}, bf16[2,128,256]{2,1,0:T(8,128)(2,1)S(1)}, u32[]{:S(2)}, u32[]{:S(2)}) collective-permute-start(bf16[2,128,256]{2,1,0:T(8,128)(2,1)S(1)} %collective-permute-done.10.refs_3_), channel_id=1, source_target_pairs={{0,1},{1,0},{2,3},{3,2},{4,5},{5,4},{6,7},{7,6},{8,9},{9,8},{10,11... | collective-permute-start | bytes 393224 | tf_op jit(solution)/shard_map/ppermute | solution.py:565
  71.9 2.2 %collective-permute-start.13 = (bf16[2,128,256]{2,1,0:T(8,128)(2,1)S(1)}, bf16[2,128,256]{2,1,0:T(8,128)(2,1)S(1)}, u32[]{:S(2)}, u32[]{:S(2)}) collective-permute-start(bf16[2,128,256]{2,1,0:T(8,128)(2,1)S(1)} %collective-permute-done.9.refs_2_), channel_id=1, source_target_pairs={{0,1},{1,0},{2,3},{3,2},{4,5},{5,4},{6,7},{7,6},{8,9},{9,8},{10,11... | collective-permute-start | bytes 393224 | tf_op jit(solution)/shard_map/ppermute | solution.py:565
  73.1 1.3 %collective-permute-start.12 = (bf16[2,128,256]{2,1,0:T(8,128)(2,1)S(1)}, bf16[2,128,256]{2,1,0:T(8,128)(2,1)S(1)}, u32[]{:S(2)}, u32[]{:S(2)}) collective-permute-start(bf16[2,128,256]{2,1,0:T(8,128)(2,1)S(1)} %collective-permute-done.8.refs_1_), channel_id=1, source_target_pairs={{0,1},{1,0},{2,3},{3,2},{4,5},{5,4},{6,7},{7,6},{8,9},{9,8},{10,11... | collective-permute-start | bytes 393224 | tf_op jit(solution)/shard_map/ppermute | solution.py:565
  79.3 6.8 %collective-permute-start.15 = (bf16[2,128,256]{2,1,0:T(8,128)(2,1)S(1)}, bf16[2,128,256]{2,1,0:T(8,128)(2,1)S(1)}, u32[]{:S(2)}, u32[]{:S(2)}) collective-permute-start(bf16[2,128,256]{2,1,0:T(8,128)(2,1)S(1)} %get-tuple-element.31), channel_id=1, source_target_pairs={{0,12},{4,8},{8,4},{12,0},{1,13},{5,9},{9,5},{13,1},{2,14},{6,10},... | collective-permute-start | bytes 393224 | tf_op jit(solution)/shard_map/ppermute | solution.py:562
  86.2 5.3 %collective-permute-start.18 = (bf16[2,128,256]{2,1,0:T(8,128)(2,1)S(1)}, bf16[2,128,256]{2,1,0:T(8,128)(2,1)S(1)}, u32[]{:S(2)}, u32[]{:S(2)}) collective-permute-start(bf16[2,128,256]{2,1,0:T(8,128)(2,1)S(1)} %select_convert_fusion.refs_0_), channel_id=1, source_target_pairs={{0,6},{2,4},{4,2},{6,0},{8,14},{10,12},{12,10},{14,8},{1,7},{3,5},... | collective-permute-start | bytes 393224 | tf_op jit(solution)/shard_map/ppermute | solution.py:564
  88.8 6.5 %collective-permute-start.17 = (bf16[2,128,256]{2,1,0:T(8,128)(2,1)S(1)}, bf16[2,128,256]{2,1,0:T(8,128)(2,1)S(1)}, u32[]{:S(2)}, u32[]{:S(2)}) collective-permute-start(bf16[2,128,256]{2,1,0:T(8,128)(2,1)S(1)} %select_convert_fusion.refs_0_), channel_id=1, source_target_pairs={{0,2},{2,0},{1,3},{3,1},{4,6},{6,4},{5,7},{7,5},{8,10},{10,8},{9,1... | collective-permute-start | bytes 393224 | tf_op jit(solution)/shard_map/ppermute | solution.py:564
  89.3 6.8 %collective-permute-start.16 = (bf16[2,128,256]{2,1,0:T(8,128)(2,1)S(1)}, bf16[2,128,256]{2,1,0:T(8,128)(2,1)S(1)}, u32[]{:S(2)}, u32[]{:S(2)}) collective-permute-start(bf16[2,128,256]{2,1,0:T(8,128)(2,1)S(1)} %select_convert_fusion.refs_0_), channel_id=1, source_target_pairs={{0,4},{4,0},{8,12},{12,8},{1,5},{5,1},{9,13},{13,9},{2,6},{6,2},{1... | collective-permute-start | bytes 393224 | tf_op jit(solution)/shard_map/ppermute | solution.py:564
  89.3 6.8 %collective-permute-start.19 = (bf16[2,128,256]{2,1,0:T(8,128)(2,1)S(1)}, bf16[2,128,256]{2,1,0:T(8,128)(2,1)S(1)}, u32[]{:S(2)}, u32[]{:S(2)}) collective-permute-start(bf16[2,128,256]{2,1,0:T(8,128)(2,1)S(1)} %select_convert_fusion.refs_0_), channel_id=1, source_target_pairs={{0,1},{1,0},{2,3},{3,2},{4,5},{5,4},{6,7},{7,6},{8,9},{9,8},{10,11... | collective-permute-start | bytes 393224 | tf_op jit(solution)/shard_map/ppermute | solution.py:565
  91.5 4.6 %collective-permute-start.22 = (bf16[2,128,256]{2,1,0:T(8,128)(2,1)S(1)}, bf16[2,128,256]{2,1,0:T(8,128)(2,1)S(1)}, u32[]{:S(2)}, u32[]{:S(2)}) collective-permute-start(bf16[2,128,256]{2,1,0:T(8,128)(2,1)S(1)} %collective-permute-done.18.refs_3_), channel_id=1, source_target_pairs={{0,1},{1,0},{2,3},{3,2},{4,5},{5,4},{6,7},{7,6},{8,9},{9,8},{10,11... | collective-permute-start | bytes 393224 | tf_op jit(solution)/shard_map/ppermute | solution.py:565
  95.3 1.7 %collective-permute-start.21 = (bf16[2,128,256]{2,1,0:T(8,128)(2,1)S(1)}, bf16[2,128,256]{2,1,0:T(8,128)(2,1)S(1)}, u32[]{:S(2)}, u32[]{:S(2)}) collective-permute-start(bf16[2,128,256]{2,1,0:T(8,128)(2,1)S(1)} %collective-permute-done.17.refs_2_), channel_id=1, source_target_pairs={{0,1},{1,0},{2,3},{3,2},{4,5},{5,4},{6,7},{7,6},{8,9},{9,8},{10,11... | collective-permute-start | bytes 393224 | tf_op jit(solution)/shard_map/ppermute | solution.py:565
  96.1 1.3 %collective-permute-start.20 = (bf16[2,128,256]{2,1,0:T(8,128)(2,1)S(1)}, bf16[2,128,256]{2,1,0:T(8,128)(2,1)S(1)}, u32[]{:S(2)}, u32[]{:S(2)}) collective-permute-start(bf16[2,128,256]{2,1,0:T(8,128)(2,1)S(1)} %collective-permute-done.16.refs_1_), channel_id=1, source_target_pairs={{0,1},{1,0},{2,3},{3,2},{4,5},{5,4},{6,7},{7,6},{8,9},{9,8},{10,11... | collective-permute-start | bytes 393224 | tf_op jit(solution)/shard_map/ppermute | solution.py:565
  103.0 5.5 %collective-permute-start.23 = (bf16[272,128]{1,0:T(8,128)(2,1)S(1)}, bf16[272,128]{1,0:T(8,128)(2,1)S(1)}, u32[]{:S(2)}, u32[]{:S(2)}) collective-permute-start(bf16[272,128]{1,0:T(8,128)(2,1)S(1)} %get-tuple-element.35), channel_id=1, source_target_pairs={{0,12},{4,8},{8,4},{12,0},{1,13},{5,9},{9,5},{13,1},{2,14},{6,10},... | collective-permute-start | bytes 208904 | tf_op jit(solution)/shard_map/ppermute | solution.py:621
  109.1 2.9 %collective-permute-start.24 = (bf16[144,128]{1,0:T(8,128)(2,1)S(1)}, bf16[144,128]{1,0:T(8,128)(2,1)S(1)}, u32[]{:S(2)}, u32[]{:S(2)}) collective-permute-start(bf16[144,128]{1,0:T(8,128)(2,1)S(1)} %get-tuple-element.37.own), channel_id=1, source_target_pairs={{0,2},{2,0},{1,3},{3,1},{4,6},{6,4},{5,7},{7,5},{8,10},{10,8},{9,1... | collective-permute-start | bytes 110600 | tf_op jit(solution)/shard_map/ppermute | solution.py:631
  109.7 3.7 %collective-permute-start.26 = (bf16[144,128]{1,0:T(8,128)(2,1)S(1)}, bf16[144,128]{1,0:T(8,128)(2,1)S(1)}, u32[]{:S(2)}, u32[]{:S(2)}) collective-permute-start(bf16[144,128]{1,0:T(8,128)(2,1)S(1)} %get-tuple-element.38), channel_id=1, source_target_pairs={{0,6},{2,4},{4,2},{6,0},{8,14},{10,12},{12,10},{14,8},{1,7},{3,5},... | collective-permute-start | bytes 110600 | tf_op jit(solution)/shard_map/ppermute | solution.py:631
  109.7 4.1 %collective-permute-start.25 = (bf16[144,128]{1,0:T(8,128)(2,1)S(1)}, bf16[144,128]{1,0:T(8,128)(2,1)S(1)}, u32[]{:S(2)}, u32[]{:S(2)}) collective-permute-start(bf16[144,128]{1,0:T(8,128)(2,1)S(1)} %get-tuple-element.38), channel_id=1, source_target_pairs={{0,4},{4,0},{8,12},{12,8},{1,5},{5,1},{9,13},{13,9},{2,6},{6,2},{1... | collective-permute-start | bytes 110600 | tf_op jit(solution)/shard_map/ppermute | solution.py:631
  113.9 4.3 %collective-permute-start.27 = (f32[8,128]{1,0:T(8,128)S(1)}, f32[8,128]{1,0:T(8,128)S(1)}, u32[]{:S(2)}, u32[]{:S(2)}) collective-permute-start(f32[8,128]{1,0:T(8,128)S(1)} %last_dots.1.dots), channel_id=1, source_target_pairs={{0,1},{1,0},{2,3},{3,2},{4,5},{5,4},{6,7},{7,6},{8,9},{9,8},{10,11... | collective-permute-start | bytes 12296 | tf_op jit(solution)/shard_map/ppermute | solution.py:640

commit v7 on v6

--- a/solution.py
+++ b/solution.py
@@ -421,33 +421,28 @@
     return functools.partial(lax.ppermute, axis_name=axis, perm=[(i, i ^ s) for i in range(n)])
 
 
-def _cut_kernel(held, which, env_h, *refs):
-    count = (len(refs) - 1) // 2
-    outs, bufs, sem = refs[:count], refs[count:-1], refs[-1]
-    loads, saves = [], []
-    for i, (out, buf) in enumerate(zip(outs, bufs)):
-        at = (1 - which[0] if i == 0 else which[0]) * held
-        loads.append(pltpu.make_async_copy(env_h.at[:, pl.ds(at, held)], buf, sem.at[0, i]))
-        saves.append(pltpu.make_async_copy(buf, out, sem.at[1, i]))
-        loads[-1].start()
-    for load, save in zip(loads, saves):
-        load.wait()
-        save.start()
-    for save in saves:
-        save.wait()
-
-
-def _cut(env, mine, held, count):
+def _cut_kernel(held, which, env_h, out, sem):
+    half = env_h.shape[0] // 2
+    moves = []
+    for i in range(2):
+        t = pl.ds(i * half, half)
+        moves.append(pltpu.make_async_copy(env_h.at[t, pl.ds(which[0] * held, held)], out.at[t], sem.at[i]))
+        moves[-1].start()
+    for c in moves:
+        c.wait()
+
+
+def _cut(env, which, held):
     shape = (env.shape[0], held, *env.shape[2:])
     return pl.pallas_call(
         functools.partial(_cut_kernel, held),
-        out_shape=tuple(HB(shape, BF16) for _ in range(count)),
+        out_shape=VM(shape, BF16),
         in_specs=_specs(SM, HB),
-        out_specs=tuple(_specs(*[HB] * count)),
-        scratch_shapes=[pltpu.VMEM(shape, BF16) for _ in range(count)] + [pltpu.SemaphoreType.DMA((2, count))],
+        out_specs=_specs(VM)[0],
+        scratch_shapes=[pltpu.SemaphoreType.DMA((2,))],
         compiler_params=pltpu.CompilerParams(vmem_limit_bytes=VMEM_LIMIT),
         name="sectors_to_send",
-    )(mine.astype(jnp.int32).reshape(1), *_hbm(env))
+    )(which.astype(jnp.int32).reshape(1), *_hbm(env))
 
 
 def _on_device(n_env, n_term, n_blk, psi, left_env, right_env, pairing, sector_dims, precond):
@@ -470,8 +465,9 @@
     group = lambda x, which: lax.dynamic_slice_in_dim(x, which * held, held, 1)
 
     if direct:
-        to_next, to_env = _cut(left_env, mine, held, 2)
-        (right_to_next,) = _cut(right_env, mine, held, 1)
+        to_next = _cut(left_env, 1 - mine, held)
+        to_env = _cut(left_env, lax.optimization_barrier((mine, to_next))[0], held)
+        right_to_next = _cut(right_env, lax.optimization_barrier((1 - mine, to_env))[0], held)
         psi_o, pre_o = other_blk(psi), other_blk(precond)
         next_left = next_term(to_next)
         far_left = other_env(to_env)

time: 119 us -> 117 us (0.983)
  local copies, waits for them, and re-layouts: 6.9 us -> 4.04 us
    unnamed x20 -> x12, local copies, waits for them, and re-layouts: 6.33 us -> 3.46 us
    ppermute x1, waiting for transfers between devices: 5.64 us -> 7.5 us  [_on_device(): next_pairing = next_term(lax.optimization_barrier((pairing, partial))[0])]
    ppermute x1, waiting for transfers between devices: 18.6 us -> 16.8 us  [_on_device(): next_left = next_term(to_next)]
    pallas_call x2 -> x3, Pallas kernels: 4.9 us -> 4.67 us  [_cut(): pl.pallas_call(functools.partial(_cut_kernel, held), out_shape=VM(shape,...]
  transfers between devices with their start and end apart: 28 -> 28, of which waited for: 16 -> 16; matrix products, arithmetic and copies ran while one was open for 0% -> 0% of each run, Pallas kernels for 8% -> 10%
where the time goes in v7:
time: 117 us
  waiting for transfers between devices  43.3 us (37%)
  starting transfers between devices  42.2 us (36%)
  Pallas kernels  26.5 us (23%)
  local copies, waits for them, and re-layouts  4.04 us (3%)
    ppermute x1, waiting for transfers between devices, _on_device(): next_left = next_term(to_next)  16.8 us
    ppermute x8, starting transfers between devices, combine(): there = [other_blk(x) for x in here]  11.1 us
    pallas_call x2, Pallas kernels, _on_device(): pl.pallas_call(functools.partial(_step_kernel, dict(cfg, n_out=len(outs))...  10.4 us
    ppermute x1, waiting for transfers between devices, _on_device(): next_pairing = next_term(lax.optimization_barrier((pairing, partial))[0])  7.5 us
    ppermute x6, starting transfers between devices, combine(): here = [shard, next_term(shard), other_env(shard), corners(shard)]  7.18 us
    ppermute x2, waiting for transfers between devices, combine(): total = partial.astype(F32) + far_term(partial).astype(F32)  7.04 us
    ppermute x2, starting transfers between devices, combine(): total = partial.astype(F32) + far_term(partial).astype(F32)  5.5 us
    pallas_call x3, Pallas kernels, _cut(): pl.pallas_call(functools.partial(_cut_kernel, held), out_shape=VM(shape,...  4.67 us
  transfers between devices with their start and end apart: 28, of which 16 were waited for; matrix products, arithmetic and copies ran while one was open for 0% of the time, Pallas kernels for 10%

profile of v7, /device:TPU:1, one launch (start us, length us, event | category | flops | bytes accessed | tf_op | source)
XLA Modules:
  0.0 117.1 jit_solution(8253290942044454541)
XLA Ops:
  0.6 1.2 %sectors_to_send.3 = bf16[8,2,128,256]{3,2,1,0:T(8,128)(2,1)S(1)} custom-call(s32[1]{0:T(128)} %bitcast.4.which, bf16[8,4,128,256]{3,2,1,0:T(8,128)(2,1)} %refs_14_.1), custom_call_target="tpu_custom_call" | custom-call | tf_op jit(solution)/shard_map/sectors_to_send/pallas_call | solution.py:437
  1.9 2.2 %collective-permute-start.5 = (bf16[8,2,128,256]{3,2,1,0:T(8,128)(2,1)S(1)}, bf16[8,2,128,256]{3,2,1,0:T(8,128)(2,1)}, u32[]{:S(2)}, u32[]{:S(2)}) collective-permute-start(bf16[8,2,128,256]{3,2,1,0:T(8,128)(2,1)S(1)} %sectors_to_send.3), channel_id=1, source_target_pairs={{0,4},{4,0},{8,12},{12,8},{1,5},{5,1},{9,13},{13,9},{2,6},{6,2},{1... | collective-permute-start | bytes 3145736 | tf_op jit(solution)/shard_map/ppermute | solution.py:472
  4.1 1.2 %sectors_to_send.4 = bf16[8,2,128,256]{3,2,1,0:T(8,128)(2,1)S(1)} custom-call(s32[1]{0:T(128)} %bitcast.5.which, bf16[8,4,128,256]{3,2,1,0:T(8,128)(2,1)} %refs_14_.1), custom_call_target="tpu_custom_call" | custom-call | tf_op jit(solution)/shard_map/sectors_to_send/pallas_call | solution.py:437
  5.3 1.3 %collective-permute-start.2 = (bf16[8,2,128,256]{3,2,1,0:T(8,128)(2,1)S(1)}, bf16[8,2,128,256]{3,2,1,0:T(8,128)(2,1)}, u32[]{:S(2)}, u32[]{:S(2)}) collective-permute-start(bf16[8,2,128,256]{3,2,1,0:T(8,128)(2,1)S(1)} %sectors_to_send.4), channel_id=1, source_target_pairs={{0,2},{2,0},{1,3},{3,1},{4,6},{6,4},{5,7},{7,5},{8,10},{10,8},{9,1... | collective-permute-start | bytes 3145736 | tf_op jit(solution)/shard_map/ppermute | solution.py:473
  6.6 1.2 %collective-permute-start.1 = (f32[4,256,256]{2,1,0:T(8,128)S(1)}, f32[4,256,256]{2,1,0:T(8,128)S(1)}, u32[]{:S(2)}, u32[]{:S(2)}) collective-permute-start(f32[4,256,256]{2,1,0:T(8,128)S(1)} %copy-done), channel_id=1, source_target_pairs={{0,1},{1,0},{2,3},{3,2},{4,5},{5,4},{6,7},{7,6},{8,9},{9,8},{10,11... | collective-permute-start | bytes 3145736 | tf_op jit(solution)/shard_map/ppermute | solution.py:471
  7.8 2.2 %sectors_to_send.5 = bf16[8,2,128,256]{3,2,1,0:T(8,128)(2,1)} custom-call(s32[1]{0:T(128)} %bitcast.6.which, bf16[8,4,128,256]{3,2,1,0:T(8,128)(2,1)} %refs_13_.1), custom_call_target="tpu_custom_call" | custom-call | tf_op jit(solution)/shard_map/sectors_to_send/pallas_call | solution.py:437
  10.3 16.8 %collective-permute-done.5.near_h.refs_15_.refs_17_ = bf16[8,2,128,256]{3,2,1,0:T(8,128)(2,1)} collective-permute-done((bf16[8,2,128,256]{3,2,1,0:T(8,128)(2,1)S(1)}, bf16[8,2,128,256]{3,2,1,0:T(8,128)(2,1)}, u32[]{:S(2)}, u32[]{:S(2)}) %collective-permute-start.5) | collective-permute-done | bytes 1048608 | tf_op jit(solution)/shard_map/ppermute | solution.py:472
  27.1 1.1 collective-permute-start.6
  28.1 3.0 %collective-permute-start = (bf16[4,256,256]{2,1,0:T(8,128)(2,1)}, bf16[4,256,256]{2,1,0:T(8,128)(2,1)}, u32[]{:S(2)}, u32[]{:S(2)}) collective-permute-start(bf16[4,256,256]{2,1,0:T(8,128)(2,1)} %psi.1), channel_id=1, source_target_pairs={{0,1},{1,0},{2,3},{3,2},{4,5},{5,4},{6,7},{7,6},{8,9},{9,8},{10,11... | collective-permute-start | bytes 1572872 | tf_op jit(solution)/shard_map/ppermute | solution.py:471
  31.4 1.6 %collective-permute-done.psi_o = bf16[4,256,256]{2,1,0:T(8,128)(2,1)} collective-permute-done((bf16[4,256,256]{2,1,0:T(8,128)(2,1)}, bf16[4,256,256]{2,1,0:T(8,128)(2,1)}, u32[]{:S(2)}, u32[]{:S(2)}) %collective-permute-start) | collective-permute-done | bytes 524320 | tf_op jit(solution)/shard_map/ppermute | solution.py:471
  33.0 1.0 copy-done.2
  34.0 1.2 %copy-done.1 = f32[4,256,256]{2,1,0:T(8,128)S(1)} copy-done((f32[4,256,256]{2,1,0:T(8,128)S(1)}, f32[4,256,256]{2,1,0:T(8,128)}, u32[]{:S(2)}) %copy-start.1) | copy-done | bytes 1048600
  35.2 1.2 %copy-done.3 = f32[4,256,256]{2,1,0:T(8,128)S(1)} copy-done((f32[4,256,256]{2,1,0:T(8,128)S(1)}, f32[4,256,256]{2,1,0:T(8,128)}, u32[]{:S(2)}) %copy-start.3) | copy-done | bytes 1048600
  36.4 4.3 %start_vector.1 = (bf16[8,256,256]{2,1,0:T(8,128)(2,1)S(1)}, f32[8,256,256]{2,1,0:T(8,128)S(1)}, f32[8,128]{1,0:T(8,128)S(1)}, f32[2,128,256]{2,1,0:T(8,128)S(1)}) custom-call(s32[28]{0:T(128)S(1)} %concatenate.7.meta, bf16[4,256,256]{2,1,0:T(8,128)(2,1)} %psi.1, bf16[4,256,256]{2,1,0:T(8,128)(2,1)} %collective-permute-done.psi_o, ...), custom_call_target="tpu_custom_call" | custom-call | tf_op jit(solution)/shard_map/start_vector/pallas_call | solution.py:509
  40.7 1.4 %collective-permute-start.3 = (s32[8,4]{0,1:T(4,128)S(1)}, s32[8,4]{0,1:T(4,128)S(1)}, u32[]{:S(2)}, u32[]{:S(2)}) collective-permute-start(s32[8,4]{0,1:T(4,128)S(1)} %copy-done.5), channel_id=1, source_target_pairs={{0,4},{4,0},{8,12},{12,8},{1,5},{5,1},{9,13},{13,9},{2,6},{6,2},{1... | collective-permute-start | bytes 392 | tf_op jit(solution)/shard_map/ppermute | solution.py:526
  42.1 7.5 %collective-permute-done.3 = s32[8,4]{0,1:T(4,128)S(1)} collective-permute-done((s32[8,4]{0,1:T(4,128)S(1)}, s32[8,4]{0,1:T(4,128)S(1)}, u32[]{:S(2)}, u32[]{:S(2)}) %collective-permute-start.3) | collective-permute-done | bytes 160 | tf_op jit(solution)/shard_map/ppermute | solution.py:526
  49.8 2.7 %first_sigma_next_terms.1 = (f32[2,128,256]{2,1,0:T(8,128)S(1)}, bf16[8,2,128,128]{3,2,1,0:T(8,128)(2,1)S(1)}) custom-call(s32[44]{0:T(128)S(1)} %concatenate.8.meta, f32[2,128,256]{2,1,0:T(8,128)S(1)} %get-tuple-element.23.acc, bf16[8,256,256]{2,1,0:T(8,128)(2,1)S(1)} %get-tuple-element.25.start.refs_8_, f32[8,128]{1,0:T(8,128)S(1)} %get-tuple-element.26.scale_ref.refs_9_, ...), custom_call_target="tpu_custom_call" | custom-call | tf_op jit(solution)/shard_map/first_sigma_next_terms/pallas_call | solution.py:529
  52.6 1.9 %first_sigma_far_rows.1 = bf16[2,128,256]{2,1,0:T(8,128)(2,1)S(1)} custom-call(f32[2,128,256]{2,1,0:T(8,128)S(1)} %get-tuple-element.28.acc, bf16[8,2,128,128]{3,2,1,0:T(8,128)(2,1)S(1)} %get-tuple-element.29.inner, bf16[8,2,128,256]{3,2,1,0:T(8,128)(2,1)} %collective-permute-done.6.far_h.refs_16_.refs_18_), custom_call_target="tpu_custom_call" | custom-call | tf_op jit(solution)/shard_map/first_sigma_far_rows/pallas_call | solution.py:538
  54.5 3.2 %collective-permute-start.7 = (bf16[2,128,256]{2,1,0:T(8,128)(2,1)S(1)}, bf16[2,128,256]{2,1,0:T(8,128)(2,1)S(1)}, u32[]{:S(2)}, u32[]{:S(2)}) collective-permute-start(bf16[2,128,256]{2,1,0:T(8,128)(2,1)S(1)} %first_sigma_far_rows.1), channel_id=1, source_target_pairs={{0,12},{4,8},{8,4},{12,0},{1,13},{5,9},{9,5},{13,1},{2,14},{6,10},... | collective-permute-start | bytes 393224 | tf_op jit(solution)/shard_map/ppermute | solution.py:558
  57.8 2.5 %collective-permute-done.7 = bf16[2,128,256]{2,1,0:T(8,128)(2,1)S(1)} collective-permute-done((bf16[2,128,256]{2,1,0:T(8,128)(2,1)S(1)}, bf16[2,128,256]{2,1,0:T(8,128)(2,1)S(1)}, u32[]{:S(2)}, u32[]{:S(2)}) %collective-permute-start.7) | collective-permute-done | bytes 131104 | tf_op jit(solution)/shard_map/ppermute | solution.py:558
  60.4 3.7 %collective-permute-start.10 = (bf16[2,128,256]{2,1,0:T(8,128)(2,1)S(1)}, bf16[2,128,256]{2,1,0:T(8,128)(2,1)S(1)}, u32[]{:S(2)}, u32[]{:S(2)}) collective-permute-start(bf16[2,128,256]{2,1,0:T(8,128)(2,1)S(1)} %select_convert_fusion.1.refs_0_), channel_id=1, source_target_pairs={{0,6},{2,4},{4,2},{6,0},{8,14},{10,12},{12,10},{14,8},{1,7},{3,5},... | collective-permute-start | bytes 393224 | tf_op jit(solution)/shard_map/ppermute | solution.py:560
  64.4 2.0 %collective-permute-start.11 = (bf16[2,128,256]{2,1,0:T(8,128)(2,1)S(1)}, bf16[2,128,256]{2,1,0:T(8,128)(2,1)S(1)}, u32[]{:S(2)}, u32[]{:S(2)}) collective-permute-start(bf16[2,128,256]{2,1,0:T(8,128)(2,1)S(1)} %select_convert_fusion.1.refs_0_), channel_id=1, source_target_pairs={{0,1},{1,0},{2,3},{3,2},{4,5},{5,4},{6,7},{7,6},{8,9},{9,8},{10,11... | collective-permute-start | bytes 393224 | tf_op jit(solution)/shard_map/ppermute | solution.py:561
  66.4 2.8 %collective-permute-start.14 = (bf16[2,128,256]{2,1,0:T(8,128)(2,1)S(1)}, bf16[2,128,256]{2,1,0:T(8,128)(2,1)S(1)}, u32[]{:S(2)}, u32[]{:S(2)}) collective-permute-start(bf16[2,128,256]{2,1,0:T(8,128)(2,1)S(1)} %collective-permute-done.10.refs_3_), channel_id=1, source_target_pairs={{0,1},{1,0},{2,3},{3,2},{4,5},{5,4},{6,7},{7,6},{8,9},{9,8},{10,11... | collective-permute-start | bytes 393224 | tf_op jit(solution)/shard_map/ppermute | solution.py:561
  69.2 0.9 collective-permute-done.9.refs_2_
  70.2 1.2 %collective-permute-start.13 = (bf16[2,128,256]{2,1,0:T(8,128)(2,1)S(1)}, bf16[2,128,256]{2,1,0:T(8,128)(2,1)S(1)}, u32[]{:S(2)}, u32[]{:S(2)}) collective-permute-start(bf16[2,128,256]{2,1,0:T(8,128)(2,1)S(1)} %collective-permute-done.9.refs_2_), channel_id=1, source_target_pairs={{0,1},{1,0},{2,3},{3,2},{4,5},{5,4},{6,7},{7,6},{8,9},{9,8},{10,11... | collective-permute-start | bytes 393224 | tf_op jit(solution)/shard_map/ppermute | solution.py:561
  71.6 0.8 collective-permute-done.13.refs_6_
  72.8 4.8 %vector_and_sigma_1.1 = (bf16[8,256,256]{2,1,0:T(8,128)(2,1)}, f32[8,256,256]{2,1,0:T(8,128)S(1)}, f32[8,128]{1,0:T(8,128)S(1)}, bf16[2,128,256]{2,1,0:T(8,128)(2,1)S(1)}) custom-call(s32[44]{0:T(128)S(1)} %concatenate.8.meta, bf16[2,128,256]{2,1,0:T(8,128)(2,1)S(1)} %select_convert_fusion.1.refs_0_, ...), custom_call_target="tpu_custom_call" | custom-call | tf_op jit(solution)/shard_map/vector_and_sigma_1/pallas_call | solution.py:585
  77.6 2.3 %collective-permute-start.15 = (bf16[2,128,256]{2,1,0:T(8,128)(2,1)S(1)}, bf16[2,128,256]{2,1,0:T(8,128)(2,1)S(1)}, u32[]{:S(2)}, u32[]{:S(2)}) collective-permute-start(bf16[2,128,256]{2,1,0:T(8,128)(2,1)S(1)} %get-tuple-element.31), channel_id=1, source_target_pairs={{0,12},{4,8},{8,4},{12,0},{1,13},{5,9},{9,5},{13,1},{2,14},{6,10},... | collective-permute-start | bytes 393224 | tf_op jit(solution)/shard_map/ppermute | solution.py:558
  79.8 4.6 %collective-permute-done.15 = bf16[2,128,256]{2,1,0:T(8,128)(2,1)S(1)} collective-permute-done((bf16[2,128,256]{2,1,0:T(8,128)(2,1)S(1)}, bf16[2,128,256]{2,1,0:T(8,128)(2,1)S(1)}, u32[]{:S(2)}, u32[]{:S(2)}) %collective-permute-start.15) | collective-permute-done | bytes 131104 | tf_op jit(solution)/shard_map/ppermute | solution.py:558
  84.5 2.6 %collective-permute-start.18 = (bf16[2,128,256]{2,1,0:T(8,128)(2,1)S(1)}, bf16[2,128,256]{2,1,0:T(8,128)(2,1)S(1)}, u32[]{:S(2)}, u32[]{:S(2)}) collective-permute-start(bf16[2,128,256]{2,1,0:T(8,128)(2,1)S(1)} %select_convert_fusion.refs_0_), channel_id=1, source_target_pairs={{0,6},{2,4},{4,2},{6,0},{8,14},{10,12},{12,10},{14,8},{1,7},{3,5},... | collective-permute-start | bytes 393224 | tf_op jit(solution)/shard_map/ppermute | solution.py:560
  87.1 0.5 collective-permute-start.17
  87.6 1.8 %collective-permute-start.19 = (bf16[2,128,256]{2,1,0:T(8,128)(2,1)S(1)}, bf16[2,128,256]{2,1,0:T(8,128)(2,1)S(1)}, u32[]{:S(2)}, u32[]{:S(2)}) collective-permute-start(bf16[2,128,256]{2,1,0:T(8,128)(2,1)S(1)} %select_convert_fusion.refs_0_), channel_id=1, source_target_pairs={{0,1},{1,0},{2,3},{3,2},{4,5},{5,4},{6,7},{7,6},{8,9},{9,8},{10,11... | collective-permute-start | bytes 393224 | tf_op jit(solution)/shard_map/ppermute | solution.py:561
  89.4 0.4 collective-permute-done.18.refs_3_
  89.8 2.5 %collective-permute-start.22 = (bf16[2,128,256]{2,1,0:T(8,128)(2,1)S(1)}, bf16[2,128,256]{2,1,0:T(8,128)(2,1)S(1)}, u32[]{:S(2)}, u32[]{:S(2)}) collective-permute-start(bf16[2,128,256]{2,1,0:T(8,128)(2,1)S(1)} %collective-permute-done.18.refs_3_), channel_id=1, source_target_pairs={{0,1},{1,0},{2,3},{3,2},{4,5},{5,4},{6,7},{7,6},{8,9},{9,8},{10,11... | collective-permute-start | bytes 393224 | tf_op jit(solution)/shard_map/ppermute | solution.py:561
  92.3 1.4 %collective-permute-done.17.refs_2_ = bf16[2,128,256]{2,1,0:T(8,128)(2,1)S(1)} collective-permute-done((bf16[2,128,256]{2,1,0:T(8,128)(2,1)S(1)}, bf16[2,128,256]{2,1,0:T(8,128)(2,1)S(1)}, u32[]{:S(2)}, u32[]{:S(2)}) %collective-permute-start.17) | collective-permute-done | bytes 131104 | tf_op jit(solution)/shard_map/ppermute | solution.py:560
  93.6 0.7 collective-permute-start.21
  94.4 1.0 collective-permute-done.21.refs_6_
  95.7 5.5 %vector_and_sigma_2.1 = (f32[3,4,64,256]{3,2,1,0:T(8,128)}, f32[8,128]{1,0:T(8,128)S(1)}, f32[272,128]{1,0:T(8,128)S(1)}, bf16[272,128]{1,0:T(8,128)(2,1)S(1)}) custom-call(s32[44]{0:T(128)S(1)} %concatenate.8.meta, bf16[2,128,256]{2,1,0:T(8,128)(2,1)S(1)} %select_convert_fusion.refs_0_, bf16[2,128,256]{2,1,0:T(8,128)(2,1)S(1)} %collective-permute-done.16.refs_1_, ...), custom_call_target="tpu_custom_call" | custom-call | tf_op jit(solution)/shard_map/vector_and_sigma_2/pallas_call | solution.py:585
  101.3 2.4 %collective-permute-start.23 = (bf16[272,128]{1,0:T(8,128)(2,1)S(1)}, bf16[272,128]{1,0:T(8,128)(2,1)S(1)}, u32[]{:S(2)}, u32[]{:S(2)}) collective-permute-start(bf16[272,128]{1,0:T(8,128)(2,1)S(1)} %get-tuple-element.35), channel_id=1, source_target_pairs={{0,12},{4,8},{8,4},{12,0},{1,13},{5,9},{9,5},{13,1},{2,14},{6,10},... | collective-permute-start | bytes 208904 | tf_op jit(solution)/shard_map/ppermute | solution.py:617
  103.7 3.1 %collective-permute-done.23.got = bf16[272,128]{1,0:T(8,128)(2,1)S(1)} collective-permute-done((bf16[272,128]{1,0:T(8,128)(2,1)S(1)}, bf16[272,128]{1,0:T(8,128)(2,1)S(1)}, u32[]{:S(2)}, u32[]{:S(2)}) %collective-permute-start.23) | collective-permute-done | bytes 69664 | tf_op jit(solution)/shard_map/ppermute | solution.py:617
  106.8 0.6 last_sums.1
  107.4 0.6 collective-permute-start.24
  108.0 2.1 %collective-permute-start.25 = (bf16[144,128]{1,0:T(8,128)(2,1)S(1)}, bf16[144,128]{1,0:T(8,128)(2,1)S(1)}, u32[]{:S(2)}, u32[]{:S(2)}) collective-permute-start(bf16[144,128]{1,0:T(8,128)(2,1)S(1)} %get-tuple-element.38), channel_id=1, source_target_pairs={{0,4},{4,0},{8,12},{12,8},{1,5},{5,1},{9,13},{13,9},{2,6},{6,2},{1... | collective-permute-start | bytes 110600 | tf_op jit(solution)/shard_map/ppermute | solution.py:627
  110.2 1.5 %collective-permute-done.26.by_both = bf16[144,128]{1,0:T(8,128)(2,1)S(1)} collective-permute-done((bf16[144,128]{1,0:T(8,128)(2,1)S(1)}, bf16[144,128]{1,0:T(8,128)(2,1)S(1)}, u32[]{:S(2)}, u32[]{:S(2)}) %collective-permute-start.26) | collective-permute-done | bytes 36896 | tf_op jit(solution)/shard_map/ppermute | solution.py:627
  111.7 0.4 collective-permute-done.25.by_term
  112.2 3.0 %collective-permute-start.27 = (f32[8,128]{1,0:T(8,128)S(1)}, f32[8,128]{1,0:T(8,128)S(1)}, u32[]{:S(2)}, u32[]{:S(2)}) collective-permute-start(f32[8,128]{1,0:T(8,128)S(1)} %last_dots.1.dots), channel_id=1, source_target_pairs={{0,1},{1,0},{2,3},{3,2},{4,5},{5,4},{6,7},{7,6},{8,9},{9,8},{10,11... | collective-permute-start | bytes 12296 | tf_op jit(solution)/shard_map/ppermute | solution.py:636
  115.1 1.3 %last_rows.1 = f32[3,4,64,256]{3,2,1,0:T(8,128)} custom-call(s32[44]{0:T(128)S(1)} %concatenate.8.meta, f32[2,64,128]{2,1,0:T(8,128)S(1)} %get-tuple-element.36.own, bf16[144,128]{1,0:T(8,128)(2,1)S(1)} %collective-permute-done.24.by_env, bf16[144,128]{1,0:T(8,128)(2,1)S(1)} %collective-permute-done.25.by_term, ...), custom_call_target="tpu_custom_call", output_to_operand_aliasing={{}: (5, {})} | custom-call | tf_op jit(solution)/shard_map/last_rows/pallas_call | solution.py:637
  116.4 0.6 subspace.1
  (44 shorter events, 2.5 us)
Async XLA Ops:
  1.9 4.7 %copy-start = (f32[4,256,256]{2,1,0:T(8,128)S(1)}, f32[4,256,256]{2,1,0:T(8,128)}, u32[]{:S(2)}) copy-start(f32[4,256,256]{2,1,0:T(8,128)} %pre.1) | copy-start | bytes 3145732
  1.9 25.2 %collective-permute-start.5 = (bf16[8,2,128,256]{3,2,1,0:T(8,128)(2,1)S(1)}, bf16[8,2,128,256]{3,2,1,0:T(8,128)(2,1)}, u32[]{:S(2)}, u32[]{:S(2)}) collective-permute-start(bf16[8,2,128,256]{3,2,1,0:T(8,128)(2,1)S(1)} %sectors_to_send.3), channel_id=1, source_target_pairs={{0,4},{4,0},{8,12},{12,8},{1,5},{5,1},{9,13},{13,9},{2,6},{6,2},{1... | collective-permute-start | bytes 3145736 | tf_op jit(solution)/shard_map/ppermute | solution.py:472
  5.3 25.8 %copy-start.5 = (s32[8,4]{0,1:T(4,128)S(1)}, s32[8,4]{0,1:T(4,128)}, u32[]{:S(2)}) copy-start(s32[8,4]{0,1:T(4,128)} %param.9) | copy-start | bytes 388
  5.3 26.0 %copy-start.4 = (s32[8]{0:T(128)S(1)}, s32[8]{0:T(128)}, u32[]{:S(2)}) copy-start(s32[8]{0:T(128)} %param.10) | copy-start | bytes 100
  5.3 27.7 %collective-permute-start.2 = (bf16[8,2,128,256]{3,2,1,0:T(8,128)(2,1)S(1)}, bf16[8,2,128,256]{3,2,1,0:T(8,128)(2,1)}, u32[]{:S(2)}, u32[]{:S(2)}) collective-permute-start(bf16[8,2,128,256]{3,2,1,0:T(8,128)(2,1)S(1)} %sectors_to_send.4), channel_id=1, source_target_pairs={{0,2},{2,0},{1,3},{3,1},{4,6},{6,4},{5,7},{7,5},{8,10},{10,8},{9,1... | collective-permute-start | bytes 3145736 | tf_op jit(solution)/shard_map/ppermute | solution.py:473
  6.6 26.4 %collective-permute-start.1 = (f32[4,256,256]{2,1,0:T(8,128)S(1)}, f32[4,256,256]{2,1,0:T(8,128)S(1)}, u32[]{:S(2)}, u32[]{:S(2)}) collective-permute-start(f32[4,256,256]{2,1,0:T(8,128)S(1)} %copy-done), channel_id=1, source_target_pairs={{0,1},{1,0},{2,3},{3,2},{4,5},{5,4},{6,7},{7,6},{8,9},{9,8},{10,11... | collective-permute-start | bytes 3145736 | tf_op jit(solution)/shard_map/ppermute | solution.py:471
  10.1 39.8 %collective-permute-start.4 = (bf16[8,2,128,256]{3,2,1,0:T(8,128)(2,1)}, bf16[8,2,128,256]{3,2,1,0:T(8,128)(2,1)}, u32[]{:S(2)}, u32[]{:S(2)}) collective-permute-start(bf16[8,2,128,256]{3,2,1,0:T(8,128)(2,1)} %sectors_to_send.5), channel_id=1, source_target_pairs={{0,4},{4,0},{8,12},{12,8},{1,5},{5,1},{9,13},{13,9},{2,6},{6,2},{1... | collective-permute-start | bytes 3145736 | tf_op jit(solution)/shard_map/ppermute | solution.py:474
  27.1 25.5 %collective-permute-start.6 = (bf16[8,2,128,256]{3,2,1,0:T(8,128)(2,1)}, bf16[8,2,128,256]{3,2,1,0:T(8,128)(2,1)}, u32[]{:S(2)}, u32[]{:S(2)}) collective-permute-start(bf16[8,2,128,256]{3,2,1,0:T(8,128)(2,1)} %collective-permute-done.5.near_h.refs_15_.refs_17_), channel_id=1, source_target_pairs={{0,2},{2,0},{1,3},{3,1},{4,6},{6,4},{5,7},{7,5},{8,10},{10,8},{9,1... | collective-permute-start | bytes 3145736 | tf_op jit(solution)/shard_map/ppermute | solution.py:475
  28.1 4.9 %collective-permute-start = (bf16[4,256,256]{2,1,0:T(8,128)(2,1)}, bf16[4,256,256]{2,1,0:T(8,128)(2,1)}, u32[]{:S(2)}, u32[]{:S(2)}) collective-permute-start(bf16[4,256,256]{2,1,0:T(8,128)(2,1)} %psi.1), channel_id=1, source_target_pairs={{0,1},{1,0},{2,3},{3,2},{4,5},{5,4},{6,7},{7,6},{8,9},{9,8},{10,11... | collective-permute-start | bytes 1572872 | tf_op jit(solution)/shard_map/ppermute | solution.py:471
  33.0 1.0 copy-start.2
  34.0 1.2 %copy-start.1 = (f32[4,256,256]{2,1,0:T(8,128)S(1)}, f32[4,256,256]{2,1,0:T(8,128)}, u32[]{:S(2)}) copy-start(f32[4,256,256]{2,1,0:T(8,128)} %pre.1) | copy-start | bytes 3145732
  35.2 1.2 %copy-start.3 = (f32[4,256,256]{2,1,0:T(8,128)S(1)}, f32[4,256,256]{2,1,0:T(8,128)}, u32[]{:S(2)}) copy-start(f32[4,256,256]{2,1,0:T(8,128)} %copy-done.2) | copy-start | bytes 3145732
  40.7 8.9 %collective-permute-start.3 = (s32[8,4]{0,1:T(4,128)S(1)}, s32[8,4]{0,1:T(4,128)S(1)}, u32[]{:S(2)}, u32[]{:S(2)}) collective-permute-start(s32[8,4]{0,1:T(4,128)S(1)} %copy-done.5), channel_id=1, source_target_pairs={{0,4},{4,0},{8,12},{12,8},{1,5},{5,1},{9,13},{13,9},{2,6},{6,2},{1... | collective-permute-start | bytes 392 | tf_op jit(solution)/shard_map/ppermute | solution.py:526
  54.5 5.8 %collective-permute-start.7 = (bf16[2,128,256]{2,1,0:T(8,128)(2,1)S(1)}, bf16[2,128,256]{2,1,0:T(8,128)(2,1)S(1)}, u32[]{:S(2)}, u32[]{:S(2)}) collective-permute-start(bf16[2,128,256]{2,1,0:T(8,128)(2,1)S(1)} %first_sigma_far_rows.1), channel_id=1, source_target_pairs={{0,12},{4,8},{8,4},{12,0},{1,13},{5,9},{9,5},{13,1},{2,14},{6,10},... | collective-permute-start | bytes 393224 | tf_op jit(solution)/shard_map/ppermute | solution.py:558
  60.4 6.1 %collective-permute-start.10 = (bf16[2,128,256]{2,1,0:T(8,128)(2,1)S(1)}, bf16[2,128,256]{2,1,0:T(8,128)(2,1)S(1)}, u32[]{:S(2)}, u32[]{:S(2)}) collective-permute-start(bf16[2,128,256]{2,1,0:T(8,128)(2,1)S(1)} %select_convert_fusion.1.refs_0_), channel_id=1, source_target_pairs={{0,6},{2,4},{4,2},{6,0},{8,14},{10,12},{12,10},{14,8},{1,7},{3,5},... | collective-permute-start | bytes 393224 | tf_op jit(solution)/shard_map/ppermute | solution.py:560
  64.1 6.1 %collective-permute-start.9 = (bf16[2,128,256]{2,1,0:T(8,128)(2,1)S(1)}, bf16[2,128,256]{2,1,0:T(8,128)(2,1)S(1)}, u32[]{:S(2)}, u32[]{:S(2)}) collective-permute-start(bf16[2,128,256]{2,1,0:T(8,128)(2,1)S(1)} %select_convert_fusion.1.refs_0_), channel_id=1, source_target_pairs={{0,2},{2,0},{1,3},{3,1},{4,6},{6,4},{5,7},{7,5},{8,10},{10,8},{9,1... | collective-permute-start | bytes 393224 | tf_op jit(solution)/shard_map/ppermute | solution.py:560
  64.2 7.2 %collective-permute-start.8 = (bf16[2,128,256]{2,1,0:T(8,128)(2,1)S(1)}, bf16[2,128,256]{2,1,0:T(8,128)(2,1)S(1)}, u32[]{:S(2)}, u32[]{:S(2)}) collective-permute-start(bf16[2,128,256]{2,1,0:T(8,128)(2,1)S(1)} %select_convert_fusion.1.refs_0_), channel_id=1, source_target_pairs={{0,4},{4,0},{8,12},{12,8},{1,5},{5,1},{9,13},{13,9},{2,6},{6,2},{1... | collective-permute-start | bytes 393224 | tf_op jit(solution)/shard_map/ppermute | solution.py:560
  64.4 7.1 %collective-permute-start.11 = (bf16[2,128,256]{2,1,0:T(8,128)(2,1)S(1)}, bf16[2,128,256]{2,1,0:T(8,128)(2,1)S(1)}, u32[]{:S(2)}, u32[]{:S(2)}) collective-permute-start(bf16[2,128,256]{2,1,0:T(8,128)(2,1)S(1)} %select_convert_fusion.1.refs_0_), channel_id=1, source_target_pairs={{0,1},{1,0},{2,3},{3,2},{4,5},{5,4},{6,7},{7,6},{8,9},{9,8},{10,11... | collective-permute-start | bytes 393224 | tf_op jit(solution)/shard_map/ppermute | solution.py:561
  66.4 5.1 %collective-permute-start.14 = (bf16[2,128,256]{2,1,0:T(8,128)(2,1)S(1)}, bf16[2,128,256]{2,1,0:T(8,128)(2,1)S(1)}, u32[]{:S(2)}, u32[]{:S(2)}) collective-permute-start(bf16[2,128,256]{2,1,0:T(8,128)(2,1)S(1)} %collective-permute-done.10.refs_3_), channel_id=1, source_target_pairs={{0,1},{1,0},{2,3},{3,2},{4,5},{5,4},{6,7},{7,6},{8,9},{9,8},{10,11... | collective-permute-start | bytes 393224 | tf_op jit(solution)/shard_map/ppermute | solution.py:561
  70.2 2.2 %collective-permute-start.13 = (bf16[2,128,256]{2,1,0:T(8,128)(2,1)S(1)}, bf16[2,128,256]{2,1,0:T(8,128)(2,1)S(1)}, u32[]{:S(2)}, u32[]{:S(2)}) collective-permute-start(bf16[2,128,256]{2,1,0:T(8,128)(2,1)S(1)} %collective-permute-done.9.refs_2_), channel_id=1, source_target_pairs={{0,1},{1,0},{2,3},{3,2},{4,5},{5,4},{6,7},{7,6},{8,9},{9,8},{10,11... | collective-permute-start | bytes 393224 | tf_op jit(solution)/shard_map/ppermute | solution.py:561
  71.4 1.3 %collective-permute-start.12 = (bf16[2,128,256]{2,1,0:T(8,128)(2,1)S(1)}, bf16[2,128,256]{2,1,0:T(8,128)(2,1)S(1)}, u32[]{:S(2)}, u32[]{:S(2)}) collective-permute-start(bf16[2,128,256]{2,1,0:T(8,128)(2,1)S(1)} %collective-permute-done.8.refs_1_), channel_id=1, source_target_pairs={{0,1},{1,0},{2,3},{3,2},{4,5},{5,4},{6,7},{7,6},{8,9},{9,8},{10,11... | collective-permute-start | bytes 393224 | tf_op jit(solution)/shard_map/ppermute | solution.py:561
  77.6 6.8 %collective-permute-start.15 = (bf16[2,128,256]{2,1,0:T(8,128)(2,1)S(1)}, bf16[2,128,256]{2,1,0:T(8,128)(2,1)S(1)}, u32[]{:S(2)}, u32[]{:S(2)}) collective-permute-start(bf16[2,128,256]{2,1,0:T(8,128)(2,1)S(1)} %get-tuple-element.31), channel_id=1, source_target_pairs={{0,12},{4,8},{8,4},{12,0},{1,13},{5,9},{9,5},{13,1},{2,14},{6,10},... | collective-permute-start | bytes 393224 | tf_op jit(solution)/shard_map/ppermute | solution.py:558
  84.5 5.3 %collective-permute-start.18 = (bf16[2,128,256]{2,1,0:T(8,128)(2,1)S(1)}, bf16[2,128,256]{2,1,0:T(8,128)(2,1)S(1)}, u32[]{:S(2)}, u32[]{:S(2)}) collective-permute-start(bf16[2,128,256]{2,1,0:T(8,128)(2,1)S(1)} %select_convert_fusion.refs_0_), channel_id=1, source_target_pairs={{0,6},{2,4},{4,2},{6,0},{8,14},{10,12},{12,10},{14,8},{1,7},{3,5},... | collective-permute-start | bytes 393224 | tf_op jit(solution)/shard_map/ppermute | solution.py:560
  87.1 6.5 %collective-permute-start.17 = (bf16[2,128,256]{2,1,0:T(8,128)(2,1)S(1)}, bf16[2,128,256]{2,1,0:T(8,128)(2,1)S(1)}, u32[]{:S(2)}, u32[]{:S(2)}) collective-permute-start(bf16[2,128,256]{2,1,0:T(8,128)(2,1)S(1)} %select_convert_fusion.refs_0_), channel_id=1, source_target_pairs={{0,2},{2,0},{1,3},{3,1},{4,6},{6,4},{5,7},{7,5},{8,10},{10,8},{9,1... | collective-permute-start | bytes 393224 | tf_op jit(solution)/shard_map/ppermute | solution.py:560
  87.6 6.8 %collective-permute-start.16 = (bf16[2,128,256]{2,1,0:T(8,128)(2,1)S(1)}, bf16[2,128,256]{2,1,0:T(8,128)(2,1)S(1)}, u32[]{:S(2)}, u32[]{:S(2)}) collective-permute-start(bf16[2,128,256]{2,1,0:T(8,128)(2,1)S(1)} %select_convert_fusion.refs_0_), channel_id=1, source_target_pairs={{0,4},{4,0},{8,12},{12,8},{1,5},{5,1},{9,13},{13,9},{2,6},{6,2},{1... | collective-permute-start | bytes 393224 | tf_op jit(solution)/shard_map/ppermute | solution.py:560
  87.6 6.8 %collective-permute-start.19 = (bf16[2,128,256]{2,1,0:T(8,128)(2,1)S(1)}, bf16[2,128,256]{2,1,0:T(8,128)(2,1)S(1)}, u32[]{:S(2)}, u32[]{:S(2)}) collective-permute-start(bf16[2,128,256]{2,1,0:T(8,128)(2,1)S(1)} %select_convert_fusion.refs_0_), channel_id=1, source_target_pairs={{0,1},{1,0},{2,3},{3,2},{4,5},{5,4},{6,7},{7,6},{8,9},{9,8},{10,11... | collective-permute-start | bytes 393224 | tf_op jit(solution)/shard_map/ppermute | solution.py:561
  89.8 4.6 %collective-permute-start.22 = (bf16[2,128,256]{2,1,0:T(8,128)(2,1)S(1)}, bf16[2,128,256]{2,1,0:T(8,128)(2,1)S(1)}, u32[]{:S(2)}, u32[]{:S(2)}) collective-permute-start(bf16[2,128,256]{2,1,0:T(8,128)(2,1)S(1)} %collective-permute-done.18.refs_3_), channel_id=1, source_target_pairs={{0,1},{1,0},{2,3},{3,2},{4,5},{5,4},{6,7},{7,6},{8,9},{9,8},{10,11... | collective-permute-start | bytes 393224 | tf_op jit(solution)/shard_map/ppermute | solution.py:561
  93.6 1.7 %collective-permute-start.21 = (bf16[2,128,256]{2,1,0:T(8,128)(2,1)S(1)}, bf16[2,128,256]{2,1,0:T(8,128)(2,1)S(1)}, u32[]{:S(2)}, u32[]{:S(2)}) collective-permute-start(bf16[2,128,256]{2,1,0:T(8,128)(2,1)S(1)} %collective-permute-done.17.refs_2_), channel_id=1, source_target_pairs={{0,1},{1,0},{2,3},{3,2},{4,5},{5,4},{6,7},{7,6},{8,9},{9,8},{10,11... | collective-permute-start | bytes 393224 | tf_op jit(solution)/shard_map/ppermute | solution.py:561
  94.4 1.3 %collective-permute-start.20 = (bf16[2,128,256]{2,1,0:T(8,128)(2,1)S(1)}, bf16[2,128,256]{2,1,0:T(8,128)(2,1)S(1)}, u32[]{:S(2)}, u32[]{:S(2)}) collective-permute-start(bf16[2,128,256]{2,1,0:T(8,128)(2,1)S(1)} %collective-permute-done.16.refs_1_), channel_id=1, source_target_pairs={{0,1},{1,0},{2,3},{3,2},{4,5},{5,4},{6,7},{7,6},{8,9},{9,8},{10,11... | collective-permute-start | bytes 393224 | tf_op jit(solution)/shard_map/ppermute | solution.py:561
  101.3 5.5 %collective-permute-start.23 = (bf16[272,128]{1,0:T(8,128)(2,1)S(1)}, bf16[272,128]{1,0:T(8,128)(2,1)S(1)}, u32[]{:S(2)}, u32[]{:S(2)}) collective-permute-start(bf16[272,128]{1,0:T(8,128)(2,1)S(1)} %get-tuple-element.35), channel_id=1, source_target_pairs={{0,12},{4,8},{8,4},{12,0},{1,13},{5,9},{9,5},{13,1},{2,14},{6,10},... | collective-permute-start | bytes 208904 | tf_op jit(solution)/shard_map/ppermute | solution.py:617
  107.4 2.9 %collective-permute-start.24 = (bf16[144,128]{1,0:T(8,128)(2,1)S(1)}, bf16[144,128]{1,0:T(8,128)(2,1)S(1)}, u32[]{:S(2)}, u32[]{:S(2)}) collective-permute-start(bf16[144,128]{1,0:T(8,128)(2,1)S(1)} %get-tuple-element.37.own), channel_id=1, source_target_pairs={{0,2},{2,0},{1,3},{3,1},{4,6},{6,4},{5,7},{7,5},{8,10},{10,8},{9,1... | collective-permute-start | bytes 110600 | tf_op jit(solution)/shard_map/ppermute | solution.py:627
  108.0 3.7 %collective-permute-start.26 = (bf16[144,128]{1,0:T(8,128)(2,1)S(1)}, bf16[144,128]{1,0:T(8,128)(2,1)S(1)}, u32[]{:S(2)}, u32[]{:S(2)}) collective-permute-start(bf16[144,128]{1,0:T(8,128)(2,1)S(1)} %get-tuple-element.38), channel_id=1, source_target_pairs={{0,6},{2,4},{4,2},{6,0},{8,14},{10,12},{12,10},{14,8},{1,7},{3,5},... | collective-permute-start | bytes 110600 | tf_op jit(solution)/shard_map/ppermute | solution.py:627
  108.0 4.1 %collective-permute-start.25 = (bf16[144,128]{1,0:T(8,128)(2,1)S(1)}, bf16[144,128]{1,0:T(8,128)(2,1)S(1)}, u32[]{:S(2)}, u32[]{:S(2)}) collective-permute-start(bf16[144,128]{1,0:T(8,128)(2,1)S(1)} %get-tuple-element.38), channel_id=1, source_target_pairs={{0,4},{4,0},{8,12},{12,8},{1,5},{5,1},{9,13},{13,9},{2,6},{6,2},{1... | collective-permute-start | bytes 110600 | tf_op jit(solution)/shard_map/ppermute | solution.py:627
  112.2 4.3 %collective-permute-start.27 = (f32[8,128]{1,0:T(8,128)S(1)}, f32[8,128]{1,0:T(8,128)S(1)}, u32[]{:S(2)}, u32[]{:S(2)}) collective-permute-start(f32[8,128]{1,0:T(8,128)S(1)} %last_dots.1.dots), channel_id=1, source_target_pairs={{0,1},{1,0},{2,3},{3,2},{4,5},{5,4},{6,7},{7,6},{8,9},{9,8},{10,11... | collective-permute-start | bytes 12296 | tf_op jit(solution)/shard_map/ppermute | solution.py:636

commit v8 on v7

--- a/solution.py
+++ b/solution.py
@@ -123,9 +123,10 @@
     return moves
 
 
-def _near_sigma_kernel(cfg, t0, meta, acc, start, scale_ref, right_h, near_h, out, inner_far, vb, right, near, inner, sem):
-    moves = [(right_h, right), (near_h, near)]
-    moves = [pltpu.make_async_copy(a, b, sem.at[i]) for i, (a, b) in enumerate(moves)]
+def _next_inner_kernel(cfg, t0, meta, start, scale_ref, right_h, near_h, inner, near, vb, right, sem):
+    cut = right.shape[0] // 2
+    parts = [(a.at[t], b.at[t]) for a, b in ((right_h, right), (near_h, near)) for t in (pl.ds(0, cut), pl.ds(cut, cut))]
+    moves = [pltpu.make_async_copy(a, b, sem.at[i]) for i, (a, b) in enumerate(parts)]
     for c in moves:
         c.start()
     scale = scale_ref[0, 0]
@@ -136,31 +137,35 @@
 
     _over(*vb.shape, 0, make)
     moves[0].wait()
-    terms, held, half = right.shape[:3]
+    moves[1].wait()
+    terms, held = right.shape[:2]
     for k in range(held):
         for t in range(terms):
             chosen = vb[meta[cfg["pair_at"] + (t0 + t) * held + k]]
             inner[t, k] = jnp.dot(right[t, k], chosen, preferred_element_type=F32).astype(BF16)
-    moves[1].wait()
+    moves[2].wait()
+    moves[3].wait()
+
+
+def _next_sigma_kernel(cfg, meta, acc, inner, near, far_h, out, far, sem):
+    terms, held, half = far.shape[:3]
+    cut = terms // 2
+    parts = [pl.ds(0, cut), pl.ds(cut, cut)]
+    moves = [pltpu.make_async_copy(far_h.at[t], far.at[t], sem.at[i]) for i, t in enumerate(parts)]
+    for c in moves:
+        c.start()
     own, other = (pl.ds(pl.multiple_of(side * half, half), half) for side in (meta[0], 1 - meta[0]))
+    totals = []
     for k in range(held):
         total = acc[k]
         for t in range(terms):
             total = total + jnp.dot(inner[t, k, :, own], near[t, k], preferred_element_type=F32)
-            inner_far[t, k] = inner[t, k, :, other]
-        out[k] = total
-
-
-def _far_sigma_kernel(acc, inner, far_h, out, far, sem):
-    held = far.shape[1]
-    moves = [pltpu.make_async_copy(far_h.at[:, k], far.at[:, k], sem.at[k]) for k in range(held)]
+        totals.append(total)
     for c in moves:
-        c.start()
-    for k in range(held):
-        moves[k].wait()
-        total = acc[k]
-        for t in range(far.shape[0]):
-            total = total + jnp.dot(inner[t, k], far[t, k], preferred_element_type=F32)
+        c.wait()
+    for k, total in enumerate(totals):
+        for t in range(terms):
+            total = total + jnp.dot(inner[t, k, :, other], far[t, k], preferred_element_type=F32)
         out[k] = total.astype(out.dtype)
 
 
@@ -526,24 +531,24 @@
         next_pairing = next_term(lax.optimization_barrier((pairing, partial))[0])
         meta = jnp.concatenate([own_meta, group(next_pairing, mine).reshape(-1)])
         piece = (terms, held, half, states)
-        partial, inner_far = pl.pallas_call(
-            functools.partial(_near_sigma_kernel, cfg, terms),
-            out_shape=(VM((held, half, width), F32), VM((terms, held, half, half), BF16)),
-            in_specs=_specs(SM, VM, VM, VM, HB, HB),
+        inner, near = pl.pallas_call(
+            functools.partial(_next_inner_kernel, cfg, terms),
+            out_shape=(VM((terms, held, half, states), BF16), VM(piece, BF16)),
+            in_specs=_specs(SM, VM, VM, HB, HB),
             out_specs=tuple(_specs(VM, VM)),
-            scratch_shapes=[pltpu.VMEM(full, BF16), *[pltpu.VMEM(piece, BF16)] * 3, dma((2,))],
+            scratch_shapes=[pltpu.VMEM(full, BF16), pltpu.VMEM(piece, BF16), dma((4,))],
             compiler_params=params,
-            name="first_sigma_next_terms",
-        )(meta, *_vmem(partial, start, scale0), *_hbm(next_right, next_left))
+            name="next_terms_inner",
+        )(meta, *_vmem(start, scale0), *_hbm(next_right, next_left))
         partial = pl.pallas_call(
-            _far_sigma_kernel,
+            functools.partial(_next_sigma_kernel, cfg),
             out_shape=VM((held, half, width), BF16),
-            in_specs=_specs(VM, VM, HB),
+            in_specs=_specs(SM, VM, VM, VM, HB),
             out_specs=_specs(VM)[0],
-            scratch_shapes=[pltpu.VMEM(piece, BF16), dma((held,))],
+            scratch_shapes=[pltpu.VMEM(piece, BF16), dma((2,))],
             compiler_params=params,
-            name="first_sigma_far_rows",
-        )(*_vmem(partial, inner_far), *_hbm(next_far_left))
+            name="next_terms_sigma",
+        )(meta, *_vmem(partial, inner, near), *_hbm(next_far_left))
 
     live_own = lax.dynamic_slice_in_dim(sector_dims, blk_pos * sec, sec)
 

time: 117 us -> 117 us (level)
  no operation moved by 1% of the time
where the time goes in v8:
time: 117 us
  waiting for transfers between devices  43.2 us (37%)
  starting transfers between devices  42.3 us (36%)
  Pallas kernels  26.3 us (22%)
  local copies, waits for them, and re-layouts  4.04 us (3%)
    ppermute x1, waiting for transfers between devices, _on_device(): next_left = next_term(to_next)  16.8 us
    ppermute x8, starting transfers between devices, combine(): there = [other_blk(x) for x in here]  11.2 us
    pallas_call x2, Pallas kernels, _on_device(): pl.pallas_call(functools.partial(_step_kernel, dict(cfg, n_out=len(outs))...  10.4 us
    ppermute x1, waiting for transfers between devices, _on_device(): next_pairing = next_term(lax.optimization_barrier((pairing, partial))[0])  7.5 us
    ppermute x6, starting transfers between devices, combine(): here = [shard, next_term(shard), other_env(shard), corners(shard)]  7.18 us
    ppermute x2, waiting for transfers between devices, combine(): total = partial.astype(F32) + far_term(partial).astype(F32)  7.04 us
    ppermute x2, starting transfers between devices, combine(): total = partial.astype(F32) + far_term(partial).astype(F32)  5.51 us
    pallas_call x3, Pallas kernels, _cut(): pl.pallas_call(functools.partial(_cut_kernel, held), out_shape=VM(shape,...  4.67 us
  transfers between devices with their start and end apart: 28, of which 16 were waited for; matrix products, arithmetic and copies ran while one was open for 0% of the time, Pallas kernels for 10%

profile of v8, /device:TPU:1, one launch (start us, length us, event | category | flops | bytes accessed | tf_op | source)
XLA Modules:
  0.0 116.9 jit_solution(3951548770276288076)
XLA Ops:
  0.6 1.2 %sectors_to_send.3 = bf16[8,2,128,256]{3,2,1,0:T(8,128)(2,1)S(1)} custom-call(s32[1]{0:T(128)} %bitcast.4.which, bf16[8,4,128,256]{3,2,1,0:T(8,128)(2,1)} %refs_14_.1), custom_call_target="tpu_custom_call" | custom-call | tf_op jit(solution)/shard_map/sectors_to_send/pallas_call | solution.py:442
  1.9 2.2 %collective-permute-start.5 = (bf16[8,2,128,256]{3,2,1,0:T(8,128)(2,1)S(1)}, bf16[8,2,128,256]{3,2,1,0:T(8,128)(2,1)}, u32[]{:S(2)}, u32[]{:S(2)}) collective-permute-start(bf16[8,2,128,256]{3,2,1,0:T(8,128)(2,1)S(1)} %sectors_to_send.3), channel_id=1, source_target_pairs={{0,4},{4,0},{8,12},{12,8},{1,5},{5,1},{9,13},{13,9},{2,6},{6,2},{1... | collective-permute-start | bytes 3145736 | tf_op jit(solution)/shard_map/ppermute | solution.py:477
  4.1 1.2 %sectors_to_send.4 = bf16[8,2,128,256]{3,2,1,0:T(8,128)(2,1)S(1)} custom-call(s32[1]{0:T(128)} %bitcast.5.which, bf16[8,4,128,256]{3,2,1,0:T(8,128)(2,1)} %refs_14_.1), custom_call_target="tpu_custom_call" | custom-call | tf_op jit(solution)/shard_map/sectors_to_send/pallas_call | solution.py:442
  5.3 1.3 %collective-permute-start.2 = (bf16[8,2,128,256]{3,2,1,0:T(8,128)(2,1)S(1)}, bf16[8,2,128,256]{3,2,1,0:T(8,128)(2,1)}, u32[]{:S(2)}, u32[]{:S(2)}) collective-permute-start(bf16[8,2,128,256]{3,2,1,0:T(8,128)(2,1)S(1)} %sectors_to_send.4), channel_id=1, source_target_pairs={{0,2},{2,0},{1,3},{3,1},{4,6},{6,4},{5,7},{7,5},{8,10},{10,8},{9,1... | collective-permute-start | bytes 3145736 | tf_op jit(solution)/shard_map/ppermute | solution.py:478
  6.6 1.2 %collective-permute-start.1 = (f32[4,256,256]{2,1,0:T(8,128)S(1)}, f32[4,256,256]{2,1,0:T(8,128)S(1)}, u32[]{:S(2)}, u32[]{:S(2)}) collective-permute-start(f32[4,256,256]{2,1,0:T(8,128)S(1)} %copy-done), channel_id=1, source_target_pairs={{0,1},{1,0},{2,3},{3,2},{4,5},{5,4},{6,7},{7,6},{8,9},{9,8},{10,11... | collective-permute-start | bytes 3145736 | tf_op jit(solution)/shard_map/ppermute | solution.py:476
  7.8 2.2 %sectors_to_send.5 = bf16[8,2,128,256]{3,2,1,0:T(8,128)(2,1)} custom-call(s32[1]{0:T(128)} %bitcast.6.which, bf16[8,4,128,256]{3,2,1,0:T(8,128)(2,1)} %refs_13_.1), custom_call_target="tpu_custom_call" | custom-call | tf_op jit(solution)/shard_map/sectors_to_send/pallas_call | solution.py:442
  10.3 16.8 %collective-permute-done.5.near_h.refs_15_.refs_17_ = bf16[8,2,128,256]{3,2,1,0:T(8,128)(2,1)} collective-permute-done((bf16[8,2,128,256]{3,2,1,0:T(8,128)(2,1)S(1)}, bf16[8,2,128,256]{3,2,1,0:T(8,128)(2,1)}, u32[]{:S(2)}, u32[]{:S(2)}) %collective-permute-start.5) | collective-permute-done | bytes 1048608 | tf_op jit(solution)/shard_map/ppermute | solution.py:477
  27.1 1.1 collective-permute-start.6
  28.1 3.0 %collective-permute-start = (bf16[4,256,256]{2,1,0:T(8,128)(2,1)}, bf16[4,256,256]{2,1,0:T(8,128)(2,1)}, u32[]{:S(2)}, u32[]{:S(2)}) collective-permute-start(bf16[4,256,256]{2,1,0:T(8,128)(2,1)} %psi.1), channel_id=1, source_target_pairs={{0,1},{1,0},{2,3},{3,2},{4,5},{5,4},{6,7},{7,6},{8,9},{9,8},{10,11... | collective-permute-start | bytes 1572872 | tf_op jit(solution)/shard_map/ppermute | solution.py:476
  31.4 1.6 %collective-permute-done.psi_o = bf16[4,256,256]{2,1,0:T(8,128)(2,1)} collective-permute-done((bf16[4,256,256]{2,1,0:T(8,128)(2,1)}, bf16[4,256,256]{2,1,0:T(8,128)(2,1)}, u32[]{:S(2)}, u32[]{:S(2)}) %collective-permute-start) | collective-permute-done | bytes 524320 | tf_op jit(solution)/shard_map/ppermute | solution.py:476
  33.0 1.0 copy-done.2
  34.0 1.2 %copy-done.1 = f32[4,256,256]{2,1,0:T(8,128)S(1)} copy-done((f32[4,256,256]{2,1,0:T(8,128)S(1)}, f32[4,256,256]{2,1,0:T(8,128)}, u32[]{:S(2)}) %copy-start.1) | copy-done | bytes 1048600
  35.2 1.2 %copy-done.3 = f32[4,256,256]{2,1,0:T(8,128)S(1)} copy-done((f32[4,256,256]{2,1,0:T(8,128)S(1)}, f32[4,256,256]{2,1,0:T(8,128)}, u32[]{:S(2)}) %copy-start.3) | copy-done | bytes 1048600
  36.4 4.3 %start_vector.1 = (bf16[8,256,256]{2,1,0:T(8,128)(2,1)S(1)}, f32[8,256,256]{2,1,0:T(8,128)S(1)}, f32[8,128]{1,0:T(8,128)S(1)}, f32[2,128,256]{2,1,0:T(8,128)S(1)}) custom-call(s32[28]{0:T(128)S(1)} %concatenate.7.meta, bf16[4,256,256]{2,1,0:T(8,128)(2,1)} %psi.1, bf16[4,256,256]{2,1,0:T(8,128)(2,1)} %collective-permute-done.psi_o, ...), custom_call_target="tpu_custom_call" | custom-call | tf_op jit(solution)/shard_map/start_vector/pallas_call | solution.py:514
  40.7 1.4 %collective-permute-start.3 = (s32[8,4]{0,1:T(4,128)S(1)}, s32[8,4]{0,1:T(4,128)S(1)}, u32[]{:S(2)}, u32[]{:S(2)}) collective-permute-start(s32[8,4]{0,1:T(4,128)S(1)} %copy-done.5), channel_id=1, source_target_pairs={{0,4},{4,0},{8,12},{12,8},{1,5},{5,1},{9,13},{13,9},{2,6},{6,2},{1... | collective-permute-start | bytes 392 | tf_op jit(solution)/shard_map/ppermute | solution.py:531
  42.1 7.5 %collective-permute-done.3 = s32[8,4]{0,1:T(4,128)S(1)} collective-permute-done((s32[8,4]{0,1:T(4,128)S(1)}, s32[8,4]{0,1:T(4,128)S(1)}, u32[]{:S(2)}, u32[]{:S(2)}) %collective-permute-start.3) | collective-permute-done | bytes 160 | tf_op jit(solution)/shard_map/ppermute | solution.py:531
  49.8 2.2 %next_terms_inner.1 = (bf16[8,2,128,256]{3,2,1,0:T(8,128)(2,1)S(1)}, bf16[8,2,128,256]{3,2,1,0:T(8,128)(2,1)S(1)}) custom-call(s32[44]{0:T(128)S(1)} %concatenate.8.meta, bf16[8,256,256]{2,1,0:T(8,128)(2,1)S(1)} %get-tuple-element.25.start.refs_8_, f32[8,128]{1,0:T(8,128)S(1)} %get-tuple-element.26.scale_ref.refs_9_, ...), custom_call_target="tpu_custom_call" | custom-call | tf_op jit(solution)/shard_map/next_terms_inner/pallas_call | solution.py:534
  52.1 2.2 %next_terms_sigma.1 = bf16[2,128,256]{2,1,0:T(8,128)(2,1)S(1)} custom-call(s32[44]{0:T(128)S(1)} %concatenate.8.meta, f32[2,128,256]{2,1,0:T(8,128)S(1)} %get-tuple-element.23.acc, bf16[8,2,128,256]{3,2,1,0:T(8,128)(2,1)S(1)} %get-tuple-element.28.inner, bf16[8,2,128,256]{3,2,1,0:T(8,128)(2,1)S(1)} %get-tuple-element.29.near, ...), custom_call_target="tpu_custom_call" | custom-call | tf_op jit(solution)/shard_map/next_terms_sigma/pallas_call | solution.py:543
  54.3 3.2 %collective-permute-start.7 = (bf16[2,128,256]{2,1,0:T(8,128)(2,1)S(1)}, bf16[2,128,256]{2,1,0:T(8,128)(2,1)S(1)}, u32[]{:S(2)}, u32[]{:S(2)}) collective-permute-start(bf16[2,128,256]{2,1,0:T(8,128)(2,1)S(1)} %next_terms_sigma.1), channel_id=1, source_target_pairs={{0,12},{4,8},{8,4},{12,0},{1,13},{5,9},{9,5},{13,1},{2,14},{6,10},... | collective-permute-start | bytes 393224 | tf_op jit(solution)/shard_map/ppermute | solution.py:563
  57.6 2.5 %collective-permute-done.7 = bf16[2,128,256]{2,1,0:T(8,128)(2,1)S(1)} collective-permute-done((bf16[2,128,256]{2,1,0:T(8,128)(2,1)S(1)}, bf16[2,128,256]{2,1,0:T(8,128)(2,1)S(1)}, u32[]{:S(2)}, u32[]{:S(2)}) %collective-permute-start.7) | collective-permute-done | bytes 131104 | tf_op jit(solution)/shard_map/ppermute | solution.py:563
  60.2 3.7 %collective-permute-start.10 = (bf16[2,128,256]{2,1,0:T(8,128)(2,1)S(1)}, bf16[2,128,256]{2,1,0:T(8,128)(2,1)S(1)}, u32[]{:S(2)}, u32[]{:S(2)}) collective-permute-start(bf16[2,128,256]{2,1,0:T(8,128)(2,1)S(1)} %select_convert_fusion.1.refs_0_), channel_id=1, source_target_pairs={{0,6},{2,4},{4,2},{6,0},{8,14},{10,12},{12,10},{14,8},{1,7},{3,5},... | collective-permute-start | bytes 393224 | tf_op jit(solution)/shard_map/ppermute | solution.py:565
  64.3 2.0 %collective-permute-start.11 = (bf16[2,128,256]{2,1,0:T(8,128)(2,1)S(1)}, bf16[2,128,256]{2,1,0:T(8,128)(2,1)S(1)}, u32[]{:S(2)}, u32[]{:S(2)}) collective-permute-start(bf16[2,128,256]{2,1,0:T(8,128)(2,1)S(1)} %select_convert_fusion.1.refs_0_), channel_id=1, source_target_pairs={{0,1},{1,0},{2,3},{3,2},{4,5},{5,4},{6,7},{7,6},{8,9},{9,8},{10,11... | collective-permute-start | bytes 393224 | tf_op jit(solution)/shard_map/ppermute | solution.py:566
  66.3 2.9 %collective-permute-start.14 = (bf16[2,128,256]{2,1,0:T(8,128)(2,1)S(1)}, bf16[2,128,256]{2,1,0:T(8,128)(2,1)S(1)}, u32[]{:S(2)}, u32[]{:S(2)}) collective-permute-start(bf16[2,128,256]{2,1,0:T(8,128)(2,1)S(1)} %collective-permute-done.10.refs_3_), channel_id=1, source_target_pairs={{0,1},{1,0},{2,3},{3,2},{4,5},{5,4},{6,7},{7,6},{8,9},{9,8},{10,11... | collective-permute-start | bytes 393224 | tf_op jit(solution)/shard_map/ppermute | solution.py:566
  69.1 0.9 collective-permute-done.9.refs_2_
  70.0 1.2 %collective-permute-start.13 = (bf16[2,128,256]{2,1,0:T(8,128)(2,1)S(1)}, bf16[2,128,256]{2,1,0:T(8,128)(2,1)S(1)}, u32[]{:S(2)}, u32[]{:S(2)}) collective-permute-start(bf16[2,128,256]{2,1,0:T(8,128)(2,1)S(1)} %collective-permute-done.9.refs_2_), channel_id=1, source_target_pairs={{0,1},{1,0},{2,3},{3,2},{4,5},{5,4},{6,7},{7,6},{8,9},{9,8},{10,11... | collective-permute-start | bytes 393224 | tf_op jit(solution)/shard_map/ppermute | solution.py:566
  71.4 0.8 collective-permute-done.13.refs_6_
  72.6 4.8 %vector_and_sigma_1.1 = (bf16[8,256,256]{2,1,0:T(8,128)(2,1)}, f32[8,256,256]{2,1,0:T(8,128)S(1)}, f32[8,128]{1,0:T(8,128)S(1)}, bf16[2,128,256]{2,1,0:T(8,128)(2,1)S(1)}) custom-call(s32[44]{0:T(128)S(1)} %concatenate.8.meta, bf16[2,128,256]{2,1,0:T(8,128)(2,1)S(1)} %select_convert_fusion.1.refs_0_, ...), custom_call_target="tpu_custom_call" | custom-call | tf_op jit(solution)/shard_map/vector_and_sigma_1/pallas_call | solution.py:590
  77.4 2.3 %collective-permute-start.15 = (bf16[2,128,256]{2,1,0:T(8,128)(2,1)S(1)}, bf16[2,128,256]{2,1,0:T(8,128)(2,1)S(1)}, u32[]{:S(2)}, u32[]{:S(2)}) collective-permute-start(bf16[2,128,256]{2,1,0:T(8,128)(2,1)S(1)} %get-tuple-element.31), channel_id=1, source_target_pairs={{0,12},{4,8},{8,4},{12,0},{1,13},{5,9},{9,5},{13,1},{2,14},{6,10},... | collective-permute-start | bytes 393224 | tf_op jit(solution)/shard_map/ppermute | solution.py:563
  79.7 4.6 %collective-permute-done.15 = bf16[2,128,256]{2,1,0:T(8,128)(2,1)S(1)} collective-permute-done((bf16[2,128,256]{2,1,0:T(8,128)(2,1)S(1)}, bf16[2,128,256]{2,1,0:T(8,128)(2,1)S(1)}, u32[]{:S(2)}, u32[]{:S(2)}) %collective-permute-start.15) | collective-permute-done | bytes 131104 | tf_op jit(solution)/shard_map/ppermute | solution.py:563
  84.3 2.6 %collective-permute-start.18 = (bf16[2,128,256]{2,1,0:T(8,128)(2,1)S(1)}, bf16[2,128,256]{2,1,0:T(8,128)(2,1)S(1)}, u32[]{:S(2)}, u32[]{:S(2)}) collective-permute-start(bf16[2,128,256]{2,1,0:T(8,128)(2,1)S(1)} %select_convert_fusion.refs_0_), channel_id=1, source_target_pairs={{0,6},{2,4},{4,2},{6,0},{8,14},{10,12},{12,10},{14,8},{1,7},{3,5},... | collective-permute-start | bytes 393224 | tf_op jit(solution)/shard_map/ppermute | solution.py:565
  86.9 0.5 collective-permute-start.17
  87.4 1.8 %collective-permute-start.19 = (bf16[2,128,256]{2,1,0:T(8,128)(2,1)S(1)}, bf16[2,128,256]{2,1,0:T(8,128)(2,1)S(1)}, u32[]{:S(2)}, u32[]{:S(2)}) collective-permute-start(bf16[2,128,256]{2,1,0:T(8,128)(2,1)S(1)} %select_convert_fusion.refs_0_), channel_id=1, source_target_pairs={{0,1},{1,0},{2,3},{3,2},{4,5},{5,4},{6,7},{7,6},{8,9},{9,8},{10,11... | collective-permute-start | bytes 393224 | tf_op jit(solution)/shard_map/ppermute | solution.py:566
  89.2 0.4 collective-permute-done.18.refs_3_
  89.6 2.5 %collective-permute-start.22 = (bf16[2,128,256]{2,1,0:T(8,128)(2,1)S(1)}, bf16[2,128,256]{2,1,0:T(8,128)(2,1)S(1)}, u32[]{:S(2)}, u32[]{:S(2)}) collective-permute-start(bf16[2,128,256]{2,1,0:T(8,128)(2,1)S(1)} %collective-permute-done.18.refs_3_), channel_id=1, source_target_pairs={{0,1},{1,0},{2,3},{3,2},{4,5},{5,4},{6,7},{7,6},{8,9},{9,8},{10,11... | collective-permute-start | bytes 393224 | tf_op jit(solution)/shard_map/ppermute | solution.py:566
  92.1 1.4 %collective-permute-done.17.refs_2_ = bf16[2,128,256]{2,1,0:T(8,128)(2,1)S(1)} collective-permute-done((bf16[2,128,256]{2,1,0:T(8,128)(2,1)S(1)}, bf16[2,128,256]{2,1,0:T(8,128)(2,1)S(1)}, u32[]{:S(2)}, u32[]{:S(2)}) %collective-permute-start.17) | collective-permute-done | bytes 131104 | tf_op jit(solution)/shard_map/ppermute | solution.py:565
  93.4 0.7 collective-permute-start.21
  94.2 1.0 collective-permute-done.21.refs_6_
  95.5 5.5 %vector_and_sigma_2.1 = (f32[3,4,64,256]{3,2,1,0:T(8,128)}, f32[8,128]{1,0:T(8,128)S(1)}, f32[272,128]{1,0:T(8,128)S(1)}, bf16[272,128]{1,0:T(8,128)(2,1)S(1)}) custom-call(s32[44]{0:T(128)S(1)} %concatenate.8.meta, bf16[2,128,256]{2,1,0:T(8,128)(2,1)S(1)} %select_convert_fusion.refs_0_, bf16[2,128,256]{2,1,0:T(8,128)(2,1)S(1)} %collective-permute-done.16.refs_1_, ...), custom_call_target="tpu_custom_call" | custom-call | tf_op jit(solution)/shard_map/vector_and_sigma_2/pallas_call | solution.py:590
  101.1 2.4 %collective-permute-start.23 = (bf16[272,128]{1,0:T(8,128)(2,1)S(1)}, bf16[272,128]{1,0:T(8,128)(2,1)S(1)}, u32[]{:S(2)}, u32[]{:S(2)}) collective-permute-start(bf16[272,128]{1,0:T(8,128)(2,1)S(1)} %get-tuple-element.35), channel_id=1, source_target_pairs={{0,12},{4,8},{8,4},{12,0},{1,13},{5,9},{9,5},{13,1},{2,14},{6,10},... | collective-permute-start | bytes 208904 | tf_op jit(solution)/shard_map/ppermute | solution.py:622
  103.5 3.1 %collective-permute-done.23.got = bf16[272,128]{1,0:T(8,128)(2,1)S(1)} collective-permute-done((bf16[272,128]{1,0:T(8,128)(2,1)S(1)}, bf16[272,128]{1,0:T(8,128)(2,1)S(1)}, u32[]{:S(2)}, u32[]{:S(2)}) %collective-permute-start.23) | collective-permute-done | bytes 69664 | tf_op jit(solution)/shard_map/ppermute | solution.py:622
  106.6 0.6 last_sums.1
  107.2 0.6 collective-permute-start.24
  107.8 2.1 %collective-permute-start.25 = (bf16[144,128]{1,0:T(8,128)(2,1)S(1)}, bf16[144,128]{1,0:T(8,128)(2,1)S(1)}, u32[]{:S(2)}, u32[]{:S(2)}) collective-permute-start(bf16[144,128]{1,0:T(8,128)(2,1)S(1)} %get-tuple-element.38), channel_id=1, source_target_pairs={{0,4},{4,0},{8,12},{12,8},{1,5},{5,1},{9,13},{13,9},{2,6},{6,2},{1... | collective-permute-start | bytes 110600 | tf_op jit(solution)/shard_map/ppermute | solution.py:632
  110.0 1.5 %collective-permute-done.26.by_both = bf16[144,128]{1,0:T(8,128)(2,1)S(1)} collective-permute-done((bf16[144,128]{1,0:T(8,128)(2,1)S(1)}, bf16[144,128]{1,0:T(8,128)(2,1)S(1)}, u32[]{:S(2)}, u32[]{:S(2)}) %collective-permute-start.26) | collective-permute-done | bytes 36896 | tf_op jit(solution)/shard_map/ppermute | solution.py:632
  111.5 0.4 collective-permute-done.25.by_term
  112.0 3.0 %collective-permute-start.27 = (f32[8,128]{1,0:T(8,128)S(1)}, f32[8,128]{1,0:T(8,128)S(1)}, u32[]{:S(2)}, u32[]{:S(2)}) collective-permute-start(f32[8,128]{1,0:T(8,128)S(1)} %last_dots.1.dots), channel_id=1, source_target_pairs={{0,1},{1,0},{2,3},{3,2},{4,5},{5,4},{6,7},{7,6},{8,9},{9,8},{10,11... | collective-permute-start | bytes 12296 | tf_op jit(solution)/shard_map/ppermute | solution.py:641
  114.9 1.3 %last_rows.1 = f32[3,4,64,256]{3,2,1,0:T(8,128)} custom-call(s32[44]{0:T(128)S(1)} %concatenate.8.meta, f32[2,64,128]{2,1,0:T(8,128)S(1)} %get-tuple-element.36.own, bf16[144,128]{1,0:T(8,128)(2,1)S(1)} %collective-permute-done.24.by_env, bf16[144,128]{1,0:T(8,128)(2,1)S(1)} %collective-permute-done.25.by_term, ...), custom_call_target="tpu_custom_call", output_to_operand_aliasing={{}: (5, {})} | custom-call | tf_op jit(solution)/shard_map/last_rows/pallas_call | solution.py:642
  116.2 0.6 subspace.1
  (44 shorter events, 2.5 us)
Async XLA Ops:
  1.9 4.7 %copy-start = (f32[4,256,256]{2,1,0:T(8,128)S(1)}, f32[4,256,256]{2,1,0:T(8,128)}, u32[]{:S(2)}) copy-start(f32[4,256,256]{2,1,0:T(8,128)} %pre.1) | copy-start | bytes 3145732
  1.9 25.2 %collective-permute-start.5 = (bf16[8,2,128,256]{3,2,1,0:T(8,128)(2,1)S(1)}, bf16[8,2,128,256]{3,2,1,0:T(8,128)(2,1)}, u32[]{:S(2)}, u32[]{:S(2)}) collective-permute-start(bf16[8,2,128,256]{3,2,1,0:T(8,128)(2,1)S(1)} %sectors_to_send.3), channel_id=1, source_target_pairs={{0,4},{4,0},{8,12},{12,8},{1,5},{5,1},{9,13},{13,9},{2,6},{6,2},{1... | collective-permute-start | bytes 3145736 | tf_op jit(solution)/shard_map/ppermute | solution.py:477
  5.3 25.8 %copy-start.5 = (s32[8,4]{0,1:T(4,128)S(1)}, s32[8,4]{0,1:T(4,128)}, u32[]{:S(2)}) copy-start(s32[8,4]{0,1:T(4,128)} %param.9) | copy-start | bytes 388
  5.3 26.0 %copy-start.4 = (s32[8]{0:T(128)S(1)}, s32[8]{0:T(128)}, u32[]{:S(2)}) copy-start(s32[8]{0:T(128)} %param.10) | copy-start | bytes 100
  5.3 27.7 %collective-permute-start.2 = (bf16[8,2,128,256]{3,2,1,0:T(8,128)(2,1)S(1)}, bf16[8,2,128,256]{3,2,1,0:T(8,128)(2,1)}, u32[]{:S(2)}, u32[]{:S(2)}) collective-permute-start(bf16[8,2,128,256]{3,2,1,0:T(8,128)(2,1)S(1)} %sectors_to_send.4), channel_id=1, source_target_pairs={{0,2},{2,0},{1,3},{3,1},{4,6},{6,4},{5,7},{7,5},{8,10},{10,8},{9,1... | collective-permute-start | bytes 3145736 | tf_op jit(solution)/shard_map/ppermute | solution.py:478
  6.6 26.4 %collective-permute-start.1 = (f32[4,256,256]{2,1,0:T(8,128)S(1)}, f32[4,256,256]{2,1,0:T(8,128)S(1)}, u32[]{:S(2)}, u32[]{:S(2)}) collective-permute-start(f32[4,256,256]{2,1,0:T(8,128)S(1)} %copy-done), channel_id=1, source_target_pairs={{0,1},{1,0},{2,3},{3,2},{4,5},{5,4},{6,7},{7,6},{8,9},{9,8},{10,11... | collective-permute-start | bytes 3145736 | tf_op jit(solution)/shard_map/ppermute | solution.py:476
  10.1 39.8 %collective-permute-start.4 = (bf16[8,2,128,256]{3,2,1,0:T(8,128)(2,1)}, bf16[8,2,128,256]{3,2,1,0:T(8,128)(2,1)}, u32[]{:S(2)}, u32[]{:S(2)}) collective-permute-start(bf16[8,2,128,256]{3,2,1,0:T(8,128)(2,1)} %sectors_to_send.5), channel_id=1, source_target_pairs={{0,4},{4,0},{8,12},{12,8},{1,5},{5,1},{9,13},{13,9},{2,6},{6,2},{1... | collective-permute-start | bytes 3145736 | tf_op jit(solution)/shard_map/ppermute | solution.py:479
  27.1 25.0 %collective-permute-start.6 = (bf16[8,2,128,256]{3,2,1,0:T(8,128)(2,1)}, bf16[8,2,128,256]{3,2,1,0:T(8,128)(2,1)}, u32[]{:S(2)}, u32[]{:S(2)}) collective-permute-start(bf16[8,2,128,256]{3,2,1,0:T(8,128)(2,1)} %collective-permute-done.5.near_h.refs_15_.refs_17_), channel_id=1, source_target_pairs={{0,2},{2,0},{1,3},{3,1},{4,6},{6,4},{5,7},{7,5},{8,10},{10,8},{9,1... | collective-permute-start | bytes 3145736 | tf_op jit(solution)/shard_map/ppermute | solution.py:480
  28.1 4.9 %collective-permute-start = (bf16[4,256,256]{2,1,0:T(8,128)(2,1)}, bf16[4,256,256]{2,1,0:T(8,128)(2,1)}, u32[]{:S(2)}, u32[]{:S(2)}) collective-permute-start(bf16[4,256,256]{2,1,0:T(8,128)(2,1)} %psi.1), channel_id=1, source_target_pairs={{0,1},{1,0},{2,3},{3,2},{4,5},{5,4},{6,7},{7,6},{8,9},{9,8},{10,11... | collective-permute-start | bytes 1572872 | tf_op jit(solution)/shard_map/ppermute | solution.py:476
  33.0 1.0 copy-start.2
  34.0 1.2 %copy-start.1 = (f32[4,256,256]{2,1,0:T(8,128)S(1)}, f32[4,256,256]{2,1,0:T(8,128)}, u32[]{:S(2)}) copy-start(f32[4,256,256]{2,1,0:T(8,128)} %pre.1) | copy-start | bytes 3145732
  35.2 1.2 %copy-start.3 = (f32[4,256,256]{2,1,0:T(8,128)S(1)}, f32[4,256,256]{2,1,0:T(8,128)}, u32[]{:S(2)}) copy-start(f32[4,256,256]{2,1,0:T(8,128)} %copy-done.2) | copy-start | bytes 3145732
  40.7 8.9 %collective-permute-start.3 = (s32[8,4]{0,1:T(4,128)S(1)}, s32[8,4]{0,1:T(4,128)S(1)}, u32[]{:S(2)}, u32[]{:S(2)}) collective-permute-start(s32[8,4]{0,1:T(4,128)S(1)} %copy-done.5), channel_id=1, source_target_pairs={{0,4},{4,0},{8,12},{12,8},{1,5},{5,1},{9,13},{13,9},{2,6},{6,2},{1... | collective-permute-start | bytes 392 | tf_op jit(solution)/shard_map/ppermute | solution.py:531
  54.3 5.8 %collective-permute-start.7 = (bf16[2,128,256]{2,1,0:T(8,128)(2,1)S(1)}, bf16[2,128,256]{2,1,0:T(8,128)(2,1)S(1)}, u32[]{:S(2)}, u32[]{:S(2)}) collective-permute-start(bf16[2,128,256]{2,1,0:T(8,128)(2,1)S(1)} %next_terms_sigma.1), channel_id=1, source_target_pairs={{0,12},{4,8},{8,4},{12,0},{1,13},{5,9},{9,5},{13,1},{2,14},{6,10},... | collective-permute-start | bytes 393224 | tf_op jit(solution)/shard_map/ppermute | solution.py:563
  60.2 6.1 %collective-permute-start.10 = (bf16[2,128,256]{2,1,0:T(8,128)(2,1)S(1)}, bf16[2,128,256]{2,1,0:T(8,128)(2,1)S(1)}, u32[]{:S(2)}, u32[]{:S(2)}) collective-permute-start(bf16[2,128,256]{2,1,0:T(8,128)(2,1)S(1)} %select_convert_fusion.1.refs_0_), channel_id=1, source_target_pairs={{0,6},{2,4},{4,2},{6,0},{8,14},{10,12},{12,10},{14,8},{1,7},{3,5},... | collective-permute-start | bytes 393224 | tf_op jit(solution)/shard_map/ppermute | solution.py:565
  63.9 6.1 %collective-permute-start.9 = (bf16[2,128,256]{2,1,0:T(8,128)(2,1)S(1)}, bf16[2,128,256]{2,1,0:T(8,128)(2,1)S(1)}, u32[]{:S(2)}, u32[]{:S(2)}) collective-permute-start(bf16[2,128,256]{2,1,0:T(8,128)(2,1)S(1)} %select_convert_fusion.1.refs_0_), channel_id=1, source_target_pairs={{0,2},{2,0},{1,3},{3,1},{4,6},{6,4},{5,7},{7,5},{8,10},{10,8},{9,1... | collective-permute-start | bytes 393224 | tf_op jit(solution)/shard_map/ppermute | solution.py:565
  64.1 7.2 %collective-permute-start.8 = (bf16[2,128,256]{2,1,0:T(8,128)(2,1)S(1)}, bf16[2,128,256]{2,1,0:T(8,128)(2,1)S(1)}, u32[]{:S(2)}, u32[]{:S(2)}) collective-permute-start(bf16[2,128,256]{2,1,0:T(8,128)(2,1)S(1)} %select_convert_fusion.1.refs_0_), channel_id=1, source_target_pairs={{0,4},{4,0},{8,12},{12,8},{1,5},{5,1},{9,13},{13,9},{2,6},{6,2},{1... | collective-permute-start | bytes 393224 | tf_op jit(solution)/shard_map/ppermute | solution.py:565
  64.3 7.1 %collective-permute-start.11 = (bf16[2,128,256]{2,1,0:T(8,128)(2,1)S(1)}, bf16[2,128,256]{2,1,0:T(8,128)(2,1)S(1)}, u32[]{:S(2)}, u32[]{:S(2)}) collective-permute-start(bf16[2,128,256]{2,1,0:T(8,128)(2,1)S(1)} %select_convert_fusion.1.refs_0_), channel_id=1, source_target_pairs={{0,1},{1,0},{2,3},{3,2},{4,5},{5,4},{6,7},{7,6},{8,9},{9,8},{10,11... | collective-permute-start | bytes 393224 | tf_op jit(solution)/shard_map/ppermute | solution.py:566
  66.3 5.1 %collective-permute-start.14 = (bf16[2,128,256]{2,1,0:T(8,128)(2,1)S(1)}, bf16[2,128,256]{2,1,0:T(8,128)(2,1)S(1)}, u32[]{:S(2)}, u32[]{:S(2)}) collective-permute-start(bf16[2,128,256]{2,1,0:T(8,128)(2,1)S(1)} %collective-permute-done.10.refs_3_), channel_id=1, source_target_pairs={{0,1},{1,0},{2,3},{3,2},{4,5},{5,4},{6,7},{7,6},{8,9},{9,8},{10,11... | collective-permute-start | bytes 393224 | tf_op jit(solution)/shard_map/ppermute | solution.py:566
  70.0 2.2 %collective-permute-start.13 = (bf16[2,128,256]{2,1,0:T(8,128)(2,1)S(1)}, bf16[2,128,256]{2,1,0:T(8,128)(2,1)S(1)}, u32[]{:S(2)}, u32[]{:S(2)}) collective-permute-start(bf16[2,128,256]{2,1,0:T(8,128)(2,1)S(1)} %collective-permute-done.9.refs_2_), channel_id=1, source_target_pairs={{0,1},{1,0},{2,3},{3,2},{4,5},{5,4},{6,7},{7,6},{8,9},{9,8},{10,11... | collective-permute-start | bytes 393224 | tf_op jit(solution)/shard_map/ppermute | solution.py:566
  71.2 1.3 %collective-permute-start.12 = (bf16[2,128,256]{2,1,0:T(8,128)(2,1)S(1)}, bf16[2,128,256]{2,1,0:T(8,128)(2,1)S(1)}, u32[]{:S(2)}, u32[]{:S(2)}) collective-permute-start(bf16[2,128,256]{2,1,0:T(8,128)(2,1)S(1)} %collective-permute-done.8.refs_1_), channel_id=1, source_target_pairs={{0,1},{1,0},{2,3},{3,2},{4,5},{5,4},{6,7},{7,6},{8,9},{9,8},{10,11... | collective-permute-start | bytes 393224 | tf_op jit(solution)/shard_map/ppermute | solution.py:566
  77.4 6.8 %collective-permute-start.15 = (bf16[2,128,256]{2,1,0:T(8,128)(2,1)S(1)}, bf16[2,128,256]{2,1,0:T(8,128)(2,1)S(1)}, u32[]{:S(2)}, u32[]{:S(2)}) collective-permute-start(bf16[2,128,256]{2,1,0:T(8,128)(2,1)S(1)} %get-tuple-element.31), channel_id=1, source_target_pairs={{0,12},{4,8},{8,4},{12,0},{1,13},{5,9},{9,5},{13,1},{2,14},{6,10},... | collective-permute-start | bytes 393224 | tf_op jit(solution)/shard_map/ppermute | solution.py:563
  84.3 5.3 %collective-permute-start.18 = (bf16[2,128,256]{2,1,0:T(8,128)(2,1)S(1)}, bf16[2,128,256]{2,1,0:T(8,128)(2,1)S(1)}, u32[]{:S(2)}, u32[]{:S(2)}) collective-permute-start(bf16[2,128,256]{2,1,0:T(8,128)(2,1)S(1)} %select_convert_fusion.refs_0_), channel_id=1, source_target_pairs={{0,6},{2,4},{4,2},{6,0},{8,14},{10,12},{12,10},{14,8},{1,7},{3,5},... | collective-permute-start | bytes 393224 | tf_op jit(solution)/shard_map/ppermute | solution.py:565
  86.9 6.5 %collective-permute-start.17 = (bf16[2,128,256]{2,1,0:T(8,128)(2,1)S(1)}, bf16[2,128,256]{2,1,0:T(8,128)(2,1)S(1)}, u32[]{:S(2)}, u32[]{:S(2)}) collective-permute-start(bf16[2,128,256]{2,1,0:T(8,128)(2,1)S(1)} %select_convert_fusion.refs_0_), channel_id=1, source_target_pairs={{0,2},{2,0},{1,3},{3,1},{4,6},{6,4},{5,7},{7,5},{8,10},{10,8},{9,1... | collective-permute-start | bytes 393224 | tf_op jit(solution)/shard_map/ppermute | solution.py:565
  87.4 6.8 %collective-permute-start.16 = (bf16[2,128,256]{2,1,0:T(8,128)(2,1)S(1)}, bf16[2,128,256]{2,1,0:T(8,128)(2,1)S(1)}, u32[]{:S(2)}, u32[]{:S(2)}) collective-permute-start(bf16[2,128,256]{2,1,0:T(8,128)(2,1)S(1)} %select_convert_fusion.refs_0_), channel_id=1, source_target_pairs={{0,4},{4,0},{8,12},{12,8},{1,5},{5,1},{9,13},{13,9},{2,6},{6,2},{1... | collective-permute-start | bytes 393224 | tf_op jit(solution)/shard_map/ppermute | solution.py:565
  87.4 6.8 %collective-permute-start.19 = (bf16[2,128,256]{2,1,0:T(8,128)(2,1)S(1)}, bf16[2,128,256]{2,1,0:T(8,128)(2,1)S(1)}, u32[]{:S(2)}, u32[]{:S(2)}) collective-permute-start(bf16[2,128,256]{2,1,0:T(8,128)(2,1)S(1)} %select_convert_fusion.refs_0_), channel_id=1, source_target_pairs={{0,1},{1,0},{2,3},{3,2},{4,5},{5,4},{6,7},{7,6},{8,9},{9,8},{10,11... | collective-permute-start | bytes 393224 | tf_op jit(solution)/shard_map/ppermute | solution.py:566
  89.6 4.6 %collective-permute-start.22 = (bf16[2,128,256]{2,1,0:T(8,128)(2,1)S(1)}, bf16[2,128,256]{2,1,0:T(8,128)(2,1)S(1)}, u32[]{:S(2)}, u32[]{:S(2)}) collective-permute-start(bf16[2,128,256]{2,1,0:T(8,128)(2,1)S(1)} %collective-permute-done.18.refs_3_), channel_id=1, source_target_pairs={{0,1},{1,0},{2,3},{3,2},{4,5},{5,4},{6,7},{7,6},{8,9},{9,8},{10,11... | collective-permute-start | bytes 393224 | tf_op jit(solution)/shard_map/ppermute | solution.py:566
  93.4 1.7 %collective-permute-start.21 = (bf16[2,128,256]{2,1,0:T(8,128)(2,1)S(1)}, bf16[2,128,256]{2,1,0:T(8,128)(2,1)S(1)}, u32[]{:S(2)}, u32[]{:S(2)}) collective-permute-start(bf16[2,128,256]{2,1,0:T(8,128)(2,1)S(1)} %collective-permute-done.17.refs_2_), channel_id=1, source_target_pairs={{0,1},{1,0},{2,3},{3,2},{4,5},{5,4},{6,7},{7,6},{8,9},{9,8},{10,11... | collective-permute-start | bytes 393224 | tf_op jit(solution)/shard_map/ppermute | solution.py:566
  94.2 1.3 %collective-permute-start.20 = (bf16[2,128,256]{2,1,0:T(8,128)(2,1)S(1)}, bf16[2,128,256]{2,1,0:T(8,128)(2,1)S(1)}, u32[]{:S(2)}, u32[]{:S(2)}) collective-permute-start(bf16[2,128,256]{2,1,0:T(8,128)(2,1)S(1)} %collective-permute-done.16.refs_1_), channel_id=1, source_target_pairs={{0,1},{1,0},{2,3},{3,2},{4,5},{5,4},{6,7},{7,6},{8,9},{9,8},{10,11... | collective-permute-start | bytes 393224 | tf_op jit(solution)/shard_map/ppermute | solution.py:566
  101.1 5.5 %collective-permute-start.23 = (bf16[272,128]{1,0:T(8,128)(2,1)S(1)}, bf16[272,128]{1,0:T(8,128)(2,1)S(1)}, u32[]{:S(2)}, u32[]{:S(2)}) collective-permute-start(bf16[272,128]{1,0:T(8,128)(2,1)S(1)} %get-tuple-element.35), channel_id=1, source_target_pairs={{0,12},{4,8},{8,4},{12,0},{1,13},{5,9},{9,5},{13,1},{2,14},{6,10},... | collective-permute-start | bytes 208904 | tf_op jit(solution)/shard_map/ppermute | solution.py:622
  107.2 2.9 %collective-permute-start.24 = (bf16[144,128]{1,0:T(8,128)(2,1)S(1)}, bf16[144,128]{1,0:T(8,128)(2,1)S(1)}, u32[]{:S(2)}, u32[]{:S(2)}) collective-permute-start(bf16[144,128]{1,0:T(8,128)(2,1)S(1)} %get-tuple-element.37.own), channel_id=1, source_target_pairs={{0,2},{2,0},{1,3},{3,1},{4,6},{6,4},{5,7},{7,5},{8,10},{10,8},{9,1... | collective-permute-start | bytes 110600 | tf_op jit(solution)/shard_map/ppermute | solution.py:632
  107.8 3.7 %collective-permute-start.26 = (bf16[144,128]{1,0:T(8,128)(2,1)S(1)}, bf16[144,128]{1,0:T(8,128)(2,1)S(1)}, u32[]{:S(2)}, u32[]{:S(2)}) collective-permute-start(bf16[144,128]{1,0:T(8,128)(2,1)S(1)} %get-tuple-element.38), channel_id=1, source_target_pairs={{0,6},{2,4},{4,2},{6,0},{8,14},{10,12},{12,10},{14,8},{1,7},{3,5},... | collective-permute-start | bytes 110600 | tf_op jit(solution)/shard_map/ppermute | solution.py:632
  107.8 4.1 %collective-permute-start.25 = (bf16[144,128]{1,0:T(8,128)(2,1)S(1)}, bf16[144,128]{1,0:T(8,128)(2,1)S(1)}, u32[]{:S(2)}, u32[]{:S(2)}) collective-permute-start(bf16[144,128]{1,0:T(8,128)(2,1)S(1)} %get-tuple-element.38), channel_id=1, source_target_pairs={{0,4},{4,0},{8,12},{12,8},{1,5},{5,1},{9,13},{13,9},{2,6},{6,2},{1... | collective-permute-start | bytes 110600 | tf_op jit(solution)/shard_map/ppermute | solution.py:632
  112.0 4.3 %collective-permute-start.27 = (f32[8,128]{1,0:T(8,128)S(1)}, f32[8,128]{1,0:T(8,128)S(1)}, u32[]{:S(2)}, u32[]{:S(2)}) collective-permute-start(f32[8,128]{1,0:T(8,128)S(1)} %last_dots.1.dots), channel_id=1, source_target_pairs={{0,1},{1,0},{2,3},{3,2},{4,5},{5,4},{6,7},{7,6},{8,9},{9,8},{10,11... | collective-permute-start | bytes 12296 | tf_op jit(solution)/shard_map/ppermute | solution.py:641
